TPU v7x, 32 devices: a whole 2x2x4 slice. The times are simulated.
32 devices in a mesh: req: 16 (over z, x, core), mdl: 2 (over y).
Axes of the slice: x: 2, y: 2, z: 4, core: 2. Of those that a mesh axis runs over, the one named last changes fastest.
Arguments:
- hidden_in: bfloat16 [2048, 2048], P('req'), may hold values from -6 to 6
- z_weight: bfloat16 [2048, 4096], P('req', 'mdl'), may hold values from -0.125 to 0.125
- x_weight: bfloat16 [2048, 4096], P('req', 'mdl'), may hold values from -0.125 to 0.125
- state_proj: bfloat16 [2048, 256], P('req'), may hold values from -0.125 to 0.125
- step_weight: bfloat16 [2048, 64], P('req', 'mdl'), may hold values from -0.125 to 0.125
- step_bias: float32 [64], P('mdl'), may hold values from -4 to -1
- decay_log: float32 [64], P('mdl'), may hold values from -2 to 1
- skip_gain: float32 [64], P('mdl'), may hold values from 0.5 to 2
- conv_inner: float32 [4, 4096], P(None, 'mdl'), may hold values from -3 to 3
- conv_state: float32 [4, 256], replicated, may hold values from -3 to 3
- norm_gain: float32 [4096], P('mdl'), may hold values from 0.1 to 1.9
- out_weight: bfloat16 [4096, 2048], P('mdl', 'req'), may hold values from -0.09375 to 0.09375
- state_pool: float32 [128, 64, 64, 128], P('req', 'mdl'), may hold values from -2.4 to 2.4
- conv_pool_inner: bfloat16 [128, 3, 4096], P('req', None, 'mdl'), may hold values from -6 to 6
- conv_pool_state: bfloat16 [128, 3, 256], P('req'), may hold values from -6 to 6
- owner_dev: int32 [128], replicated, may hold values from 0 to 15, as said below
- state_page: int32 [128], replicated, may hold values from 0 to 7, as said below
- conv_page: int32 [128], replicated, may hold values from 0 to 7, as said below
- accepted: int32 [128], replicated, may hold values from 1 to 16
Outputs:
- mixed: bfloat16 [2048, 2048], P('req', 'mdl')
- new_states: float32 [128, 64, 64, 128], P('req', 'mdl')
- conv_inner_out: bfloat16 [128, 3, 4096], P('req', None, 'mdl')
- conv_state_out: bfloat16 [128, 3, 256], P('req')
Inputs may be any that keep to these rules, and one draw needn't show every extreme that they name: `owner_dev`: request r of device i = r // 8 has its owner among devices i to i + 7 along req, counted modulo the axis size; among the 8 requests of one device at most 2 name the same owner, and exactly 2 do for one owner; every owner is named by exactly 8 requests in all. `state_page`: the requests of one owner have distinct state slots. `conv_page`: the requests of one owner have distinct convolution pages.
All inputs are finite; a program needn't handle non-finite values.
Results may differ from a plain program's by a relative error of at most 0.0069.
Values may be sent and summed in bfloat16 or wider, within the bound.
No kernel may reach another device: no remote copies, remote signals or barrier semaphores. Data moves between devices by JAX's collectives and lax.ppermute only.
A program may use at most 128 MiB of HBM per device.

v0:
```python
import jax
import jax.numpy as jnp
from jax import lax
from jax.sharding import PartitionSpec as P

KCONV = 4
CAP = 2
WINDOW = 8


HIGH = lax.Precision.HIGHEST
EPSILON = 1e-05


def from_behind(value, axis, steps):
    count = lax.axis_size(axis)
    pairs = [(source, (source + steps) % count) for source in range(count)]
    return lax.ppermute(value, axis, pairs)


def one_hot_apply(table, values, shape):
    flat = values.reshape(table.shape[1], -1)
    return (
        jnp.dot(table, flat, preferred_element_type=jnp.float32).astype(jnp.bfloat16).reshape(shape)
    )


def route_tables(owner_dev, state_page, conv_page, accepted, groups, per_dev, this_dev):
    owner_grid = owner_dev.reshape(groups, per_dev)
    home_grid = jnp.arange(groups, dtype=jnp.int32)[:, None]
    offset_grid = (owner_grid - home_grid + groups) % groups
    positions = jnp.arange(per_dev, dtype=jnp.int32)
    earlier = positions[None, :] < positions[:, None]
    pair_rank = jnp.sum((owner_grid[:, :, None] == owner_grid[:, None, :]) & earlier[None], axis=2)
    slot_grid = offset_grid * CAP + pair_rank
    send_at = lax.dynamic_slice_in_dim(slot_grid, this_dev, 1, 0)[0]
    buffer_rows = jnp.arange(WINDOW * CAP, dtype=jnp.int32)
    send_table = (buffer_rows[:, None] == send_at[None, :]).astype(jnp.bfloat16)
    arrive_at = slot_grid.reshape(-1)
    slot_match = (owner_dev[None, :] == this_dev) & (state_page[None, :] == positions[:, None])
    pick_from = jnp.sum(jnp.where(slot_match, arrive_at[None, :], 0), axis=1)
    conv_of = jnp.sum(jnp.where(slot_match, conv_page[None, :], 0), axis=1)
    kept_count = jnp.sum(jnp.where(slot_match, accepted[None, :], 0), axis=1)
    gather_table = (buffer_rows[None, :] == pick_from[:, None]).astype(jnp.bfloat16)
    place_table = (positions[:, None] == conv_of[None, :]).astype(jnp.bfloat16)
    return (send_table, gather_table, place_table, conv_of, kept_count)


def project_in(rows, z_weight, x_weight, state_proj, step_weight):
    pieces = (
        lax.all_gather(z_weight, "req", axis=0, tiled=True),
        lax.all_gather(x_weight, "req", axis=0, tiled=True),
        lax.all_gather(state_proj, "req", axis=0, tiled=True),
        lax.all_gather(step_weight, "req", axis=0, tiled=True),
    )
    gate_pre, inner_raw, state_full, step_raw = tuple(
        (jnp.dot(rows, piece, preferred_element_type=jnp.float32) for piece in pieces)
    )
    state_raw = state_full.astype(jnp.bfloat16)
    packed = jnp.concatenate([inner_raw.astype(jnp.bfloat16), state_raw], axis=1)
    return (gate_pre, packed, step_raw.astype(jnp.bfloat16))


def mix_requests(
    packed, step_raw, history, kernel, step_bias, decay_log, skip_gain, state_pool, kept_count
):
    per_dev, draft, channels = packed.shape
    heads, head_dim, state_width = (state_pool.shape[1], state_pool.shape[2], state_pool.shape[3])
    inner = heads * head_dim
    series = jnp.concatenate([history, packed], axis=1)
    series_f = series.astype(jnp.float32)
    conv_sum = kernel[0] * series_f[:, 0:draft]
    for tap in range(1, KCONV):
        conv_sum = conv_sum + kernel[tap] * series_f[:, tap : tap + draft]
    active = jax.nn.silu(conv_sum)
    inputs_x = active[:, :, :inner].reshape(per_dev, draft, heads, head_dim)
    b_rows = active[:, :, inner : inner + state_width]
    c_rows = active[:, :, inner + state_width :]
    step_size = jax.nn.softplus(step_raw.astype(jnp.float32) + step_bias)
    log_decay = jnp.cumsum(step_size * -jnp.exp(decay_log), axis=1)
    step_order = jnp.arange(draft, dtype=jnp.int32)
    causal = (step_order[None, :] <= step_order[:, None])[None, :, :, None]
    spread = log_decay[:, :, None, :] - log_decay[:, None, :, :]
    decay_table = jnp.where(causal, jnp.exp(jnp.where(causal, spread, 0.0)), 0.0)
    scores = jnp.einsum("stn,sun->stu", c_rows, b_rows, precision=HIGH)
    weights = decay_table * scores[:, :, :, None] * step_size[:, None, :, :]
    within = jnp.einsum("stuh,suhp->sthp", weights, inputs_x, precision=HIGH)
    carried = (
        jnp.einsum("stn,shpn->sthp", c_rows, state_pool, precision=HIGH)
        * jnp.exp(log_decay)[:, :, :, None]
    )
    outputs = within + carried + skip_gain[:, None] * inputs_x
    at_end = (step_order[None, :] == (kept_count - 1)[:, None])[:, :, None]
    end_decay = jnp.sum(jnp.where(at_end, log_decay, 0.0), axis=1)
    before = (step_order[None, :] < kept_count[:, None])[:, :, None]
    gap = end_decay[:, None, :] - log_decay
    select_weight = jnp.where(before, jnp.exp(jnp.where(before, gap, 0.0)), 0.0) * step_size
    chosen = jnp.exp(end_decay)[:, :, None, None] * state_pool + jnp.einsum(
        "suh,suhp,sun->shpn", select_weight, inputs_x, b_rows, precision=HIGH
    )
    series_rows = jnp.arange(series.shape[1], dtype=jnp.int32)
    window = (
        series_rows[None, None, :]
        == kept_count[:, None, None] + jnp.arange(KCONV - 1, dtype=jnp.int32)[None, :, None]
    ).astype(jnp.bfloat16)
    edge_rows = jnp.einsum(
        "sir,src->sic", window, series, preferred_element_type=jnp.float32
    ).astype(jnp.bfloat16)
    return (outputs.reshape(per_dev, draft, inner).astype(jnp.bfloat16), chosen, edge_rows)


def finish(mixed_rows, gate_pre, norm_gain, out_weight):
    gated = mixed_rows.astype(jnp.float32) * jax.nn.silu(gate_pre)
    inner_total = gated.shape[1] * lax.axis_size("mdl")
    squares = lax.psum(jnp.sum(gated * gated, axis=1), "mdl")
    normed = (gated * lax.rsqrt(squares[:, None] / inner_total + EPSILON) * norm_gain).astype(
        jnp.bfloat16
    )
    terms = jnp.dot(
        normed,
        lax.all_gather(out_weight, "req", axis=1, tiled=True),
        preferred_element_type=jnp.float32,
    )
    return lax.psum_scatter(terms, "mdl", scatter_dimension=1, tiled=True).astype(jnp.bfloat16)


def on_device(
    hidden_in,
    z_weight,
    x_weight,
    state_proj,
    step_weight,
    step_bias,
    decay_log,
    skip_gain,
    conv_inner,
    conv_state,
    norm_gain,
    out_weight,
    state_pool,
    conv_pool_inner,
    conv_pool_state,
    owner_dev,
    state_page,
    conv_page,
    accepted,
):
    groups = lax.axis_size("req")
    this_dev = lax.axis_index("req")
    per_dev = state_pool.shape[0]
    draft = hidden_in.shape[0] // per_dev
    slots = WINDOW * CAP
    send_table, gather_table, place_table, conv_of, kept_count = route_tables(
        owner_dev, state_page, conv_page, accepted, groups, per_dev, this_dev
    )
    history = jnp.concatenate([conv_pool_inner[conv_of], conv_pool_state[conv_of]], axis=2)
    kernel = jnp.concatenate([conv_inner, conv_state], axis=1)
    gate_pre, packed, step_raw = project_in(hidden_in, z_weight, x_weight, state_proj, step_weight)
    channels = packed.shape[1]
    payload = jnp.concatenate([packed, step_raw], axis=1)
    total_cols = payload.shape[1]
    outgoing = one_hot_apply(send_table, payload, (slots, draft, total_cols))
    incoming = jnp.concatenate(
        [
            from_behind(outgoing[offset * CAP : (offset + 1) * CAP], "req", offset)
            for offset in range(WINDOW)
        ],
        axis=0,
    )
    owned = one_hot_apply(gather_table, incoming, (per_dev, draft, total_cols))
    mixed_rows, chosen, edge_rows = mix_requests(
        owned[:, :, :channels],
        owned[:, :, channels:],
        history,
        kernel,
        step_bias,
        decay_log,
        skip_gain,
        state_pool,
        kept_count,
    )
    inner_local = mixed_rows.shape[2]
    returning = one_hot_apply(gather_table.T, mixed_rows, (slots, draft, inner_local))
    arrived = jnp.concatenate(
        [
            from_behind(returning[offset * CAP : (offset + 1) * CAP], "req", -offset)
            for offset in range(WINDOW)
        ],
        axis=0,
    )
    home_rows = one_hot_apply(send_table.T, arrived, (per_dev * draft, inner_local))
    mixed = finish(home_rows, gate_pre, norm_gain, out_weight)
    placed = one_hot_apply(place_table, edge_rows, edge_rows.shape)
    inner_cols = conv_pool_inner.shape[2]
    return (mixed, chosen, placed[:, :, :inner_cols], placed[:, :, inner_cols:])


def solution(mesh):
    return jax.shard_map(
        on_device,
        mesh=mesh,
        in_specs=(
            P("req", None),
            P("req", "mdl"),
            P("req", "mdl"),
            P("req", None),
            P("req", "mdl"),
            P("mdl"),
            P("mdl"),
            P("mdl"),
            P(None, "mdl"),
            P(),
            P("mdl"),
            P("mdl", "req"),
            P("req", "mdl", None, None),
            P("req", None, "mdl"),
            P("req", None, None),
            P(),
            P(),
            P(),
            P(),
        ),
        out_specs=(
            P("req", "mdl"),
            P("req", "mdl", None, None),
            P("req", None, "mdl"),
            P("req", None, None),
        ),
        check_vma=False,
    )
```

profile of v0, /device:TPU:1, one launch (start us, length us, event | category | flops | bytes accessed | tf_op | source)
XLA Modules:
  0.0 360.3 jit_solution(4869039299910708247)
XLA Ops:
  13.5 23.6 %all_gather.17 = bf16[2048,32]{0,1:T(8,128)(2,1)S(1)} all-gather(bf16[128,32]{0,1:T(8,128)(2,1)} %param.23), channel_id=1, replica_groups=mesh['req'=16,'mdl'=2] {'req'}, dimensions={0}, use_global_device_ids=true | all-gather | bytes 139264 | tf_op jit(solution)/shard_map/all_gather | solution.py:54
  37.9 12.8 %all-gather.7.cloned.1.call-done = bf16[2048,256]{1,0:T(8,128)(2,1)} async-done(((bf16[128,256]{1,0:T(8,128)(2,1)}), bf16[2048,256]{1,0:T(8,128)(2,1)}) %all-gather.7.cloned.1.call-update) | async-done | bytes 1048592 | tf_op jit(solution)/shard_map/all_gather | solution.py:53
  50.7 1.5 convolution_convert_fusion.7
  52.3 74.5 %all-gather.5.cloned.1.call-done = bf16[2048,2048]{1,0:T(8,128)(2,1)} async-done(((bf16[128,2048]{1,0:T(8,128)(2,1)}), bf16[2048,2048]{1,0:T(8,128)(2,1)}) %all-gather.5.cloned.1.call-update) | async-done | bytes 8388624 | tf_op jit(solution)/shard_map/all_gather | solution.py:52
  126.7 4.6 %convolution_convert_fusion.6 = bf16[128,2048]{1,0:T(8,128)(2,1)S(1)} fusion(bf16[128,2048]{1,0:T(8,128)(2,1)S(1)} %copy-done, bf16[2048,2048]{1,0:T(8,128)(2,1)} %all-gather.5.cloned.1.call-done), kind=kOutput, calls=%fused_computation.11 | convolution fusion | flops 1074003968 | bytes 9437184 | tf_op jit(solution)/shard_map/dot_general | solution.py:57
  135.4 0.9 slice.145
  136.7 0.9 slice.147
  137.7 1.5 collective-permute-start.2
  139.8 1.0 collective-permute-start.4
  142.3 3.7 %collective-permute-start.5 = (bf16[2,16,2336]{2,1,0:T(8,128)(2,1)S(1)}, bf16[2,16,2336]{2,1,0:T(8,128)(2,1)S(1)}, u32[]{:S(2)}, u32[]{:S(2)}) collective-permute-start(bf16[2,16,2336]{2,1,0:T(8,128)(2,1)S(1)} %slice.153), channel_id=1, source_target_pairs={{0,10},{2,12},{4,14},{6,16},{8,18},{10,20},{12,22},{14,24},{16,26}... | collective-permute-start | bytes 448520 | tf_op jit(solution)/shard_map/ppermute | solution.py:18
  146.0 0.9 constant_dynamic-update-slice_fusion.9
  147.6 0.9 constant_dynamic-update-slice_fusion.8
  148.5 5.8 %collective-permute-done.2 = bf16[2,16,2336]{2,1,0:T(8,128)(2,1)} collective-permute-done((bf16[2,16,2336]{2,1,0:T(8,128)(2,1)}, bf16[2,16,2336]{2,1,0:T(8,128)(2,1)}, u32[]{:S(2)}, u32[]{:S(2)}) %collective-permute-start.2) | collective-permute-done | bytes 149536 | tf_op jit(solution)/shard_map/ppermute | solution.py:18
  154.3 0.9 constant_dynamic-update-slice_fusion.7
  155.3 1.7 collective-permute-done.3
  157.0 0.9 constant_dynamic-update-slice_fusion.6
  157.9 1.3 collective-permute-done.5
  159.2 25.3 %collective-permute-done.6 = bf16[2,16,2336]{2,1,0:T(8,128)(2,1)S(1)} collective-permute-done((bf16[2,16,2336]{2,1,0:T(8,128)(2,1)S(1)}, bf16[2,16,2336]{2,1,0:T(8,128)(2,1)S(1)}, u32[]{:S(2)}, u32[]{:S(2)}) %collective-permute-start.6) | collective-permute-done | bytes 149536 | tf_op jit(solution)/shard_map/ppermute | solution.py:18
  184.5 0.9 collective-permute-done.7
  185.5 1.4 reshape.221
  187.2 1.0 reshape.222
  189.8 1.0 copy-done.3
  190.8 1.1 slice.209
  191.9 2.0 reshape.223
  196.2 0.9 copy.92
  197.1 0.9 copy.94
  198.1 1.1 fusion.31
  199.2 4.5 %fusion.5 = f32[8,32,64,16]{2,3,1,0:T(8,128)S(1)} fusion(f32[8,16,32,64]{3,2,1,0:T(8,128)S(1)} %reshape.223, f32[8,16,32]{1,2,0:T(8,128)S(1)} %copy.92, f32[8,16,16]{2,1,0:T(8,128)S(1)} %fusion.31, f32[8,16,32]{1,2,0:T(8,128)} %copy.90, pred[16,16]{1,0:T(8,128)(4,1)S(1)} %iota_compare_fusion.2), kind=kOutput, calls=%fused_computation.16 | convolution fusion | flops 50659328 | bytes 2138368 | tf_op jit(solution)/shard_map/stuh,suhp->sthp/dot_general | solution.py:87
  203.7 22.3 %fusion.3 = bf16[8,16,32,64]{3,1,2,0:T(8,128)(2,1)S(1)} fusion(f32[8,32,64,16]{2,3,1,0:T(8,128)S(1)} %fusion.5, f32[8,16,32,64]{3,2,1,0:T(8,128)S(1)} %reshape.223, f32[8,32,64,128]{3,2,1,0:T(8,128)} %param.31, f32[32]{0:T(128)S(1)} %copy-done.11, f32[8,16,32]{1,2,0:T(8,128)S(1)} %copy.94, f32[8,16,2304]{2,1,0:T(8,128)} %copy-done.3), kind=kOutput, calls=%fused_computation.14 | convolution fusion | flops 403963904 | bytes 11092096 | tf_op jit(solution)/shard_map/stn,shpn->sthp/dot_general | solution.py:89
  226.0 1.2 copy.96
  227.3 2.0 convert_element_type.68
  230.8 2.9 collective-permute-start.10
  233.8 0.9 collective-permute-start.11
  235.0 2.7 collective-permute-start.13
  238.5 3.1 collective-permute-start.15
  241.6 3.2 collective-permute-done.11
  244.8 4.4 %collective-permute-done.12 = bf16[2,16,2048]{2,1,0:T(8,128)(2,1)S(1)} collective-permute-done((bf16[2,16,2048]{2,1,0:T(8,128)(2,1)S(1)}, bf16[2,16,2048]{2,1,0:T(8,128)(2,1)S(1)}, u32[]{:S(2)}, u32[]{:S(2)}) %collective-permute-start.12) | collective-permute-done | bytes 131104 | tf_op jit(solution)/shard_map/ppermute | solution.py:18
  249.2 3.5 collective-permute-done.13
  252.7 5.6 %collective-permute-done.14 = bf16[2,16,2048]{2,1,0:T(8,128)(2,1)S(1)} collective-permute-done((bf16[2,16,2048]{2,1,0:T(8,128)(2,1)S(1)}, bf16[2,16,2048]{2,1,0:T(8,128)(2,1)S(1)}, u32[]{:S(2)}, u32[]{:S(2)}) %collective-permute-start.14) | collective-permute-done | bytes 131104 | tf_op jit(solution)/shard_map/ppermute | solution.py:18
  258.3 11.0 %collective-permute-done.15 = bf16[2,16,2048]{2,1,0:T(8,128)(2,1)S(1)} collective-permute-done((bf16[2,16,2048]{2,1,0:T(8,128)(2,1)S(1)}, bf16[2,16,2048]{2,1,0:T(8,128)(2,1)S(1)}, u32[]{:S(2)}, u32[]{:S(2)}) %collective-permute-start.15) | collective-permute-done | bytes 131104 | tf_op jit(solution)/shard_map/ppermute | solution.py:18
  269.9 1.3 fusion
  271.2 2.4 reshape.227
  273.7 6.0 %multiply_reduce_fusion = (f32[128]{0:T(128)S(1)}, f32[128,2048]{1,0:T(8,128)}) fusion(f32[128,2048]{1,0:T(8,128)} %reshape.227, bf16[128,2048]{1,0:T(8,128)(2,1)S(1)} %copy-done, bf16[2048,2048]{1,0:T(8,128)(2,1)} %all-gather.9.cloned.1.call-done), kind=kOutput, calls=%fused_computation.36 | convolution fusion | flops 1075576704 | bytes 11010560 | tf_op jit(solution)/shard_map/dot_general | solution.py:57
  279.6 3.8 %psum.7 = f32[128]{0:T(128)S(1)} all-reduce(f32[128]{0:T(128)S(1)} %get-tuple-element.31), channel_id=1, replica_groups=mesh['req'=16,'mdl'=2] {'mdl'}, use_global_device_ids=true, to_apply=%region_5.6 | all-reduce | flops 128 | bytes 1024 | tf_op jit(solution)/shard_map/psum | solution.py:115
  283.4 41.5 %all-gather.11.cloned.1.call-done = bf16[2048,2048]{1,0:T(8,128)(2,1)} async-done(((bf16[2048,128]{1,0:T(8,128)(2,1)}), bf16[2048,2048]{1,0:T(8,128)(2,1)}) %all-gather.11.cloned.1.call-update) | async-done | bytes 8388624 | tf_op jit(solution)/shard_map/all_gather | solution.py:121
  324.9 6.7 %fusion.22 = f32[128,2048]{1,0:T(8,128)} fusion(bf16[2048,2048]{1,0:T(8,128)(2,1)} %all-gather.11.cloned.1.call-done, f32[2048]{0:T(1024)S(1)} %copy-done.12, f32[128]{0:T(128)S(1)} %add_rsqrt_fusion, f32[128,2048]{1,0:T(8,128)} %reshape.227, f32[128,2048]{1,0:T(8,128)} %get-tuple-element.32), kind=kOutput, calls=%fused_computation.46 | convolution fusion | flops 1075838976 | bytes 11543040 | tf_op jit(solution)/shard_map/dot_general | solution.py:119
  334.2 17.8 %multiply_add_fusion = f32[8,32,64,128]{3,2,1,0:T(8,128)} fusion(f32[8,32,64,128]{3,2,1,0:T(8,128)} %param.31, f32[8,32]{1,0:T(8,128)S(1)} %exp.41, f32[8,16,32,64]{3,2,1,0:T(8,128)S(1)} %broadcast_multiply_fusion, f32[8,16,2304]{2,1,0:T(8,128)} %copy-done.3), kind=kOutput, calls=%fused_computation.7 | convolution fusion | flops 406847488 | bytes 17892352 | tf_op jit(solution)/shard_map/suh,suhp,sun->shpn/dot_general | solution.py:98
  352.0 1.8 convert_element_type.74
  (134 shorter events, 24.1 us)
Async XLA Ops:
  7.2 30.0 %copy-start = (bf16[128,2048]{1,0:T(8,128)(2,1)S(1)}, bf16[128,2048]{1,0:T(8,128)(2,1)}, u32[]{:S(2)}) copy-start(bf16[128,2048]{1,0:T(8,128)(2,1)} %param.19) | copy-start | bytes 1572868
  7.2 30.4 %copy-start.13 = (f32[32]{0:T(128)S(1)}, f32[32]{0:T(128)}, u32[]{:S(2)}) copy-start(f32[32]{0:T(128)} %param.25) | copy-start | bytes 388
  7.2 30.5 %copy-start.8 = (f32[4,2048]{1,0:T(4,128)S(1)}, f32[4,2048]{1,0:T(4,128)}, u32[]{:S(2)}) copy-start(f32[4,2048]{1,0:T(4,128)} %param.27) | copy-start | bytes 98308
  7.2 30.7 %copy-start.9 = (f32[4,256]{1,0:T(4,128)S(1)}, f32[4,256]{1,0:T(4,128)}, u32[]{:S(2)}) copy-start(f32[4,256]{1,0:T(4,128)} %param.28) | copy-start | bytes 12292
  7.2 43.5 %all-gather.7.cloned.1.call-start = ((), (), s32[]{:S(2)}) async-start(), calls=%async_computation.2 | async-start | bytes 1114112 | tf_op jit(solution)/shard_map/all_gather | solution.py:53
  7.9 118.8 %all-gather.5.cloned.1.call-start = ((), (), s32[]{:S(2)}) async-start(), calls=%async_computation.1 | async-start | bytes 8912896 | tf_op jit(solution)/shard_map/all_gather | solution.py:52
  8.7 265.0 %all-gather.9.cloned.1.call-start = ((), (), s32[]{:S(2)}) async-start(), calls=%async_computation.3 | async-start | bytes 8912896 | tf_op jit(solution)/shard_map/all_gather | solution.py:51
  9.4 315.5 %all-gather.11.cloned.1.call-start = ((), (), s32[]{:S(2)}) async-start(), calls=%async_computation.4 | async-start | bytes 8912896 | tf_op jit(solution)/shard_map/all_gather | solution.py:121
  10.0 342.0 %reduce-scatter.2.cloned.1.call-start = ((), (), s32[]{:S(2)}) async-start(), calls=%async_computation.5 | async-start | bytes 1572864 | tf_op jit(solution)/shard_map/reduce_scatter | solution.py:124
  132.6 1.2 copy-start.2
  132.6 2.1 copy-start.6
  133.7 7.9 %collective-permute-start = (bf16[2,16,2336]{2,1,0:T(8,128)(2,1)S(1)}, bf16[2,16,2336]{2,1,0:T(8,128)(2,1)S(1)}, u32[]{:S(2)}, u32[]{:S(2)}) collective-permute-start(bf16[2,16,2336]{2,1,0:T(8,128)(2,1)S(1)} %slice.143), channel_id=1, source_target_pairs={{0,0},{2,2},{4,4},{6,6},{8,8},{10,10},{12,12},{14,14},{16,16},{18,... | collective-permute-start | bytes 448520 | tf_op jit(solution)/shard_map/ppermute | solution.py:18
  136.3 10.6 %collective-permute-start.1 = (bf16[2,16,2336]{2,1,0:T(8,128)(2,1)}, bf16[2,16,2336]{2,1,0:T(8,128)(2,1)}, u32[]{:S(2)}, u32[]{:S(2)}) collective-permute-start(bf16[2,16,2336]{2,1,0:T(8,128)(2,1)} %slice.145), channel_id=1, source_target_pairs={{0,2},{2,4},{4,6},{6,8},{8,10},{10,12},{12,14},{14,16},{16,18},{18... | collective-permute-start | bytes 448520 | tf_op jit(solution)/shard_map/ppermute | solution.py:18
  137.7 16.7 %collective-permute-start.2 = (bf16[2,16,2336]{2,1,0:T(8,128)(2,1)}, bf16[2,16,2336]{2,1,0:T(8,128)(2,1)}, u32[]{:S(2)}, u32[]{:S(2)}) collective-permute-start(bf16[2,16,2336]{2,1,0:T(8,128)(2,1)} %slice.147), channel_id=1, source_target_pairs={{0,4},{2,6},{4,8},{6,10},{8,12},{10,14},{12,16},{14,18},{16,20},{1... | collective-permute-start | bytes 448520 | tf_op jit(solution)/shard_map/ppermute | solution.py:18
  139.5 17.5 %collective-permute-start.3 = (bf16[2,16,2336]{2,1,0:T(8,128)(2,1)S(1)}, bf16[2,16,2336]{2,1,0:T(8,128)(2,1)}, u32[]{:S(2)}, u32[]{:S(2)}) collective-permute-start(bf16[2,16,2336]{2,1,0:T(8,128)(2,1)S(1)} %slice.149), channel_id=1, source_target_pairs={{0,6},{2,8},{4,10},{6,12},{8,14},{10,16},{12,18},{14,20},{16,22},{... | collective-permute-start | bytes 448520 | tf_op jit(solution)/shard_map/ppermute | solution.py:18
  139.8 18.1 %collective-permute-start.4 = (bf16[2,16,2336]{2,1,0:T(8,128)(2,1)S(1)}, bf16[2,16,2336]{2,1,0:T(8,128)(2,1)S(1)}, u32[]{:S(2)}, u32[]{:S(2)}) collective-permute-start(bf16[2,16,2336]{2,1,0:T(8,128)(2,1)S(1)} %slice.151), channel_id=1, source_target_pairs={{0,8},{2,10},{4,12},{6,14},{8,16},{10,18},{12,20},{14,22},{16,24},... | collective-permute-start | bytes 448520 | tf_op jit(solution)/shard_map/ppermute | solution.py:18
  141.6 0.7 copy-start.7
  142.3 16.9 %collective-permute-start.5 = (bf16[2,16,2336]{2,1,0:T(8,128)(2,1)S(1)}, bf16[2,16,2336]{2,1,0:T(8,128)(2,1)S(1)}, u32[]{:S(2)}, u32[]{:S(2)}) collective-permute-start(bf16[2,16,2336]{2,1,0:T(8,128)(2,1)S(1)} %slice.153), channel_id=1, source_target_pairs={{0,10},{2,12},{4,14},{6,16},{8,18},{10,20},{12,22},{14,24},{16,26}... | collective-permute-start | bytes 448520 | tf_op jit(solution)/shard_map/ppermute | solution.py:18
  146.9 37.6 %collective-permute-start.6 = (bf16[2,16,2336]{2,1,0:T(8,128)(2,1)S(1)}, bf16[2,16,2336]{2,1,0:T(8,128)(2,1)S(1)}, u32[]{:S(2)}, u32[]{:S(2)}) collective-permute-start(bf16[2,16,2336]{2,1,0:T(8,128)(2,1)S(1)} %slice.155), channel_id=1, source_target_pairs={{0,12},{2,14},{4,16},{6,18},{8,20},{10,22},{12,24},{14,26},{16,28}... | collective-permute-start | bytes 448520 | tf_op jit(solution)/shard_map/ppermute | solution.py:18
  154.3 31.1 %collective-permute-start.7 = (bf16[2,16,2336]{2,1,0:T(8,128)(2,1)S(1)}, bf16[2,16,2336]{2,1,0:T(8,128)(2,1)S(1)}, u32[]{:S(2)}, u32[]{:S(2)}) collective-permute-start(bf16[2,16,2336]{2,1,0:T(8,128)(2,1)S(1)} %slice.157), channel_id=1, source_target_pairs={{0,14},{2,16},{4,18},{6,20},{8,22},{10,24},{12,26},{14,28},{16,30}... | collective-permute-start | bytes 448520 | tf_op jit(solution)/shard_map/ppermute | solution.py:18
  188.3 0.8 copy-start.4
  189.8 1.0 copy-start.3
  191.9 2.0 copy-start.10
  199.2 4.5 %copy-start.11 = (f32[32]{0:T(128)S(1)}, f32[32]{0:T(128)}, u32[]{:S(2)}) copy-start(f32[32]{0:T(128)} %param.26) | copy-start | bytes 388
  230.7 4.3 %collective-permute-start.8 = (bf16[2,16,2048]{2,1,0:T(8,128)(2,1)S(1)}, bf16[2,16,2048]{2,1,0:T(8,128)(2,1)S(1)}, u32[]{:S(2)}, u32[]{:S(2)}) collective-permute-start(bf16[2,16,2048]{2,1,0:T(8,128)(2,1)S(1)} %bitcast.95), channel_id=1, source_target_pairs={{0,0},{2,2},{4,4},{6,6},{8,8},{10,10},{12,12},{14,14},{16,16},{18,... | collective-permute-start | bytes 393224 | tf_op jit(solution)/shard_map/ppermute | solution.py:18
  230.7 7.0 %collective-permute-start.9 = (bf16[2,16,2048]{2,1,0:T(8,128)(2,1)S(1)}, bf16[2,16,2048]{2,1,0:T(8,128)(2,1)S(1)}, u32[]{:S(2)}, u32[]{:S(2)}) collective-permute-start(bf16[2,16,2048]{2,1,0:T(8,128)(2,1)S(1)} %bitcast.94), channel_id=1, source_target_pairs={{0,30},{2,0},{4,2},{6,4},{8,6},{10,8},{12,10},{14,12},{16,14},{18,... | collective-permute-start | bytes 393224 | tf_op jit(solution)/shard_map/ppermute | solution.py:18
  230.8 7.6 %collective-permute-start.10 = (bf16[2,16,2048]{2,1,0:T(8,128)(2,1)S(1)}, bf16[2,16,2048]{2,1,0:T(8,128)(2,1)S(1)}, u32[]{:S(2)}, u32[]{:S(2)}) collective-permute-start(bf16[2,16,2048]{2,1,0:T(8,128)(2,1)S(1)} %bitcast.93), channel_id=1, source_target_pairs={{0,28},{2,30},{4,0},{6,2},{8,4},{10,6},{12,8},{14,10},{16,12},{18,... | collective-permute-start | bytes 393224 | tf_op jit(solution)/shard_map/ppermute | solution.py:18
  233.8 11.0 %collective-permute-start.11 = (bf16[2,16,2048]{2,1,0:T(8,128)(2,1)S(1)}, bf16[2,16,2048]{2,1,0:T(8,128)(2,1)S(1)}, u32[]{:S(2)}, u32[]{:S(2)}) collective-permute-start(bf16[2,16,2048]{2,1,0:T(8,128)(2,1)S(1)} %bitcast.92), channel_id=1, source_target_pairs={{0,26},{2,28},{4,30},{6,0},{8,2},{10,4},{12,6},{14,8},{16,10},{18,... | collective-permute-start | bytes 393224 | tf_op jit(solution)/shard_map/ppermute | solution.py:18
  234.7 14.4 %collective-permute-start.12 = (bf16[2,16,2048]{2,1,0:T(8,128)(2,1)S(1)}, bf16[2,16,2048]{2,1,0:T(8,128)(2,1)S(1)}, u32[]{:S(2)}, u32[]{:S(2)}) collective-permute-start(bf16[2,16,2048]{2,1,0:T(8,128)(2,1)S(1)} %bitcast.91), channel_id=1, source_target_pairs={{0,24},{2,26},{4,28},{6,30},{8,0},{10,2},{12,4},{14,6},{16,8},{18,... | collective-permute-start | bytes 393224 | tf_op jit(solution)/shard_map/ppermute | solution.py:18
  235.0 17.6 %collective-permute-start.13 = (bf16[2,16,2048]{2,1,0:T(8,128)(2,1)S(1)}, bf16[2,16,2048]{2,1,0:T(8,128)(2,1)S(1)}, u32[]{:S(2)}, u32[]{:S(2)}) collective-permute-start(bf16[2,16,2048]{2,1,0:T(8,128)(2,1)S(1)} %bitcast.90), channel_id=1, source_target_pairs={{0,22},{2,24},{4,26},{6,28},{8,30},{10,0},{12,2},{14,4},{16,6},{18... | collective-permute-start | bytes 393224 | tf_op jit(solution)/shard_map/ppermute | solution.py:18
  237.7 20.6 %collective-permute-start.14 = (bf16[2,16,2048]{2,1,0:T(8,128)(2,1)S(1)}, bf16[2,16,2048]{2,1,0:T(8,128)(2,1)S(1)}, u32[]{:S(2)}, u32[]{:S(2)}) collective-permute-start(bf16[2,16,2048]{2,1,0:T(8,128)(2,1)S(1)} %bitcast.89), channel_id=1, source_target_pairs={{0,20},{2,22},{4,24},{6,26},{8,28},{10,30},{12,0},{14,2},{16,4},{1... | collective-permute-start | bytes 393224 | tf_op jit(solution)/shard_map/ppermute | solution.py:18
  238.5 30.8 %collective-permute-start.15 = (bf16[2,16,2048]{2,1,0:T(8,128)(2,1)S(1)}, bf16[2,16,2048]{2,1,0:T(8,128)(2,1)S(1)}, u32[]{:S(2)}, u32[]{:S(2)}) collective-permute-start(bf16[2,16,2048]{2,1,0:T(8,128)(2,1)S(1)} %bitcast.88), channel_id=1, source_target_pairs={{0,18},{2,20},{4,22},{6,24},{8,26},{10,28},{12,30},{14,0},{16,2},{... | collective-permute-start | bytes 393224 | tf_op jit(solution)/shard_map/ppermute | solution.py:18
  273.7 51.3 %copy-start.12 = (f32[2048]{0:T(1024)S(1)}, f32[2048]{0:T(1024)}, u32[]{:S(2)}) copy-start(f32[2048]{0:T(1024)} %param.29) | copy-start | bytes 24580
  324.9 6.8 %copy-start.5 = (bf16[8,16,2304]{2,1,0:T(8,128)(2,1)S(1)}, bf16[8,16,2304]{2,1,0:T(8,128)(2,1)}, u32[]{:S(2)}) copy-start(bf16[8,16,2304]{2,1,0:T(8,128)(2,1)} %copy-done.4) | copy-start | bytes 1769476
  334.2 19.6 %copy-start.1 = (bf16[128,2048]{1,0:T(8,128)(2,1)S(1)}, bf16[128,2048]{1,0:T(8,128)(2,1)}, u32[]{:S(2)}) copy-start(bf16[128,2048]{1,0:T(8,128)(2,1)} %param.19) | copy-start | bytes 1572868
Sparse Core Ops, SparseCore 0:
  10.2 40.4 all-gather.6
  52.9 73.7 all-gather.4
  128.9 99.4 all-gather.8
  230.4 94.4 all-gather.10
  331.7 18.0 reduce-scatter.1
where the time goes:
time: 361 us; the launch traced here: 360 us
  waiting for transfers between devices  194 us (54%)
  matrix products  68.1 us (19%)
  local copies, waits for them, and re-layouts  30.9 us (9%)
  blocking collectives  27.4 us (8%)
  starting transfers between devices  18.1 us (5%)
  between operations  14.4 us (4%)
  other arithmetic  7.38 us (2%)
    all_gather x1, waiting for transfers between devices, project_in(): lax.all_gather(x_weight, 'req', axis=0, tiled=True)  74.5 us
    ppermute x16, waiting for transfers between devices, from_behind(): return lax.ppermute(value, axis, pairs)  62.7 us
    all_gather x1, waiting for transfers between devices, finish(): lax.all_gather(out_weight, 'req', axis=1, tiled=True)  41.5 us
    all_gather x1, blocking collectives, project_in(): lax.all_gather(step_weight, 'req', axis=0, tiled=True)  23.6 us
    dot_general x1, matrix products, mix_requests(): jnp.einsum('stn,shpn->sthp', c_rows, state_pool, precision=HIGH)  22.3 us
    ppermute x16, starting transfers between devices, from_behind(): return lax.ppermute(value, axis, pairs)  17.9 us
    dot_general x1, matrix products, mix_requests(): jnp.einsum('suh,suhp,sun->shpn', select_weight, inputs_x, b_rows, precisi...  17.8 us
    all_gather x1, waiting for transfers between devices, project_in(): lax.all_gather(state_proj, 'req', axis=0, tiled=True)  12.8 us
  transfers between devices with their start and end apart: 21, of which 13 were waited for; matrix products, arithmetic and copies ran while one was open for 27% of the time, Pallas kernels for 0%

commit v1 on v0

v1 whole, which is shorter than its diff:
```python
import jax
import jax.numpy as jnp
from jax import lax
from jax.experimental import pallas as pl
from jax.experimental.pallas import tpu as pltpu
from jax.sharding import Mesh, PartitionSpec as P

KCONV = 4
CAP = 2
WINDOW = 8
LANES = 128
EPSILON = 1e-05
HIGH = lax.Precision.HIGHEST
BF16 = jnp.bfloat16
F32 = jnp.float32

RING = ("slab", "side", "core")


def round_up(value, unit):
    return -(-value // unit) * unit


def factor(count):
    core = 2 if count % 2 == 0 else 1
    chips = count // core
    side = 1
    while (2 * side) ** 2 <= chips and chips % (2 * side) == 0:
        side *= 2
    return chips // side, side, core


def rotate(value, axis, steps):
    count = lax.axis_size(axis)
    if steps % count == 0:
        return value
    pairs = [(source, (source + steps) % count) for source in range(count)]
    return lax.ppermute(value, axis, pairs)


def gather_axis(value, axis, dim):
    count = lax.axis_size(axis)
    if count == 1:
        return value
    if count > 2:
        return lax.all_gather(value, axis, axis=dim, tiled=True)
    peer = rotate(value, axis, 1)
    first = lax.axis_index(axis) == 0
    return jnp.concatenate(
        [jnp.where(first, value, peer), jnp.where(first, peer, value)], axis=dim
    )


def place(pieces, slots):
    full = jnp.zeros((len(pieces),) + pieces[0].shape, pieces[0].dtype)
    for piece, slot in zip(pieces, slots):
        full = lax.dynamic_update_slice_in_dim(full, piece[None], slot, 0)
    return full


def one_hot_apply(table, values, shape):
    flat = values.reshape(table.shape[1], -1)
    return jnp.dot(table, flat, preferred_element_type=F32).astype(BF16).reshape(shape)


def route_tables(owner_dev, state_page, conv_page, accepted, groups, per_dev, this_dev):
    owner_grid = owner_dev.reshape(groups, per_dev)
    home_grid = jnp.arange(groups, dtype=jnp.int32)[:, None]
    offset_grid = (owner_grid - home_grid + groups) % groups
    positions = jnp.arange(per_dev, dtype=jnp.int32)
    earlier = positions[None, :] < positions[:, None]
    pair_rank = jnp.sum((owner_grid[:, :, None] == owner_grid[:, None, :]) & earlier[None], axis=2)
    slot_grid = offset_grid * CAP + pair_rank
    send_at = lax.dynamic_slice_in_dim(slot_grid, this_dev, 1, 0)[0]
    buffer_rows = jnp.arange(WINDOW * CAP, dtype=jnp.int32)
    send_table = (buffer_rows[:, None] == send_at[None, :]).astype(BF16)
    arrive_at = slot_grid.reshape(-1)
    slot_match = (owner_dev[None, :] == this_dev) & (state_page[None, :] == positions[:, None])
    pick_from = jnp.sum(jnp.where(slot_match, arrive_at[None, :], 0), axis=1)
    conv_of = jnp.sum(jnp.where(slot_match, conv_page[None, :], 0), axis=1)
    kept_count = jnp.sum(jnp.where(slot_match, accepted[None, :], 0), axis=1)
    gather_table = (buffer_rows[None, :] == pick_from[:, None]).astype(BF16)
    return (send_table, gather_table, conv_of, kept_count)


def series_tables(conv_of, kept_count, per_dev, draft, hist_pad):
    rows = per_dev * draft
    keep = KCONV - 1
    row = jnp.arange(rows, dtype=jnp.int32)
    step = row % draft
    page_row = jnp.repeat(conv_of, draft) * keep
    columns = jnp.arange(rows + hist_pad, dtype=jnp.int32)
    shifts = []
    for delay in range(1, KCONV):
        source = jnp.where(step >= delay, row - delay, rows + page_row + keep + step - delay)
        shifts.append((columns[None, :] == source[:, None]).astype(BF16))
    out_row = jnp.arange(hist_pad, dtype=jnp.int32)
    out_page, out_at = out_row // keep, out_row % keep
    match = conv_of[None, :] == out_page[:, None]
    slot_of = jnp.sum(jnp.where(match, jnp.arange(per_dev, dtype=jnp.int32)[None, :], 0), axis=1)
    kept_of = jnp.sum(jnp.where(match, kept_count[None, :], 0), axis=1)
    at = kept_of + out_at
    source = jnp.where(at < keep, rows + out_page * keep + at, slot_of * draft + at - keep)
    edges = (columns[None, :] == source[:, None]).astype(BF16)
    kept_row = jnp.repeat(kept_count, draft)
    before = jnp.broadcast_to((step < kept_row)[:, None], (rows, LANES)).astype(F32)
    end_row = row - step + kept_row - 1
    at_end = (row[None, :] == end_row[:, None]).astype(F32)
    causal = ((row[:, None] // draft == row[None, :] // draft) & (row[None, :] <= row[:, None])).astype(F32)
    return jnp.stack(shifts), edges, before, at_end, causal


def split_pair(value):
    high = value.astype(BF16)
    return high, (value - high.astype(F32)).astype(BF16)


def convolve(series, current, taps, shift_ref):
    total = taps[KCONV - 1 : KCONV] * current
    for delay in range(1, KCONV):
        moved = jnp.dot(shift_ref[delay - 1], series, preferred_element_type=F32)
        total = total + taps[KCONV - 1 - delay : KCONV - delay] * moved
    return total / (1.0 + jnp.exp(-total))


def mixer_kernel(
    sizes,
    order_ref,
    x_ref,
    aux_ref,
    select_ref,
    shift_ref,
    edge_ref,
    before_ref,
    at_end_ref,
    causal_ref,
    hist_ref,
    hist_state_ref,
    taps_ref,
    taps_state_ref,
    skip_ref,
    bias_ref,
    rate_ref,
    state_ref,
    y_ref,
    new_state_ref,
    conv_ref,
    conv_state_ref,
    b_scr,
    c_scr,
    scores_scr,
    log_scr,
    sel_scr,
    end_scr,
    log_t_scr,
    step_t_scr,
):
    chunks, per_dev, draft, heads, head_dim, state_width = sizes
    rows = per_dev * draft
    width = heads * head_dim
    group = pl.program_id(0)
    causal = causal_ref[...]

    @pl.when(group == 0)
    def prepare():
        aux = jnp.dot(aux_ref[0], select_ref[0], preferred_element_type=F32)
        for chunk in range(1, chunks):
            aux = aux + jnp.dot(aux_ref[chunk], select_ref[chunk], preferred_element_type=F32)
        maps = aux[:, : 2 * state_width]
        series = jnp.concatenate([maps.astype(BF16), hist_state_ref[...]], axis=0)
        active = convolve(series, maps, taps_state_ref[...], shift_ref)
        conv_state_ref[...] = jnp.dot(edge_ref[...], series, preferred_element_type=F32).astype(BF16)
        b_rows, c_rows = active[:, :state_width], active[:, state_width:]
        b_scr[...] = b_rows
        c_scr[...] = c_rows
        scores_scr[...] = lax.dot_general(
            c_rows, b_rows, (((1,), (1,)), ((), ())), precision=HIGH, preferred_element_type=F32
        ) * causal
        raw = aux[:, 2 * state_width :] + bias_ref[...]
        step_size = jnp.maximum(raw, 0.0) + jnp.log1p(jnp.exp(-jnp.abs(raw)))
        log_decay = jnp.dot(causal, step_size * rate_ref[...], precision=HIGH, preferred_element_type=F32)
        end = jnp.dot(at_end_ref[...], log_decay, precision=HIGH, preferred_element_type=F32)
        kept = before_ref[...] > 0.0
        chosen = jnp.where(kept, jnp.exp(jnp.where(kept, end - log_decay, 0.0)), 0.0) * step_size
        decay_end = jnp.exp(end)
        for chunk in range(chunks):
            part = slice(chunk * heads, (chunk + 1) * heads)
            log_scr[chunk] = log_decay[:, part]
            sel_scr[chunk] = chosen[:, part]
            end_scr[chunk] = decay_end[:, part]
        log_t_scr[...] = log_decay.T
        step_t_scr[...] = step_size.T

    x_rows = x_ref[0]
    series = jnp.concatenate([x_rows, hist_ref[0]], axis=0)
    active = convolve(series, x_rows.astype(F32), taps_ref[0], shift_ref)
    conv_ref[0] = jnp.dot(edge_ref[...], series, preferred_element_type=F32).astype(BF16)
    scores = scores_scr[...]
    log_here = log_scr[group]
    sel_here = sel_scr[group]
    end_here = end_scr[group]
    within, growth, picks = [], [], []
    for head in range(heads):
        lanes = slice(head * head_dim, (head + 1) * head_dim)
        at = group * heads + head
        log_row = log_t_scr[pl.ds(at, 1), :]
        step_row = step_t_scr[pl.ds(at, 1), :]
        spread = jnp.where(causal > 0.0, log_here[:, head : head + 1] - log_row, -1e30)
        weight = jnp.exp(spread) * (scores * step_row)
        within.append(
            jnp.dot(weight.astype(BF16), active[:, lanes].astype(BF16), preferred_element_type=F32)
        )
        growth.append(jnp.broadcast_to(jnp.exp(log_here[:, head : head + 1]), (rows, head_dim)))
        picks.append(jnp.broadcast_to(sel_here[:, head : head + 1], (rows, head_dim)))
    within = jnp.concatenate(within, axis=1)
    growth = jnp.concatenate(growth, axis=1)
    picked = active[:, :width] * jnp.concatenate(picks, axis=1)
    carried = []
    for slot in range(per_dev):
        part = slice(slot * draft, (slot + 1) * draft)
        state = state_ref[slot].reshape(width, state_width)
        carried.append(
            lax.dot_general(
                c_scr[part, :].astype(BF16),
                state.astype(BF16),
                (((1,), (1,)), ((), ())),
                preferred_element_type=F32,
            )
        )
        x_high, x_low = split_pair(picked[part])
        b_high, b_low = split_pair(b_scr[part, :])
        update = lax.dot_general(
            jnp.concatenate([x_high, x_low, x_high], axis=0),
            jnp.concatenate([b_high, b_high, b_low], axis=0),
            (((0,), (0,)), ((), ())),
            preferred_element_type=F32,
        )
        for head in range(heads):
            keep = end_here[slot * draft : slot * draft + 1, head : head + 1]
            lanes = slice(head * head_dim, (head + 1) * head_dim)
            new_state_ref[slot, head] = keep * state[lanes] + update[lanes]
    carried = jnp.concatenate(carried, axis=0)
    outputs = within + growth * carried + skip_ref[0][:, :width] * active[:, :width]
    if width < y_ref.shape[2]:
        outputs = jnp.concatenate(
            [outputs, jnp.zeros((rows, y_ref.shape[2] - width), F32)], axis=1
        )
    y_ref[0] = outputs.astype(BF16)


def mix_requests(
    packed,
    order,
    select,
    tables,
    history,
    history_state,
    taps,
    taps_state,
    skip_lanes,
    bias,
    rate,
    state_pool,
):
    chunks, rows, packed_width = packed.shape
    per_dev, all_heads, head_dim, state_width = state_pool.shape
    heads = all_heads // chunks
    draft = rows // per_dev
    lanes = history.shape[2]
    aux_lanes = packed_width - lanes
    hist_pad = history.shape[1]
    shifts, edges, before, at_end, causal = tables
    sizes = (chunks, per_dev, draft, heads, head_dim, state_width)

    def whole(array):
        zeros = (0,) * array.ndim
        return pl.BlockSpec(array.shape, lambda group, order_ref: zeros)

    def by_group(block):
        return pl.BlockSpec(
            (1,) + block, lambda group, order_ref: (group,) + (0,) * len(block)
        )

    state_spec = pl.BlockSpec(
        (per_dev, heads, head_dim, state_width), lambda group, order_ref: (0, group, 0, 0)
    )
    step_lanes = select.shape[2] - 2 * state_width
    grid_spec = pltpu.PrefetchScalarGridSpec(
        num_scalar_prefetch=1,
        grid=(chunks,),
        in_specs=[
            pl.BlockSpec((1, rows, lanes), lambda group, order_ref: (order_ref[group], 0, 0)),
            pl.BlockSpec((chunks, rows, aux_lanes), lambda group, order_ref: (0, 0, lanes // aux_lanes)),
            whole(select),
            whole(shifts),
            whole(edges),
            whole(before),
            whole(at_end),
            whole(causal),
            by_group((hist_pad, lanes)),
            whole(history_state),
            by_group((KCONV, lanes)),
            whole(taps_state),
            by_group((1, lanes)),
            whole(bias),
            whole(rate),
            state_spec,
        ],
        out_specs=[
            by_group((rows, lanes)),
            state_spec,
            by_group((hist_pad, lanes)),
            pl.BlockSpec((hist_pad, 2 * state_width), lambda group, order_ref: (0, 0)),
        ],
        scratch_shapes=[
            pltpu.VMEM((rows, state_width), F32),
            pltpu.VMEM((rows, state_width), F32),
            pltpu.VMEM((rows, rows), F32),
            pltpu.VMEM((chunks, rows, heads), F32),
            pltpu.VMEM((chunks, rows, heads), F32),
            pltpu.VMEM((chunks, rows, heads), F32),
            pltpu.VMEM((step_lanes, rows), F32),
            pltpu.VMEM((step_lanes, rows), F32),
        ],
    )
    return pl.pallas_call(
        lambda *refs: mixer_kernel(sizes, *refs),
        grid_spec=grid_spec,
        out_shape=(
            jax.ShapeDtypeStruct((chunks, rows, lanes), BF16),
            jax.ShapeDtypeStruct(state_pool.shape, F32),
            jax.ShapeDtypeStruct((chunks, hist_pad, lanes), BF16),
            jax.ShapeDtypeStruct((hist_pad, 2 * state_width), BF16),
        ),
        compiler_params=pltpu.CompilerParams(vmem_limit_bytes=32 * 1024 * 1024),
        cost_estimate=pl.CostEstimate(
            flops=2 * 4 * rows * rows * all_heads * head_dim,
            bytes_accessed=2 * 4 * state_pool.size,
            transcendentals=rows * rows * all_heads,
        ),
    )(
        order,
        packed,
        packed,
        select,
        shifts,
        edges,
        before,
        at_end,
        causal,
        history,
        history_state,
        taps,
        taps_state,
        skip_lanes,
        bias,
        rate,
        state_pool,
    )


def by_chunk(array, chunks, lanes):
    rows, width = array.shape
    parts = array.reshape(rows, chunks, width // chunks).transpose(1, 0, 2)
    return jnp.pad(parts, ((0, 0), (0, 0), (0, lanes - width // chunks)))


def spread_weight(weight, chunks):
    me = lax.axis_index("slab")
    pieces = [
        rotate(lax.dynamic_index_in_dim(weight, (me + step) % chunks, 0, keepdims=False), "slab", step)
        for step in range(chunks)
    ]
    full = place(pieces, [(me - step) % chunks for step in range(chunks)])
    full = full.reshape(-1, full.shape[2])
    full = gather_axis(full, "side", 0)
    return gather_axis(full, "core", 0)


def on_device(
    hidden_in,
    z_weight,
    x_weight,
    state_proj,
    step_weight,
    step_bias,
    decay_log,
    skip_gain,
    conv_inner,
    conv_state,
    norm_gain,
    out_weight,
    state_pool,
    conv_pool_inner,
    conv_pool_state,
    owner_dev,
    state_page,
    conv_page,
    accepted,
):
    groups = lax.axis_size(RING)
    chunks, sides, cores = (lax.axis_size(name) for name in RING)
    this_dev = lax.axis_index(RING)
    me = lax.axis_index("slab")
    splits = lax.axis_size("mdl")
    part = lax.axis_index("mdl")
    per_dev, all_heads, head_dim, state_width = state_pool.shape
    rows, depth = hidden_in.shape
    draft = rows // per_dev
    inner = all_heads * head_dim
    slots = WINDOW * CAP
    chunk_width = inner // chunks
    lanes = round_up(chunk_width, LANES)
    map_width = 2 * state_width // chunks
    heads = all_heads // chunks
    aux_lanes = round_up(map_width + heads, LANES)
    keep = KCONV - 1
    hist_rows = per_dev * keep
    hist_pad = round_up(hist_rows, 32)

    send_table, gather_table, conv_of, kept_count = route_tables(
        owner_dev, state_page, conv_page, accepted, groups, per_dev, this_dev
    )

    block = depth // groups
    columns = hidden_in.reshape(rows, chunks, sides, cores, block).transpose(0, 3, 2, 1, 4)
    columns = columns.reshape(rows, splits, depth // splits)
    share = lax.dynamic_index_in_dim(columns, part, 1, keepdims=False)
    outgoing = one_hot_apply(send_table, share, (slots, draft, depth // splits))
    incoming = jnp.concatenate(
        [
            rotate(outgoing[offset * CAP : (offset + 1) * CAP], RING, offset)
            for offset in range(WINDOW)
        ],
        axis=0,
    )
    owned = one_hot_apply(gather_table, incoming, (rows, depth // splits))
    owned_all = jnp.stack([rotate(owned, "slab", step) for step in range(chunks)])
    owned_all = gather_axis(owned_all, "mdl", 2)

    packed_weight = jnp.concatenate(
        [
            by_chunk(x_weight, chunks, lanes),
            by_chunk(state_proj, chunks, map_width),
            by_chunk(step_weight, chunks, aux_lanes - map_width),
        ],
        axis=2,
    )
    packed_full = spread_weight(packed_weight, chunks)
    gate_full = spread_weight(by_chunk(z_weight, chunks, lanes), chunks)
    out_full = lax.all_gather(out_weight, RING, axis=1, tiled=True)

    owned_flat = owned_all.reshape(chunks * rows, depth)
    packed = jnp.dot(owned_flat, packed_full, preferred_element_type=F32).astype(BF16)
    packed = packed.reshape(chunks, rows, lanes + aux_lanes)
    packed = jnp.stack([rotate(packed[step], "slab", -step) for step in range(chunks)])
    gate = jnp.dot(owned_flat, gate_full, preferred_element_type=F32).astype(BF16)
    gate = gate.reshape(chunks, rows, lanes)
    gate = jnp.stack([rotate(gate[step], "slab", -step) for step in range(chunks)])

    order = (jnp.arange(chunks, dtype=jnp.int32) - me) % chunks
    home_chunk = (jnp.arange(chunks, dtype=jnp.int32) + me) % chunks
    lane = jnp.arange(aux_lanes, dtype=jnp.int32)[None, :]
    step_lanes = round_up(all_heads, LANES)
    target = jnp.where(
        lane < map_width,
        home_chunk[:, None] * map_width + lane,
        jnp.where(
            lane < map_width + heads,
            2 * state_width + home_chunk[:, None] * heads + lane - map_width,
            -1,
        ),
    )
    select = (
        target[:, :, None] == jnp.arange(2 * state_width + step_lanes, dtype=jnp.int32)
    ).astype(BF16)
    tables = series_tables(conv_of, kept_count, per_dev, draft, hist_pad)
    pad_rows = ((0, hist_pad - hist_rows), (0, 0))
    history = by_chunk(
        jnp.pad(conv_pool_inner.reshape(hist_rows, inner), pad_rows), chunks, lanes
    )
    history_state = jnp.pad(conv_pool_state.reshape(hist_rows, 2 * state_width), pad_rows)
    pad_heads = (0, step_lanes - all_heads)
    y_rows, new_states, conv_rows, conv_state_rows = mix_requests(
        packed,
        order,
        select,
        tables,
        history,
        history_state,
        by_chunk(conv_inner, chunks, lanes),
        conv_state,
        by_chunk(jnp.repeat(skip_gain, head_dim)[None], chunks, lanes),
        jnp.pad(step_bias, pad_heads)[None],
        jnp.pad(-jnp.exp(decay_log), pad_heads)[None],
        state_pool,
    )

    gate_here = jnp.roll(gate, me, axis=0).astype(F32)[:, :, :chunk_width]
    gated = y_rows[:, :, :chunk_width].astype(F32) * (gate_here / (1.0 + jnp.exp(-gate_here)))
    squares = jnp.sum(gated * gated, axis=(0, 2))
    scaled = (gated * norm_gain.reshape(chunks, 1, chunk_width)).astype(BF16)
    scaled = scaled.transpose(1, 0, 2).reshape(rows, inner)
    terms = jnp.dot(scaled, out_full, preferred_element_type=F32)
    wide = depth // splits
    if splits == 2:
        squares = squares + rotate(squares, "mdl", 1)
        mine = lax.dynamic_slice_in_dim(terms, part * wide, wide, 1)
        other = lax.dynamic_slice_in_dim(terms, (1 - part) * wide, wide, 1)
        total = mine + rotate(other.astype(BF16), "mdl", 1).astype(F32)
    else:
        squares = lax.psum(squares, "mdl")
        total = lax.psum_scatter(terms, "mdl", scatter_dimension=1, tiled=True)
    scale = lax.rsqrt(squares / (inner * splits) + EPSILON)
    mixed_rows = (total * scale[:, None]).astype(BF16)

    returning = one_hot_apply(
        gather_table.T, mixed_rows.reshape(per_dev, draft, wide), (slots, draft, wide)
    )
    arrived = jnp.concatenate(
        [
            rotate(returning[offset * CAP : (offset + 1) * CAP], RING, -offset)
            for offset in range(WINDOW)
        ],
        axis=0,
    )
    mixed = one_hot_apply(send_table.T, arrived, (rows, wide))
    conv_rows = conv_rows[:, :hist_rows, :chunk_width].transpose(1, 0, 2)
    return (
        mixed,
        new_states,
        conv_rows.reshape(per_dev, keep, inner),
        conv_state_rows[:hist_rows].reshape(per_dev, keep, 2 * state_width),
    )


def solution(mesh):
    slab, side, core = factor(mesh.shape["req"])
    split_mesh = Mesh(
        mesh.devices.reshape(slab, side, core, mesh.shape["mdl"]), RING + ("mdl",)
    )
    return jax.shard_map(
        on_device,
        mesh=split_mesh,
        in_specs=(
            P(RING, None),
            P(RING, "mdl"),
            P(RING, "mdl"),
            P(RING, None),
            P(RING, "mdl"),
            P("mdl"),
            P("mdl"),
            P("mdl"),
            P(None, "mdl"),
            P(),
            P("mdl"),
            P("mdl", RING),
            P(RING, "mdl", None, None),
            P(RING, None, "mdl"),
            P(RING, None, None),
            P(),
            P(),
            P(),
            P(),
        ),
        out_specs=(
            P(RING, "mdl"),
            P(RING, "mdl", None, None),
            P(RING, None, "mdl"),
            P(RING, None, None),
        ),
        check_vma=False,
    )
```

time: 361 us -> 240 us (0.66)
  waiting for transfers between devices: 194 us -> 99.5 us
  matrix products: 68.1 us -> 8.96 us
  starting transfers between devices: 18.1 us -> 69.3 us
  blocking collectives: 27.4 us -> 0 us
  Pallas kernels: 0 us -> 10.8 us
  local copies, waits for them, and re-layouts: 30.9 us -> 25.2 us
    all_gather x4 -> x1, waiting for transfers between devices: 129 us -> 0.02 us  [on_device(): out_full = lax.all_gather(out_weight, RING, axis=1, tiled=True)]
    dot_general x15 -> x7, matrix products: 68.1 us -> 8.96 us  [the longest x1 4.66 us: on_device(): terms = jnp.dot(scaled, out_full, preferred_element_type=F32)]
    ppermute x16 -> x36, starting transfers between devices: 17.9 us -> 69.3 us  [rotate(): return lax.ppermute(value, axis, pairs)]
    ppermute x16 -> x36, waiting for transfers between devices: 62.7 us -> 98.8 us  [rotate(): return lax.ppermute(value, axis, pairs)]
    all_gather x1 -> x0, blocking collectives: 23.6 us -> none  [project_in(): lax.all_gather(step_weight, 'req', axis=0, tiled=True)]
    pallas_call x0 -> x1, Pallas kernels: none -> 10.8 us  [mix_requests(): pl.pallas_call(lambda *refs: mixer_kernel(sizes, *refs), grid_spec=grid_s...]
    convert_element_type x4 -> x1, local copies, waits for them, and re-layouts: 5.82 us -> 0.04 us  [on_device(): total = mine + rotate(other.astype(BF16), 'mdl', 1).astype(F32)]
    select_n x1 -> x11, other arithmetic: 0.01 us -> 5.02 us  [the longest x5 4.9 us: gather_axis(): jnp.where(first, value, peer)]
  transfers between devices with their start and end apart: 21 -> 37, of which waited for: 13 -> 15; matrix products, arithmetic and copies ran while one was open for 27% -> 15% of each run, Pallas kernels for 0% -> 5%
where the time goes in v1:
time: 240 us; the launch traced here: 238 us
  waiting for transfers between devices  99.5 us (41%)
  starting transfers between devices  69.3 us (29%)
  local copies, waits for them, and re-layouts  25.2 us (10%)
  between operations  15.2 us (6%)
  Pallas kernels  10.8 us (4%)
  other arithmetic  9.31 us (4%)
  matrix products  8.96 us (4%)
    ppermute x36, waiting for transfers between devices, rotate(): return lax.ppermute(value, axis, pairs)  98.8 us
    ppermute x36, starting transfers between devices, rotate(): return lax.ppermute(value, axis, pairs)  69.3 us
    pallas_call x1, Pallas kernels, mix_requests(): pl.pallas_call(lambda *refs: mixer_kernel(sizes, *refs), grid_spec=grid_s...  10.8 us
    unnamed x91, local copies, waits for them, and re-layouts  10 us
    select_n x5, other arithmetic, gather_axis(): jnp.where(first, value, peer)  4.9 us
  transfers between devices with their start and end apart: 37, of which 15 were waited for; matrix products, arithmetic and copies ran while one was open for 15% of the time, Pallas kernels for 5%

profile of v1, /device:TPU:1, one launch (start us, length us, event | category | flops | bytes accessed | tf_op | source)
XLA Modules:
  0.0 238.3 jit_solution(16927359669547894510)
XLA Ops:
  8.9 1.3 copy.93
  11.5 2.7 %collective-permute-start = (bf16[2,16,1024]{2,1,0:T(8,128)(2,1)S(1)}, bf16[2,16,1024]{2,1,0:T(8,128)(2,1)}, u32[]{:S(2)}, u32[]{:S(2)}) collective-permute-start(bf16[2,16,1024]{2,1,0:T(8,128)(2,1)S(1)} %bitcast.233), channel_id=1, source_target_pairs={{0,2},{2,4},{4,6},{6,8},{8,10},{10,12},{12,14},{14,16},{16,18},{18... | collective-permute-start | bytes 196616 | tf_op jit(solution)/shard_map/ppermute | solution.py:38
  14.1 1.3 collective-permute-start.1
  17.1 1.3 collective-permute-start.3
  19.0 2.5 %collective-permute-start.4 = (bf16[2,16,1024]{2,1,0:T(8,128)(2,1)}, bf16[2,16,1024]{2,1,0:T(8,128)(2,1)S(1)}, u32[]{:S(2)}, u32[]{:S(2)}) collective-permute-start(bf16[2,16,1024]{2,1,0:T(8,128)(2,1)} %bitcast.172), channel_id=1, source_target_pairs={{0,10},{2,12},{4,14},{6,16},{8,18},{10,20},{12,22},{14,24},{16,26}... | collective-permute-start | bytes 196616 | tf_op jit(solution)/shard_map/ppermute | solution.py:38
  28.0 2.2 collective-permute-start.5
  32.7 1.2 collective-permute-start.11
  36.4 1.6 collective-permute-start.13
  38.0 5.4 %collective-permute-done.5 = bf16[2,16,1024]{2,1,0:T(8,128)(2,1)S(1)} collective-permute-done((bf16[2,16,1024]{2,1,0:T(8,128)(2,1)S(1)}, bf16[2,16,1024]{2,1,0:T(8,128)(2,1)S(1)}, u32[]{:S(2)}, u32[]{:S(2)}) %collective-permute-start.5) | collective-permute-done | bytes 65568 | tf_op jit(solution)/shard_map/ppermute | solution.py:38
  43.5 9.4 %collective-permute-done.6 = bf16[2,16,1024]{2,1,0:T(8,128)(2,1)S(1)} collective-permute-done((bf16[2,16,1024]{2,1,0:T(8,128)(2,1)S(1)}, bf16[2,16,1024]{2,1,0:T(8,128)(2,1)S(1)}, u32[]{:S(2)}, u32[]{:S(2)}) %collective-permute-start.6) | collective-permute-done | bytes 65568 | tf_op jit(solution)/shard_map/ppermute | solution.py:38
  54.5 5.7 %collective-permute-done.19 = bf16[128,512]{1,0:T(8,128)(2,1)} collective-permute-done((bf16[128,512]{1,0:T(8,128)(2,1)}, bf16[128,512]{1,0:T(8,128)(2,1)}, u32[]{:S(2)}, u32[]{:S(2)}) %collective-permute-start.19) | collective-permute-done | bytes 131104 | tf_op jit(solution)/shard_map/ppermute | solution.py:38
  60.1 0.9 bitcast_dynamic-update-slice_fusion.11
  61.1 9.0 %collective-permute-done.20 = bf16[128,512]{1,0:T(8,128)(2,1)} collective-permute-done((bf16[128,512]{1,0:T(8,128)(2,1)}, bf16[128,512]{1,0:T(8,128)(2,1)}, u32[]{:S(2)}, u32[]{:S(2)}) %collective-permute-start.20) | collective-permute-done | bytes 131104 | tf_op jit(solution)/shard_map/ppermute | solution.py:38
  70.1 7.3 %collective-permute-start.7 = (bf16[128,1024]{1,0:T(8,128)(2,1)S(1)}, bf16[128,1024]{1,0:T(8,128)(2,1)S(1)}, u32[]{:S(2)}, u32[]{:S(2)}) collective-permute-start(bf16[128,1024]{1,0:T(8,128)(2,1)S(1)} %reshape.560), channel_id=1, source_target_pairs={{0,8},{8,16},{16,24},{24,0},{1,9},{9,17},{17,25},{25,1},{2,10},{10... | collective-permute-start | bytes 786440 | tf_op jit(solution)/shard_map/ppermute | solution.py:38
  77.4 0.9 bitcast_dynamic-update-slice_fusion.10
  78.3 4.7 %collective-permute-start.8 = (bf16[128,1024]{1,0:T(8,128)(2,1)S(1)}, bf16[128,1024]{1,0:T(8,128)(2,1)S(1)}, u32[]{:S(2)}, u32[]{:S(2)}) collective-permute-start(bf16[128,1024]{1,0:T(8,128)(2,1)S(1)} %reshape.560), channel_id=1, source_target_pairs={{0,16},{8,24},{16,0},{24,8},{1,17},{9,25},{17,1},{25,9},{2,18},{10... | collective-permute-start | bytes 786440 | tf_op jit(solution)/shard_map/ppermute | solution.py:38
  83.1 4.5 %collective-permute-start.9 = (bf16[128,1024]{1,0:T(8,128)(2,1)S(1)}, bf16[128,1024]{1,0:T(8,128)(2,1)S(1)}, u32[]{:S(2)}, u32[]{:S(2)}) collective-permute-start(bf16[128,1024]{1,0:T(8,128)(2,1)S(1)} %reshape.560), channel_id=1, source_target_pairs={{0,24},{8,0},{16,8},{24,16},{1,25},{9,1},{17,9},{25,17},{2,26},{10... | collective-permute-start | bytes 786440 | tf_op jit(solution)/shard_map/ppermute | solution.py:38
  87.5 0.9 bitcast_dynamic-update-slice_fusion.2
  88.5 0.9 bitcast_dynamic-update-slice_fusion.1
  89.5 0.9 bitcast_dynamic-update-slice_fusion
  90.4 1.5 collective-permute-start.14
  92.9 17.4 %collective-permute-done.8 = bf16[128,1024]{1,0:T(8,128)(2,1)S(1)} collective-permute-done((bf16[128,1024]{1,0:T(8,128)(2,1)S(1)}, bf16[128,1024]{1,0:T(8,128)(2,1)S(1)}, u32[]{:S(2)}, u32[]{:S(2)}) %collective-permute-start.8) | collective-permute-done | bytes 262176 | tf_op jit(solution)/shard_map/ppermute | solution.py:38
  110.3 1.1 pad_maximum_fusion.2
  111.4 1.3 collective-permute-start.10
  113.0 1.1 pad_maximum_fusion.3
  114.6 4.0 %collective-permute-done.14 = bf16[512,640]{1,0:T(8,128)(2,1)} collective-permute-done((bf16[512,640]{1,0:T(8,128)(2,1)S(1)}, bf16[512,640]{1,0:T(8,128)(2,1)}, u32[]{:S(2)}, u32[]{:S(2)}) %collective-permute-start.14) | collective-permute-done | bytes 655392 | tf_op jit(solution)/shard_map/ppermute | solution.py:38
  118.7 1.2 broadcast_select_fusion.7
  120.3 16.3 %collective-permute-done.10 = bf16[4,128,1024]{2,1,0:T(8,128)(2,1)} collective-permute-done((bf16[4,128,1024]{2,1,0:T(8,128)(2,1)}, bf16[4,128,1024]{2,1,0:T(8,128)(2,1)}, u32[]{:S(2)}, u32[]{:S(2)}) %collective-permute-start.10) | collective-permute-done | bytes 1048608 | tf_op jit(solution)/shard_map/ppermute | solution.py:38
  136.7 1.4 broadcast_select_fusion.5
  138.3 1.6 broadcast_select_fusion.3
  139.9 1.2 fusion.12
  141.2 13.9 %collective-permute-start.24 = (bf16[128,512]{1,0:T(8,128)(2,1)S(1)}, bf16[128,512]{1,0:T(8,128)(2,1)S(1)}, u32[]{:S(2)}, u32[]{:S(2)}) collective-permute-start(bf16[128,512]{1,0:T(8,128)(2,1)S(1)} %get-tuple-element.67), channel_id=1, source_target_pairs={{0,24},{8,0},{16,8},{24,16},{1,25},{9,1},{17,9},{25,17},{2,26},{10... | collective-permute-start | bytes 393224 | tf_op jit(solution)/shard_map/ppermute | solution.py:38
  155.2 4.4 %collective-permute-start.25 = (bf16[128,512]{1,0:T(8,128)(2,1)S(1)}, bf16[128,512]{1,0:T(8,128)(2,1)S(1)}, u32[]{:S(2)}, u32[]{:S(2)}) collective-permute-start(bf16[128,512]{1,0:T(8,128)(2,1)S(1)} %get-tuple-element.66), channel_id=1, source_target_pairs={{0,16},{8,24},{16,0},{24,8},{1,17},{9,25},{17,1},{25,9},{2,18},{10... | collective-permute-start | bytes 393224 | tf_op jit(solution)/shard_map/ppermute | solution.py:38
  159.6 2.3 collective-permute-done.24
  161.9 9.3 %collective-permute-done.25 = bf16[128,512]{1,0:T(8,128)(2,1)S(1)} collective-permute-done((bf16[128,512]{1,0:T(8,128)(2,1)S(1)}, bf16[128,512]{1,0:T(8,128)(2,1)S(1)}, u32[]{:S(2)}, u32[]{:S(2)}) %collective-permute-start.25) | collective-permute-done | bytes 131104 | tf_op jit(solution)/shard_map/ppermute | solution.py:38
  171.8 1.8 fusion.8
  173.8 1.4 collective-permute-start.18
  175.2 4.3 %collective-permute-done.16 = bf16[128,640]{1,0:T(8,128)(2,1)S(1)} collective-permute-done((bf16[128,640]{1,0:T(8,128)(2,1)S(1)}, bf16[128,640]{1,0:T(8,128)(2,1)S(1)}, u32[]{:S(2)}, u32[]{:S(2)}) %collective-permute-start.16) | collective-permute-done | bytes 163872 | tf_op jit(solution)/shard_map/ppermute | solution.py:38
  179.5 8.1 %collective-permute-done.17 = bf16[128,640]{1,0:T(8,128)(2,1)S(1)} collective-permute-done((bf16[128,640]{1,0:T(8,128)(2,1)S(1)}, bf16[128,640]{1,0:T(8,128)(2,1)S(1)}, u32[]{:S(2)}, u32[]{:S(2)}) %collective-permute-start.17) | collective-permute-done | bytes 163872 | tf_op jit(solution)/shard_map/ppermute | solution.py:38
  187.9 10.8 %shard_map.210 = (bf16[4,128,512]{2,1,0:T(8,128)(2,1)S(1)}, f32[8,32,64,128]{3,2,1,0:T(8,128)}, bf16[4,32,512]{2,1,0:T(8,128)(2,1)S(1)}, bf16[32,256]{1,0:T(8,128)(2,1)S(1)}) custom-call(s32[4]{0:T(128)S(1)} %and_select_fusion.5.refs_0_, bf16[4,128,640]{2,1,0:T(8,128)(2,1)S(1)} %pad_maximum_fusion.4.refs_1_.refs_2_, ...), custom_call_target="tpu_custom_call" | custom-call | flops 268435456 | bytes 16777216 | tf_op jit(solution)/shard_map/pallas_call | solution.py:326
  199.5 4.7 %fusion.50 = f32[128,2048]{1,0:T(8,128)S(1)} fusion(bf16[128,2048]{0,1:T(8,128)(2,1)S(1)} %bitcast.181, bf16[2048,2048]{1,0:T(8,128)(2,1)} %all-gather.2.cloned.1.call-done), kind=kOutput, calls=%fused_computation.171 | convolution fusion | flops 1073741824 | bytes 9961472 | tf_op jit(solution)/shard_map/dot_general | solution.py:504
  204.2 1.4 collective-permute-start.27
  205.8 5.0 %collective-permute-done.28 = f32[128]{0:T(128)S(1)} collective-permute-done((f32[128]{0:T(128)S(1)}, f32[128]{0:T(128)S(1)}, u32[]{:S(2)}, u32[]{:S(2)}) %collective-permute-start.28) | collective-permute-done | bytes 544 | tf_op jit(solution)/shard_map/ppermute | solution.py:38
  211.9 3.2 %collective-permute-start.33 = (bf16[2,16,1024]{2,1,0:T(8,128)(2,1)S(1)}, bf16[2,16,1024]{2,1,0:T(8,128)(2,1)S(1)}, u32[]{:S(2)}, u32[]{:S(2)}) collective-permute-start(bf16[2,16,1024]{2,1,0:T(8,128)(2,1)S(1)} %bitcast.251), channel_id=1, source_target_pairs={{0,22},{2,24},{4,26},{6,28},{8,30},{10,0},{12,2},{14,4},{16,6},{18... | collective-permute-start | bytes 196616 | tf_op jit(solution)/shard_map/ppermute | solution.py:38
  215.1 3.0 %collective-permute-start.34 = (bf16[2,16,1024]{2,1,0:T(8,128)(2,1)S(1)}, bf16[2,16,1024]{2,1,0:T(8,128)(2,1)S(1)}, u32[]{:S(2)}, u32[]{:S(2)}) collective-permute-start(bf16[2,16,1024]{2,1,0:T(8,128)(2,1)S(1)} %bitcast.250), channel_id=1, source_target_pairs={{0,20},{2,22},{4,24},{6,26},{8,28},{10,30},{12,0},{14,2},{16,4},{1... | collective-permute-start | bytes 196616 | tf_op jit(solution)/shard_map/ppermute | solution.py:38
  219.5 2.3 collective-permute-start.30
  221.8 3.0 %collective-permute-start.31 = (bf16[2,16,1024]{2,1,0:T(8,128)(2,1)S(1)}, bf16[2,16,1024]{2,1,0:T(8,128)(2,1)S(1)}, u32[]{:S(2)}, u32[]{:S(2)}) collective-permute-start(bf16[2,16,1024]{2,1,0:T(8,128)(2,1)S(1)} %bitcast.247), channel_id=1, source_target_pairs={{0,26},{2,28},{4,30},{6,0},{8,2},{10,4},{12,6},{14,8},{16,10},{18,... | collective-permute-start | bytes 196616 | tf_op jit(solution)/shard_map/ppermute | solution.py:38
  224.8 1.2 collective-permute-start.32
  (230 shorter events, 29.9 us)
Async XLA Ops:
  7.2 192.3 %all-gather.2.cloned.1.call-start = ((), (), s32[]{:S(2)}) async-start(), calls=%async_computation | async-start | bytes 8912896 | tf_op jit(solution)/shard_map/all_gather | solution.py:451
  10.4 11.4 %copy-start.11 = (bf16[128,256]{1,0:T(8,128)(2,1)S(1)}, bf16[128,256]{1,0:T(8,128)(2,1)}, u32[]{:S(2)}) copy-start(bf16[128,256]{1,0:T(8,128)(2,1)} %param.22) | copy-start | bytes 196612
  10.4 11.6 %copy-start.13 = (bf16[128,32]{0,1:T(8,128)(2,1)S(1)}, bf16[128,32]{0,1:T(8,128)(2,1)}, u32[]{:S(2)}) copy-start(bf16[128,32]{0,1:T(8,128)(2,1)} %param.23) | copy-start | bytes 24580
  11.5 16.6 %collective-permute-start = (bf16[2,16,1024]{2,1,0:T(8,128)(2,1)S(1)}, bf16[2,16,1024]{2,1,0:T(8,128)(2,1)}, u32[]{:S(2)}, u32[]{:S(2)}) collective-permute-start(bf16[2,16,1024]{2,1,0:T(8,128)(2,1)S(1)} %bitcast.233), channel_id=1, source_target_pairs={{0,2},{2,4},{4,6},{6,8},{8,10},{10,12},{12,14},{14,16},{16,18},{18... | collective-permute-start | bytes 196616 | tf_op jit(solution)/shard_map/ppermute | solution.py:38
  14.1 16.1 %collective-permute-start.1 = (bf16[2,16,1024]{2,1,0:T(8,128)(2,1)S(1)}, bf16[2,16,1024]{2,1,0:T(8,128)(2,1)}, u32[]{:S(2)}, u32[]{:S(2)}) collective-permute-start(bf16[2,16,1024]{2,1,0:T(8,128)(2,1)S(1)} %bitcast.232), channel_id=1, source_target_pairs={{0,4},{2,6},{4,8},{6,10},{8,12},{10,14},{12,16},{14,18},{16,20},{1... | collective-permute-start | bytes 196616 | tf_op jit(solution)/shard_map/ppermute | solution.py:38
  16.1 16.5 %collective-permute-start.2 = (bf16[2,16,1024]{2,1,0:T(8,128)(2,1)}, bf16[2,16,1024]{2,1,0:T(8,128)(2,1)}, u32[]{:S(2)}, u32[]{:S(2)}) collective-permute-start(bf16[2,16,1024]{2,1,0:T(8,128)(2,1)} %bitcast.174), channel_id=1, source_target_pairs={{0,6},{2,8},{4,10},{6,12},{8,14},{10,16},{12,18},{14,20},{16,22},{... | collective-permute-start | bytes 196616 | tf_op jit(solution)/shard_map/ppermute | solution.py:38
  17.1 17.7 %collective-permute-start.3 = (bf16[2,16,1024]{2,1,0:T(8,128)(2,1)}, bf16[2,16,1024]{2,1,0:T(8,128)(2,1)}, u32[]{:S(2)}, u32[]{:S(2)}) collective-permute-start(bf16[2,16,1024]{2,1,0:T(8,128)(2,1)} %bitcast.173), channel_id=1, source_target_pairs={{0,8},{2,10},{4,12},{6,14},{8,16},{10,18},{12,20},{14,22},{16,24},... | collective-permute-start | bytes 196616 | tf_op jit(solution)/shard_map/ppermute | solution.py:38
  19.0 17.3 %collective-permute-start.4 = (bf16[2,16,1024]{2,1,0:T(8,128)(2,1)}, bf16[2,16,1024]{2,1,0:T(8,128)(2,1)S(1)}, u32[]{:S(2)}, u32[]{:S(2)}) collective-permute-start(bf16[2,16,1024]{2,1,0:T(8,128)(2,1)} %bitcast.172), channel_id=1, source_target_pairs={{0,10},{2,12},{4,14},{6,16},{8,18},{10,20},{12,22},{14,24},{16,26}... | collective-permute-start | bytes 196616 | tf_op jit(solution)/shard_map/ppermute | solution.py:38
  28.0 15.4 %collective-permute-start.5 = (bf16[2,16,1024]{2,1,0:T(8,128)(2,1)S(1)}, bf16[2,16,1024]{2,1,0:T(8,128)(2,1)S(1)}, u32[]{:S(2)}, u32[]{:S(2)}) collective-permute-start(bf16[2,16,1024]{2,1,0:T(8,128)(2,1)S(1)} %bitcast.235), channel_id=1, source_target_pairs={{0,12},{2,14},{4,16},{6,18},{8,20},{10,22},{12,24},{14,26},{16,28}... | collective-permute-start | bytes 196616 | tf_op jit(solution)/shard_map/ppermute | solution.py:38
  30.2 22.7 %collective-permute-start.6 = (bf16[2,16,1024]{2,1,0:T(8,128)(2,1)S(1)}, bf16[2,16,1024]{2,1,0:T(8,128)(2,1)S(1)}, u32[]{:S(2)}, u32[]{:S(2)}) collective-permute-start(bf16[2,16,1024]{2,1,0:T(8,128)(2,1)S(1)} %bitcast.234), channel_id=1, source_target_pairs={{0,14},{2,16},{4,18},{6,20},{8,22},{10,24},{12,26},{14,28},{16,30}... | collective-permute-start | bytes 196616 | tf_op jit(solution)/shard_map/ppermute | solution.py:38
  32.7 50.4 %collective-permute-start.11 = (bf16[128,640]{1,0:T(8,128)(2,1)}, bf16[128,640]{1,0:T(8,128)(2,1)}, u32[]{:S(2)}, u32[]{:S(2)}) collective-permute-start(bf16[128,640]{1,0:T(8,128)(2,1)} %bitcast.13), channel_id=1, source_target_pairs={{0,8},{8,16},{16,24},{24,0},{1,9},{9,17},{17,25},{25,1},{2,10},{10... | collective-permute-start | bytes 491528 | tf_op jit(solution)/shard_map/ppermute | solution.py:38
  34.8 53.7 %collective-permute-start.12 = (bf16[128,640]{1,0:T(8,128)(2,1)}, bf16[128,640]{1,0:T(8,128)(2,1)}, u32[]{:S(2)}, u32[]{:S(2)}) collective-permute-start(bf16[128,640]{1,0:T(8,128)(2,1)} %bitcast.15), channel_id=1, source_target_pairs={{0,16},{8,24},{16,0},{24,8},{1,17},{9,25},{17,1},{25,9},{2,18},{10... | collective-permute-start | bytes 491528 | tf_op jit(solution)/shard_map/ppermute | solution.py:38
  36.4 53.1 %collective-permute-start.13 = (bf16[128,640]{1,0:T(8,128)(2,1)S(1)}, bf16[128,640]{1,0:T(8,128)(2,1)}, u32[]{:S(2)}, u32[]{:S(2)}) collective-permute-start(bf16[128,640]{1,0:T(8,128)(2,1)S(1)} %bitcast.229), channel_id=1, source_target_pairs={{0,24},{8,0},{16,8},{24,16},{1,25},{9,1},{17,9},{25,17},{2,26},{10... | collective-permute-start | bytes 491528 | tf_op jit(solution)/shard_map/ppermute | solution.py:38
  43.4 16.7 %collective-permute-start.19 = (bf16[128,512]{1,0:T(8,128)(2,1)}, bf16[128,512]{1,0:T(8,128)(2,1)}, u32[]{:S(2)}, u32[]{:S(2)}) collective-permute-start(bf16[128,512]{1,0:T(8,128)(2,1)} %bitcast.31), channel_id=1, source_target_pairs={{0,8},{8,16},{16,24},{24,0},{1,9},{9,17},{17,25},{25,1},{2,10},{10... | collective-permute-start | bytes 393224 | tf_op jit(solution)/shard_map/ppermute | solution.py:38
  52.9 17.1 %collective-permute-start.20 = (bf16[128,512]{1,0:T(8,128)(2,1)}, bf16[128,512]{1,0:T(8,128)(2,1)}, u32[]{:S(2)}, u32[]{:S(2)}) collective-permute-start(bf16[128,512]{1,0:T(8,128)(2,1)} %bitcast.33), channel_id=1, source_target_pairs={{0,16},{8,24},{16,0},{24,8},{1,17},{9,25},{17,1},{25,9},{2,18},{10... | collective-permute-start | bytes 393224 | tf_op jit(solution)/shard_map/ppermute | solution.py:38
  54.3 58.5 %copy-start.17 = (f32[32]{0:T(128)S(1)}, f32[32]{0:T(128)}, u32[]{:S(2)}) copy-start(f32[32]{0:T(128)} %param.24) | copy-start | bytes 388
  60.1 18.2 %collective-permute-start.21 = (bf16[128,512]{1,0:T(8,128)(2,1)S(1)}, bf16[128,512]{1,0:T(8,128)(2,1)S(1)}, u32[]{:S(2)}, u32[]{:S(2)}) collective-permute-start(bf16[128,512]{1,0:T(8,128)(2,1)S(1)} %bitcast.230), channel_id=1, source_target_pairs={{0,24},{8,0},{16,8},{24,16},{1,25},{9,1},{17,9},{25,17},{2,26},{10... | collective-permute-start | bytes 393224 | tf_op jit(solution)/shard_map/ppermute | solution.py:38
  70.1 22.8 %collective-permute-start.7 = (bf16[128,1024]{1,0:T(8,128)(2,1)S(1)}, bf16[128,1024]{1,0:T(8,128)(2,1)S(1)}, u32[]{:S(2)}, u32[]{:S(2)}) collective-permute-start(bf16[128,1024]{1,0:T(8,128)(2,1)S(1)} %reshape.560), channel_id=1, source_target_pairs={{0,8},{8,16},{16,24},{24,0},{1,9},{9,17},{17,25},{25,1},{2,10},{10... | collective-permute-start | bytes 786440 | tf_op jit(solution)/shard_map/ppermute | solution.py:38
  78.3 32.0 %collective-permute-start.8 = (bf16[128,1024]{1,0:T(8,128)(2,1)S(1)}, bf16[128,1024]{1,0:T(8,128)(2,1)S(1)}, u32[]{:S(2)}, u32[]{:S(2)}) collective-permute-start(bf16[128,1024]{1,0:T(8,128)(2,1)S(1)} %reshape.560), channel_id=1, source_target_pairs={{0,16},{8,24},{16,0},{24,8},{1,17},{9,25},{17,1},{25,9},{2,18},{10... | collective-permute-start | bytes 786440 | tf_op jit(solution)/shard_map/ppermute | solution.py:38
  83.1 27.2 %collective-permute-start.9 = (bf16[128,1024]{1,0:T(8,128)(2,1)S(1)}, bf16[128,1024]{1,0:T(8,128)(2,1)S(1)}, u32[]{:S(2)}, u32[]{:S(2)}) collective-permute-start(bf16[128,1024]{1,0:T(8,128)(2,1)S(1)} %reshape.560), channel_id=1, source_target_pairs={{0,24},{8,0},{16,8},{24,16},{1,25},{9,1},{17,9},{25,17},{2,26},{10... | collective-permute-start | bytes 786440 | tf_op jit(solution)/shard_map/ppermute | solution.py:38
  88.5 24.4 %collective-permute-start.22 = (bf16[512,512]{1,0:T(8,128)(2,1)S(1)}, bf16[512,512]{1,0:T(8,128)(2,1)S(1)}, u32[]{:S(2)}, u32[]{:S(2)}) collective-permute-start(bf16[512,512]{1,0:T(8,128)(2,1)S(1)} %bitcast.183), channel_id=1, source_target_pairs={{0,4},{4,0},{1,5},{5,1},{2,6},{6,2},{3,7},{7,3},{8,12},{12,8},{9,1... | collective-permute-start | bytes 1572872 | tf_op jit(solution)/shard_map/ppermute | solution.py:38
  90.4 28.2 %collective-permute-start.14 = (bf16[512,640]{1,0:T(8,128)(2,1)S(1)}, bf16[512,640]{1,0:T(8,128)(2,1)}, u32[]{:S(2)}, u32[]{:S(2)}) collective-permute-start(bf16[512,640]{1,0:T(8,128)(2,1)S(1)} %bitcast.182), channel_id=1, source_target_pairs={{0,4},{4,0},{1,5},{5,1},{2,6},{6,2},{3,7},{7,3},{8,12},{12,8},{9,1... | collective-permute-start | bytes 1966088 | tf_op jit(solution)/shard_map/ppermute | solution.py:38
  92.9 18.6 %copy-start.2 = (bf16[128,1024]{1,0:T(8,128)(2,1)}, bf16[128,1024]{1,0:T(8,128)(2,1)S(1)}, u32[]{:S(2)}) copy-start(bf16[128,1024]{1,0:T(8,128)(2,1)S(1)} %collective-permute-done.7) | copy-start | bytes 786436
  111.4 25.2 %collective-permute-start.10 = (bf16[4,128,1024]{2,1,0:T(8,128)(2,1)}, bf16[4,128,1024]{2,1,0:T(8,128)(2,1)}, u32[]{:S(2)}, u32[]{:S(2)}) collective-permute-start(bf16[4,128,1024]{2,1,0:T(8,128)(2,1)} %pad_maximum_fusion.2), channel_id=1, source_target_pairs={{0,1},{1,0},{2,3},{3,2},{4,5},{5,4},{6,7},{7,6},{8,9},{9,8},{10,11... | collective-permute-start | bytes 3145736 | tf_op jit(solution)/shard_map/ppermute | solution.py:38
  114.0 24.3 %collective-permute-start.23 = (bf16[1024,512]{1,0:T(8,128)(2,1)}, bf16[1024,512]{1,0:T(8,128)(2,1)}, u32[]{:S(2)}, u32[]{:S(2)}) collective-permute-start(bf16[1024,512]{1,0:T(8,128)(2,1)} %pad_maximum_fusion.3), channel_id=1, source_target_pairs={{0,2},{2,0},{1,3},{3,1},{4,6},{6,4},{5,7},{7,5},{8,10},{10,8},{9,1... | collective-permute-start | bytes 3145736 | tf_op jit(solution)/shard_map/ppermute | solution.py:38
  114.6 22.0 %copy-start.3 = (bf16[128,1024]{1,0:T(8,128)(2,1)S(1)}, bf16[128,1024]{1,0:T(8,128)(2,1)}, u32[]{:S(2)}) copy-start(bf16[128,1024]{1,0:T(8,128)(2,1)} %copy-done.2) | copy-start | bytes 786436
  114.6 22.0 %copy-start.5 = (bf16[128,1024]{1,0:T(8,128)(2,1)S(1)}, bf16[128,1024]{1,0:T(8,128)(2,1)}, u32[]{:S(2)}) copy-start(bf16[128,1024]{1,0:T(8,128)(2,1)} %copy-done.4) | copy-start | bytes 786436
  114.6 22.0 %copy-start.7 = (bf16[128,1024]{1,0:T(8,128)(2,1)S(1)}, bf16[128,1024]{1,0:T(8,128)(2,1)}, u32[]{:S(2)}) copy-start(bf16[128,1024]{1,0:T(8,128)(2,1)} %copy-done.6) | copy-start | bytes 786436
  120.0 51.2 %collective-permute-start.15 = (bf16[1024,640]{1,0:T(8,128)(2,1)S(1)}, bf16[1024,640]{1,0:T(8,128)(2,1)S(1)}, u32[]{:S(2)}, u32[]{:S(2)}) collective-permute-start(bf16[1024,640]{1,0:T(8,128)(2,1)S(1)} %pad_maximum_fusion.1), channel_id=1, source_target_pairs={{0,2},{2,0},{1,3},{3,1},{4,6},{6,4},{5,7},{7,5},{8,10},{10,8},{9,1... | collective-permute-start | bytes 3932168 | tf_op jit(solution)/shard_map/ppermute | solution.py:38
  141.2 20.6 %collective-permute-start.24 = (bf16[128,512]{1,0:T(8,128)(2,1)S(1)}, bf16[128,512]{1,0:T(8,128)(2,1)S(1)}, u32[]{:S(2)}, u32[]{:S(2)}) collective-permute-start(bf16[128,512]{1,0:T(8,128)(2,1)S(1)} %get-tuple-element.67), channel_id=1, source_target_pairs={{0,24},{8,0},{16,8},{24,16},{1,25},{9,1},{17,9},{25,17},{2,26},{10... | collective-permute-start | bytes 393224 | tf_op jit(solution)/shard_map/ppermute | solution.py:38
  155.2 16.0 %collective-permute-start.25 = (bf16[128,512]{1,0:T(8,128)(2,1)S(1)}, bf16[128,512]{1,0:T(8,128)(2,1)S(1)}, u32[]{:S(2)}, u32[]{:S(2)}) collective-permute-start(bf16[128,512]{1,0:T(8,128)(2,1)S(1)} %get-tuple-element.66), channel_id=1, source_target_pairs={{0,16},{8,24},{16,0},{24,8},{1,17},{9,25},{17,1},{25,9},{2,18},{10... | collective-permute-start | bytes 393224 | tf_op jit(solution)/shard_map/ppermute | solution.py:38
  159.6 11.6 %collective-permute-start.26 = (bf16[128,512]{1,0:T(8,128)(2,1)S(1)}, bf16[128,512]{1,0:T(8,128)(2,1)S(1)}, u32[]{:S(2)}, u32[]{:S(2)}) collective-permute-start(bf16[128,512]{1,0:T(8,128)(2,1)S(1)} %get-tuple-element.65), channel_id=1, source_target_pairs={{0,8},{8,16},{16,24},{24,0},{1,9},{9,17},{17,25},{25,1},{2,10},{10... | collective-permute-start | bytes 393224 | tf_op jit(solution)/shard_map/ppermute | solution.py:38
  171.3 16.6 %slice-start = ((s8[8388608]{0:T(1024)(128)(4,1)}), s8[4194304]{0:T(1024)(128)(4,1)S(1)}, s32[]{:S(2)}) async-start(s8[8388608]{0:T(1024)(128)(4,1)} %bitcast.177), calls=%async_computation.1 | async-start | bytes 8388608
  171.8 16.1 %slice-start.1 = ((s8[8388608]{0:T(1024)(128)(4,1)}), s8[4194304]{0:T(1024)(128)(4,1)S(1)}, s32[]{:S(2)}) async-start(s8[8388608]{0:T(1024)(128)(4,1)} %bitcast.177), calls=%async_computation.2 | async-start | bytes 8388608
  173.6 14.3 %copy-start = (f32[4,2048]{1,0:T(4,128)S(1)}, f32[4,2048]{1,0:T(4,128)}, u32[]{:S(2)}) copy-start(f32[4,2048]{1,0:T(4,128)} %param.27) | copy-start | bytes 98308
  173.6 14.3 %copy-start.1 = (f32[4,256]{1,0:T(4,128)S(1)}, f32[4,256]{1,0:T(4,128)}, u32[]{:S(2)}) copy-start(f32[4,256]{1,0:T(4,128)} %refs_12_.1) | copy-start | bytes 12292
  173.7 5.8 %collective-permute-start.16 = (bf16[128,640]{1,0:T(8,128)(2,1)S(1)}, bf16[128,640]{1,0:T(8,128)(2,1)S(1)}, u32[]{:S(2)}, u32[]{:S(2)}) collective-permute-start(bf16[128,640]{1,0:T(8,128)(2,1)S(1)} %get-tuple-element.52), channel_id=1, source_target_pairs={{0,24},{8,0},{16,8},{24,16},{1,25},{9,1},{17,9},{25,17},{2,26},{10... | collective-permute-start | bytes 491528 | tf_op jit(solution)/shard_map/ppermute | solution.py:38
  173.8 13.9 %collective-permute-start.17 = (bf16[128,640]{1,0:T(8,128)(2,1)S(1)}, bf16[128,640]{1,0:T(8,128)(2,1)S(1)}, u32[]{:S(2)}, u32[]{:S(2)}) collective-permute-start(bf16[128,640]{1,0:T(8,128)(2,1)S(1)} %get-tuple-element.51), channel_id=1, source_target_pairs={{0,16},{8,24},{16,0},{24,8},{1,17},{9,25},{17,1},{25,9},{2,18},{10... | collective-permute-start | bytes 491528 | tf_op jit(solution)/shard_map/ppermute | solution.py:38
  173.8 13.8 %collective-permute-start.18 = (bf16[128,640]{1,0:T(8,128)(2,1)S(1)}, bf16[128,640]{1,0:T(8,128)(2,1)S(1)}, u32[]{:S(2)}, u32[]{:S(2)}) collective-permute-start(bf16[128,640]{1,0:T(8,128)(2,1)S(1)} %get-tuple-element.50), channel_id=1, source_target_pairs={{0,8},{8,16},{16,24},{24,0},{1,9},{9,17},{17,25},{25,1},{2,10},{10... | collective-permute-start | bytes 491528 | tf_op jit(solution)/shard_map/ppermute | solution.py:38
  204.2 6.6 %collective-permute-start.27 = (bf16[128,1024]{1,0:T(8,128)(2,1)S(1)}, bf16[128,1024]{1,0:T(8,128)(2,1)S(1)}, u32[]{:S(2)}, u32[]{:S(2)}) collective-permute-start(bf16[128,1024]{1,0:T(8,128)(2,1)S(1)} %dynamic-slice_convert_fusion), channel_id=1, source_target_pairs={{0,1},{1,0},{2,3},{3,2},{4,5},{5,4},{6,7},{7,6},{8,9},{9,8},{10,11... | collective-permute-start | bytes 786440 | tf_op jit(solution)/shard_map/ppermute | solution.py:38
  205.6 5.2 %collective-permute-start.28 = (f32[128]{0:T(128)S(1)}, f32[128]{0:T(128)S(1)}, u32[]{:S(2)}, u32[]{:S(2)}) collective-permute-start(f32[128]{0:T(128)S(1)} %get-tuple-element.43), channel_id=1, source_target_pairs={{0,1},{1,0},{2,3},{3,2},{4,5},{5,4},{6,7},{7,6},{8,9},{9,8},{10,11... | collective-permute-start | bytes 1544 | tf_op jit(solution)/shard_map/ppermute | solution.py:38
  211.9 9.9 %collective-permute-start.33 = (bf16[2,16,1024]{2,1,0:T(8,128)(2,1)S(1)}, bf16[2,16,1024]{2,1,0:T(8,128)(2,1)S(1)}, u32[]{:S(2)}, u32[]{:S(2)}) collective-permute-start(bf16[2,16,1024]{2,1,0:T(8,128)(2,1)S(1)} %bitcast.251), channel_id=1, source_target_pairs={{0,22},{2,24},{4,26},{6,28},{8,30},{10,0},{12,2},{14,4},{16,6},{18... | collective-permute-start | bytes 196616 | tf_op jit(solution)/shard_map/ppermute | solution.py:38
  215.1 9.6 %collective-permute-start.34 = (bf16[2,16,1024]{2,1,0:T(8,128)(2,1)S(1)}, bf16[2,16,1024]{2,1,0:T(8,128)(2,1)S(1)}, u32[]{:S(2)}, u32[]{:S(2)}) collective-permute-start(bf16[2,16,1024]{2,1,0:T(8,128)(2,1)S(1)} %bitcast.250), channel_id=1, source_target_pairs={{0,20},{2,22},{4,24},{6,26},{8,28},{10,30},{12,0},{14,2},{16,4},{1... | collective-permute-start | bytes 196616 | tf_op jit(solution)/shard_map/ppermute | solution.py:38
  218.1 9.5 %collective-permute-start.35 = (bf16[2,16,1024]{2,1,0:T(8,128)(2,1)S(1)}, bf16[2,16,1024]{2,1,0:T(8,128)(2,1)S(1)}, u32[]{:S(2)}, u32[]{:S(2)}) collective-permute-start(bf16[2,16,1024]{2,1,0:T(8,128)(2,1)S(1)} %bitcast.241), channel_id=1, source_target_pairs={{0,18},{2,20},{4,22},{6,24},{8,26},{10,28},{12,30},{14,0},{16,2},{... | collective-permute-start | bytes 196616 | tf_op jit(solution)/shard_map/ppermute | solution.py:38
  219.0 8.7 %collective-permute-start.29 = (bf16[2,16,1024]{2,1,0:T(8,128)(2,1)S(1)}, bf16[2,16,1024]{2,1,0:T(8,128)(2,1)S(1)}, u32[]{:S(2)}, u32[]{:S(2)}) collective-permute-start(bf16[2,16,1024]{2,1,0:T(8,128)(2,1)S(1)} %bitcast.243), channel_id=1, source_target_pairs={{0,30},{2,0},{4,2},{6,4},{8,6},{10,8},{12,10},{14,12},{16,14},{18,... | collective-permute-start | bytes 196616 | tf_op jit(solution)/shard_map/ppermute | solution.py:38
  219.5 8.3 %collective-permute-start.30 = (bf16[2,16,1024]{2,1,0:T(8,128)(2,1)S(1)}, bf16[2,16,1024]{2,1,0:T(8,128)(2,1)S(1)}, u32[]{:S(2)}, u32[]{:S(2)}) collective-permute-start(bf16[2,16,1024]{2,1,0:T(8,128)(2,1)S(1)} %bitcast.245), channel_id=1, source_target_pairs={{0,28},{2,30},{4,0},{6,2},{8,4},{10,6},{12,8},{14,10},{16,12},{18,... | collective-permute-start | bytes 196616 | tf_op jit(solution)/shard_map/ppermute | solution.py:38
  221.8 6.8 %collective-permute-start.31 = (bf16[2,16,1024]{2,1,0:T(8,128)(2,1)S(1)}, bf16[2,16,1024]{2,1,0:T(8,128)(2,1)S(1)}, u32[]{:S(2)}, u32[]{:S(2)}) collective-permute-start(bf16[2,16,1024]{2,1,0:T(8,128)(2,1)S(1)} %bitcast.247), channel_id=1, source_target_pairs={{0,26},{2,28},{4,30},{6,0},{8,2},{10,4},{12,6},{14,8},{16,10},{18,... | collective-permute-start | bytes 196616 | tf_op jit(solution)/shard_map/ppermute | solution.py:38
  224.8 4.6 %collective-permute-start.32 = (bf16[2,16,1024]{2,1,0:T(8,128)(2,1)S(1)}, bf16[2,16,1024]{2,1,0:T(8,128)(2,1)S(1)}, u32[]{:S(2)}, u32[]{:S(2)}) collective-permute-start(bf16[2,16,1024]{2,1,0:T(8,128)(2,1)S(1)} %bitcast.237), channel_id=1, source_target_pairs={{0,24},{2,26},{4,28},{6,30},{8,0},{10,2},{12,4},{14,6},{16,8},{18,... | collective-permute-start | bytes 196616 | tf_op jit(solution)/shard_map/ppermute | solution.py:38
  (13 other events, 38.6 us)
Sparse Core Ops, SparseCore 0:
  10.2 123.2 all-gather.1

commit v2 on v1

v2 whole, which is shorter than its diff:
```python
import jax
import jax.numpy as jnp
from jax import lax
from jax.experimental import pallas as pl
from jax.experimental.pallas import tpu as pltpu
from jax.sharding import Mesh, PartitionSpec as P

KCONV = 4
CAP = 2
WINDOW = 8
LANES = 128
QUICK = pl.CostEstimate(flops=1000, bytes_accessed=1000, transcendentals=0)
VMEM_LIMIT = 56 * 1024 * 1024
EPSILON = 1e-05
HIGH = lax.Precision.HIGHEST
BF16 = jnp.bfloat16
F32 = jnp.float32

RING = ("far", "near", "side", "core")
SLABS = ("far", "near")


def round_up(value, unit):
    return -(-value // unit) * unit


def factor(count):
    core, near = 2, 2
    chips = count // core
    side = 1
    while (2 * side) ** 2 <= chips:
        side *= 2
    return chips // side // near, near, side, core


def rotate(value, axis, steps):
    count = lax.axis_size(axis)
    if steps % count == 0:
        return value
    pairs = [(source, (source + steps) % count) for source in range(count)]
    return lax.ppermute(value, axis, pairs)


def gather_axis(value, axis, dim):
    count = lax.axis_size(axis)
    if count == 1:
        return value
    if count > 2:
        return lax.all_gather(value, axis, axis=dim, tiled=True)
    peer = rotate(value, axis, 1)
    first = lax.axis_index(axis) == 0
    return jnp.concatenate(
        [jnp.where(first, value, peer), jnp.where(first, peer, value)], axis=dim
    )


def place(pieces, slots):
    full = jnp.zeros((len(pieces),) + pieces[0].shape, pieces[0].dtype)
    for piece, slot in zip(pieces, slots):
        full = lax.dynamic_update_slice_in_dim(full, piece[None], slot, 0)
    return full


def one_hot_apply(table, values, shape):
    flat = values.reshape(table.shape[1], -1)
    return jnp.dot(table, flat, preferred_element_type=F32).astype(BF16).reshape(shape)


def route_tables(owner_dev, state_page, conv_page, accepted, groups, per_dev, this_dev):
    owner_grid = owner_dev.reshape(groups, per_dev)
    home_grid = jnp.arange(groups, dtype=jnp.int32)[:, None]
    offset_grid = (owner_grid - home_grid + groups) % groups
    positions = jnp.arange(per_dev, dtype=jnp.int32)
    earlier = positions[None, :] < positions[:, None]
    pair_rank = jnp.sum((owner_grid[:, :, None] == owner_grid[:, None, :]) & earlier[None], axis=2)
    slot_grid = offset_grid * CAP + pair_rank
    send_at = lax.dynamic_slice_in_dim(slot_grid, this_dev, 1, 0)[0]
    buffer_rows = jnp.arange(WINDOW * CAP, dtype=jnp.int32)
    send_table = (buffer_rows[:, None] == send_at[None, :]).astype(BF16)
    arrive_at = slot_grid.reshape(-1)
    slot_match = (owner_dev[None, :] == this_dev) & (state_page[None, :] == positions[:, None])
    pick_from = jnp.sum(jnp.where(slot_match, arrive_at[None, :], 0), axis=1)
    conv_of = jnp.sum(jnp.where(slot_match, conv_page[None, :], 0), axis=1)
    kept_count = jnp.sum(jnp.where(slot_match, accepted[None, :], 0), axis=1)
    gather_table = (buffer_rows[None, :] == pick_from[:, None]).astype(BF16)
    return (send_table, gather_table, conv_of, kept_count)


def tables_kernel(sizes, conv_ref, kept_ref, moves_ref, masks_ref):
    per_dev, draft, hist_pad = sizes
    rows = per_dev * draft
    keep = KCONV - 1
    width = rows + hist_pad

    def pick(slot, scalars):
        return sum(jnp.where(slot == at, scalars[at], 0) for at in range(per_dev))

    row = lax.broadcasted_iota(jnp.int32, (rows, width), 0)
    column = lax.broadcasted_iota(jnp.int32, (rows, width), 1)
    step = row % draft
    page_row = pick(row // draft, conv_ref) * keep
    for delay in range(1, KCONV):
        source = jnp.where(step >= delay, row - delay, rows + page_row + keep + step - delay)
        moves_ref[(delay - 1) * rows : delay * rows, :] = (column == source).astype(F32).astype(BF16)
    out_row = lax.broadcasted_iota(jnp.int32, (hist_pad, width), 0)
    column = lax.broadcasted_iota(jnp.int32, (hist_pad, width), 1)
    out_page, out_at = out_row // keep, out_row % keep
    source = jnp.full((hist_pad, width), -1, jnp.int32)
    for slot in range(per_dev):
        at = kept_ref[slot] + out_at
        held = jnp.where(at < keep, rows + out_page * keep + at, slot * draft + at - keep)
        source = jnp.where(out_page == conv_ref[slot], held, source)
    moves_ref[keep * rows : keep * rows + hist_pad, :] = (column == source).astype(F32).astype(BF16)
    row = lax.broadcasted_iota(jnp.int32, (rows, rows), 0)
    column = lax.broadcasted_iota(jnp.int32, (rows, rows), 1)
    step = row % draft
    kept = pick(row // draft, kept_ref)
    masks_ref[0] = (step < kept).astype(F32)
    masks_ref[1] = (column == row - step + kept - 1).astype(F32)
    masks_ref[2] = ((row // draft == column // draft) & (column <= row)).astype(F32)


def series_tables(conv_of, kept_count, per_dev, draft, hist_pad):
    rows = per_dev * draft
    smem = pl.BlockSpec(memory_space=pltpu.SMEM)
    return pl.pallas_call(
        lambda *refs: tables_kernel((per_dev, draft, hist_pad), *refs),
        in_specs=[smem, smem],
        out_specs=[pl.BlockSpec(memory_space=pltpu.VMEM)] * 2,
        out_shape=[
            jax.ShapeDtypeStruct(((KCONV - 1) * rows + hist_pad, rows + hist_pad), BF16),
            jax.ShapeDtypeStruct((3, rows, rows), F32),
        ],
    )(conv_of, kept_count)


def split_pair(value):
    high = value.astype(BF16)
    return high, (value - high.astype(F32)).astype(BF16)


def convolve(series, current, taps, moves_ref):
    rows = current.shape[0]
    total = taps[KCONV - 1 : KCONV] * current
    for delay in range(1, KCONV):
        move = moves_ref[(delay - 1) * rows : delay * rows, :]
        moved = jnp.dot(move, series, preferred_element_type=F32)
        total = total + taps[KCONV - 1 - delay : KCONV - delay] * moved
    return total / (1.0 + jnp.exp(-total))


def mixer_kernel(
    sizes,
    order_ref,
    *refs,
):
    chunks, per_dev, draft, heads, head_dim, state_width = sizes
    x_refs, aux_refs, refs = refs[:chunks], refs[chunks : 2 * chunks], refs[2 * chunks :]
    (
        select_ref,
        moves_ref,
        masks_ref,
        hist_ref,
        hist_state_ref,
        taps_ref,
        taps_state_ref,
        skip_ref,
        step_ref,
        state_ref,
        y_ref,
        new_state_ref,
        conv_ref,
        conv_state_ref,
        b_scr,
        c_scr,
        scores_scr,
        log_scr,
        sel_scr,
        end_scr,
        log_t_scr,
        step_t_scr,
    ) = refs
    rows = per_dev * draft
    width = heads * head_dim
    group = pl.program_id(0)
    causal = masks_ref[2]
    edges = moves_ref[(KCONV - 1) * rows :, :]

    @pl.when(group == 0)
    def prepare():
        aux = jnp.dot(aux_refs[0][...], select_ref[0], preferred_element_type=F32)
        for chunk in range(1, chunks):
            aux = aux + jnp.dot(aux_refs[chunk][...], select_ref[chunk], preferred_element_type=F32)
        maps = aux[:, : 2 * state_width]
        series = jnp.concatenate([maps.astype(BF16), hist_state_ref[...]], axis=0)
        active = convolve(series, maps, taps_state_ref[...], moves_ref)
        conv_state_ref[...] = jnp.dot(edges, series, preferred_element_type=F32).astype(BF16)
        b_rows, c_rows = active[:, :state_width], active[:, state_width:]
        b_scr[...] = b_rows
        c_scr[...] = c_rows
        scores_scr[...] = lax.dot_general(
            c_rows, b_rows, (((1,), (1,)), ((), ())), precision=HIGH, preferred_element_type=F32
        ) * causal
        raw = aux[:, 2 * state_width :] + step_ref[:1, :]
        step_size = jnp.maximum(raw, 0.0) + jnp.log1p(jnp.exp(-jnp.abs(raw)))
        log_decay = jnp.dot(causal, step_size * step_ref[1:2, :], precision=HIGH, preferred_element_type=F32)
        end = jnp.dot(masks_ref[1], log_decay, precision=HIGH, preferred_element_type=F32)
        kept = masks_ref[0] > 0.0
        chosen = jnp.where(kept, jnp.exp(jnp.where(kept, end - log_decay, 0.0)), 0.0) * step_size
        decay_end = jnp.exp(end)
        for chunk in range(chunks):
            part = slice(chunk * heads, (chunk + 1) * heads)
            log_scr[chunk] = log_decay[:, part]
            sel_scr[chunk] = chosen[:, part]
            end_scr[chunk] = decay_end[:, part]
        log_t_scr[...] = log_decay.T
        step_t_scr[...] = step_size.T

    x_rows = x_refs[0][...]
    for chunk in range(1, chunks):
        x_rows = jnp.where(order_ref[group] == chunk, x_refs[chunk][...], x_rows)
    series = jnp.concatenate([x_rows, hist_ref[...]], axis=0)
    active = convolve(series, x_rows.astype(F32), taps_ref[...], moves_ref)
    conv_ref[...] = jnp.dot(edges, series, preferred_element_type=F32).astype(BF16)
    scores = scores_scr[...]
    log_here = log_scr[group]
    sel_here = sel_scr[group]
    end_here = end_scr[group]
    within, growth, picks = [], [], []
    for head in range(heads):
        lanes = slice(head * head_dim, (head + 1) * head_dim)
        at = group * heads + head
        log_row = log_t_scr[pl.ds(at, 1), :]
        step_row = step_t_scr[pl.ds(at, 1), :]
        spread = jnp.where(causal > 0.0, log_here[:, head : head + 1] - log_row, -1e30)
        weight = jnp.exp(spread) * (scores * step_row)
        x_head = active[:, lanes]
        within.append(
            jnp.dot(weight.astype(BF16), x_head.astype(BF16), preferred_element_type=F32)
            + skip_ref[at] * x_head
        )
        growth.append(jnp.broadcast_to(jnp.exp(log_here[:, head : head + 1]), (rows, head_dim)))
        picks.append(jnp.broadcast_to(sel_here[:, head : head + 1], (rows, head_dim)))
    within = jnp.concatenate(within, axis=1)
    growth = jnp.concatenate(growth, axis=1)
    picked = active * jnp.concatenate(picks, axis=1)
    carried = []
    for slot in range(per_dev):
        part = slice(slot * draft, (slot + 1) * draft)
        state = state_ref[slot].reshape(width, state_width)
        carried.append(
            lax.dot_general(
                c_scr[part, :].astype(BF16),
                state.astype(BF16),
                (((1,), (1,)), ((), ())),
                preferred_element_type=F32,
            )
        )
        x_high, x_low = split_pair(picked[part])
        b_high, b_low = split_pair(b_scr[part, :])
        update = lax.dot_general(
            jnp.concatenate([x_high, x_low, x_high], axis=0),
            jnp.concatenate([b_high, b_high, b_low], axis=0),
            (((0,), (0,)), ((), ())),
            preferred_element_type=F32,
        )
        for head in range(heads):
            keep = end_here[slot * draft : slot * draft + 1, head : head + 1]
            lanes = slice(head * head_dim, (head + 1) * head_dim)
            new_state_ref[slot, head] = keep * state[lanes] + update[lanes]
    carried = jnp.concatenate(carried, axis=0)
    y_ref[...] = (within + growth * carried).astype(BF16)


def mix_requests(
    packed,
    order,
    select,
    tables,
    history,
    history_state,
    taps,
    taps_state,
    skip_gain,
    steps,
    state_pool,
):
    rows, packed_width = packed[0].shape
    chunks = len(packed)
    per_dev, all_heads, head_dim, state_width = state_pool.shape
    hist_pad, inner = history.shape
    heads = all_heads // chunks
    draft = rows // per_dev
    lanes = inner // chunks
    aux_lanes = packed_width - lanes
    moves, masks = tables
    sizes = (chunks, per_dev, draft, heads, head_dim, state_width)

    def whole(array):
        zeros = (0,) * array.ndim
        return pl.BlockSpec(array.shape, lambda group, order_ref: zeros)

    def by_group(height):
        return pl.BlockSpec((height, lanes), lambda group, order_ref: (0, group))

    x_spec = pl.BlockSpec((rows, lanes), lambda group, order_ref: (0, 0))
    aux_spec = pl.BlockSpec(
        (rows, aux_lanes), lambda group, order_ref: (0, lanes // aux_lanes)
    )

    state_spec = pl.BlockSpec(
        (per_dev, heads, head_dim, state_width), lambda group, order_ref: (0, group, 0, 0)
    )
    step_lanes = select.shape[2] - 2 * state_width
    grid_spec = pltpu.PrefetchScalarGridSpec(
        num_scalar_prefetch=1,
        grid=(chunks,),
        in_specs=[
            *[x_spec] * chunks,
            *[aux_spec] * chunks,
            whole(select),
            whole(moves),
            whole(masks),
            by_group(hist_pad),
            whole(history_state),
            by_group(KCONV),
            whole(taps_state),
            pl.BlockSpec(memory_space=pltpu.SMEM),
            whole(steps),
            state_spec,
        ],
        out_specs=[
            by_group(rows),
            state_spec,
            by_group(hist_pad),
            pl.BlockSpec((hist_pad, 2 * state_width), lambda group, order_ref: (0, 0)),
        ],
        scratch_shapes=[
            pltpu.VMEM((rows, state_width), F32),
            pltpu.VMEM((rows, state_width), F32),
            pltpu.VMEM((rows, rows), F32),
            pltpu.VMEM((chunks, rows, heads), F32),
            pltpu.VMEM((chunks, rows, heads), F32),
            pltpu.VMEM((chunks, rows, heads), F32),
            pltpu.VMEM((step_lanes, rows), F32),
            pltpu.VMEM((step_lanes, rows), F32),
        ],
    )
    return pl.pallas_call(
        lambda *refs: mixer_kernel(sizes, *refs),
        grid_spec=grid_spec,
        out_shape=(
            jax.ShapeDtypeStruct((rows, inner), BF16),
            jax.ShapeDtypeStruct(state_pool.shape, F32),
            jax.ShapeDtypeStruct((hist_pad, inner), BF16),
            jax.ShapeDtypeStruct((hist_pad, 2 * state_width), BF16),
        ),
        compiler_params=pltpu.CompilerParams(vmem_limit_bytes=VMEM_LIMIT),
        cost_estimate=pl.CostEstimate(
            flops=64 * rows * rows * all_heads * head_dim,
            bytes_accessed=8 * state_pool.size,
            transcendentals=rows * rows * all_heads,
        ),
    )(
        order,
        *packed,
        *packed,
        select,
        moves,
        masks,
        history,
        history_state,
        taps,
        taps_state,
        skip_gain,
        steps,
        state_pool,
    )


def by_chunk(array, chunks, lanes):
    rows, width = array.shape
    parts = array.reshape(rows, chunks, width // chunks).transpose(1, 0, 2)
    return jnp.pad(parts, ((0, 0), (0, 0), (0, lanes - width // chunks)))


def swap(value, axis):
    return rotate(value, axis, 1)


def near_half(weight):
    me = lax.axis_index("near")
    keep = lax.dynamic_index_in_dim(weight, me, 0, keepdims=False)
    give = lax.dynamic_index_in_dim(weight, 1 - me, 0, keepdims=False)
    take = swap(give, "near")
    return jnp.concatenate([jnp.where(me == 0, keep, take), jnp.where(me == 0, take, keep)])


def tie(value, *others):
    return lax.optimization_barrier((value,) + others)[0]


def out_kernel(place_ref, own_ref, peer_ref, *refs):
    weight_refs, out_ref = refs[:8], refs[8]
    rows = own_ref.shape[0]
    both = jnp.concatenate([own_ref[...], peer_ref[...]], axis=0)
    for pair in range(4):
        weight = jnp.concatenate([weight_refs[2 * pair][...], weight_refs[2 * pair + 1][...]], axis=1)
        total = jnp.dot(both, weight, preferred_element_type=F32)
        for at in range(2):
            start = place_ref[(2 * pair + at) % 4] * LANES
            lanes = pl.ds(pl.multiple_of(start, LANES), LANES)
            out_ref[pair // 2, :, lanes] = total[:, at * LANES : (at + 1) * LANES]


def project_out(own, peer, weights, place_of):
    rows, depth = own.shape
    whole = pl.BlockSpec(memory_space=pltpu.VMEM)
    return pl.pallas_call(
        out_kernel,
        in_specs=[pl.BlockSpec(memory_space=pltpu.SMEM)] + [whole] * 10,
        out_specs=whole,
        out_shape=jax.ShapeDtypeStruct((2, 2 * rows, 4 * LANES), F32),
        compiler_params=pltpu.CompilerParams(vmem_limit_bytes=24 * 1024 * 1024),
        cost_estimate=QUICK,
    )(place_of, own, peer, *weights)


def on_device(
    hidden_in,
    z_weight,
    x_weight,
    state_proj,
    step_weight,
    step_bias,
    decay_log,
    skip_gain,
    conv_inner,
    conv_state,
    norm_gain,
    out_weight,
    state_pool,
    conv_pool_inner,
    conv_pool_state,
    owner_dev,
    state_page,
    conv_page,
    accepted,
):
    groups = lax.axis_size(RING)
    fars, nears, sides, cores = (lax.axis_size(name) for name in RING)
    splits = lax.axis_size("mdl")
    paired = (fars, nears, sides, cores, splits) == (2, 2, 2, 2, 2)
    paired = paired and hidden_in.shape[1] == groups * LANES
    chunks = fars * nears if paired else nears
    this_dev = lax.axis_index(RING)
    near_at = lax.axis_index("near")
    me = lax.axis_index(SLABS) if paired else near_at
    part = lax.axis_index("mdl")
    per_dev, all_heads, head_dim, state_width = state_pool.shape
    rows, depth = hidden_in.shape
    draft = rows // per_dev
    inner = all_heads * head_dim
    slots = WINDOW * CAP
    chunk_width = inner // chunks
    lanes = chunk_width
    map_width = 2 * state_width // chunks
    heads = all_heads // chunks
    aux_lanes = round_up(map_width + heads, LANES)
    keep = KCONV - 1
    hist_rows = per_dev * keep
    hist_pad = round_up(hist_rows, 32)

    send_table, gather_table, conv_of, kept_count = route_tables(
        owner_dev, state_page, conv_page, accepted, groups, per_dev, this_dev
    )

    order = (jnp.arange(chunks, dtype=jnp.int32) - me) % chunks
    home_chunk = (jnp.arange(chunks, dtype=jnp.int32) + me) % chunks
    lane = jnp.arange(aux_lanes, dtype=jnp.int32)[None, :]
    step_lanes = round_up(all_heads, LANES)
    target = jnp.where(
        lane < map_width,
        home_chunk[:, None] * map_width + lane,
        jnp.where(
            lane < map_width + heads,
            2 * state_width + home_chunk[:, None] * heads + lane - map_width,
            -1,
        ),
    )
    select = (
        target[:, :, None] == jnp.arange(2 * state_width + step_lanes, dtype=jnp.int32)
    ).astype(BF16)
    tables = series_tables(conv_of, kept_count, per_dev, draft, hist_pad)
    pad_rows = ((0, hist_pad - hist_rows), (0, 0))
    history = jnp.pad(conv_pool_inner.reshape(hist_rows, inner), pad_rows)
    history_state = jnp.pad(conv_pool_state.reshape(hist_rows, 2 * state_width), pad_rows)
    pad_heads = ((0, 0), (0, step_lanes - all_heads))
    steps = jnp.pad(jnp.stack([step_bias, -jnp.exp(decay_log)]), pad_heads)


    block = depth // groups
    columns = hidden_in.reshape(rows, fars, nears, sides, cores, block).transpose(0, 4, 3, 1, 2, 5)
    columns = columns.reshape(rows, splits, depth // splits)
    share = lax.dynamic_index_in_dim(columns, part, 1, keepdims=False)
    outgoing = one_hot_apply(send_table, share, (slots, draft, depth // splits))
    incoming = [
        rotate(outgoing[offset * CAP : (offset + 1) * CAP], RING, offset) for offset in range(WINDOW)
    ]

    packed_weight = jnp.concatenate(
        [
            by_chunk(x_weight, chunks, lanes),
            by_chunk(state_proj, chunks, map_width),
            by_chunk(step_weight, chunks, aux_lanes - map_width),
            by_chunk(z_weight, chunks, lanes),
        ],
        axis=2,
    )
    split = lanes + aux_lanes
    width = split + lanes
    far, side, core = (lax.axis_index(name) for name in ("far", "side", "core"))
    if paired:
        pieces = [
            rotate(
                lax.dynamic_index_in_dim(packed_weight, (me + step) % chunks, 0, keepdims=False),
                SLABS,
                step,
            )
            for step in range(chunks)
        ]
        across = swap(pieces[0], "side")
        incoming, pieces, across, select, history, history_state, steps, tables = (
            lax.optimization_barrier(
                (incoming, pieces, across, select, history, history_state, steps, tables)
            )
        )
        owned = one_hot_apply(gather_table, jnp.concatenate(incoming), (rows, depth // splits))
        owned, pieces = lax.optimization_barrier((owned, pieces))
        rows_of = [rotate(owned, SLABS, step) for step in range(chunks)]
        rows_peer = swap(owned, "mdl")
        slabs = [(me - step) % chunks for step in range(chunks)]
        held = place(pieces, slabs)
        across = place([across] + [swap(piece, "side") for piece in pieces[1:]], slabs)
        rows_of, rows_peer, across, held = lax.optimization_barrier((rows_of, rows_peer, across, held))
        rows_rest = swap(jnp.stack(rows_of[1:]), "mdl")
        at_core, at_side, at_half = core == 0, side == 0, part == 0
        held_peer, across_peer = swap(held, "core"), swap(across, "core")

        def full(columns):
            own = [value[:, :, columns].reshape(-1, columns.stop - columns.start) for value in (held, across)]
            peer = [
                value[:, :, columns].reshape(-1, columns.stop - columns.start)
                for value in (held_peer, across_peer)
            ]
            parts = []
            for first, second in ((own, peer), (peer, own)):
                low = [jnp.where(at_core, first[at], second[at]) for at in range(2)]
                parts += [jnp.where(at_side, low[0], low[1]), jnp.where(at_side, low[1], low[0])]
            return jnp.concatenate(parts)

        packed_full, gate_full = full(slice(0, split)), full(slice(split, width))
        out_far, out_side = swap(out_weight, "far"), swap(out_weight, "side")
        rows_rest, packed_full, gate_full, out_far, out_side = lax.optimization_barrier(
            (rows_rest, packed_full, gate_full, out_far, out_side)
        )
        own_rows = jnp.concatenate(rows_of)
        peer_rows = jnp.concatenate([rows_peer, rows_rest.reshape(-1, depth // splits)])
        all_rows = jnp.concatenate(
            [jnp.where(at_half, own_rows, peer_rows), jnp.where(at_half, peer_rows, own_rows)], axis=1
        )
        packed = jnp.dot(all_rows, packed_full, preferred_element_type=F32).astype(BF16)
        packed = packed.reshape(chunks, rows, split)
        packed = [rotate(packed[step], SLABS, -step) for step in range(chunks)]
        gate = jnp.dot(all_rows, gate_full, preferred_element_type=F32).astype(BF16)
        gate = gate.reshape(chunks, rows, lanes)
        out_across = swap(out_far, "side")
        packed, gate, out_across = lax.optimization_barrier((packed, gate, out_across))
        gate = [rotate(gate[step], SLABS, -step) for step in range(chunks)]
        out_columns = []
        for column in (out_weight, out_side, out_far, out_across):
            out_columns += [column, swap(column, "core")]
    else:
        owned = one_hot_apply(gather_table, jnp.concatenate(incoming), (rows, depth // splits))
        owned = lax.all_gather(owned, "mdl", axis=1, tiled=True)
        owned = jnp.concatenate([owned, swap(owned, "near")])
        weight = near_half(packed_weight)
        for name in ("far", "side", "core"):
            weight = lax.all_gather(weight, name, axis=0, tiled=True)
        total = jnp.dot(owned, weight, preferred_element_type=F32).astype(BF16)
        total = [total[:rows], swap(total[rows:], "near")]
        packed = [value[:, :split] for value in total]
        gate = [value[:, split:] for value in total]
        out_columns = lax.all_gather(out_weight, RING, axis=1, tiled=True)

    y_rows, new_states, conv_rows, conv_state_rows = mix_requests(
        packed,
        order,
        select,
        tables,
        history,
        history_state,
        conv_inner,
        conv_state,
        skip_gain,
        steps,
        state_pool,
    )

    gate_here = []
    for chunk in range(chunks):
        value = gate[0]
        for step in range(1, chunks):
            value = jnp.where(me == (chunk - step) % chunks, gate[step], value)
        gate_here.append(value)
    gate_here = jnp.concatenate(gate_here, axis=1).astype(F32)
    gated = y_rows.astype(F32) * (gate_here / (1.0 + jnp.exp(-gate_here)))
    squares = jnp.sum(gated * gated, axis=1)
    scaled = (gated * norm_gain).astype(BF16)
    wide = depth // splits
    total_inner = inner * splits
    if paired:
        squares = squares + swap(squares, "mdl")
        scale = lax.rsqrt(squares / total_inner + EPSILON)
        scale = jnp.concatenate([scale, swap(scale, "near")])
        columns_at = jnp.stack(
            [2 * at_side + at_core for at_side in (side, 1 - side) for at_core in (core, 1 - core)]
        )
        terms = project_out(scaled, swap(scaled, "near"), out_columns, columns_at)
        here = far == part
        mine = jnp.where(here, terms[0], terms[1])
        other = jnp.where(here, terms[1], terms[0]).astype(BF16)
        total = (mine + swap(other, "mdl").astype(F32)) * scale[:, None]
        total = total.astype(BF16).reshape(2, rows, wide // 2)
        given = swap(total[1], "near")
        mixed_rows = jnp.concatenate(
            [jnp.where(near_at == 0, total[0], given), jnp.where(near_at == 0, given, total[0])], axis=1
        )
    else:
        terms = jnp.dot(scaled, out_columns, preferred_element_type=F32)
        squares = lax.psum(squares, "mdl")
        total = lax.psum_scatter(terms, "mdl", scatter_dimension=1, tiled=True)
        scale = lax.rsqrt(squares / total_inner + EPSILON)
        mixed_rows = (total * scale[:, None]).astype(BF16)

    returning = one_hot_apply(
        gather_table.T, mixed_rows.reshape(per_dev, draft, wide), (slots, draft, wide)
    )
    arrived = jnp.concatenate(
        [
            rotate(returning[offset * CAP : (offset + 1) * CAP], RING, -offset)
            for offset in range(WINDOW)
        ],
        axis=0,
    )
    mixed = one_hot_apply(send_table.T, arrived, (rows, wide))
    return (
        mixed,
        new_states,
        conv_rows[:hist_rows].reshape(per_dev, keep, inner),
        conv_state_rows[:hist_rows].reshape(per_dev, keep, 2 * state_width),
    )


def solution(mesh):
    sizes = factor(mesh.shape["req"])
    split_mesh = Mesh(mesh.devices.reshape(*sizes, mesh.shape["mdl"]), RING + ("mdl",))
    return jax.shard_map(
        on_device,
        mesh=split_mesh,
        in_specs=(
            P(RING, None),
            P(RING, "mdl"),
            P(RING, "mdl"),
            P(RING, None),
            P(RING, "mdl"),
            P("mdl"),
            P("mdl"),
            P("mdl"),
            P(None, "mdl"),
            P(),
            P("mdl"),
            P("mdl", RING),
            P(RING, "mdl", None, None),
            P(RING, None, "mdl"),
            P(RING, None, None),
            P(),
            P(),
            P(),
            P(),
        ),
        out_specs=(
            P(RING, "mdl"),
            P(RING, "mdl", None, None),
            P(RING, None, "mdl"),
            P(RING, None, None),
        ),
        check_vma=False,
    )
```

time: 240 us -> 200 us (0.83)
  starting transfers between devices: 69.3 us -> 49.8 us
  between operations: 15.2 us -> 1.56 us
  waiting for transfers between devices: 99.5 us -> 90.7 us
  Pallas kernels: 10.8 us -> 17.7 us
  other arithmetic: 9.31 us -> 15.6 us
  local copies, waits for them, and re-layouts: 25.2 us -> 19.5 us
  matrix products: 8.96 us -> 4.3 us
    ppermute x36 -> x46, starting transfers between devices: 69.3 us -> 49.8 us  [rotate(): return lax.ppermute(value, axis, pairs)]
    ppermute x36 -> x46, waiting for transfers between devices: 98.8 us -> 90.7 us  [rotate(): return lax.ppermute(value, axis, pairs)]
    unnamed x91 -> x83, local copies, waits for them, and re-layouts: 10 us -> 4.6 us
    concatenate x3 -> x4, other arithmetic: 1.35 us -> 6.32 us  [the longest x2 6.29 us: full(): return jnp.concatenate(parts)]
    dot_general x3 -> x2, matrix products: 7.71 us -> 3.06 us  [the longest x1 1.81 us: on_device(): jnp.dot(all_rows, packed_full, preferred_element_type=F32).astype(BF16)]
    pallas_call x0 -> x2, Pallas kernels: none -> 4.39 us  [the longest x1 2.86 us: project_out(): pl.pallas_call(out_kernel, in_specs=[pl.BlockSpec(memory_space=pltpu.SMEM...]
    pallas_call x1, Pallas kernels: 10.8 us -> 13.3 us  [mix_requests(): pl.pallas_call(lambda *refs: mixer_kernel(sizes, *refs), grid_spec=grid_s...]
    select_n x9 -> x5, other arithmetic: 4.93 us -> 4.37 us  [the longest x2 3.73 us: full(): jnp.where(at_side, low[0], low[1])]
  transfers between devices with their start and end apart: 37 -> 46, of which waited for: 15 -> 17; matrix products, arithmetic and copies ran while one was open for 15% -> 16% of each run, Pallas kernels for 5% -> 9%
where the time goes in v2:
time: 200 us; the launch traced here: 199 us
  waiting for transfers between devices  90.7 us (45%)
  starting transfers between devices  49.8 us (25%)
  local copies, waits for them, and re-layouts  19.5 us (10%)
  Pallas kernels  17.7 us (9%)
  other arithmetic  15.6 us (8%)
  matrix products  4.3 us (2%)
    ppermute x46, waiting for transfers between devices, rotate(): return lax.ppermute(value, axis, pairs)  90.7 us
    ppermute x46, starting transfers between devices, rotate(): return lax.ppermute(value, axis, pairs)  49.8 us
    pallas_call x1, Pallas kernels, mix_requests(): pl.pallas_call(lambda *refs: mixer_kernel(sizes, *refs), grid_spec=grid_s...  13.3 us
    concatenate x2, other arithmetic, full(): return jnp.concatenate(parts)  6.29 us
    dynamic_update_slice x8, local copies, waits for them, and re-layouts, place(): full = lax.dynamic_update_slice_in_dim(full, piece[None], slot, 0)  5.86 us
    unnamed x83, local copies, waits for them, and re-layouts  4.6 us
  transfers between devices with their start and end apart: 46, of which 17 were waited for; matrix products, arithmetic and copies ran while one was open for 16% of the time, Pallas kernels for 9%

profile of v2, /device:TPU:1, one launch (start us, length us, event | category | flops | bytes accessed | tf_op | source)
XLA Modules:
  0.0 199.1 jit_solution(15829786870515839239)
XLA Ops:
  0.7 1.3 copy.71
  3.6 2.7 %collective-permute-start = (bf16[2,16,1024]{2,1,0:T(8,128)(2,1)S(1)}, bf16[2,16,1024]{2,1,0:T(8,128)(2,1)S(1)}, u32[]{:S(2)}, u32[]{:S(2)}) collective-permute-start(bf16[2,16,1024]{2,1,0:T(8,128)(2,1)S(1)} %bitcast.228), channel_id=1, source_target_pairs={{0,2},{2,4},{4,6},{6,8},{8,10},{10,12},{12,14},{14,16},{16,18},{18... | collective-permute-start | bytes 196616 | tf_op jit(solution)/shard_map/ppermute | solution.py:41
  6.3 1.3 collective-permute-start.1
  8.0 1.4 collective-permute-start.3
  9.4 2.5 %collective-permute-start.4 = (bf16[2,16,1024]{2,1,0:T(8,128)(2,1)S(1)}, bf16[2,16,1024]{2,1,0:T(8,128)(2,1)S(1)}, u32[]{:S(2)}, u32[]{:S(2)}) collective-permute-start(bf16[2,16,1024]{2,1,0:T(8,128)(2,1)S(1)} %bitcast.224), channel_id=1, source_target_pairs={{0,10},{2,12},{4,14},{6,16},{8,18},{10,20},{12,22},{14,24},{16,26}... | collective-permute-start | bytes 196616 | tf_op jit(solution)/shard_map/ppermute | solution.py:41
  15.6 1.2 collective-permute-start.7
  16.8 2.3 %collective-permute-start.8 = (bf16[128,1152]{1,0:T(8,128)(2,1)S(1)}, bf16[128,1152]{1,0:T(8,128)(2,1)S(1)}, u32[]{:S(2)}, u32[]{:S(2)}) collective-permute-start(bf16[128,1152]{1,0:T(8,128)(2,1)S(1)} %bitcast.198), channel_id=1, source_target_pairs={{0,16},{8,24},{16,0},{24,8},{1,17},{9,25},{17,1},{25,9},{2,18},{10... | collective-permute-start | bytes 884744 | tf_op jit(solution)/shard_map/ppermute | solution.py:41
  19.2 1.1 collective-permute-start.9
  22.1 1.3 collective-permute-start.5
  24.1 1.5 shard_map.210
  25.6 22.4 %collective-permute-done.5 = bf16[2,16,1024]{2,1,0:T(8,128)(2,1)S(1)} collective-permute-done((bf16[2,16,1024]{2,1,0:T(8,128)(2,1)S(1)}, bf16[2,16,1024]{2,1,0:T(8,128)(2,1)S(1)}, u32[]{:S(2)}, u32[]{:S(2)}) %collective-permute-start.5) | collective-permute-done | bytes 65568 | tf_op jit(solution)/shard_map/ppermute | solution.py:41
  48.6 4.9 %collective-permute-done.6 = bf16[2,16,1024]{2,1,0:T(8,128)(2,1)S(1)} collective-permute-done((bf16[2,16,1024]{2,1,0:T(8,128)(2,1)S(1)}, bf16[2,16,1024]{2,1,0:T(8,128)(2,1)S(1)}, u32[]{:S(2)}, u32[]{:S(2)}) %collective-permute-start.6) | collective-permute-done | bytes 65568 | tf_op jit(solution)/shard_map/ppermute | solution.py:41
  54.4 1.6 collective-permute-start.12
  56.0 1.6 collective-permute-start.13
  57.7 1.3 collective-permute-start.14
  58.9 1.1 broadcast.222.clone
  60.8 1.1 broadcast.222.clone.1
  64.9 2.2 %collective-permute-done.15 = bf16[128,1152]{1,0:T(8,128)(2,1)S(1)} collective-permute-done((bf16[128,1152]{1,0:T(8,128)(2,1)S(1)}, bf16[128,1152]{1,0:T(8,128)(2,1)S(1)}, u32[]{:S(2)}, u32[]{:S(2)}) %collective-permute-start.15) | collective-permute-done | bytes 294944 | tf_op jit(solution)/shard_map/ppermute | solution.py:41
  67.8 6.5 %collective-permute-done.16 = bf16[128,1152]{1,0:T(8,128)(2,1)S(1)} collective-permute-done((bf16[128,1152]{1,0:T(8,128)(2,1)S(1)}, bf16[128,1152]{1,0:T(8,128)(2,1)S(1)}, u32[]{:S(2)}, u32[]{:S(2)}) %collective-permute-start.16) | collective-permute-done | bytes 294944 | tf_op jit(solution)/shard_map/ppermute | solution.py:41
  75.0 5.6 %collective-permute-done.17 = bf16[128,1152]{1,0:T(8,128)(2,1)S(1)} collective-permute-done((bf16[128,1152]{1,0:T(8,128)(2,1)S(1)}, bf16[128,1152]{1,0:T(8,128)(2,1)S(1)}, u32[]{:S(2)}, u32[]{:S(2)}) %collective-permute-start.17) | collective-permute-done | bytes 294944 | tf_op jit(solution)/shard_map/ppermute | solution.py:41
  81.4 3.2 %collective-permute-start.19 = (bf16[4,128,1152]{2,1,0:T(8,128)(2,1)}, bf16[4,128,1152]{2,1,0:T(8,128)(2,1)}, u32[]{:S(2)}, u32[]{:S(2)}) collective-permute-start(bf16[4,128,1152]{2,1,0:T(8,128)(2,1)} %bitcast_dynamic-update-slice_fusion), channel_id=1, source_target_pairs={{0,2},{2,0},{1,3},{3,1},{4,6},{6,4},{5,7},{7,5},{8,10},{10,8},{9,1... | collective-permute-start | bytes 3538952 | tf_op jit(solution)/shard_map/ppermute | solution.py:41
  87.6 1.5 collective-permute-done.20
  89.1 2.0 %broadcast_select_fusion.9 = (bf16[4,128,640]{2,1,0:T(8,128)(2,1)S(1)}, bf16[4,128,640]{2,1,0:T(8,128)(2,1)S(1)}, bf16[4,128,640]{2,1,0:T(8,128)(2,1)S(1)}, bf16[4,128,640]{2,1,0:T(8,128)(2,1)S(1)}) fusion(pred[]{:T(512)S(6)} %eq.154, bf16[4,128,1152]{2,1,0:T(8,128)(2,1)} %collective-permute-done.19, ...), kind=kLoop, calls=%fused_computation.37 | loop fusion | flops 2621440 | bytes 5242882 | tf_op jit(solution)/shard_map/jit(_where)/select_n | solution.py:559
  91.1 1.7 broadcast_select_fusion.17
  93.0 6.2 %pad_maximum_fusion = bf16[2048,640]{1,0:T(8,128)(2,1)S(1)} fusion(bf16[512,640]{1,0:T(8,128)(2,1)S(1)} %bitcast.178, bf16[512,640]{1,0:T(8,128)(2,1)S(1)} %bitcast.177, bf16[512,640]{1,0:T(8,128)(2,1)S(1)} %bitcast.176, bf16[512,640]{1,0:T(8,128)(2,1)S(1)} %bitcast.175), kind=kLoop, calls=%fused_computation.6 | loop fusion | flops 10485760 | bytes 5242880 | tf_op jit(solution)/shard_map/concatenate | solution.py:560
  99.1 11.5 %collective-permute-done.21.refs_4_ = bf16[2048,128]{1,0:T(8,128)(2,1)S(1)} collective-permute-done((bf16[2048,128]{1,0:T(8,128)(2,1)S(1)}, bf16[2048,128]{1,0:T(8,128)(2,1)S(1)}, u32[]{:S(2)}, u32[]{:S(2)}) %collective-permute-start.21) | collective-permute-done | bytes 524320 | tf_op jit(solution)/shard_map/ppermute | solution.py:41
  111.2 1.8 fusion.4
  114.0 1.3 collective-permute-start.25
  115.2 1.2 fusion.5
  116.5 3.6 %collective-permute-done.23.refs_2_.refs_6_ = bf16[128,640]{1,0:T(8,128)(2,1)S(1)} collective-permute-done((bf16[128,640]{1,0:T(8,128)(2,1)S(1)}, bf16[128,640]{1,0:T(8,128)(2,1)S(1)}, u32[]{:S(2)}, u32[]{:S(2)}) %collective-permute-start.23) | collective-permute-done | bytes 163872 | tf_op jit(solution)/shard_map/ppermute | solution.py:41
  120.0 1.6 collective-permute-start.33
  121.7 5.3 %collective-permute-done.24.refs_3_.refs_7_ = bf16[128,640]{1,0:T(8,128)(2,1)S(1)} collective-permute-done((bf16[128,640]{1,0:T(8,128)(2,1)S(1)}, bf16[128,640]{1,0:T(8,128)(2,1)S(1)}, u32[]{:S(2)}, u32[]{:S(2)}) %collective-permute-start.24) | collective-permute-done | bytes 163872 | tf_op jit(solution)/shard_map/ppermute | solution.py:41
  127.0 2.7 %collective-permute-start.27 = (bf16[128,512]{1,0:T(8,128)(2,1)S(1)}, bf16[128,512]{1,0:T(8,128)(2,1)S(1)}, u32[]{:S(2)}, u32[]{:S(2)}) collective-permute-start(bf16[128,512]{1,0:T(8,128)(2,1)S(1)} %get-tuple-element.157), channel_id=1, source_target_pairs={{0,8},{8,16},{16,24},{24,0},{1,9},{9,17},{17,25},{25,1},{2,10},{10... | collective-permute-start | bytes 393224 | tf_op jit(solution)/shard_map/ppermute | solution.py:41
  129.7 2.0 %collective-permute-start.28 = (bf16[128,512]{1,0:T(8,128)(2,1)S(1)}, bf16[128,512]{1,0:T(8,128)(2,1)S(1)}, u32[]{:S(2)}, u32[]{:S(2)}) collective-permute-start(bf16[128,512]{1,0:T(8,128)(2,1)S(1)} %get-tuple-element.156), channel_id=1, source_target_pairs={{0,16},{8,24},{16,0},{24,8},{1,17},{9,25},{17,1},{25,9},{2,18},{10... | collective-permute-start | bytes 393224 | tf_op jit(solution)/shard_map/ppermute | solution.py:41
  131.7 2.3 %collective-permute-start.29 = (bf16[128,512]{1,0:T(8,128)(2,1)S(1)}, bf16[128,512]{1,0:T(8,128)(2,1)S(1)}, u32[]{:S(2)}, u32[]{:S(2)}) collective-permute-start(bf16[128,512]{1,0:T(8,128)(2,1)S(1)} %get-tuple-element.155), channel_id=1, source_target_pairs={{0,24},{8,0},{16,8},{24,16},{1,25},{9,1},{17,9},{25,17},{2,26},{10... | collective-permute-start | bytes 393224 | tf_op jit(solution)/shard_map/ppermute | solution.py:41
  134.0 13.3 %shard_map.211 = (bf16[128,2048]{1,0:T(8,128)(2,1)}, f32[8,32,64,128]{3,2,1,0:T(8,128)}, bf16[32,2048]{1,0:T(8,128)(2,1)}, bf16[32,256]{1,0:T(8,128)(2,1)}) custom-call(s32[4]{0:T(128)} %get-tuple-element.168.refs_0_, bf16[128,640]{1,0:T(8,128)(2,1)} %get-tuple-element.83.refs_1_.refs_5_, bf16[128,640]{1,0:T(8,128)(2,1)} %copy-done.1, ...), custom_call_target="tpu_custom_call" | custom-call | flops 2147483648 | bytes 16777216 | tf_op jit(solution)/shard_map/pallas_call | solution.py:349
  147.3 1.4 collective-permute-start.32
  148.8 1.6 multiply_reduce_fusion
  151.1 12.6 %collective-permute-done.30.peer_ref = bf16[128,2048]{1,0:T(8,128)(2,1)} collective-permute-done((bf16[128,2048]{1,0:T(8,128)(2,1)S(1)}, bf16[128,2048]{1,0:T(8,128)(2,1)}, u32[]{:S(2)}, u32[]{:S(2)}) %collective-permute-start.30) | collective-permute-done | bytes 524320 | tf_op jit(solution)/shard_map/ppermute | solution.py:41
  163.7 2.9 %shard_map.212 = f32[2,256,512]{2,1,0:T(8,128)S(1)} custom-call(s32[4]{0:T(128)S(1)} %pad_add_fusion.place_ref, bf16[128,2048]{1,0:T(8,128)(2,1)S(1)} %get-tuple-element.138.own_ref, bf16[128,2048]{1,0:T(8,128)(2,1)} %collective-permute-done.30.peer_ref, bf16[2048,128]{1,0:T(8,128)(2,1)S(1)} %copy-done, ...), custom_call_target="tpu_custom_call" | custom-call | flops 1000 | bytes 1000 | tf_op jit(solution)/shard_map/pallas_call | solution.py:419
  167.3 2.1 %collective-permute-done.37 = f32[128]{0:T(128)S(1)} collective-permute-done((f32[128]{0:T(128)S(1)}, f32[128]{0:T(128)S(1)}, u32[]{:S(2)}, u32[]{:S(2)}) %collective-permute-start.37) | collective-permute-done | bytes 544 | tf_op jit(solution)/shard_map/ppermute | solution.py:41
  169.3 3.8 %collective-permute-done.35 = bf16[256,512]{1,0:T(8,128)(2,1)S(1)} collective-permute-done((bf16[256,512]{1,0:T(8,128)(2,1)S(1)}, bf16[256,512]{1,0:T(8,128)(2,1)S(1)}, u32[]{:S(2)}, u32[]{:S(2)}) %collective-permute-start.35) | collective-permute-done | bytes 262176 | tf_op jit(solution)/shard_map/ppermute | solution.py:41
  174.0 3.2 %collective-permute-done.38 = bf16[128,512]{1,0:T(8,128)(2,1)S(1)} collective-permute-done((bf16[128,512]{1,0:T(8,128)(2,1)S(1)}, bf16[128,512]{1,0:T(8,128)(2,1)S(1)}, u32[]{:S(2)}, u32[]{:S(2)}) %collective-permute-start.38) | collective-permute-done | bytes 131104 | tf_op jit(solution)/shard_map/ppermute | solution.py:41
  178.2 3.4 %collective-permute-start.39 = (bf16[2,16,1024]{2,1,0:T(8,128)(2,1)S(1)}, bf16[2,16,1024]{2,1,0:T(8,128)(2,1)S(1)}, u32[]{:S(2)}, u32[]{:S(2)}) collective-permute-start(bf16[2,16,1024]{2,1,0:T(8,128)(2,1)S(1)} %bitcast.244), channel_id=1, source_target_pairs={{0,30},{2,0},{4,2},{6,4},{8,6},{10,8},{12,10},{14,12},{16,14},{18,... | collective-permute-start | bytes 196616 | tf_op jit(solution)/shard_map/ppermute | solution.py:41
  182.9 1.4 collective-permute-start.42
  184.2 3.0 %collective-permute-start.43 = (bf16[2,16,1024]{2,1,0:T(8,128)(2,1)S(1)}, bf16[2,16,1024]{2,1,0:T(8,128)(2,1)S(1)}, u32[]{:S(2)}, u32[]{:S(2)}) collective-permute-start(bf16[2,16,1024]{2,1,0:T(8,128)(2,1)S(1)} %bitcast.236), channel_id=1, source_target_pairs={{0,22},{2,24},{4,26},{6,28},{8,30},{10,0},{12,2},{14,4},{16,6},{18... | collective-permute-start | bytes 196616 | tf_op jit(solution)/shard_map/ppermute | solution.py:41
  187.4 2.6 %collective-permute-start.45 = (bf16[2,16,1024]{2,1,0:T(8,128)(2,1)S(1)}, bf16[2,16,1024]{2,1,0:T(8,128)(2,1)S(1)}, u32[]{:S(2)}, u32[]{:S(2)}) collective-permute-start(bf16[2,16,1024]{2,1,0:T(8,128)(2,1)S(1)} %bitcast.230), channel_id=1, source_target_pairs={{0,18},{2,20},{4,22},{6,24},{8,26},{10,28},{12,30},{14,0},{16,2},{... | collective-permute-start | bytes 196616 | tf_op jit(solution)/shard_map/ppermute | solution.py:41
  192.0 5.0 %collective-permute-done.45 = bf16[2,16,1024]{2,1,0:T(8,128)(2,1)S(1)} collective-permute-done((bf16[2,16,1024]{2,1,0:T(8,128)(2,1)S(1)}, bf16[2,16,1024]{2,1,0:T(8,128)(2,1)S(1)}, u32[]{:S(2)}, u32[]{:S(2)}) %collective-permute-start.45) | collective-permute-done | bytes 65568 | tf_op jit(solution)/shard_map/ppermute | solution.py:41
  (210 shorter events, 28.7 us)
Async XLA Ops:
  3.6 12.0 %collective-permute-start = (bf16[2,16,1024]{2,1,0:T(8,128)(2,1)S(1)}, bf16[2,16,1024]{2,1,0:T(8,128)(2,1)S(1)}, u32[]{:S(2)}, u32[]{:S(2)}) collective-permute-start(bf16[2,16,1024]{2,1,0:T(8,128)(2,1)S(1)} %bitcast.228), channel_id=1, source_target_pairs={{0,2},{2,4},{4,6},{6,8},{8,10},{10,12},{12,14},{14,16},{16,18},{18... | collective-permute-start | bytes 196616 | tf_op jit(solution)/shard_map/ppermute | solution.py:41
  6.3 10.6 %collective-permute-start.1 = (bf16[2,16,1024]{2,1,0:T(8,128)(2,1)S(1)}, bf16[2,16,1024]{2,1,0:T(8,128)(2,1)S(1)}, u32[]{:S(2)}, u32[]{:S(2)}) collective-permute-start(bf16[2,16,1024]{2,1,0:T(8,128)(2,1)S(1)} %bitcast.227), channel_id=1, source_target_pairs={{0,4},{2,6},{4,8},{6,10},{8,12},{10,14},{12,16},{14,18},{16,20},{1... | collective-permute-start | bytes 196616 | tf_op jit(solution)/shard_map/ppermute | solution.py:41
  7.6 11.6 %collective-permute-start.2 = (bf16[2,16,1024]{2,1,0:T(8,128)(2,1)S(1)}, bf16[2,16,1024]{2,1,0:T(8,128)(2,1)S(1)}, u32[]{:S(2)}, u32[]{:S(2)}) collective-permute-start(bf16[2,16,1024]{2,1,0:T(8,128)(2,1)S(1)} %bitcast.226), channel_id=1, source_target_pairs={{0,6},{2,8},{4,10},{6,12},{8,14},{10,16},{12,18},{14,20},{16,22},{... | collective-permute-start | bytes 196616 | tf_op jit(solution)/shard_map/ppermute | solution.py:41
  8.0 12.2 %collective-permute-start.3 = (bf16[2,16,1024]{2,1,0:T(8,128)(2,1)S(1)}, bf16[2,16,1024]{2,1,0:T(8,128)(2,1)S(1)}, u32[]{:S(2)}, u32[]{:S(2)}) collective-permute-start(bf16[2,16,1024]{2,1,0:T(8,128)(2,1)S(1)} %bitcast.225), channel_id=1, source_target_pairs={{0,8},{2,10},{4,12},{6,14},{8,16},{10,18},{12,20},{14,22},{16,24},... | collective-permute-start | bytes 196616 | tf_op jit(solution)/shard_map/ppermute | solution.py:41
  9.4 12.8 %collective-permute-start.4 = (bf16[2,16,1024]{2,1,0:T(8,128)(2,1)S(1)}, bf16[2,16,1024]{2,1,0:T(8,128)(2,1)S(1)}, u32[]{:S(2)}, u32[]{:S(2)}) collective-permute-start(bf16[2,16,1024]{2,1,0:T(8,128)(2,1)S(1)} %bitcast.224), channel_id=1, source_target_pairs={{0,10},{2,12},{4,14},{6,16},{8,18},{10,20},{12,22},{14,24},{16,26}... | collective-permute-start | bytes 196616 | tf_op jit(solution)/shard_map/ppermute | solution.py:41
  14.7 33.3 %copy-start.16 = (f32[32]{0:T(128)S(1)}, f32[32]{0:T(128)}, u32[]{:S(2)}) copy-start(f32[32]{0:T(128)} %param.24) | copy-start | bytes 388
  15.6 37.9 %collective-permute-start.7 = (bf16[128,1152]{1,0:T(8,128)(2,1)S(1)}, bf16[128,1152]{1,0:T(8,128)(2,1)S(1)}, u32[]{:S(2)}, u32[]{:S(2)}) collective-permute-start(bf16[128,1152]{1,0:T(8,128)(2,1)S(1)} %bitcast.199), channel_id=1, source_target_pairs={{0,8},{8,16},{16,24},{24,0},{1,9},{9,17},{17,25},{25,1},{2,10},{10... | collective-permute-start | bytes 884744 | tf_op jit(solution)/shard_map/ppermute | solution.py:41
  16.8 36.7 %collective-permute-start.8 = (bf16[128,1152]{1,0:T(8,128)(2,1)S(1)}, bf16[128,1152]{1,0:T(8,128)(2,1)S(1)}, u32[]{:S(2)}, u32[]{:S(2)}) collective-permute-start(bf16[128,1152]{1,0:T(8,128)(2,1)S(1)} %bitcast.198), channel_id=1, source_target_pairs={{0,16},{8,24},{16,0},{24,8},{1,17},{9,25},{17,1},{25,9},{2,18},{10... | collective-permute-start | bytes 884744 | tf_op jit(solution)/shard_map/ppermute | solution.py:41
  19.2 34.4 %collective-permute-start.9 = (bf16[128,1152]{1,0:T(8,128)(2,1)S(1)}, bf16[128,1152]{1,0:T(8,128)(2,1)S(1)}, u32[]{:S(2)}, u32[]{:S(2)}) collective-permute-start(bf16[128,1152]{1,0:T(8,128)(2,1)S(1)} %bitcast.197), channel_id=1, source_target_pairs={{0,24},{8,0},{16,8},{24,16},{1,25},{9,1},{17,9},{25,17},{2,26},{10... | collective-permute-start | bytes 884744 | tf_op jit(solution)/shard_map/ppermute | solution.py:41
  20.2 33.3 %collective-permute-start.10 = (bf16[128,1152]{1,0:T(8,128)(2,1)S(1)}, bf16[128,1152]{1,0:T(8,128)(2,1)S(1)}, u32[]{:S(2)}, u32[]{:S(2)}) collective-permute-start(bf16[128,1152]{1,0:T(8,128)(2,1)S(1)} %bitcast.188), channel_id=1, source_target_pairs={{0,4},{4,0},{1,5},{5,1},{2,6},{6,2},{3,7},{7,3},{8,12},{12,8},{9,1... | collective-permute-start | bytes 884744 | tf_op jit(solution)/shard_map/ppermute | solution.py:41
  22.1 25.9 %collective-permute-start.5 = (bf16[2,16,1024]{2,1,0:T(8,128)(2,1)S(1)}, bf16[2,16,1024]{2,1,0:T(8,128)(2,1)S(1)}, u32[]{:S(2)}, u32[]{:S(2)}) collective-permute-start(bf16[2,16,1024]{2,1,0:T(8,128)(2,1)S(1)} %bitcast.241), channel_id=1, source_target_pairs={{0,12},{2,14},{4,16},{6,18},{8,20},{10,22},{12,24},{14,26},{16,28}... | collective-permute-start | bytes 196616 | tf_op jit(solution)/shard_map/ppermute | solution.py:41
  48.0 5.5 %collective-permute-start.6 = (bf16[2,16,1024]{2,1,0:T(8,128)(2,1)S(1)}, bf16[2,16,1024]{2,1,0:T(8,128)(2,1)S(1)}, u32[]{:S(2)}, u32[]{:S(2)}) collective-permute-start(bf16[2,16,1024]{2,1,0:T(8,128)(2,1)S(1)} %bitcast.239), channel_id=1, source_target_pairs={{0,14},{2,16},{4,18},{6,20},{8,22},{10,24},{12,26},{14,28},{16,30}... | collective-permute-start | bytes 196616 | tf_op jit(solution)/shard_map/ppermute | solution.py:41
  54.4 27.0 %collective-permute-start.11 = (bf16[128,1024]{1,0:T(8,128)(2,1)S(1)}, bf16[128,1024]{1,0:T(8,128)(2,1)S(1)}, u32[]{:S(2)}, u32[]{:S(2)}) collective-permute-start(bf16[128,1024]{1,0:T(8,128)(2,1)S(1)} %reshape.303), channel_id=1, source_target_pairs={{0,8},{8,16},{16,24},{24,0},{1,9},{9,17},{17,25},{25,1},{2,10},{10... | collective-permute-start | bytes 786440 | tf_op jit(solution)/shard_map/ppermute | solution.py:41
  54.4 26.9 %collective-permute-start.12 = (bf16[128,1024]{1,0:T(8,128)(2,1)S(1)}, bf16[128,1024]{1,0:T(8,128)(2,1)S(1)}, u32[]{:S(2)}, u32[]{:S(2)}) collective-permute-start(bf16[128,1024]{1,0:T(8,128)(2,1)S(1)} %reshape.303), channel_id=1, source_target_pairs={{0,16},{8,24},{16,0},{24,8},{1,17},{9,25},{17,1},{25,9},{2,18},{10... | collective-permute-start | bytes 786440 | tf_op jit(solution)/shard_map/ppermute | solution.py:41
  56.0 25.3 %collective-permute-start.13 = (bf16[128,1024]{1,0:T(8,128)(2,1)S(1)}, bf16[128,1024]{1,0:T(8,128)(2,1)S(1)}, u32[]{:S(2)}, u32[]{:S(2)}) collective-permute-start(bf16[128,1024]{1,0:T(8,128)(2,1)S(1)} %reshape.303), channel_id=1, source_target_pairs={{0,24},{8,0},{16,8},{24,16},{1,25},{9,1},{17,9},{25,17},{2,26},{10... | collective-permute-start | bytes 786440 | tf_op jit(solution)/shard_map/ppermute | solution.py:41
  57.7 23.7 %collective-permute-start.14 = (bf16[128,1024]{1,0:T(8,128)(2,1)S(1)}, bf16[128,1024]{1,0:T(8,128)(2,1)S(1)}, u32[]{:S(2)}, u32[]{:S(2)}) collective-permute-start(bf16[128,1024]{1,0:T(8,128)(2,1)S(1)} %reshape.303), channel_id=1, source_target_pairs={{0,1},{1,0},{2,3},{3,2},{4,5},{5,4},{6,7},{7,6},{8,9},{9,8},{10,11... | collective-permute-start | bytes 786440 | tf_op jit(solution)/shard_map/ppermute | solution.py:41
  58.9 8.1 %collective-permute-start.15 = (bf16[128,1152]{1,0:T(8,128)(2,1)S(1)}, bf16[128,1152]{1,0:T(8,128)(2,1)S(1)}, u32[]{:S(2)}, u32[]{:S(2)}) collective-permute-start(bf16[128,1152]{1,0:T(8,128)(2,1)S(1)} %collective-permute-done.7), channel_id=1, source_target_pairs={{0,4},{4,0},{1,5},{5,1},{2,6},{6,2},{3,7},{7,3},{8,12},{12,8},{9,1... | collective-permute-start | bytes 884744 | tf_op jit(solution)/shard_map/ppermute | solution.py:41
  61.9 22.7 %copy-start = (bf16[2048,128]{1,0:T(8,128)(2,1)S(1)}, bf16[2048,128]{1,0:T(8,128)(2,1)}, u32[]{:S(2)}) copy-start(bf16[2048,128]{1,0:T(8,128)(2,1)} %refs_0_.1) | copy-start | bytes 1572868
  67.1 7.2 %collective-permute-start.16 = (bf16[128,1152]{1,0:T(8,128)(2,1)S(1)}, bf16[128,1152]{1,0:T(8,128)(2,1)S(1)}, u32[]{:S(2)}, u32[]{:S(2)}) collective-permute-start(bf16[128,1152]{1,0:T(8,128)(2,1)S(1)} %collective-permute-done.8), channel_id=1, source_target_pairs={{0,4},{4,0},{1,5},{5,1},{2,6},{6,2},{3,7},{7,3},{8,12},{12,8},{9,1... | collective-permute-start | bytes 884744 | tf_op jit(solution)/shard_map/ppermute | solution.py:41
  74.3 6.3 %collective-permute-start.17 = (bf16[128,1152]{1,0:T(8,128)(2,1)S(1)}, bf16[128,1152]{1,0:T(8,128)(2,1)S(1)}, u32[]{:S(2)}, u32[]{:S(2)}) collective-permute-start(bf16[128,1152]{1,0:T(8,128)(2,1)S(1)} %collective-permute-done.9), channel_id=1, source_target_pairs={{0,4},{4,0},{1,5},{5,1},{2,6},{6,2},{3,7},{7,3},{8,12},{12,8},{9,1... | collective-permute-start | bytes 884744 | tf_op jit(solution)/shard_map/ppermute | solution.py:41
  81.4 6.0 %collective-permute-start.19 = (bf16[4,128,1152]{2,1,0:T(8,128)(2,1)}, bf16[4,128,1152]{2,1,0:T(8,128)(2,1)}, u32[]{:S(2)}, u32[]{:S(2)}) collective-permute-start(bf16[4,128,1152]{2,1,0:T(8,128)(2,1)} %bitcast_dynamic-update-slice_fusion), channel_id=1, source_target_pairs={{0,2},{2,0},{1,3},{3,1},{4,6},{6,4},{5,7},{7,5},{8,10},{10,8},{9,1... | collective-permute-start | bytes 3538952 | tf_op jit(solution)/shard_map/ppermute | solution.py:41
  84.6 4.5 %collective-permute-start.20 = (bf16[4,128,1152]{2,1,0:T(8,128)(2,1)}, bf16[4,128,1152]{2,1,0:T(8,128)(2,1)}, u32[]{:S(2)}, u32[]{:S(2)}) collective-permute-start(bf16[4,128,1152]{2,1,0:T(8,128)(2,1)} %bitcast_dynamic-update-slice_fusion.4), channel_id=1, source_target_pairs={{0,2},{2,0},{1,3},{3,1},{4,6},{6,4},{5,7},{7,5},{8,10},{10,8},{9,1... | collective-permute-start | bytes 3538952 | tf_op jit(solution)/shard_map/ppermute | solution.py:41
  84.6 26.0 %collective-permute-start.21 = (bf16[2048,128]{1,0:T(8,128)(2,1)S(1)}, bf16[2048,128]{1,0:T(8,128)(2,1)S(1)}, u32[]{:S(2)}, u32[]{:S(2)}) collective-permute-start(bf16[2048,128]{1,0:T(8,128)(2,1)S(1)} %copy-done), channel_id=1, source_target_pairs={{0,16},{16,0},{1,17},{17,1},{2,18},{18,2},{3,19},{19,3},{4,20},{20... | collective-permute-start | bytes 1572872 | tf_op jit(solution)/shard_map/ppermute | solution.py:41
  85.5 25.1 %collective-permute-start.22 = (bf16[2048,128]{1,0:T(8,128)(2,1)S(1)}, bf16[2048,128]{1,0:T(8,128)(2,1)S(1)}, u32[]{:S(2)}, u32[]{:S(2)}) collective-permute-start(bf16[2048,128]{1,0:T(8,128)(2,1)S(1)} %copy-done), channel_id=1, source_target_pairs={{0,4},{4,0},{1,5},{5,1},{2,6},{6,2},{3,7},{7,3},{8,12},{12,8},{9,1... | collective-permute-start | bytes 1572872 | tf_op jit(solution)/shard_map/ppermute | solution.py:41
  86.1 64.5 %collective-permute-start.31 = (bf16[2048,128]{1,0:T(8,128)(2,1)S(1)}, bf16[2048,128]{1,0:T(8,128)(2,1)S(1)}, u32[]{:S(2)}, u32[]{:S(2)}) collective-permute-start(bf16[2048,128]{1,0:T(8,128)(2,1)S(1)} %copy-done), channel_id=1, source_target_pairs={{0,2},{2,0},{1,3},{3,1},{4,6},{6,4},{5,7},{7,5},{8,10},{10,8},{9,1... | collective-permute-start | bytes 1572872 | tf_op jit(solution)/shard_map/ppermute | solution.py:41
  87.4 23.2 %collective-permute-start.18 = (bf16[3,128,1024]{2,1,0:T(8,128)(2,1)S(1)}, bf16[3,128,1024]{2,1,0:T(8,128)(2,1)S(1)}, u32[]{:S(2)}, u32[]{:S(2)}) collective-permute-start(bf16[3,128,1024]{2,1,0:T(8,128)(2,1)S(1)} %pad_maximum_fusion.10), channel_id=1, source_target_pairs={{0,1},{1,0},{2,3},{3,2},{4,5},{5,4},{6,7},{7,6},{8,9},{9,8},{10,11... | collective-permute-start | bytes 2359304 | tf_op jit(solution)/shard_map/ppermute | solution.py:41
  110.6 16.3 %collective-permute-start.26 = (bf16[2048,128]{1,0:T(8,128)(2,1)S(1)}, bf16[2048,128]{1,0:T(8,128)(2,1)S(1)}, u32[]{:S(2)}, u32[]{:S(2)}) collective-permute-start(bf16[2048,128]{1,0:T(8,128)(2,1)S(1)} %collective-permute-done.21.refs_4_), channel_id=1, source_target_pairs={{0,4},{4,0},{1,5},{5,1},{2,6},{6,2},{3,7},{7,3},{8,12},{12,8},{9,1... | collective-permute-start | bytes 1572872 | tf_op jit(solution)/shard_map/ppermute | solution.py:41
  113.8 6.3 %collective-permute-start.23 = (bf16[128,640]{1,0:T(8,128)(2,1)S(1)}, bf16[128,640]{1,0:T(8,128)(2,1)S(1)}, u32[]{:S(2)}, u32[]{:S(2)}) collective-permute-start(bf16[128,640]{1,0:T(8,128)(2,1)S(1)} %get-tuple-element.145), channel_id=1, source_target_pairs={{0,24},{8,0},{16,8},{24,16},{1,25},{9,1},{17,9},{25,17},{2,26},{10... | collective-permute-start | bytes 491528 | tf_op jit(solution)/shard_map/ppermute | solution.py:41
  113.9 13.0 %collective-permute-start.24 = (bf16[128,640]{1,0:T(8,128)(2,1)S(1)}, bf16[128,640]{1,0:T(8,128)(2,1)S(1)}, u32[]{:S(2)}, u32[]{:S(2)}) collective-permute-start(bf16[128,640]{1,0:T(8,128)(2,1)S(1)} %get-tuple-element.144), channel_id=1, source_target_pairs={{0,16},{8,24},{16,0},{24,8},{1,17},{9,25},{17,1},{25,9},{2,18},{10... | collective-permute-start | bytes 491528 | tf_op jit(solution)/shard_map/ppermute | solution.py:41
  114.0 13.0 %collective-permute-start.25 = (bf16[128,640]{1,0:T(8,128)(2,1)S(1)}, bf16[128,640]{1,0:T(8,128)(2,1)S(1)}, u32[]{:S(2)}, u32[]{:S(2)}) collective-permute-start(bf16[128,640]{1,0:T(8,128)(2,1)S(1)} %get-tuple-element.143), channel_id=1, source_target_pairs={{0,8},{8,16},{16,24},{24,0},{1,9},{9,17},{17,25},{25,1},{2,10},{10... | collective-permute-start | bytes 491528 | tf_op jit(solution)/shard_map/ppermute | solution.py:41
  120.0 30.8 %collective-permute-start.33 = (bf16[2048,128]{1,0:T(8,128)(2,1)S(1)}, bf16[2048,128]{1,0:T(8,128)(2,1)}, u32[]{:S(2)}, u32[]{:S(2)}) collective-permute-start(bf16[2048,128]{1,0:T(8,128)(2,1)S(1)} %collective-permute-done.21.refs_4_), channel_id=1, source_target_pairs={{0,2},{2,0},{1,3},{3,1},{4,6},{6,4},{5,7},{7,5},{8,10},{10,8},{9,1... | collective-permute-start | bytes 1572872 | tf_op jit(solution)/shard_map/ppermute | solution.py:41
  127.0 20.3 %collective-permute-start.27 = (bf16[128,512]{1,0:T(8,128)(2,1)S(1)}, bf16[128,512]{1,0:T(8,128)(2,1)S(1)}, u32[]{:S(2)}, u32[]{:S(2)}) collective-permute-start(bf16[128,512]{1,0:T(8,128)(2,1)S(1)} %get-tuple-element.157), channel_id=1, source_target_pairs={{0,8},{8,16},{16,24},{24,0},{1,9},{9,17},{17,25},{25,1},{2,10},{10... | collective-permute-start | bytes 393224 | tf_op jit(solution)/shard_map/ppermute | solution.py:41
  129.7 19.0 %collective-permute-start.28 = (bf16[128,512]{1,0:T(8,128)(2,1)S(1)}, bf16[128,512]{1,0:T(8,128)(2,1)S(1)}, u32[]{:S(2)}, u32[]{:S(2)}) collective-permute-start(bf16[128,512]{1,0:T(8,128)(2,1)S(1)} %get-tuple-element.156), channel_id=1, source_target_pairs={{0,16},{8,24},{16,0},{24,8},{1,17},{9,25},{17,1},{25,9},{2,18},{10... | collective-permute-start | bytes 393224 | tf_op jit(solution)/shard_map/ppermute | solution.py:41
  131.7 17.1 %collective-permute-start.29 = (bf16[128,512]{1,0:T(8,128)(2,1)S(1)}, bf16[128,512]{1,0:T(8,128)(2,1)S(1)}, u32[]{:S(2)}, u32[]{:S(2)}) collective-permute-start(bf16[128,512]{1,0:T(8,128)(2,1)S(1)} %get-tuple-element.155), channel_id=1, source_target_pairs={{0,24},{8,0},{16,8},{24,16},{1,25},{9,1},{17,9},{25,17},{2,26},{10... | collective-permute-start | bytes 393224 | tf_op jit(solution)/shard_map/ppermute | solution.py:41
  147.3 3.5 %collective-permute-start.32 = (bf16[2048,128]{1,0:T(8,128)(2,1)S(1)}, bf16[2048,128]{1,0:T(8,128)(2,1)}, u32[]{:S(2)}, u32[]{:S(2)}) collective-permute-start(bf16[2048,128]{1,0:T(8,128)(2,1)S(1)} %collective-permute-done.22.refs_2_), channel_id=1, source_target_pairs={{0,2},{2,0},{1,3},{3,1},{4,6},{6,4},{5,7},{7,5},{8,10},{10,8},{9,1... | collective-permute-start | bytes 1572872 | tf_op jit(solution)/shard_map/ppermute | solution.py:41
  148.7 2.4 %collective-permute-start.34 = (bf16[2048,128]{1,0:T(8,128)(2,1)S(1)}, bf16[2048,128]{1,0:T(8,128)(2,1)}, u32[]{:S(2)}, u32[]{:S(2)}) collective-permute-start(bf16[2048,128]{1,0:T(8,128)(2,1)S(1)} %collective-permute-done.26.refs_6_), channel_id=1, source_target_pairs={{0,2},{2,0},{1,3},{3,1},{4,6},{6,4},{5,7},{7,5},{8,10},{10,8},{9,1... | collective-permute-start | bytes 1572872 | tf_op jit(solution)/shard_map/ppermute | solution.py:41
  150.4 13.2 %collective-permute-start.30 = (bf16[128,2048]{1,0:T(8,128)(2,1)S(1)}, bf16[128,2048]{1,0:T(8,128)(2,1)}, u32[]{:S(2)}, u32[]{:S(2)}) collective-permute-start(bf16[128,2048]{1,0:T(8,128)(2,1)S(1)} %get-tuple-element.138.own_ref), channel_id=1, source_target_pairs={{0,8},{8,0},{1,9},{9,1},{2,10},{10,2},{3,11},{11,3},{4,12},{12,4},... | collective-permute-start | bytes 1572872 | tf_op jit(solution)/shard_map/ppermute | solution.py:41
  150.6 16.3 %collective-permute-start.36 = (f32[128]{0:T(128)S(1)}, f32[128]{0:T(128)S(1)}, u32[]{:S(2)}, u32[]{:S(2)}) collective-permute-start(f32[128]{0:T(128)S(1)} %get-tuple-element.137), channel_id=1, source_target_pairs={{0,1},{1,0},{2,3},{3,2},{4,5},{5,4},{6,7},{7,6},{8,9},{9,8},{10,11... | collective-permute-start | bytes 1544 | tf_op jit(solution)/shard_map/ppermute | solution.py:41
  166.6 6.6 %collective-permute-start.35 = (bf16[256,512]{1,0:T(8,128)(2,1)S(1)}, bf16[256,512]{1,0:T(8,128)(2,1)S(1)}, u32[]{:S(2)}, u32[]{:S(2)}) collective-permute-start(bf16[256,512]{1,0:T(8,128)(2,1)S(1)} %fusion.14), channel_id=1, source_target_pairs={{0,1},{1,0},{2,3},{3,2},{4,5},{5,4},{6,7},{7,6},{8,9},{9,8},{10,11... | collective-permute-start | bytes 786440 | tf_op jit(solution)/shard_map/ppermute | solution.py:41
  166.9 2.5 %collective-permute-start.37 = (f32[128]{0:T(128)S(1)}, f32[128]{0:T(128)S(1)}, u32[]{:S(2)}, u32[]{:S(2)}) collective-permute-start(f32[128]{0:T(128)S(1)} %add_rsqrt_fusion), channel_id=1, source_target_pairs={{0,8},{8,0},{1,9},{9,1},{2,10},{10,2},{3,11},{11,3},{4,12},{12,4},... | collective-permute-start | bytes 1544 | tf_op jit(solution)/shard_map/ppermute | solution.py:41
  173.3 3.9 %collective-permute-start.38 = (bf16[128,512]{1,0:T(8,128)(2,1)S(1)}, bf16[128,512]{1,0:T(8,128)(2,1)S(1)}, u32[]{:S(2)}, u32[]{:S(2)}) collective-permute-start(bf16[128,512]{1,0:T(8,128)(2,1)S(1)} %slice.241), channel_id=1, source_target_pairs={{0,8},{8,0},{1,9},{9,1},{2,10},{10,2},{3,11},{11,3},{4,12},{12,4},... | collective-permute-start | bytes 393224 | tf_op jit(solution)/shard_map/ppermute | solution.py:41
  178.2 9.1 %collective-permute-start.39 = (bf16[2,16,1024]{2,1,0:T(8,128)(2,1)S(1)}, bf16[2,16,1024]{2,1,0:T(8,128)(2,1)S(1)}, u32[]{:S(2)}, u32[]{:S(2)}) collective-permute-start(bf16[2,16,1024]{2,1,0:T(8,128)(2,1)S(1)} %bitcast.244), channel_id=1, source_target_pairs={{0,30},{2,0},{4,2},{6,4},{8,6},{10,8},{12,10},{14,12},{16,14},{18,... | collective-permute-start | bytes 196616 | tf_op jit(solution)/shard_map/ppermute | solution.py:41
  181.6 5.7 %collective-permute-start.40 = (bf16[2,16,1024]{2,1,0:T(8,128)(2,1)S(1)}, bf16[2,16,1024]{2,1,0:T(8,128)(2,1)S(1)}, u32[]{:S(2)}, u32[]{:S(2)}) collective-permute-start(bf16[2,16,1024]{2,1,0:T(8,128)(2,1)S(1)} %bitcast.243), channel_id=1, source_target_pairs={{0,28},{2,30},{4,0},{6,2},{8,4},{10,6},{12,8},{14,10},{16,12},{18,... | collective-permute-start | bytes 196616 | tf_op jit(solution)/shard_map/ppermute | solution.py:41
  182.4 9.1 %collective-permute-start.41 = (bf16[2,16,1024]{2,1,0:T(8,128)(2,1)S(1)}, bf16[2,16,1024]{2,1,0:T(8,128)(2,1)S(1)}, u32[]{:S(2)}, u32[]{:S(2)}) collective-permute-start(bf16[2,16,1024]{2,1,0:T(8,128)(2,1)S(1)} %bitcast.232), channel_id=1, source_target_pairs={{0,26},{2,28},{4,30},{6,0},{8,2},{10,4},{12,6},{14,8},{16,10},{18,... | collective-permute-start | bytes 196616 | tf_op jit(solution)/shard_map/ppermute | solution.py:41
  182.9 8.8 %collective-permute-start.42 = (bf16[2,16,1024]{2,1,0:T(8,128)(2,1)S(1)}, bf16[2,16,1024]{2,1,0:T(8,128)(2,1)S(1)}, u32[]{:S(2)}, u32[]{:S(2)}) collective-permute-start(bf16[2,16,1024]{2,1,0:T(8,128)(2,1)S(1)} %bitcast.234), channel_id=1, source_target_pairs={{0,24},{2,26},{4,28},{6,30},{8,0},{10,2},{12,4},{14,6},{16,8},{18,... | collective-permute-start | bytes 196616 | tf_op jit(solution)/shard_map/ppermute | solution.py:41
  184.2 7.5 %collective-permute-start.43 = (bf16[2,16,1024]{2,1,0:T(8,128)(2,1)S(1)}, bf16[2,16,1024]{2,1,0:T(8,128)(2,1)S(1)}, u32[]{:S(2)}, u32[]{:S(2)}) collective-permute-start(bf16[2,16,1024]{2,1,0:T(8,128)(2,1)S(1)} %bitcast.236), channel_id=1, source_target_pairs={{0,22},{2,24},{4,26},{6,28},{8,30},{10,0},{12,2},{14,4},{16,6},{18... | collective-permute-start | bytes 196616 | tf_op jit(solution)/shard_map/ppermute | solution.py:41
  187.3 4.7 %collective-permute-start.44 = (bf16[2,16,1024]{2,1,0:T(8,128)(2,1)S(1)}, bf16[2,16,1024]{2,1,0:T(8,128)(2,1)S(1)}, u32[]{:S(2)}, u32[]{:S(2)}) collective-permute-start(bf16[2,16,1024]{2,1,0:T(8,128)(2,1)S(1)} %bitcast.238), channel_id=1, source_target_pairs={{0,20},{2,22},{4,24},{6,26},{8,28},{10,30},{12,0},{14,2},{16,4},{1... | collective-permute-start | bytes 196616 | tf_op jit(solution)/shard_map/ppermute | solution.py:41
  187.4 9.7 %collective-permute-start.45 = (bf16[2,16,1024]{2,1,0:T(8,128)(2,1)S(1)}, bf16[2,16,1024]{2,1,0:T(8,128)(2,1)S(1)}, u32[]{:S(2)}, u32[]{:S(2)}) collective-permute-start(bf16[2,16,1024]{2,1,0:T(8,128)(2,1)S(1)} %bitcast.230), channel_id=1, source_target_pairs={{0,18},{2,20},{4,22},{6,24},{8,26},{10,28},{12,30},{14,0},{16,2},{... | collective-permute-start | bytes 196616 | tf_op jit(solution)/shard_map/ppermute | solution.py:41
  (19 other events, 183.3 us)

commit v3 on v2

--- a/solution.py
+++ b/solution.py
@@ -117,7 +117,9 @@
     kept = pick(row // draft, kept_ref)
     masks_ref[0] = (step < kept).astype(F32)
     masks_ref[1] = (column == row - step + kept - 1).astype(F32)
-    masks_ref[2] = ((row // draft == column // draft) & (column <= row)).astype(F32)
+    same = row // draft == column // draft
+    masks_ref[2] = (same & (column <= row)).astype(F32)
+    masks_ref[3] = (same & (column >= row)).astype(F32)
 
 
 def series_tables(conv_of, kept_count, per_dev, draft, hist_pad):
@@ -129,7 +131,7 @@
         out_specs=[pl.BlockSpec(memory_space=pltpu.VMEM)] * 2,
         out_shape=[
             jax.ShapeDtypeStruct(((KCONV - 1) * rows + hist_pad, rows + hist_pad), BF16),
-            jax.ShapeDtypeStruct((3, rows, rows), F32),
+            jax.ShapeDtypeStruct((4, rows, rows), F32),
         ],
     )(conv_of, kept_count)
 
@@ -149,11 +151,7 @@
     return total / (1.0 + jnp.exp(-total))
 
 
-def mixer_kernel(
-    sizes,
-    order_ref,
-    *refs,
-):
+def mixer_kernel(sizes, order_ref, *refs):
     chunks, per_dev, draft, heads, head_dim, state_width = sizes
     x_refs, aux_refs, refs = refs[:chunks], refs[chunks : 2 * chunks], refs[2 * chunks :]
     (
@@ -168,22 +166,21 @@
         step_ref,
         state_ref,
         y_ref,
-        new_state_ref,
+        picked_ref,
+        b_ref,
+        end_ref,
         conv_ref,
         conv_state_ref,
-        b_scr,
         c_scr,
         scores_scr,
         log_scr,
-        sel_scr,
-        end_scr,
         log_t_scr,
         step_t_scr,
+        sel_t_scr,
     ) = refs
     rows = per_dev * draft
     width = heads * head_dim
     group = pl.program_id(0)
-    causal = masks_ref[2]
     edges = moves_ref[(KCONV - 1) * rows :, :]
 
     @pl.when(group == 0)
@@ -196,80 +193,125 @@
         active = convolve(series, maps, taps_state_ref[...], moves_ref)
         conv_state_ref[...] = jnp.dot(edges, series, preferred_element_type=F32).astype(BF16)
         b_rows, c_rows = active[:, :state_width], active[:, state_width:]
-        b_scr[...] = b_rows
-        c_scr[...] = c_rows
+        c_high, c_low = split_pair(c_rows.T)
+        c_scr[:state_width, :rows] = c_high
+        c_scr[:state_width, rows:] = c_low
+        c_scr[state_width:, :rows] = c_high
+        c_scr[state_width:, rows:] = jnp.zeros_like(c_low)
+        b_ref[...] = b_rows
         scores_scr[...] = lax.dot_general(
-            c_rows, b_rows, (((1,), (1,)), ((), ())), precision=HIGH, preferred_element_type=F32
-        ) * causal
+            b_rows, c_rows, (((1,), (1,)), ((), ())), precision=HIGH, preferred_element_type=F32
+        ) * masks_ref[3]
         raw = aux[:, 2 * state_width :] + step_ref[:1, :]
         step_size = jnp.maximum(raw, 0.0) + jnp.log1p(jnp.exp(-jnp.abs(raw)))
-        log_decay = jnp.dot(causal, step_size * step_ref[1:2, :], precision=HIGH, preferred_element_type=F32)
+        log_decay = jnp.dot(
+            masks_ref[2], step_size * step_ref[1:2, :], precision=HIGH, preferred_element_type=F32
+        )
         end = jnp.dot(masks_ref[1], log_decay, precision=HIGH, preferred_element_type=F32)
         kept = masks_ref[0] > 0.0
         chosen = jnp.where(kept, jnp.exp(jnp.where(kept, end - log_decay, 0.0)), 0.0) * step_size
-        decay_end = jnp.exp(end)
+        end_ref[...] = jnp.exp(end)
         for chunk in range(chunks):
-            part = slice(chunk * heads, (chunk + 1) * heads)
-            log_scr[chunk] = log_decay[:, part]
-            sel_scr[chunk] = chosen[:, part]
-            end_scr[chunk] = decay_end[:, part]
+            log_scr[chunk] = log_decay[:, chunk * heads : (chunk + 1) * heads]
         log_t_scr[...] = log_decay.T
         step_t_scr[...] = step_size.T
+        sel_t_scr[...] = chosen.T
 
     x_rows = x_refs[0][...]
     for chunk in range(1, chunks):
         x_rows = jnp.where(order_ref[group] == chunk, x_refs[chunk][...], x_rows)
     series = jnp.concatenate([x_rows, hist_ref[...]], axis=0)
-    active = convolve(series, x_rows.astype(F32), taps_ref[...], moves_ref)
+    active = convolve(series, x_rows.astype(F32), taps_ref[...], moves_ref).T
     conv_ref[...] = jnp.dot(edges, series, preferred_element_type=F32).astype(BF16)
-    scores = scores_scr[...]
     log_here = log_scr[group]
-    sel_here = sel_scr[group]
-    end_here = end_scr[group]
-    within, growth, picks = [], [], []
+    slot_of = lax.broadcasted_iota(jnp.int32, (width, rows), 1) // draft
+    c_all = c_scr[...]
+    carried = jnp.zeros((width, rows), F32)
+    for slot in range(per_dev):
+        high, low = split_pair(state_ref[slot].reshape(width, state_width))
+        read = jnp.dot(jnp.concatenate([high, low], axis=1), c_all, preferred_element_type=F32)
+        carried = jnp.where(slot_of == slot, read[:, :rows] + read[:, rows:], carried)
+    outputs, picked = [], []
     for head in range(heads):
-        lanes = slice(head * head_dim, (head + 1) * head_dim)
+        part = slice(head * head_dim, (head + 1) * head_dim)
         at = group * heads + head
         log_row = log_t_scr[pl.ds(at, 1), :]
-        step_row = step_t_scr[pl.ds(at, 1), :]
-        spread = jnp.where(causal > 0.0, log_here[:, head : head + 1] - log_row, -1e30)
-        weight = jnp.exp(spread) * (scores * step_row)
-        x_head = active[:, lanes]
-        within.append(
-            jnp.dot(weight.astype(BF16), x_head.astype(BF16), preferred_element_type=F32)
-            + skip_ref[at] * x_head
-        )
-        growth.append(jnp.broadcast_to(jnp.exp(log_here[:, head : head + 1]), (rows, head_dim)))
-        picks.append(jnp.broadcast_to(sel_here[:, head : head + 1], (rows, head_dim)))
-    within = jnp.concatenate(within, axis=1)
-    growth = jnp.concatenate(growth, axis=1)
-    picked = active * jnp.concatenate(picks, axis=1)
-    carried = []
-    for slot in range(per_dev):
-        part = slice(slot * draft, (slot + 1) * draft)
-        state = state_ref[slot].reshape(width, state_width)
-        carried.append(
-            lax.dot_general(
-                c_scr[part, :].astype(BF16),
-                state.astype(BF16),
-                (((1,), (1,)), ((), ())),
-                preferred_element_type=F32,
-            )
-        )
-        x_high, x_low = split_pair(picked[part])
-        b_high, b_low = split_pair(b_scr[part, :])
-        update = lax.dot_general(
-            jnp.concatenate([x_high, x_low, x_high], axis=0),
-            jnp.concatenate([b_high, b_high, b_low], axis=0),
-            (((0,), (0,)), ((), ())),
+        spread = jnp.where(masks_ref[3] > 0.0, log_row - log_here[:, head : head + 1], -1e30)
+        weight = (jnp.exp(spread) * scores_scr[...]).astype(BF16)
+        x_head = active[part]
+        within = jnp.dot(
+            (x_head * step_t_scr[pl.ds(at, 1), :]).astype(BF16), weight, preferred_element_type=F32
+        )
+        outputs.append(within + jnp.exp(log_row) * carried[part] + skip_ref[at] * x_head)
+        picked.append(x_head * sel_t_scr[pl.ds(at, 1), :])
+    y_ref[...] = jnp.concatenate(outputs, axis=0).T.astype(BF16)
+    x_high, x_low = split_pair(jnp.concatenate(picked, axis=0))
+    picked_ref[:, :rows] = x_high
+    picked_ref[:, rows:] = x_low
+
+
+def update_kernel(sizes, picked_ref, b_ref, end_ref, state_ref, new_state_ref, b_scr, end_scr):
+    steps, per_dev, draft, heads, head_dim, state_width = sizes
+    rows = per_dev * draft
+    group = pl.program_id(0)
+
+    @pl.when(group == 0)
+    def prepare():
+        slot = lax.broadcasted_iota(jnp.int32, (rows, state_width), 0) // draft
+        for at in range(per_dev):
+            high, low = split_pair(jnp.where(slot == at, b_ref[...], 0.0))
+            lanes = slice(at * state_width, (at + 1) * state_width)
+            b_scr[:rows, lanes] = high
+            b_scr[rows : 2 * rows, lanes] = high
+            b_scr[2 * rows :, lanes] = low
+        for step in range(steps):
+            end_scr[step] = end_ref[:, step * heads : (step + 1) * heads]
+
+    end_here = end_scr[group]
+    picked = jnp.concatenate([picked_ref[...], picked_ref[:, :rows]], axis=1)
+    for pair in range(0, per_dev, 2):
+        update = jnp.dot(
+            picked,
+            b_scr[:, pair * state_width : (pair + 2) * state_width],
             preferred_element_type=F32,
         )
-        for head in range(heads):
-            keep = end_here[slot * draft : slot * draft + 1, head : head + 1]
-            lanes = slice(head * head_dim, (head + 1) * head_dim)
-            new_state_ref[slot, head] = keep * state[lanes] + update[lanes]
-    carried = jnp.concatenate(carried, axis=0)
-    y_ref[...] = (within + growth * carried).astype(BF16)
+        for slot in range(pair, pair + 2):
+            lanes = slice((slot - pair) * state_width, (slot - pair + 1) * state_width)
+            for head in range(heads):
+                part = slice(head * head_dim, (head + 1) * head_dim)
+                keep = end_here[slot * draft : slot * draft + 1, head : head + 1]
+                new_state_ref[slot, head] = keep * state_ref[slot, head] + update[part, lanes]
+
+
+def update_states(picked, b_rows, ends, state_pool):
+    per_dev, all_heads, head_dim, state_width = state_pool.shape
+    rows = b_rows.shape[0]
+    steps = 4
+    heads = all_heads // steps
+    sizes = (steps, per_dev, rows // per_dev, heads, head_dim, state_width)
+    state_spec = pl.BlockSpec((per_dev, heads, head_dim, state_width), lambda group: (0, group, 0, 0))
+    return pl.pallas_call(
+        lambda *refs: update_kernel(sizes, *refs),
+        grid=(steps,),
+        in_specs=[
+            pl.BlockSpec((heads * head_dim, 2 * rows), lambda group: (group, 0)),
+            pl.BlockSpec(b_rows.shape, lambda group: (0, 0)),
+            pl.BlockSpec(ends.shape, lambda group: (0, 0)),
+            state_spec,
+        ],
+        out_specs=state_spec,
+        scratch_shapes=[
+            pltpu.VMEM((3 * rows, per_dev * state_width), BF16),
+            pltpu.VMEM((steps, rows, heads), F32),
+        ],
+        out_shape=jax.ShapeDtypeStruct(state_pool.shape, F32),
+        compiler_params=pltpu.CompilerParams(vmem_limit_bytes=VMEM_LIMIT),
+        cost_estimate=pl.CostEstimate(
+            flops=64 * rows * rows * all_heads * head_dim,
+            bytes_accessed=8 * state_pool.size,
+            transcendentals=0,
+        ),
+    )(picked, b_rows, ends, state_pool)
 
 
 def mix_requests(
@@ -331,17 +373,17 @@
         ],
         out_specs=[
             by_group(rows),
-            state_spec,
+            pl.BlockSpec((heads * head_dim, 2 * rows), lambda group, order_ref: (group, 0)),
+            pl.BlockSpec((rows, state_width), lambda group, order_ref: (0, 0)),
+            pl.BlockSpec((rows, step_lanes), lambda group, order_ref: (0, 0)),
             by_group(hist_pad),
             pl.BlockSpec((hist_pad, 2 * state_width), lambda group, order_ref: (0, 0)),
         ],
         scratch_shapes=[
-            pltpu.VMEM((rows, state_width), F32),
-            pltpu.VMEM((rows, state_width), F32),
+            pltpu.VMEM((2 * state_width, 2 * rows), BF16),
             pltpu.VMEM((rows, rows), F32),
             pltpu.VMEM((chunks, rows, heads), F32),
-            pltpu.VMEM((chunks, rows, heads), F32),
-            pltpu.VMEM((chunks, rows, heads), F32),
+            pltpu.VMEM((step_lanes, rows), F32),
             pltpu.VMEM((step_lanes, rows), F32),
             pltpu.VMEM((step_lanes, rows), F32),
         ],
@@ -351,7 +393,9 @@
         grid_spec=grid_spec,
         out_shape=(
             jax.ShapeDtypeStruct((rows, inner), BF16),
-            jax.ShapeDtypeStruct(state_pool.shape, F32),
+            jax.ShapeDtypeStruct((inner, 2 * rows), BF16),
+            jax.ShapeDtypeStruct((rows, state_width), F32),
+            jax.ShapeDtypeStruct((rows, step_lanes), F32),
             jax.ShapeDtypeStruct((hist_pad, inner), BF16),
             jax.ShapeDtypeStruct((hist_pad, 2 * state_width), BF16),
         ),
@@ -401,7 +445,7 @@
 
 
 def out_kernel(place_ref, own_ref, peer_ref, *refs):
-    weight_refs, out_ref = refs[:8], refs[8]
+    weight_refs, own_out_ref, both_out_ref = refs[:8], refs[8], refs[9]
     rows = own_ref.shape[0]
     both = jnp.concatenate([own_ref[...], peer_ref[...]], axis=0)
     for pair in range(4):
@@ -410,7 +454,11 @@
         for at in range(2):
             start = place_ref[(2 * pair + at) % 4] * LANES
             lanes = pl.ds(pl.multiple_of(start, LANES), LANES)
-            out_ref[pair // 2, :, lanes] = total[:, at * LANES : (at + 1) * LANES]
+            columns = slice(at * LANES, (at + 1) * LANES)
+            own_out_ref[pair // 2, :, lanes] = total[:rows, columns]
+            for group in range(2):
+                part = total[group * rows : (group + 1) * rows, columns]
+                both_out_ref[pair // 2, group, :, lanes] = part.astype(BF16)
 
 
 def project_out(own, peer, weights, place_of):
@@ -419,8 +467,11 @@
     return pl.pallas_call(
         out_kernel,
         in_specs=[pl.BlockSpec(memory_space=pltpu.SMEM)] + [whole] * 10,
-        out_specs=whole,
-        out_shape=jax.ShapeDtypeStruct((2, 2 * rows, 4 * LANES), F32),
+        out_specs=[whole, whole],
+        out_shape=[
+            jax.ShapeDtypeStruct((2, rows, 4 * LANES), F32),
+            jax.ShapeDtypeStruct((2, 2, rows, 4 * LANES), BF16),
+        ],
         compiler_params=pltpu.CompilerParams(vmem_limit_bytes=24 * 1024 * 1024),
         cost_estimate=QUICK,
     )(place_of, own, peer, *weights)
@@ -475,38 +526,45 @@
         owner_dev, state_page, conv_page, accepted, groups, per_dev, this_dev
     )
 
-    order = (jnp.arange(chunks, dtype=jnp.int32) - me) % chunks
-    home_chunk = (jnp.arange(chunks, dtype=jnp.int32) + me) % chunks
-    lane = jnp.arange(aux_lanes, dtype=jnp.int32)[None, :]
-    step_lanes = round_up(all_heads, LANES)
-    target = jnp.where(
-        lane < map_width,
-        home_chunk[:, None] * map_width + lane,
-        jnp.where(
-            lane < map_width + heads,
-            2 * state_width + home_chunk[:, None] * heads + lane - map_width,
-            -1,
-        ),
-    )
-    select = (
-        target[:, :, None] == jnp.arange(2 * state_width + step_lanes, dtype=jnp.int32)
-    ).astype(BF16)
-    tables = series_tables(conv_of, kept_count, per_dev, draft, hist_pad)
-    pad_rows = ((0, hist_pad - hist_rows), (0, 0))
-    history = jnp.pad(conv_pool_inner.reshape(hist_rows, inner), pad_rows)
-    history_state = jnp.pad(conv_pool_state.reshape(hist_rows, 2 * state_width), pad_rows)
-    pad_heads = ((0, 0), (0, step_lanes - all_heads))
-    steps = jnp.pad(jnp.stack([step_bias, -jnp.exp(decay_log)]), pad_heads)
-
-
     block = depth // groups
     columns = hidden_in.reshape(rows, fars, nears, sides, cores, block).transpose(0, 4, 3, 1, 2, 5)
     columns = columns.reshape(rows, splits, depth // splits)
     share = lax.dynamic_index_in_dim(columns, part, 1, keepdims=False)
     outgoing = one_hot_apply(send_table, share, (slots, draft, depth // splits))
-    incoming = [
-        rotate(outgoing[offset * CAP : (offset + 1) * CAP], RING, offset) for offset in range(WINDOW)
-    ]
+
+    def prepare(after):
+        conv_now, kept_now, pool_inner, pool_state, bias, rate = lax.optimization_barrier(
+            (conv_of, kept_count, conv_pool_inner, conv_pool_state, step_bias, decay_log, after)
+        )[:6]
+        order = (jnp.arange(chunks, dtype=jnp.int32) - me) % chunks
+        home_chunk = (jnp.arange(chunks, dtype=jnp.int32) + me) % chunks
+        lane = jnp.arange(aux_lanes, dtype=jnp.int32)[None, :]
+        step_lanes = round_up(all_heads, LANES)
+        target = jnp.where(
+            lane < map_width,
+            home_chunk[:, None] * map_width + lane,
+            jnp.where(
+                lane < map_width + heads,
+                2 * state_width + home_chunk[:, None] * heads + lane - map_width,
+                -1,
+            ),
+        )
+        select = (
+            target[:, :, None] == jnp.arange(2 * state_width + step_lanes, dtype=jnp.int32)
+        ).astype(BF16)
+        tables = series_tables(conv_now, kept_now, per_dev, draft, hist_pad)
+        pad_rows = ((0, hist_pad - hist_rows), (0, 0))
+        history = jnp.pad(pool_inner.reshape(hist_rows, inner), pad_rows)
+        history_state = jnp.pad(pool_state.reshape(hist_rows, 2 * state_width), pad_rows)
+        pad_heads = ((0, 0), (0, step_lanes - all_heads))
+        steps = jnp.pad(jnp.stack([bias, -jnp.exp(rate)]), pad_heads)
+        return order, select, tables, history, history_state, steps
+
+    def route(slots_out):
+        return [
+            rotate(slots_out[offset * CAP : (offset + 1) * CAP], RING, offset)
+            for offset in range(WINDOW)
+        ]
 
     packed_weight = jnp.concatenate(
         [
@@ -521,6 +579,8 @@
     width = split + lanes
     far, side, core = (lax.axis_index(name) for name in ("far", "side", "core"))
     if paired:
+        incoming = route(outgoing)
+        packed_weight, early = lax.optimization_barrier((packed_weight, incoming[: WINDOW - 2]))
         pieces = [
             rotate(
                 lax.dynamic_index_in_dim(packed_weight, (me + step) % chunks, 0, keepdims=False),
@@ -529,21 +589,21 @@
             )
             for step in range(chunks)
         ]
-        across = swap(pieces[0], "side")
-        incoming, pieces, across, select, history, history_state, steps, tables = (
-            lax.optimization_barrier(
-                (incoming, pieces, across, select, history, history_state, steps, tables)
-            )
+        side_own = swap(pieces[0], "side")
+        extras = prepare(early)
+        incoming, pieces, side_own, extras = lax.optimization_barrier(
+            (early + incoming[WINDOW - 2 :], pieces, side_own, extras)
         )
         owned = one_hot_apply(gather_table, jnp.concatenate(incoming), (rows, depth // splits))
         owned, pieces = lax.optimization_barrier((owned, pieces))
         rows_of = [rotate(owned, SLABS, step) for step in range(chunks)]
-        rows_peer = swap(owned, "mdl")
         slabs = [(me - step) % chunks for step in range(chunks)]
+        across = swap(jnp.stack(pieces[1:]), "side")
         held = place(pieces, slabs)
-        across = place([across] + [swap(piece, "side") for piece in pieces[1:]], slabs)
-        rows_of, rows_peer, across, held = lax.optimization_barrier((rows_of, rows_peer, across, held))
-        rows_rest = swap(jnp.stack(rows_of[1:]), "mdl")
+        rows_of, across, held = lax.optimization_barrier((rows_of, across, held))
+        across = place([side_own] + [across[at] for at in range(chunks - 1)], slabs)
+        own_rows = jnp.concatenate(rows_of)
+        peer_rows = swap(own_rows, "mdl")
         at_core, at_side, at_half = core == 0, side == 0, part == 0
         held_peer, across_peer = swap(held, "core"), swap(across, "core")
 
@@ -561,11 +621,9 @@
 
         packed_full, gate_full = full(slice(0, split)), full(slice(split, width))
         out_far, out_side = swap(out_weight, "far"), swap(out_weight, "side")
-        rows_rest, packed_full, gate_full, out_far, out_side = lax.optimization_barrier(
-            (rows_rest, packed_full, gate_full, out_far, out_side)
-        )
-        own_rows = jnp.concatenate(rows_of)
-        peer_rows = jnp.concatenate([rows_peer, rows_rest.reshape(-1, depth // splits)])
+        own_rows, peer_rows, packed_full, gate_full, out_far, out_side = lax.optimization_barrier(
+            (own_rows, peer_rows, packed_full, gate_full, out_far, out_side)
+        )
         all_rows = jnp.concatenate(
             [jnp.where(at_half, own_rows, peer_rows), jnp.where(at_half, peer_rows, own_rows)], axis=1
         )
@@ -581,6 +639,8 @@
         for column in (out_weight, out_side, out_far, out_across):
             out_columns += [column, swap(column, "core")]
     else:
+        incoming = route(outgoing)
+        extras = prepare(outgoing)
         owned = one_hot_apply(gather_table, jnp.concatenate(incoming), (rows, depth // splits))
         owned = lax.all_gather(owned, "mdl", axis=1, tiled=True)
         owned = jnp.concatenate([owned, swap(owned, "near")])
@@ -593,7 +653,8 @@
         gate = [value[:, split:] for value in total]
         out_columns = lax.all_gather(out_weight, RING, axis=1, tiled=True)
 
-    y_rows, new_states, conv_rows, conv_state_rows = mix_requests(
+    order, select, tables, history, history_state, steps = extras
+    y_rows, picked, b_rows, ends, conv_rows, conv_state_rows = mix_requests(
         packed,
         order,
         select,
@@ -617,24 +678,29 @@
     gated = y_rows.astype(F32) * (gate_here / (1.0 + jnp.exp(-gate_here)))
     squares = jnp.sum(gated * gated, axis=1)
     scaled = (gated * norm_gain).astype(BF16)
+    new_states = update_states(picked, tie(b_rows, scaled), ends, state_pool)
     wide = depth // splits
     total_inner = inner * splits
     if paired:
         squares = squares + swap(squares, "mdl")
         scale = lax.rsqrt(squares / total_inner + EPSILON)
-        scale = jnp.concatenate([scale, swap(scale, "near")])
         columns_at = jnp.stack(
             [2 * at_side + at_core for at_side in (side, 1 - side) for at_core in (core, 1 - core)]
         )
-        terms = project_out(scaled, swap(scaled, "near"), out_columns, columns_at)
+        terms, given = project_out(scaled, tie(swap(scaled, "near"), new_states), out_columns, columns_at)
         here = far == part
         mine = jnp.where(here, terms[0], terms[1])
-        other = jnp.where(here, terms[1], terms[0]).astype(BF16)
-        total = (mine + swap(other, "mdl").astype(F32)) * scale[:, None]
-        total = total.astype(BF16).reshape(2, rows, wide // 2)
-        given = swap(total[1], "near")
+        other = jnp.where(here, given[1, 0], given[0, 0])
+        peer_mine = jnp.where(here, given[0, 1], given[1, 1])
+        peer_other = jnp.where(here, given[1, 1], given[0, 1])
+        over_y = swap(other, "mdl")
+        over_near = swap(peer_mine, "near")
+        over_both = lax.ppermute(peer_other, ("near", "mdl"), [(0, 3), (1, 2), (2, 1), (3, 0)])
+        here = (mine + over_y.astype(F32)) * scale[:, None]
+        there = (over_near.astype(F32) + over_both.astype(F32)) * scale[:, None]
+        here, there = here.astype(BF16), there.astype(BF16)
         mixed_rows = jnp.concatenate(
-            [jnp.where(near_at == 0, total[0], given), jnp.where(near_at == 0, given, total[0])], axis=1
+            [jnp.where(near_at == 0, here, there), jnp.where(near_at == 0, there, here)], axis=1
         )
     else:
         terms = jnp.dot(scaled, out_columns, preferred_element_type=F32)

time: 200 us -> 185 us (0.925)
  waiting for transfers between devices: 90.7 us -> 71.8 us
  Pallas kernels: 17.7 us -> 22.9 us
  local copies, waits for them, and re-layouts: 19.5 us -> 16.6 us
  starting transfers between devices: 49.8 us -> 52.1 us
    ppermute x46 -> x42, waiting for transfers between devices: 90.7 us -> 69.8 us  [rotate(): return lax.ppermute(value, axis, pairs)]
    pallas_call x0 -> x1, Pallas kernels: none -> 8.75 us  [update_states(): pl.pallas_call(lambda *refs: update_kernel(sizes, *refs), grid=(steps,),...]
    pallas_call x1, Pallas kernels: 13.3 us -> 9.72 us  [mix_requests(): pl.pallas_call(lambda *refs: mixer_kernel(sizes, *refs), grid_spec=grid_s...]
    dynamic_update_slice x8, local copies, waits for them, and re-layouts: 5.86 us -> 3.08 us  [place(): full = lax.dynamic_update_slice_in_dim(full, piece[None], slot, 0)]
    ppermute x46 -> x42, starting transfers between devices: 49.8 us -> 50.5 us  [rotate(): return lax.ppermute(value, axis, pairs)]
  transfers between devices with their start and end apart: 46 -> 43, of which waited for: 17 -> 13; matrix products, arithmetic and copies ran while one was open for 16% -> 15% of each run, Pallas kernels for 9% -> 12%
where the time goes in v3:
time: 185 us; the launch traced here: 184 us
  waiting for transfers between devices  71.8 us (39%)
  starting transfers between devices  52.1 us (28%)
  Pallas kernels  22.9 us (12%)
  local copies, waits for them, and re-layouts  16.6 us (9%)
  other arithmetic  14.9 us (8%)
  matrix products  4.3 us (2%)
    ppermute x42, waiting for transfers between devices, rotate(): return lax.ppermute(value, axis, pairs)  69.8 us
    ppermute x42, starting transfers between devices, rotate(): return lax.ppermute(value, axis, pairs)  50.5 us
    pallas_call x1, Pallas kernels, mix_requests(): pl.pallas_call(lambda *refs: mixer_kernel(sizes, *refs), grid_spec=grid_s...  9.72 us
    pallas_call x1, Pallas kernels, update_states(): pl.pallas_call(lambda *refs: update_kernel(sizes, *refs), grid=(steps,),...  8.75 us
    concatenate x2, other arithmetic, full(): return jnp.concatenate(parts)  6.26 us
    unnamed x83, local copies, waits for them, and re-layouts  4.51 us
  transfers between devices with their start and end apart: 43, of which 13 were waited for; matrix products, arithmetic and copies ran while one was open for 15% of the time, Pallas kernels for 12%

profile of v3, /device:TPU:1, one launch (start us, length us, event | category | flops | bytes accessed | tf_op | source)
XLA Modules:
  0.0 184.3 jit_solution(16835168592527772329)
XLA Ops:
  0.7 1.3 copy.74
  3.6 2.7 %collective-permute-start = (bf16[2,16,1024]{2,1,0:T(8,128)(2,1)S(1)}, bf16[2,16,1024]{2,1,0:T(8,128)(2,1)S(1)}, u32[]{:S(2)}, u32[]{:S(2)}) collective-permute-start(bf16[2,16,1024]{2,1,0:T(8,128)(2,1)S(1)} %bitcast.219), channel_id=1, source_target_pairs={{0,2},{2,4},{4,6},{6,8},{8,10},{10,12},{12,14},{14,16},{16,18},{18... | collective-permute-start | bytes 196616 | tf_op jit(solution)/shard_map/ppermute | solution.py:41
  6.3 1.3 collective-permute-start.1
  8.0 1.4 collective-permute-start.3
  9.4 2.5 %collective-permute-start.4 = (bf16[2,16,1024]{2,1,0:T(8,128)(2,1)S(1)}, bf16[2,16,1024]{2,1,0:T(8,128)(2,1)S(1)}, u32[]{:S(2)}, u32[]{:S(2)}) collective-permute-start(bf16[2,16,1024]{2,1,0:T(8,128)(2,1)S(1)} %bitcast.222), channel_id=1, source_target_pairs={{0,10},{2,12},{4,14},{6,16},{8,18},{10,20},{12,22},{14,24},{16,26}... | collective-permute-start | bytes 196616 | tf_op jit(solution)/shard_map/ppermute | solution.py:41
  12.9 0.9 fusion.11.refs_9_
  15.4 2.1 %collective-permute-start.5 = (bf16[2,16,1024]{2,1,0:T(8,128)(2,1)S(1)}, bf16[2,16,1024]{2,1,0:T(8,128)(2,1)S(1)}, u32[]{:S(2)}, u32[]{:S(2)}) collective-permute-start(bf16[2,16,1024]{2,1,0:T(8,128)(2,1)S(1)} %bitcast.224), channel_id=1, source_target_pairs={{0,12},{2,14},{4,16},{6,18},{8,20},{10,22},{12,24},{14,26},{16,28}... | collective-permute-start | bytes 196616 | tf_op jit(solution)/shard_map/ppermute | solution.py:41
  18.8 1.9 %collective-permute-start.8 = (bf16[128,1152]{1,0:T(8,128)(2,1)S(1)}, bf16[128,1152]{1,0:T(8,128)(2,1)S(1)}, u32[]{:S(2)}, u32[]{:S(2)}) collective-permute-start(bf16[128,1152]{1,0:T(8,128)(2,1)S(1)} %bitcast.192), channel_id=1, source_target_pairs={{0,16},{8,24},{16,0},{24,8},{1,17},{9,25},{17,1},{25,9},{2,18},{10... | collective-permute-start | bytes 884744 | tf_op jit(solution)/shard_map/ppermute | solution.py:41
  20.9 1.6 collective-permute-start.9
  23.6 1.5 shard_map.210
  26.4 2.1 %collective-permute-start.6 = (bf16[2,16,1024]{2,1,0:T(8,128)(2,1)S(1)}, bf16[2,16,1024]{2,1,0:T(8,128)(2,1)S(1)}, u32[]{:S(2)}, u32[]{:S(2)}) collective-permute-start(bf16[2,16,1024]{2,1,0:T(8,128)(2,1)S(1)} %bitcast.223), channel_id=1, source_target_pairs={{0,14},{2,16},{4,18},{6,20},{8,22},{10,24},{12,26},{14,28},{16,30}... | collective-permute-start | bytes 196616 | tf_op jit(solution)/shard_map/ppermute | solution.py:41
  29.1 21.6 %collective-permute-done.6 = bf16[2,16,1024]{2,1,0:T(8,128)(2,1)S(1)} collective-permute-done((bf16[2,16,1024]{2,1,0:T(8,128)(2,1)S(1)}, bf16[2,16,1024]{2,1,0:T(8,128)(2,1)S(1)}, u32[]{:S(2)}, u32[]{:S(2)}) %collective-permute-start.6) | collective-permute-done | bytes 65568 | tf_op jit(solution)/shard_map/ppermute | solution.py:41
  52.3 2.6 %collective-permute-start.13 = (bf16[128,1024]{1,0:T(8,128)(2,1)S(1)}, bf16[128,1024]{1,0:T(8,128)(2,1)S(1)}, u32[]{:S(2)}, u32[]{:S(2)}) collective-permute-start(bf16[128,1024]{1,0:T(8,128)(2,1)S(1)} %reshape.298), channel_id=1, source_target_pairs={{0,24},{8,0},{16,8},{24,16},{1,25},{9,1},{17,9},{25,17},{2,26},{10... | collective-permute-start | bytes 786440 | tf_op jit(solution)/shard_map/ppermute | solution.py:41
  55.1 1.1 broadcast.224.clone
  59.3 2.5 %collective-permute-done.11 = bf16[128,1024]{1,0:T(8,128)(2,1)S(1)} collective-permute-done((bf16[128,1024]{1,0:T(8,128)(2,1)S(1)}, bf16[128,1024]{1,0:T(8,128)(2,1)S(1)}, u32[]{:S(2)}, u32[]{:S(2)}) %collective-permute-start.11) | collective-permute-done | bytes 262176 | tf_op jit(solution)/shard_map/ppermute | solution.py:41
  61.8 10.3 %collective-permute-done.12 = bf16[128,1024]{1,0:T(8,128)(2,1)S(1)} collective-permute-done((bf16[128,1024]{1,0:T(8,128)(2,1)S(1)}, bf16[128,1024]{1,0:T(8,128)(2,1)S(1)}, u32[]{:S(2)}, u32[]{:S(2)}) %collective-permute-start.12) | collective-permute-done | bytes 262176 | tf_op jit(solution)/shard_map/ppermute | solution.py:41
  72.1 4.0 %collective-permute-done.14 = bf16[3,128,1152]{2,1,0:T(8,128)(2,1)S(1)} collective-permute-done((bf16[3,128,1152]{2,1,0:T(8,128)(2,1)S(1)}, bf16[3,128,1152]{2,1,0:T(8,128)(2,1)S(1)}, u32[]{:S(2)}, u32[]{:S(2)}) %collective-permute-start.14) | collective-permute-done | bytes 884768 | tf_op jit(solution)/shard_map/ppermute | solution.py:41
  76.1 1.1 collective-permute-start.16
  77.4 1.5 collective-permute-start.18
  79.0 1.0 constant_dynamic-update-slice_fusion.8
  79.9 1.3 collective-permute-start.15
  81.4 1.5 broadcast_select_fusion.17
  83.0 1.8 broadcast_select_fusion.9
  85.0 6.1 %pad_maximum_fusion = bf16[2048,640]{1,0:T(8,128)(2,1)S(1)} fusion(bf16[512,640]{1,0:T(8,128)(2,1)S(1)} %bitcast.173, bf16[512,640]{1,0:T(8,128)(2,1)S(1)} %bitcast.172, bf16[512,640]{1,0:T(8,128)(2,1)S(1)} %bitcast.171, bf16[512,640]{1,0:T(8,128)(2,1)S(1)} %bitcast.170), kind=kLoop, calls=%fused_computation.6 | loop fusion | flops 10485760 | bytes 5242880 | tf_op jit(solution)/shard_map/concatenate | solution.py:620
  91.1 11.6 %collective-permute-done.18.refs_4_ = bf16[2048,128]{1,0:T(8,128)(2,1)S(1)} collective-permute-done((bf16[2048,128]{1,0:T(8,128)(2,1)S(1)}, bf16[2048,128]{1,0:T(8,128)(2,1)S(1)}, u32[]{:S(2)}, u32[]{:S(2)}) %collective-permute-start.18) | collective-permute-done | bytes 524320 | tf_op jit(solution)/shard_map/ppermute | solution.py:41
  102.6 1.0 collective-permute-done.15
  103.7 1.5 collective-permute-start.23
  105.3 1.8 fusion.4
  107.8 2.0 %collective-permute-start.20 = (bf16[128,640]{1,0:T(8,128)(2,1)S(1)}, bf16[128,640]{1,0:T(8,128)(2,1)S(1)}, u32[]{:S(2)}, u32[]{:S(2)}) collective-permute-start(bf16[128,640]{1,0:T(8,128)(2,1)S(1)} %get-tuple-element.187), channel_id=1, source_target_pairs={{0,24},{8,0},{16,8},{24,16},{1,25},{9,1},{17,9},{25,17},{2,26},{10... | collective-permute-start | bytes 491528 | tf_op jit(solution)/shard_map/ppermute | solution.py:41
  110.2 1.2 fusion.5
  112.3 11.2 %collective-permute-done.21.refs_3_.refs_7_ = bf16[128,640]{1,0:T(8,128)(2,1)S(1)} collective-permute-done((bf16[128,640]{1,0:T(8,128)(2,1)S(1)}, bf16[128,640]{1,0:T(8,128)(2,1)S(1)}, u32[]{:S(2)}, u32[]{:S(2)}) %collective-permute-start.21) | collective-permute-done | bytes 163872 | tf_op jit(solution)/shard_map/ppermute | solution.py:41
  124.0 2.0 %collective-permute-start.25 = (bf16[128,512]{1,0:T(8,128)(2,1)S(1)}, bf16[128,512]{1,0:T(8,128)(2,1)S(1)}, u32[]{:S(2)}, u32[]{:S(2)}) collective-permute-start(bf16[128,512]{1,0:T(8,128)(2,1)S(1)} %get-tuple-element.201), channel_id=1, source_target_pairs={{0,16},{8,24},{16,0},{24,8},{1,17},{9,25},{17,1},{25,9},{2,18},{10... | collective-permute-start | bytes 393224 | tf_op jit(solution)/shard_map/ppermute | solution.py:41
  126.0 2.3 %collective-permute-start.26 = (bf16[128,512]{1,0:T(8,128)(2,1)S(1)}, bf16[128,512]{1,0:T(8,128)(2,1)S(1)}, u32[]{:S(2)}, u32[]{:S(2)}) collective-permute-start(bf16[128,512]{1,0:T(8,128)(2,1)S(1)} %get-tuple-element.200), channel_id=1, source_target_pairs={{0,24},{8,0},{16,8},{24,16},{1,25},{9,1},{17,9},{25,17},{2,26},{10... | collective-permute-start | bytes 393224 | tf_op jit(solution)/shard_map/ppermute | solution.py:41
  128.2 9.7 %shard_map.211 = (bf16[128,2048]{1,0:T(8,128)(2,1)}, bf16[2048,256]{1,0:T(8,128)(2,1)}, f32[128,128]{1,0:T(8,128)}, f32[128,128]{1,0:T(8,128)}, bf16[32,2048]{1,0:T(8,128)(2,1)}, /*index=5*/bf16[32,256]{1,0:T(8,128)(2,1)}) custom-call(s32[4]{0:T(128)} %and_select_fusion.1.refs_0_, bf16[128,640]{1,0:T(8,128)(2,1)} %get-tuple-element.117.refs_1_.refs_5_, ...), custom_call_target="tpu_custom_call" | custom-call | flops 2147483648 | bytes 16777216 | tf_op jit(solution)/shard_map/pallas_call | solution.py:391
  138.1 1.6 multiply_convert_fusion
  140.1 1.9 %collective-permute-start.28 = (bf16[2048,128]{1,0:T(8,128)(2,1)S(1)}, bf16[2048,128]{1,0:T(8,128)(2,1)}, u32[]{:S(2)}, u32[]{:S(2)}) collective-permute-start(bf16[2048,128]{1,0:T(8,128)(2,1)S(1)} %copy-done), channel_id=1, source_target_pairs={{0,2},{2,0},{1,3},{3,1},{4,6},{6,4},{5,7},{7,5},{8,10},{10,8},{9,1... | collective-permute-start | bytes 1572872 | tf_op jit(solution)/shard_map/ppermute | solution.py:41
  142.7 8.7 %shard_map.212 = f32[8,32,64,128]{3,2,1,0:T(8,128)} custom-call(bf16[2048,256]{1,0:T(8,128)(2,1)} %get-tuple-element.129.refs_0_, f32[128,128]{1,0:T(8,128)} %get-tuple-element.131.refs_1_, f32[128,128]{1,0:T(8,128)} %get-tuple-element.132.refs_2_, f32[8,32,64,128]{3,2,1,0:T(8,128)} %refs_3_.1), custom_call_target="tpu_custom_call" | custom-call | flops 2147483648 | bytes 16777216 | tf_op jit(solution)/shard_map/pallas_call | solution.py:293
  151.4 1.2 collective-permute-start.33
  152.7 2.9 %shard_map.213 = (f32[2,128,512]{2,1,0:T(8,128)S(1)}, bf16[2,2,128,512]{3,2,1,0:T(8,128)(2,1)S(1)}) custom-call(s32[4]{0:T(128)S(1)} %pad_add_fusion.place_ref, bf16[128,2048]{1,0:T(8,128)(2,1)S(1)} %get-tuple-element.179.own_ref, bf16[128,2048]{1,0:T(8,128)(2,1)S(1)} %collective-permute-done.27.peer_ref, bf16[2048,128]{1,0:T(8,128)(2,1)S(1)} %copy-done, ...), custom_call_target="tpu_custom_call" | custom-call | flops 1000 | bytes 1000 | tf_op jit(solution)/shard_map/pallas_call | solution.py:467
  155.6 1.6 collective-permute-start.35
  157.3 1.1 collective-permute-start.32
  158.4 2.0 %collective-permute-done.35 = bf16[128,512]{1,0:T(8,128)(2,1)S(1)} collective-permute-done((bf16[128,512]{1,0:T(8,128)(2,1)S(1)}, bf16[128,512]{1,0:T(8,128)(2,1)S(1)}, u32[]{:S(2)}, u32[]{:S(2)}) %collective-permute-start.35) | collective-permute-done | bytes 131104 | tf_op jit(solution)/shard_map/ppermute | solution.py:698
  163.0 4.1 %collective-permute-start.36 = (bf16[2,16,1024]{2,1,0:T(8,128)(2,1)S(1)}, bf16[2,16,1024]{2,1,0:T(8,128)(2,1)S(1)}, u32[]{:S(2)}, u32[]{:S(2)}) collective-permute-start(bf16[2,16,1024]{2,1,0:T(8,128)(2,1)S(1)} %bitcast.238), channel_id=1, source_target_pairs={{0,30},{2,0},{4,2},{6,4},{8,6},{10,8},{12,10},{14,12},{16,14},{18,... | collective-permute-start | bytes 196616 | tf_op jit(solution)/shard_map/ppermute | solution.py:41
  167.1 1.5 collective-permute-start.37
  168.6 1.5 collective-permute-start.38
  171.7 1.8 collective-permute-start.41
  173.4 1.7 collective-permute-start.42
  177.1 5.2 %collective-permute-done.42 = bf16[2,16,1024]{2,1,0:T(8,128)(2,1)S(1)} collective-permute-done((bf16[2,16,1024]{2,1,0:T(8,128)(2,1)S(1)}, bf16[2,16,1024]{2,1,0:T(8,128)(2,1)S(1)}, u32[]{:S(2)}, u32[]{:S(2)}) %collective-permute-start.42) | collective-permute-done | bytes 65568 | tf_op jit(solution)/shard_map/ppermute | solution.py:41
  (205 shorter events, 25.8 us)
Async XLA Ops:
  3.6 11.8 %collective-permute-start = (bf16[2,16,1024]{2,1,0:T(8,128)(2,1)S(1)}, bf16[2,16,1024]{2,1,0:T(8,128)(2,1)S(1)}, u32[]{:S(2)}, u32[]{:S(2)}) collective-permute-start(bf16[2,16,1024]{2,1,0:T(8,128)(2,1)S(1)} %bitcast.219), channel_id=1, source_target_pairs={{0,2},{2,4},{4,6},{6,8},{8,10},{10,12},{12,14},{14,16},{16,18},{18... | collective-permute-start | bytes 196616 | tf_op jit(solution)/shard_map/ppermute | solution.py:41
  6.3 11.3 %collective-permute-start.1 = (bf16[2,16,1024]{2,1,0:T(8,128)(2,1)S(1)}, bf16[2,16,1024]{2,1,0:T(8,128)(2,1)S(1)}, u32[]{:S(2)}, u32[]{:S(2)}) collective-permute-start(bf16[2,16,1024]{2,1,0:T(8,128)(2,1)S(1)} %bitcast.218), channel_id=1, source_target_pairs={{0,4},{2,6},{4,8},{6,10},{8,12},{10,14},{12,16},{14,18},{16,20},{1... | collective-permute-start | bytes 196616 | tf_op jit(solution)/shard_map/ppermute | solution.py:41
  7.6 9.9 %collective-permute-start.2 = (bf16[2,16,1024]{2,1,0:T(8,128)(2,1)S(1)}, bf16[2,16,1024]{2,1,0:T(8,128)(2,1)S(1)}, u32[]{:S(2)}, u32[]{:S(2)}) collective-permute-start(bf16[2,16,1024]{2,1,0:T(8,128)(2,1)S(1)} %bitcast.220), channel_id=1, source_target_pairs={{0,6},{2,8},{4,10},{6,12},{8,14},{10,16},{12,18},{14,20},{16,22},{... | collective-permute-start | bytes 196616 | tf_op jit(solution)/shard_map/ppermute | solution.py:41
  8.0 9.5 %collective-permute-start.3 = (bf16[2,16,1024]{2,1,0:T(8,128)(2,1)S(1)}, bf16[2,16,1024]{2,1,0:T(8,128)(2,1)S(1)}, u32[]{:S(2)}, u32[]{:S(2)}) collective-permute-start(bf16[2,16,1024]{2,1,0:T(8,128)(2,1)S(1)} %bitcast.221), channel_id=1, source_target_pairs={{0,8},{2,10},{4,12},{6,14},{8,16},{10,18},{12,20},{14,22},{16,24},... | collective-permute-start | bytes 196616 | tf_op jit(solution)/shard_map/ppermute | solution.py:41
  9.4 8.2 %collective-permute-start.4 = (bf16[2,16,1024]{2,1,0:T(8,128)(2,1)S(1)}, bf16[2,16,1024]{2,1,0:T(8,128)(2,1)S(1)}, u32[]{:S(2)}, u32[]{:S(2)}) collective-permute-start(bf16[2,16,1024]{2,1,0:T(8,128)(2,1)S(1)} %bitcast.222), channel_id=1, source_target_pairs={{0,10},{2,12},{4,14},{6,16},{8,18},{10,20},{12,22},{14,24},{16,26}... | collective-permute-start | bytes 196616 | tf_op jit(solution)/shard_map/ppermute | solution.py:41
  15.4 11.0 %collective-permute-start.5 = (bf16[2,16,1024]{2,1,0:T(8,128)(2,1)S(1)}, bf16[2,16,1024]{2,1,0:T(8,128)(2,1)S(1)}, u32[]{:S(2)}, u32[]{:S(2)}) collective-permute-start(bf16[2,16,1024]{2,1,0:T(8,128)(2,1)S(1)} %bitcast.224), channel_id=1, source_target_pairs={{0,12},{2,14},{4,16},{6,18},{8,20},{10,22},{12,24},{14,26},{16,28}... | collective-permute-start | bytes 196616 | tf_op jit(solution)/shard_map/ppermute | solution.py:41
  18.1 32.6 %collective-permute-start.7 = (bf16[128,1152]{1,0:T(8,128)(2,1)S(1)}, bf16[128,1152]{1,0:T(8,128)(2,1)S(1)}, u32[]{:S(2)}, u32[]{:S(2)}) collective-permute-start(bf16[128,1152]{1,0:T(8,128)(2,1)S(1)} %bitcast.191), channel_id=1, source_target_pairs={{0,8},{8,16},{16,24},{24,0},{1,9},{9,17},{17,25},{25,1},{2,10},{10... | collective-permute-start | bytes 884744 | tf_op jit(solution)/shard_map/ppermute | solution.py:41
  18.8 31.9 %collective-permute-start.8 = (bf16[128,1152]{1,0:T(8,128)(2,1)S(1)}, bf16[128,1152]{1,0:T(8,128)(2,1)S(1)}, u32[]{:S(2)}, u32[]{:S(2)}) collective-permute-start(bf16[128,1152]{1,0:T(8,128)(2,1)S(1)} %bitcast.192), channel_id=1, source_target_pairs={{0,16},{8,24},{16,0},{24,8},{1,17},{9,25},{17,1},{25,9},{2,18},{10... | collective-permute-start | bytes 884744 | tf_op jit(solution)/shard_map/ppermute | solution.py:41
  20.9 29.8 %collective-permute-start.9 = (bf16[128,1152]{1,0:T(8,128)(2,1)S(1)}, bf16[128,1152]{1,0:T(8,128)(2,1)S(1)}, u32[]{:S(2)}, u32[]{:S(2)}) collective-permute-start(bf16[128,1152]{1,0:T(8,128)(2,1)S(1)} %bitcast.193), channel_id=1, source_target_pairs={{0,24},{8,0},{16,8},{24,16},{1,25},{9,1},{17,9},{25,17},{2,26},{10... | collective-permute-start | bytes 884744 | tf_op jit(solution)/shard_map/ppermute | solution.py:41
  22.5 28.2 %collective-permute-start.10 = (bf16[128,1152]{1,0:T(8,128)(2,1)S(1)}, bf16[128,1152]{1,0:T(8,128)(2,1)S(1)}, u32[]{:S(2)}, u32[]{:S(2)}) collective-permute-start(bf16[128,1152]{1,0:T(8,128)(2,1)S(1)} %bitcast.186), channel_id=1, source_target_pairs={{0,4},{4,0},{1,5},{5,1},{2,6},{6,2},{3,7},{7,3},{8,12},{12,8},{9,1... | collective-permute-start | bytes 884744 | tf_op jit(solution)/shard_map/ppermute | solution.py:41
  26.4 24.3 %collective-permute-start.6 = (bf16[2,16,1024]{2,1,0:T(8,128)(2,1)S(1)}, bf16[2,16,1024]{2,1,0:T(8,128)(2,1)S(1)}, u32[]{:S(2)}, u32[]{:S(2)}) collective-permute-start(bf16[2,16,1024]{2,1,0:T(8,128)(2,1)S(1)} %bitcast.223), channel_id=1, source_target_pairs={{0,14},{2,16},{4,18},{6,20},{8,22},{10,24},{12,26},{14,28},{16,30}... | collective-permute-start | bytes 196616 | tf_op jit(solution)/shard_map/ppermute | solution.py:41
  51.6 10.2 %collective-permute-start.11 = (bf16[128,1024]{1,0:T(8,128)(2,1)S(1)}, bf16[128,1024]{1,0:T(8,128)(2,1)S(1)}, u32[]{:S(2)}, u32[]{:S(2)}) collective-permute-start(bf16[128,1024]{1,0:T(8,128)(2,1)S(1)} %reshape.298), channel_id=1, source_target_pairs={{0,8},{8,16},{16,24},{24,0},{1,9},{9,17},{17,25},{25,1},{2,10},{10... | collective-permute-start | bytes 786440 | tf_op jit(solution)/shard_map/ppermute | solution.py:41
  51.6 20.5 %collective-permute-start.12 = (bf16[128,1024]{1,0:T(8,128)(2,1)S(1)}, bf16[128,1024]{1,0:T(8,128)(2,1)S(1)}, u32[]{:S(2)}, u32[]{:S(2)}) collective-permute-start(bf16[128,1024]{1,0:T(8,128)(2,1)S(1)} %reshape.298), channel_id=1, source_target_pairs={{0,16},{8,24},{16,0},{24,8},{1,17},{9,25},{17,1},{25,9},{2,18},{10... | collective-permute-start | bytes 786440 | tf_op jit(solution)/shard_map/ppermute | solution.py:41
  52.3 19.8 %collective-permute-start.13 = (bf16[128,1024]{1,0:T(8,128)(2,1)S(1)}, bf16[128,1024]{1,0:T(8,128)(2,1)S(1)}, u32[]{:S(2)}, u32[]{:S(2)}) collective-permute-start(bf16[128,1024]{1,0:T(8,128)(2,1)S(1)} %reshape.298), channel_id=1, source_target_pairs={{0,24},{8,0},{16,8},{24,16},{1,25},{9,1},{17,9},{25,17},{2,26},{10... | collective-permute-start | bytes 786440 | tf_op jit(solution)/shard_map/ppermute | solution.py:41
  55.0 21.1 %collective-permute-start.14 = (bf16[3,128,1152]{2,1,0:T(8,128)(2,1)S(1)}, bf16[3,128,1152]{2,1,0:T(8,128)(2,1)S(1)}, u32[]{:S(2)}, u32[]{:S(2)}) collective-permute-start(bf16[3,128,1152]{2,1,0:T(8,128)(2,1)S(1)} %pad_maximum_fusion.9), channel_id=1, source_target_pairs={{0,4},{4,0},{1,5},{5,1},{2,6},{6,2},{3,7},{7,3},{8,12},{12,8},{9,1... | collective-permute-start | bytes 2654216 | tf_op jit(solution)/shard_map/ppermute | solution.py:41
  58.4 18.9 %copy-start = (bf16[2048,128]{1,0:T(8,128)(2,1)S(1)}, bf16[2048,128]{1,0:T(8,128)(2,1)}, u32[]{:S(2)}) copy-start(bf16[2048,128]{1,0:T(8,128)(2,1)} %refs_0_.1) | copy-start | bytes 1572868
  76.1 5.2 %collective-permute-start.16 = (bf16[4,128,1152]{2,1,0:T(8,128)(2,1)}, bf16[4,128,1152]{2,1,0:T(8,128)(2,1)}, u32[]{:S(2)}, u32[]{:S(2)}) collective-permute-start(bf16[4,128,1152]{2,1,0:T(8,128)(2,1)} %constant_dynamic-update-slice_fusion.12), channel_id=1, source_target_pairs={{0,2},{2,0},{1,3},{3,1},{4,6},{6,4},{5,7},{7,5},{8,10},{10,8},{9,1... | collective-permute-start | bytes 3538952 | tf_op jit(solution)/shard_map/ppermute | solution.py:41
  77.3 4.2 %collective-permute-start.17 = (bf16[4,128,1152]{2,1,0:T(8,128)(2,1)S(1)}, bf16[4,128,1152]{2,1,0:T(8,128)(2,1)}, u32[]{:S(2)}, u32[]{:S(2)}) collective-permute-start(bf16[4,128,1152]{2,1,0:T(8,128)(2,1)S(1)} %slice_dynamic-update-slice_fusion), channel_id=1, source_target_pairs={{0,2},{2,0},{1,3},{3,1},{4,6},{6,4},{5,7},{7,5},{8,10},{10,8},{9,1... | collective-permute-start | bytes 3538952 | tf_op jit(solution)/shard_map/ppermute | solution.py:41
  77.4 25.3 %collective-permute-start.18 = (bf16[2048,128]{1,0:T(8,128)(2,1)S(1)}, bf16[2048,128]{1,0:T(8,128)(2,1)S(1)}, u32[]{:S(2)}, u32[]{:S(2)}) collective-permute-start(bf16[2048,128]{1,0:T(8,128)(2,1)S(1)} %copy-done), channel_id=1, source_target_pairs={{0,16},{16,0},{1,17},{17,1},{2,18},{18,2},{3,19},{19,3},{4,20},{20... | collective-permute-start | bytes 1572872 | tf_op jit(solution)/shard_map/ppermute | solution.py:41
  78.9 23.8 %collective-permute-start.19 = (bf16[2048,128]{1,0:T(8,128)(2,1)S(1)}, bf16[2048,128]{1,0:T(8,128)(2,1)S(1)}, u32[]{:S(2)}, u32[]{:S(2)}) collective-permute-start(bf16[2048,128]{1,0:T(8,128)(2,1)S(1)} %copy-done), channel_id=1, source_target_pairs={{0,4},{4,0},{1,5},{5,1},{2,6},{6,2},{3,7},{7,3},{8,12},{12,8},{9,1... | collective-permute-start | bytes 1572872 | tf_op jit(solution)/shard_map/ppermute | solution.py:41
  79.9 23.7 %collective-permute-start.15 = (bf16[512,1024]{1,0:T(8,128)(2,1)S(1)}, bf16[512,1024]{1,0:T(8,128)(2,1)S(1)}, u32[]{:S(2)}, u32[]{:S(2)}) collective-permute-start(bf16[512,1024]{1,0:T(8,128)(2,1)S(1)} %constant_dynamic-update-slice_fusion.8), channel_id=1, source_target_pairs={{0,1},{1,0},{2,3},{3,2},{4,5},{5,4},{6,7},{7,6},{8,9},{9,8},{10,11... | collective-permute-start | bytes 3145736 | tf_op jit(solution)/shard_map/ppermute | solution.py:41
  103.7 19.9 %collective-permute-start.23 = (bf16[2048,128]{1,0:T(8,128)(2,1)S(1)}, bf16[2048,128]{1,0:T(8,128)(2,1)S(1)}, u32[]{:S(2)}, u32[]{:S(2)}) collective-permute-start(bf16[2048,128]{1,0:T(8,128)(2,1)S(1)} %collective-permute-done.18.refs_4_), channel_id=1, source_target_pairs={{0,4},{4,0},{1,5},{5,1},{2,6},{6,2},{3,7},{7,3},{8,12},{12,8},{9,1... | collective-permute-start | bytes 1572872 | tf_op jit(solution)/shard_map/ppermute | solution.py:41
  107.8 4.5 %collective-permute-start.20 = (bf16[128,640]{1,0:T(8,128)(2,1)S(1)}, bf16[128,640]{1,0:T(8,128)(2,1)S(1)}, u32[]{:S(2)}, u32[]{:S(2)}) collective-permute-start(bf16[128,640]{1,0:T(8,128)(2,1)S(1)} %get-tuple-element.187), channel_id=1, source_target_pairs={{0,24},{8,0},{16,8},{24,16},{1,25},{9,1},{17,9},{25,17},{2,26},{10... | collective-permute-start | bytes 491528 | tf_op jit(solution)/shard_map/ppermute | solution.py:41
  109.8 13.7 %collective-permute-start.21 = (bf16[128,640]{1,0:T(8,128)(2,1)S(1)}, bf16[128,640]{1,0:T(8,128)(2,1)S(1)}, u32[]{:S(2)}, u32[]{:S(2)}) collective-permute-start(bf16[128,640]{1,0:T(8,128)(2,1)S(1)} %get-tuple-element.186), channel_id=1, source_target_pairs={{0,16},{8,24},{16,0},{24,8},{1,17},{9,25},{17,1},{25,9},{2,18},{10... | collective-permute-start | bytes 491528 | tf_op jit(solution)/shard_map/ppermute | solution.py:41
  109.8 13.7 %collective-permute-start.22 = (bf16[128,640]{1,0:T(8,128)(2,1)S(1)}, bf16[128,640]{1,0:T(8,128)(2,1)S(1)}, u32[]{:S(2)}, u32[]{:S(2)}) collective-permute-start(bf16[128,640]{1,0:T(8,128)(2,1)S(1)} %get-tuple-element.185), channel_id=1, source_target_pairs={{0,8},{8,16},{16,24},{24,0},{1,9},{9,17},{17,25},{25,1},{2,10},{10... | collective-permute-start | bytes 491528 | tf_op jit(solution)/shard_map/ppermute | solution.py:41
  112.3 15.9 %copy-start.1 = (bf16[128,640]{1,0:T(8,128)(2,1)}, bf16[128,640]{1,0:T(8,128)(2,1)S(1)}, u32[]{:S(2)}) copy-start(bf16[128,640]{1,0:T(8,128)(2,1)S(1)} %collective-permute-done.20.refs_2_.refs_6_) | copy-start | bytes 491524
  123.6 14.4 %collective-permute-start.24 = (bf16[128,512]{1,0:T(8,128)(2,1)S(1)}, bf16[128,512]{1,0:T(8,128)(2,1)S(1)}, u32[]{:S(2)}, u32[]{:S(2)}) collective-permute-start(bf16[128,512]{1,0:T(8,128)(2,1)S(1)} %get-tuple-element.202), channel_id=1, source_target_pairs={{0,8},{8,16},{16,24},{24,0},{1,9},{9,17},{17,25},{25,1},{2,10},{10... | collective-permute-start | bytes 393224 | tf_op jit(solution)/shard_map/ppermute | solution.py:41
  124.0 14.0 %collective-permute-start.25 = (bf16[128,512]{1,0:T(8,128)(2,1)S(1)}, bf16[128,512]{1,0:T(8,128)(2,1)S(1)}, u32[]{:S(2)}, u32[]{:S(2)}) collective-permute-start(bf16[128,512]{1,0:T(8,128)(2,1)S(1)} %get-tuple-element.201), channel_id=1, source_target_pairs={{0,16},{8,24},{16,0},{24,8},{1,17},{9,25},{17,1},{25,9},{2,18},{10... | collective-permute-start | bytes 393224 | tf_op jit(solution)/shard_map/ppermute | solution.py:41
  125.9 12.1 %copy-start.15 = (f32[2048]{0:T(1024)S(1)}, f32[2048]{0:T(1024)}, u32[]{:S(2)}) copy-start(f32[2048]{0:T(1024)} %param.29) | copy-start | bytes 24580
  126.0 12.0 %collective-permute-start.26 = (bf16[128,512]{1,0:T(8,128)(2,1)S(1)}, bf16[128,512]{1,0:T(8,128)(2,1)S(1)}, u32[]{:S(2)}, u32[]{:S(2)}) collective-permute-start(bf16[128,512]{1,0:T(8,128)(2,1)S(1)} %get-tuple-element.200), channel_id=1, source_target_pairs={{0,24},{8,0},{16,8},{24,16},{1,25},{9,1},{17,9},{25,17},{2,26},{10... | collective-permute-start | bytes 393224 | tf_op jit(solution)/shard_map/ppermute | solution.py:41
  139.7 11.8 %collective-permute-start.27 = (bf16[128,2048]{1,0:T(8,128)(2,1)S(1)}, bf16[128,2048]{1,0:T(8,128)(2,1)S(1)}, u32[]{:S(2)}, u32[]{:S(2)}) collective-permute-start(bf16[128,2048]{1,0:T(8,128)(2,1)S(1)} %get-tuple-element.179.own_ref), channel_id=1, source_target_pairs={{0,8},{8,0},{1,9},{9,1},{2,10},{10,2},{3,11},{11,3},{4,12},{12,4},... | collective-permute-start | bytes 1572872 | tf_op jit(solution)/shard_map/ppermute | solution.py:41
  140.1 12.6 %collective-permute-start.28 = (bf16[2048,128]{1,0:T(8,128)(2,1)S(1)}, bf16[2048,128]{1,0:T(8,128)(2,1)}, u32[]{:S(2)}, u32[]{:S(2)}) collective-permute-start(bf16[2048,128]{1,0:T(8,128)(2,1)S(1)} %copy-done), channel_id=1, source_target_pairs={{0,2},{2,0},{1,3},{3,1},{4,6},{6,4},{5,7},{7,5},{8,10},{10,8},{9,1... | collective-permute-start | bytes 1572872 | tf_op jit(solution)/shard_map/ppermute | solution.py:41
  142.0 10.7 %collective-permute-start.30 = (bf16[2048,128]{1,0:T(8,128)(2,1)S(1)}, bf16[2048,128]{1,0:T(8,128)(2,1)}, u32[]{:S(2)}, u32[]{:S(2)}) collective-permute-start(bf16[2048,128]{1,0:T(8,128)(2,1)S(1)} %collective-permute-done.18.refs_4_), channel_id=1, source_target_pairs={{0,2},{2,0},{1,3},{3,1},{4,6},{6,4},{5,7},{7,5},{8,10},{10,8},{9,1... | collective-permute-start | bytes 1572872 | tf_op jit(solution)/shard_map/ppermute | solution.py:41
  142.1 10.6 %collective-permute-start.29 = (bf16[2048,128]{1,0:T(8,128)(2,1)S(1)}, bf16[2048,128]{1,0:T(8,128)(2,1)}, u32[]{:S(2)}, u32[]{:S(2)}) collective-permute-start(bf16[2048,128]{1,0:T(8,128)(2,1)S(1)} %collective-permute-done.19.refs_2_), channel_id=1, source_target_pairs={{0,2},{2,0},{1,3},{3,1},{4,6},{6,4},{5,7},{7,5},{8,10},{10,8},{9,1... | collective-permute-start | bytes 1572872 | tf_op jit(solution)/shard_map/ppermute | solution.py:41
  142.5 10.2 %collective-permute-start.31 = (bf16[2048,128]{1,0:T(8,128)(2,1)S(1)}, bf16[2048,128]{1,0:T(8,128)(2,1)}, u32[]{:S(2)}, u32[]{:S(2)}) collective-permute-start(bf16[2048,128]{1,0:T(8,128)(2,1)S(1)} %collective-permute-done.23.refs_6_), channel_id=1, source_target_pairs={{0,2},{2,0},{1,3},{3,1},{4,6},{6,4},{5,7},{7,5},{8,10},{10,8},{9,1... | collective-permute-start | bytes 1572872 | tf_op jit(solution)/shard_map/ppermute | solution.py:41
  151.4 7.0 %collective-permute-start.33 = (f32[128]{0:T(128)S(1)}, f32[128]{0:T(128)S(1)}, u32[]{:S(2)}, u32[]{:S(2)}) collective-permute-start(f32[128]{0:T(128)S(1)} %get-tuple-element.180), channel_id=1, source_target_pairs={{0,1},{1,0},{2,3},{3,2},{4,5},{5,4},{6,7},{7,6},{8,9},{9,8},{10,11... | collective-permute-start | bytes 1544 | tf_op jit(solution)/shard_map/ppermute | solution.py:41
  155.6 4.8 %collective-permute-start.35 = (bf16[128,512]{1,0:T(8,128)(2,1)S(1)}, bf16[128,512]{1,0:T(8,128)(2,1)S(1)}, u32[]{:S(2)}, u32[]{:S(2)}) collective-permute-start(bf16[128,512]{1,0:T(8,128)(2,1)S(1)} %get-tuple-element.198), channel_id=1, source_target_pairs={{0,9},{1,8},{8,1},{9,0},{2,11},{3,10},{10,3},{11,2},{4,13},{5,12},... | collective-permute-start | bytes 393224 | tf_op jit(solution)/shard_map/ppermute | solution.py:698
  157.2 3.9 %collective-permute-start.34 = (bf16[128,512]{1,0:T(8,128)(2,1)S(1)}, bf16[128,512]{1,0:T(8,128)(2,1)S(1)}, u32[]{:S(2)}, u32[]{:S(2)}) collective-permute-start(bf16[128,512]{1,0:T(8,128)(2,1)S(1)} %get-tuple-element.199), channel_id=1, source_target_pairs={{0,8},{8,0},{1,9},{9,1},{2,10},{10,2},{3,11},{11,3},{4,12},{12,4},... | collective-permute-start | bytes 393224 | tf_op jit(solution)/shard_map/ppermute | solution.py:41
  157.3 4.4 %collective-permute-start.32 = (bf16[128,512]{1,0:T(8,128)(2,1)S(1)}, bf16[128,512]{1,0:T(8,128)(2,1)S(1)}, u32[]{:S(2)}, u32[]{:S(2)}) collective-permute-start(bf16[128,512]{1,0:T(8,128)(2,1)S(1)} %get-tuple-element.197), channel_id=1, source_target_pairs={{0,1},{1,0},{2,3},{3,2},{4,5},{5,4},{6,7},{7,6},{8,9},{9,8},{10,11... | collective-permute-start | bytes 393224 | tf_op jit(solution)/shard_map/ppermute | solution.py:41
  161.9 13.2 %copy-start.10 = (bf16[32,2048]{1,0:T(8,128)(2,1)S(1)}, bf16[32,2048]{1,0:T(8,128)(2,1)}, u32[]{:S(2)}) copy-start(bf16[32,2048]{1,0:T(8,128)(2,1)} %get-tuple-element.138) | copy-start | bytes 393220
  162.0 13.9 %copy-start.13 = (bf16[32,256]{1,0:T(8,128)(2,1)S(1)}, bf16[32,256]{1,0:T(8,128)(2,1)}, u32[]{:S(2)}) copy-start(bf16[32,256]{1,0:T(8,128)(2,1)} %get-tuple-element.139) | copy-start | bytes 49156
  163.0 8.7 %collective-permute-start.36 = (bf16[2,16,1024]{2,1,0:T(8,128)(2,1)S(1)}, bf16[2,16,1024]{2,1,0:T(8,128)(2,1)S(1)}, u32[]{:S(2)}, u32[]{:S(2)}) collective-permute-start(bf16[2,16,1024]{2,1,0:T(8,128)(2,1)S(1)} %bitcast.238), channel_id=1, source_target_pairs={{0,30},{2,0},{4,2},{6,4},{8,6},{10,8},{12,10},{14,12},{16,14},{18,... | collective-permute-start | bytes 196616 | tf_op jit(solution)/shard_map/ppermute | solution.py:41
  167.1 6.3 %collective-permute-start.37 = (bf16[2,16,1024]{2,1,0:T(8,128)(2,1)S(1)}, bf16[2,16,1024]{2,1,0:T(8,128)(2,1)S(1)}, u32[]{:S(2)}, u32[]{:S(2)}) collective-permute-start(bf16[2,16,1024]{2,1,0:T(8,128)(2,1)S(1)} %bitcast.237), channel_id=1, source_target_pairs={{0,28},{2,30},{4,0},{6,2},{8,4},{10,6},{12,8},{14,10},{16,12},{18,... | collective-permute-start | bytes 196616 | tf_op jit(solution)/shard_map/ppermute | solution.py:41
  168.6 8.1 %collective-permute-start.38 = (bf16[2,16,1024]{2,1,0:T(8,128)(2,1)S(1)}, bf16[2,16,1024]{2,1,0:T(8,128)(2,1)S(1)}, u32[]{:S(2)}, u32[]{:S(2)}) collective-permute-start(bf16[2,16,1024]{2,1,0:T(8,128)(2,1)S(1)} %bitcast.228), channel_id=1, source_target_pairs={{0,26},{2,28},{4,30},{6,0},{8,2},{10,4},{12,6},{14,8},{16,10},{18,... | collective-permute-start | bytes 196616 | tf_op jit(solution)/shard_map/ppermute | solution.py:41
  170.2 6.6 %collective-permute-start.39 = (bf16[2,16,1024]{2,1,0:T(8,128)(2,1)S(1)}, bf16[2,16,1024]{2,1,0:T(8,128)(2,1)S(1)}, u32[]{:S(2)}, u32[]{:S(2)}) collective-permute-start(bf16[2,16,1024]{2,1,0:T(8,128)(2,1)S(1)} %bitcast.230), channel_id=1, source_target_pairs={{0,24},{2,26},{4,28},{6,30},{8,0},{10,2},{12,4},{14,6},{16,8},{18,... | collective-permute-start | bytes 196616 | tf_op jit(solution)/shard_map/ppermute | solution.py:41
  170.9 6.0 %collective-permute-start.40 = (bf16[2,16,1024]{2,1,0:T(8,128)(2,1)S(1)}, bf16[2,16,1024]{2,1,0:T(8,128)(2,1)S(1)}, u32[]{:S(2)}, u32[]{:S(2)}) collective-permute-start(bf16[2,16,1024]{2,1,0:T(8,128)(2,1)S(1)} %bitcast.232), channel_id=1, source_target_pairs={{0,22},{2,24},{4,26},{6,28},{8,30},{10,0},{12,2},{14,4},{16,6},{18... | collective-permute-start | bytes 196616 | tf_op jit(solution)/shard_map/ppermute | solution.py:41
  171.7 5.3 %collective-permute-start.41 = (bf16[2,16,1024]{2,1,0:T(8,128)(2,1)S(1)}, bf16[2,16,1024]{2,1,0:T(8,128)(2,1)S(1)}, u32[]{:S(2)}, u32[]{:S(2)}) collective-permute-start(bf16[2,16,1024]{2,1,0:T(8,128)(2,1)S(1)} %bitcast.234), channel_id=1, source_target_pairs={{0,20},{2,22},{4,24},{6,26},{8,28},{10,30},{12,0},{14,2},{16,4},{1... | collective-permute-start | bytes 196616 | tf_op jit(solution)/shard_map/ppermute | solution.py:41
  173.4 8.8 %collective-permute-start.42 = (bf16[2,16,1024]{2,1,0:T(8,128)(2,1)S(1)}, bf16[2,16,1024]{2,1,0:T(8,128)(2,1)S(1)}, u32[]{:S(2)}, u32[]{:S(2)}) collective-permute-start(bf16[2,16,1024]{2,1,0:T(8,128)(2,1)S(1)} %bitcast.226), channel_id=1, source_target_pairs={{0,18},{2,20},{4,22},{6,24},{8,26},{10,28},{12,30},{14,0},{16,2},{... | collective-permute-start | bytes 196616 | tf_op jit(solution)/shard_map/ppermute | solution.py:41
  (17 other events, 98.8 us)

commit v4 on v3

--- a/solution.py
+++ b/solution.py
@@ -601,40 +601,46 @@
         across = swap(jnp.stack(pieces[1:]), "side")
         held = place(pieces, slabs)
         rows_of, across, held = lax.optimization_barrier((rows_of, across, held))
+        out_far, out_side = swap(out_weight, "far"), swap(out_weight, "side")
         across = place([side_own] + [across[at] for at in range(chunks - 1)], slabs)
-        own_rows = jnp.concatenate(rows_of)
-        peer_rows = swap(own_rows, "mdl")
-        at_core, at_side, at_half = core == 0, side == 0, part == 0
-        held_peer, across_peer = swap(held, "core"), swap(across, "core")
-
-        def full(columns):
-            own = [value[:, :, columns].reshape(-1, columns.stop - columns.start) for value in (held, across)]
-            peer = [
-                value[:, :, columns].reshape(-1, columns.stop - columns.start)
-                for value in (held_peer, across_peer)
+        held, across = held.reshape(-1, width), across.reshape(-1, width)
+        weights = jnp.concatenate([held, across, swap(held, "core"), swap(across, "core")])
+        early_own = jnp.concatenate(rows_of[1:3])
+        late_own = jnp.concatenate([rows_of[3], rows_of[0]])
+        early_peer = swap(early_own, "mdl")
+        early_own, early_peer, late_own, weights, out_side = lax.optimization_barrier(
+            (early_own, early_peer, late_own, weights, out_side)
+        )
+
+        def project(own, peer):
+            low = jnp.where(part == core, own, peer)
+            high = jnp.where(part == core, peer, own)
+            quarter = depth // 4
+            lhs = [
+                lax.dynamic_slice_in_dim(value, at_side * quarter, quarter, 1)
+                for value in (low, high)
+                for at_side in (side, 1 - side)
             ]
-            parts = []
-            for first, second in ((own, peer), (peer, own)):
-                low = [jnp.where(at_core, first[at], second[at]) for at in range(2)]
-                parts += [jnp.where(at_side, low[0], low[1]), jnp.where(at_side, low[1], low[0])]
-            return jnp.concatenate(parts)
-
-        packed_full, gate_full = full(slice(0, split)), full(slice(split, width))
-        out_far, out_side = swap(out_weight, "far"), swap(out_weight, "side")
-        own_rows, peer_rows, packed_full, gate_full, out_far, out_side = lax.optimization_barrier(
-            (own_rows, peer_rows, packed_full, gate_full, out_far, out_side)
-        )
-        all_rows = jnp.concatenate(
-            [jnp.where(at_half, own_rows, peer_rows), jnp.where(at_half, peer_rows, own_rows)], axis=1
-        )
-        packed = jnp.dot(all_rows, packed_full, preferred_element_type=F32).astype(BF16)
-        packed = packed.reshape(chunks, rows, split)
-        packed = [rotate(packed[step], SLABS, -step) for step in range(chunks)]
-        gate = jnp.dot(all_rows, gate_full, preferred_element_type=F32).astype(BF16)
-        gate = gate.reshape(chunks, rows, lanes)
+            total = jnp.dot(jnp.concatenate(lhs, axis=1), weights, preferred_element_type=F32)
+            return total.astype(BF16)
+
+        late_peer = swap(late_own, "mdl")
+        early = project(early_own, early_peer)
+        packed_1 = rotate(early[:rows, :split], SLABS, -1)
+        packed_2 = rotate(early[rows:, :split], SLABS, -2)
+        late = project(late_own, late_peer)
+        packed_3 = rotate(late[:rows, :split], SLABS, -3)
+        early, late, packed_1, packed_2, packed_3, out_far = lax.optimization_barrier(
+            (early, late, packed_1, packed_2, packed_3, out_far)
+        )
+        packed = [late[rows:, :split], packed_1, packed_2, packed_3]
+        gate = [
+            late[rows:, split:],
+            rotate(early[:rows, split:], SLABS, -1),
+            rotate(early[rows:, split:], SLABS, -2),
+            rotate(late[:rows, split:], SLABS, -3),
+        ]
         out_across = swap(out_far, "side")
-        packed, gate, out_across = lax.optimization_barrier((packed, gate, out_across))
-        gate = [rotate(gate[step], SLABS, -step) for step in range(chunks)]
         out_columns = []
         for column in (out_weight, out_side, out_far, out_across):
             out_columns += [column, swap(column, "core")]

time: 185 us -> 180 us (0.973)
  other arithmetic: 14.9 us -> 9.21 us
  waiting for transfers between devices: 71.8 us -> 68.1 us
  local copies, waits for them, and re-layouts: 16.6 us -> 19.1 us
    ppermute x42 -> x43, waiting for transfers between devices: 69.8 us -> 66 us  [rotate(): return lax.ppermute(value, axis, pairs)]
    select_n x3 -> x2, other arithmetic: 3.51 us -> 0.2 us  [project(): low = jnp.where(part == core, own, peer)]
    concatenate x2, other arithmetic: 6.26 us -> 3.86 us  [the longest x1 2.88 us: on_device(): jnp.concatenate([held, across, swap(held, 'core'), swap(across, 'core')])]
    ppermute x42 -> x43, starting transfers between devices: 50.5 us -> 52.4 us  [rotate(): return lax.ppermute(value, axis, pairs)]
    unnamed x83 -> x85, local copies, waits for them, and re-layouts: 4.51 us -> 5.43 us
  transfers between devices with their start and end apart: 43 -> 44, of which waited for: 13 -> 13; matrix products, arithmetic and copies ran while one was open for 15% -> 14% of each run, Pallas kernels for 12% -> 13%
where the time goes in v4:
time: 180 us; the launch traced here: 179 us
  waiting for transfers between devices  68.1 us (38%)
  starting transfers between devices  53.9 us (30%)
  Pallas kernels  22.9 us (13%)
  local copies, waits for them, and re-layouts  19.1 us (11%)
  other arithmetic  9.21 us (5%)
  matrix products  4.35 us (2%)
    ppermute x43, waiting for transfers between devices, rotate(): return lax.ppermute(value, axis, pairs)  66 us
    ppermute x43, starting transfers between devices, rotate(): return lax.ppermute(value, axis, pairs)  52.4 us
    pallas_call x1, Pallas kernels, mix_requests(): pl.pallas_call(lambda *refs: mixer_kernel(sizes, *refs), grid_spec=grid_s...  9.72 us
    pallas_call x1, Pallas kernels, update_states(): pl.pallas_call(lambda *refs: update_kernel(sizes, *refs), grid=(steps,),...  8.75 us
    unnamed x85, local copies, waits for them, and re-layouts  5.43 us
  transfers between devices with their start and end apart: 44, of which 13 were waited for; matrix products, arithmetic and copies ran while one was open for 14% of the time, Pallas kernels for 13%

profile of v4, /device:TPU:1, one launch (start us, length us, event | category | flops | bytes accessed | tf_op | source)
XLA Modules:
  0.0 179.3 jit_solution(15344003856805630466)
XLA Ops:
  0.7 1.3 copy.74
  3.6 2.7 %collective-permute-start = (bf16[2,16,1024]{2,1,0:T(8,128)(2,1)S(1)}, bf16[2,16,1024]{2,1,0:T(8,128)(2,1)S(1)}, u32[]{:S(2)}, u32[]{:S(2)}) collective-permute-start(bf16[2,16,1024]{2,1,0:T(8,128)(2,1)S(1)} %bitcast.177), channel_id=1, source_target_pairs={{0,2},{2,4},{4,6},{6,8},{8,10},{10,12},{12,14},{14,16},{16,18},{18... | collective-permute-start | bytes 196616 | tf_op jit(solution)/shard_map/ppermute | solution.py:41
  6.3 1.3 collective-permute-start.1
  8.0 1.4 collective-permute-start.3
  9.4 2.5 %collective-permute-start.4 = (bf16[2,16,1024]{2,1,0:T(8,128)(2,1)S(1)}, bf16[2,16,1024]{2,1,0:T(8,128)(2,1)S(1)}, u32[]{:S(2)}, u32[]{:S(2)}) collective-permute-start(bf16[2,16,1024]{2,1,0:T(8,128)(2,1)S(1)} %bitcast.180), channel_id=1, source_target_pairs={{0,10},{2,12},{4,14},{6,16},{8,18},{10,20},{12,22},{14,24},{16,26}... | collective-permute-start | bytes 196616 | tf_op jit(solution)/shard_map/ppermute | solution.py:41
  15.4 2.1 %collective-permute-start.5 = (bf16[2,16,1024]{2,1,0:T(8,128)(2,1)S(1)}, bf16[2,16,1024]{2,1,0:T(8,128)(2,1)S(1)}, u32[]{:S(2)}, u32[]{:S(2)}) collective-permute-start(bf16[2,16,1024]{2,1,0:T(8,128)(2,1)S(1)} %bitcast.182), channel_id=1, source_target_pairs={{0,12},{2,14},{4,16},{6,18},{8,20},{10,22},{12,24},{14,26},{16,28}... | collective-permute-start | bytes 196616 | tf_op jit(solution)/shard_map/ppermute | solution.py:41
  18.8 1.9 %collective-permute-start.8 = (bf16[128,1152]{1,0:T(8,128)(2,1)S(1)}, bf16[128,1152]{1,0:T(8,128)(2,1)S(1)}, u32[]{:S(2)}, u32[]{:S(2)}) collective-permute-start(bf16[128,1152]{1,0:T(8,128)(2,1)S(1)} %bitcast.150), channel_id=1, source_target_pairs={{0,16},{8,24},{16,0},{24,8},{1,17},{9,25},{17,1},{25,9},{2,18},{10... | collective-permute-start | bytes 884744 | tf_op jit(solution)/shard_map/ppermute | solution.py:41
  20.9 1.6 collective-permute-start.9
  23.6 1.6 shard_map.210
  26.4 2.1 %collective-permute-start.6 = (bf16[2,16,1024]{2,1,0:T(8,128)(2,1)S(1)}, bf16[2,16,1024]{2,1,0:T(8,128)(2,1)S(1)}, u32[]{:S(2)}, u32[]{:S(2)}) collective-permute-start(bf16[2,16,1024]{2,1,0:T(8,128)(2,1)S(1)} %bitcast.181), channel_id=1, source_target_pairs={{0,14},{2,16},{4,18},{6,20},{8,22},{10,24},{12,26},{14,28},{16,30}... | collective-permute-start | bytes 196616 | tf_op jit(solution)/shard_map/ppermute | solution.py:41
  29.1 21.6 %collective-permute-done.6 = bf16[2,16,1024]{2,1,0:T(8,128)(2,1)S(1)} collective-permute-done((bf16[2,16,1024]{2,1,0:T(8,128)(2,1)S(1)}, bf16[2,16,1024]{2,1,0:T(8,128)(2,1)S(1)}, u32[]{:S(2)}, u32[]{:S(2)}) %collective-permute-start.6) | collective-permute-done | bytes 65568 | tf_op jit(solution)/shard_map/ppermute | solution.py:41
  52.3 2.6 %collective-permute-start.13 = (bf16[128,1024]{1,0:T(8,128)(2,1)S(1)}, bf16[128,1024]{1,0:T(8,128)(2,1)S(1)}, u32[]{:S(2)}, u32[]{:S(2)}) collective-permute-start(bf16[128,1024]{1,0:T(8,128)(2,1)S(1)} %reshape.252), channel_id=1, source_target_pairs={{0,24},{8,0},{16,8},{24,16},{1,25},{9,1},{17,9},{25,17},{2,26},{10... | collective-permute-start | bytes 786440 | tf_op jit(solution)/shard_map/ppermute | solution.py:41
  55.1 1.1 broadcast.204.clone
  59.3 2.5 %collective-permute-done.11 = bf16[128,1024]{1,0:T(8,128)(2,1)S(1)} collective-permute-done((bf16[128,1024]{1,0:T(8,128)(2,1)S(1)}, bf16[128,1024]{1,0:T(8,128)(2,1)S(1)}, u32[]{:S(2)}, u32[]{:S(2)}) %collective-permute-start.11) | collective-permute-done | bytes 262176 | tf_op jit(solution)/shard_map/ppermute | solution.py:41
  61.8 10.3 %collective-permute-done.12 = bf16[128,1024]{1,0:T(8,128)(2,1)S(1)} collective-permute-done((bf16[128,1024]{1,0:T(8,128)(2,1)S(1)}, bf16[128,1024]{1,0:T(8,128)(2,1)S(1)}, u32[]{:S(2)}, u32[]{:S(2)}) %collective-permute-start.12) | collective-permute-done | bytes 262176 | tf_op jit(solution)/shard_map/ppermute | solution.py:41
  72.1 4.0 %collective-permute-done.14 = bf16[3,128,1152]{2,1,0:T(8,128)(2,1)S(1)} collective-permute-done((bf16[3,128,1152]{2,1,0:T(8,128)(2,1)S(1)}, bf16[3,128,1152]{2,1,0:T(8,128)(2,1)S(1)}, u32[]{:S(2)}, u32[]{:S(2)}) %collective-permute-start.14) | collective-permute-done | bytes 884768 | tf_op jit(solution)/shard_map/ppermute | solution.py:41
  76.2 1.1 collective-permute-start.17
  77.4 1.5 collective-permute-start.23
  80.9 1.3 collective-permute-start.15
  83.2 2.9 %pad_maximum_fusion = bf16[2048,1152]{1,0:T(8,128)(2,1)S(1)} fusion(bf16[512,1152]{1,0:T(8,128)(2,1)} %collective-permute-done.17, bf16[512,1152]{1,0:T(8,128)(2,1)} %collective-permute-done.16, bf16[512,1152]{1,0:T(8,128)(2,1)S(1)} %bitcast.137, bf16[512,1152]{1,0:T(8,128)(2,1)} %bitcast.25), kind=kLoop, calls=%fused_computation.4 | loop fusion | flops 18874368 | bytes 9437184 | tf_op jit(solution)/shard_map/concatenate | solution.py:607
  86.1 4.4 %collective-permute-done.18.refs_2_ = bf16[2048,128]{1,0:T(8,128)(2,1)S(1)} collective-permute-done((bf16[2048,128]{1,0:T(8,128)(2,1)S(1)}, bf16[2048,128]{1,0:T(8,128)(2,1)S(1)}, u32[]{:S(2)}, u32[]{:S(2)}) %collective-permute-start.18) | collective-permute-done | bytes 524320 | tf_op jit(solution)/shard_map/ppermute | solution.py:41
  90.5 3.0 %collective-permute-done.15 = bf16[256,1024]{1,0:T(8,128)(2,1)S(1)} collective-permute-done((bf16[256,1024]{1,0:T(8,128)(2,1)S(1)}, bf16[256,1024]{1,0:T(8,128)(2,1)S(1)}, u32[]{:S(2)}, u32[]{:S(2)}) %collective-permute-start.15) | collective-permute-done | bytes 524320 | tf_op jit(solution)/shard_map/ppermute | solution.py:41
  93.7 1.3 collective-permute-start.19
  95.0 1.6 convolution_convert_fusion.5
  97.2 2.2 %collective-permute-start.20 = (bf16[128,640]{1,0:T(8,128)(2,1)}, bf16[128,640]{1,0:T(8,128)(2,1)S(1)}, u32[]{:S(2)}, u32[]{:S(2)}) collective-permute-start(bf16[128,640]{1,0:T(8,128)(2,1)} %get-tuple-element.180), channel_id=1, source_target_pairs={{0,24},{8,0},{16,8},{24,16},{1,25},{9,1},{17,9},{25,17},{2,26},{10... | collective-permute-start | bytes 491528 | tf_op jit(solution)/shard_map/ppermute | solution.py:41
  99.5 5.9 %collective-permute-done.19 = bf16[256,1024]{1,0:T(8,128)(2,1)S(1)} collective-permute-done((bf16[256,1024]{1,0:T(8,128)(2,1)S(1)}, bf16[256,1024]{1,0:T(8,128)(2,1)S(1)}, u32[]{:S(2)}, u32[]{:S(2)}) %collective-permute-start.19) | collective-permute-done | bytes 524320 | tf_op jit(solution)/shard_map/ppermute | solution.py:41
  105.6 1.6 convolution_convert_fusion.4
  107.9 7.0 %collective-permute-done.21.refs_3_.refs_7_ = bf16[128,640]{1,0:T(8,128)(2,1)S(1)} collective-permute-done((bf16[128,640]{1,0:T(8,128)(2,1)S(1)}, bf16[128,640]{1,0:T(8,128)(2,1)S(1)}, u32[]{:S(2)}, u32[]{:S(2)}) %collective-permute-start.21) | collective-permute-done | bytes 163872 | tf_op jit(solution)/shard_map/ppermute | solution.py:41
  115.7 3.2 %collective-permute-start.25 = (bf16[128,512]{1,0:T(8,128)(2,1)S(1)}, bf16[128,512]{1,0:T(8,128)(2,1)S(1)}, u32[]{:S(2)}, u32[]{:S(2)}) collective-permute-start(bf16[128,512]{1,0:T(8,128)(2,1)S(1)} %get-tuple-element.178), channel_id=1, source_target_pairs={{0,16},{8,24},{16,0},{24,8},{1,17},{9,25},{17,1},{25,9},{2,18},{10... | collective-permute-start | bytes 393224 | tf_op jit(solution)/shard_map/ppermute | solution.py:41
  118.8 1.1 collective-permute-start.26
  119.9 1.6 collective-permute-start.31
  121.5 9.7 %shard_map.211 = (bf16[128,2048]{1,0:T(8,128)(2,1)}, bf16[2048,256]{1,0:T(8,128)(2,1)}, f32[128,128]{1,0:T(8,128)}, f32[128,128]{1,0:T(8,128)}, bf16[32,2048]{1,0:T(8,128)(2,1)}, /*index=5*/bf16[32,256]{1,0:T(8,128)(2,1)}) custom-call(s32[4]{0:T(128)} %and_select_fusion.1.refs_0_, bf16[128,640]{1,0:T(8,128)(2,1)} %slice.175.refs_1_.refs_5_, ...), custom_call_target="tpu_custom_call" | custom-call | flops 2147483648 | bytes 16777216 | tf_op jit(solution)/shard_map/pallas_call | solution.py:391
  131.4 1.6 multiply_convert_fusion
  133.3 3.2 %collective-permute-start.28 = (bf16[2048,128]{1,0:T(8,128)(2,1)S(1)}, bf16[2048,128]{1,0:T(8,128)(2,1)}, u32[]{:S(2)}, u32[]{:S(2)}) collective-permute-start(bf16[2048,128]{1,0:T(8,128)(2,1)S(1)} %copy-done), channel_id=1, source_target_pairs={{0,2},{2,0},{1,3},{3,1},{4,6},{6,4},{5,7},{7,5},{8,10},{10,8},{9,1... | collective-permute-start | bytes 1572872 | tf_op jit(solution)/shard_map/ppermute | solution.py:41
  137.1 8.7 %shard_map.212 = f32[8,32,64,128]{3,2,1,0:T(8,128)} custom-call(bf16[2048,256]{1,0:T(8,128)(2,1)} %get-tuple-element.127.refs_0_, f32[128,128]{1,0:T(8,128)} %get-tuple-element.129.refs_1_, f32[128,128]{1,0:T(8,128)} %get-tuple-element.130.refs_2_, f32[8,32,64,128]{3,2,1,0:T(8,128)} %refs_3_.1), custom_call_target="tpu_custom_call" | custom-call | flops 2147483648 | bytes 16777216 | tf_op jit(solution)/shard_map/pallas_call | solution.py:293
  145.8 1.2 collective-permute-start.34
  147.1 2.9 %shard_map.213 = (f32[2,128,512]{2,1,0:T(8,128)S(1)}, bf16[2,2,128,512]{3,2,1,0:T(8,128)(2,1)S(1)}) custom-call(s32[4]{0:T(128)S(1)} %pad_add_fusion.place_ref, bf16[128,2048]{1,0:T(8,128)(2,1)S(1)} %get-tuple-element.167.own_ref, bf16[128,2048]{1,0:T(8,128)(2,1)S(1)} %collective-permute-done.27.peer_ref, bf16[2048,128]{1,0:T(8,128)(2,1)S(1)} %copy-done, ...), custom_call_target="tpu_custom_call" | custom-call | flops 1000 | bytes 1000 | tf_op jit(solution)/shard_map/pallas_call | solution.py:467
  150.0 1.5 collective-permute-start.36
  151.6 1.1 collective-permute-start.33
  152.7 2.1 %collective-permute-done.36 = bf16[128,512]{1,0:T(8,128)(2,1)S(1)} collective-permute-done((bf16[128,512]{1,0:T(8,128)(2,1)S(1)}, bf16[128,512]{1,0:T(8,128)(2,1)S(1)}, u32[]{:S(2)}, u32[]{:S(2)}) %collective-permute-start.36) | collective-permute-done | bytes 131104 | tf_op jit(solution)/shard_map/ppermute | solution.py:704
  154.9 1.4 collective-permute-done.35
  158.3 2.7 %collective-permute-start.37 = (bf16[2,16,1024]{2,1,0:T(8,128)(2,1)S(1)}, bf16[2,16,1024]{2,1,0:T(8,128)(2,1)S(1)}, u32[]{:S(2)}, u32[]{:S(2)}) collective-permute-start(bf16[2,16,1024]{2,1,0:T(8,128)(2,1)S(1)} %bitcast.196), channel_id=1, source_target_pairs={{0,30},{2,0},{4,2},{6,4},{8,6},{10,8},{12,10},{14,12},{16,14},{18,... | collective-permute-start | bytes 196616 | tf_op jit(solution)/shard_map/ppermute | solution.py:41
  161.0 2.5 %collective-permute-start.38 = (bf16[2,16,1024]{2,1,0:T(8,128)(2,1)S(1)}, bf16[2,16,1024]{2,1,0:T(8,128)(2,1)S(1)}, u32[]{:S(2)}, u32[]{:S(2)}) collective-permute-start(bf16[2,16,1024]{2,1,0:T(8,128)(2,1)S(1)} %bitcast.195), channel_id=1, source_target_pairs={{0,28},{2,30},{4,0},{6,2},{8,4},{10,6},{12,8},{14,10},{16,12},{18,... | collective-permute-start | bytes 196616 | tf_op jit(solution)/shard_map/ppermute | solution.py:41
  163.5 1.6 collective-permute-start.39
  165.2 1.0 collective-permute-start.41
  166.3 2.1 %collective-permute-start.42 = (bf16[2,16,1024]{2,1,0:T(8,128)(2,1)S(1)}, bf16[2,16,1024]{2,1,0:T(8,128)(2,1)S(1)}, u32[]{:S(2)}, u32[]{:S(2)}) collective-permute-start(bf16[2,16,1024]{2,1,0:T(8,128)(2,1)S(1)} %bitcast.192), channel_id=1, source_target_pairs={{0,20},{2,22},{4,24},{6,26},{8,28},{10,30},{12,0},{14,2},{16,4},{1... | collective-permute-start | bytes 196616 | tf_op jit(solution)/shard_map/ppermute | solution.py:41
  168.4 1.8 collective-permute-start.43
  172.8 4.4 %collective-permute-done.43 = bf16[2,16,1024]{2,1,0:T(8,128)(2,1)S(1)} collective-permute-done((bf16[2,16,1024]{2,1,0:T(8,128)(2,1)S(1)}, bf16[2,16,1024]{2,1,0:T(8,128)(2,1)S(1)}, u32[]{:S(2)}, u32[]{:S(2)}) %collective-permute-start.43) | collective-permute-done | bytes 65568 | tf_op jit(solution)/shard_map/ppermute | solution.py:41
  (215 shorter events, 28.0 us)
Async XLA Ops:
  3.6 11.8 %collective-permute-start = (bf16[2,16,1024]{2,1,0:T(8,128)(2,1)S(1)}, bf16[2,16,1024]{2,1,0:T(8,128)(2,1)S(1)}, u32[]{:S(2)}, u32[]{:S(2)}) collective-permute-start(bf16[2,16,1024]{2,1,0:T(8,128)(2,1)S(1)} %bitcast.177), channel_id=1, source_target_pairs={{0,2},{2,4},{4,6},{6,8},{8,10},{10,12},{12,14},{14,16},{16,18},{18... | collective-permute-start | bytes 196616 | tf_op jit(solution)/shard_map/ppermute | solution.py:41
  6.3 11.3 %collective-permute-start.1 = (bf16[2,16,1024]{2,1,0:T(8,128)(2,1)S(1)}, bf16[2,16,1024]{2,1,0:T(8,128)(2,1)S(1)}, u32[]{:S(2)}, u32[]{:S(2)}) collective-permute-start(bf16[2,16,1024]{2,1,0:T(8,128)(2,1)S(1)} %bitcast.176), channel_id=1, source_target_pairs={{0,4},{2,6},{4,8},{6,10},{8,12},{10,14},{12,16},{14,18},{16,20},{1... | collective-permute-start | bytes 196616 | tf_op jit(solution)/shard_map/ppermute | solution.py:41
  7.6 9.9 %collective-permute-start.2 = (bf16[2,16,1024]{2,1,0:T(8,128)(2,1)S(1)}, bf16[2,16,1024]{2,1,0:T(8,128)(2,1)S(1)}, u32[]{:S(2)}, u32[]{:S(2)}) collective-permute-start(bf16[2,16,1024]{2,1,0:T(8,128)(2,1)S(1)} %bitcast.178), channel_id=1, source_target_pairs={{0,6},{2,8},{4,10},{6,12},{8,14},{10,16},{12,18},{14,20},{16,22},{... | collective-permute-start | bytes 196616 | tf_op jit(solution)/shard_map/ppermute | solution.py:41
  8.0 9.5 %collective-permute-start.3 = (bf16[2,16,1024]{2,1,0:T(8,128)(2,1)S(1)}, bf16[2,16,1024]{2,1,0:T(8,128)(2,1)S(1)}, u32[]{:S(2)}, u32[]{:S(2)}) collective-permute-start(bf16[2,16,1024]{2,1,0:T(8,128)(2,1)S(1)} %bitcast.179), channel_id=1, source_target_pairs={{0,8},{2,10},{4,12},{6,14},{8,16},{10,18},{12,20},{14,22},{16,24},... | collective-permute-start | bytes 196616 | tf_op jit(solution)/shard_map/ppermute | solution.py:41
  9.4 8.2 %collective-permute-start.4 = (bf16[2,16,1024]{2,1,0:T(8,128)(2,1)S(1)}, bf16[2,16,1024]{2,1,0:T(8,128)(2,1)S(1)}, u32[]{:S(2)}, u32[]{:S(2)}) collective-permute-start(bf16[2,16,1024]{2,1,0:T(8,128)(2,1)S(1)} %bitcast.180), channel_id=1, source_target_pairs={{0,10},{2,12},{4,14},{6,16},{8,18},{10,20},{12,22},{14,24},{16,26}... | collective-permute-start | bytes 196616 | tf_op jit(solution)/shard_map/ppermute | solution.py:41
  15.4 11.0 %collective-permute-start.5 = (bf16[2,16,1024]{2,1,0:T(8,128)(2,1)S(1)}, bf16[2,16,1024]{2,1,0:T(8,128)(2,1)S(1)}, u32[]{:S(2)}, u32[]{:S(2)}) collective-permute-start(bf16[2,16,1024]{2,1,0:T(8,128)(2,1)S(1)} %bitcast.182), channel_id=1, source_target_pairs={{0,12},{2,14},{4,16},{6,18},{8,20},{10,22},{12,24},{14,26},{16,28}... | collective-permute-start | bytes 196616 | tf_op jit(solution)/shard_map/ppermute | solution.py:41
  18.1 32.6 %collective-permute-start.7 = (bf16[128,1152]{1,0:T(8,128)(2,1)S(1)}, bf16[128,1152]{1,0:T(8,128)(2,1)S(1)}, u32[]{:S(2)}, u32[]{:S(2)}) collective-permute-start(bf16[128,1152]{1,0:T(8,128)(2,1)S(1)} %bitcast.149), channel_id=1, source_target_pairs={{0,8},{8,16},{16,24},{24,0},{1,9},{9,17},{17,25},{25,1},{2,10},{10... | collective-permute-start | bytes 884744 | tf_op jit(solution)/shard_map/ppermute | solution.py:41
  18.8 31.9 %collective-permute-start.8 = (bf16[128,1152]{1,0:T(8,128)(2,1)S(1)}, bf16[128,1152]{1,0:T(8,128)(2,1)S(1)}, u32[]{:S(2)}, u32[]{:S(2)}) collective-permute-start(bf16[128,1152]{1,0:T(8,128)(2,1)S(1)} %bitcast.150), channel_id=1, source_target_pairs={{0,16},{8,24},{16,0},{24,8},{1,17},{9,25},{17,1},{25,9},{2,18},{10... | collective-permute-start | bytes 884744 | tf_op jit(solution)/shard_map/ppermute | solution.py:41
  20.9 29.8 %collective-permute-start.9 = (bf16[128,1152]{1,0:T(8,128)(2,1)S(1)}, bf16[128,1152]{1,0:T(8,128)(2,1)S(1)}, u32[]{:S(2)}, u32[]{:S(2)}) collective-permute-start(bf16[128,1152]{1,0:T(8,128)(2,1)S(1)} %bitcast.151), channel_id=1, source_target_pairs={{0,24},{8,0},{16,8},{24,16},{1,25},{9,1},{17,9},{25,17},{2,26},{10... | collective-permute-start | bytes 884744 | tf_op jit(solution)/shard_map/ppermute | solution.py:41
  22.5 28.2 %collective-permute-start.10 = (bf16[128,1152]{1,0:T(8,128)(2,1)S(1)}, bf16[128,1152]{1,0:T(8,128)(2,1)S(1)}, u32[]{:S(2)}, u32[]{:S(2)}) collective-permute-start(bf16[128,1152]{1,0:T(8,128)(2,1)S(1)} %bitcast.146), channel_id=1, source_target_pairs={{0,4},{4,0},{1,5},{5,1},{2,6},{6,2},{3,7},{7,3},{8,12},{12,8},{9,1... | collective-permute-start | bytes 884744 | tf_op jit(solution)/shard_map/ppermute | solution.py:41
  26.4 24.3 %collective-permute-start.6 = (bf16[2,16,1024]{2,1,0:T(8,128)(2,1)S(1)}, bf16[2,16,1024]{2,1,0:T(8,128)(2,1)S(1)}, u32[]{:S(2)}, u32[]{:S(2)}) collective-permute-start(bf16[2,16,1024]{2,1,0:T(8,128)(2,1)S(1)} %bitcast.181), channel_id=1, source_target_pairs={{0,14},{2,16},{4,18},{6,20},{8,22},{10,24},{12,26},{14,28},{16,30}... | collective-permute-start | bytes 196616 | tf_op jit(solution)/shard_map/ppermute | solution.py:41
  51.6 10.2 %collective-permute-start.11 = (bf16[128,1024]{1,0:T(8,128)(2,1)S(1)}, bf16[128,1024]{1,0:T(8,128)(2,1)S(1)}, u32[]{:S(2)}, u32[]{:S(2)}) collective-permute-start(bf16[128,1024]{1,0:T(8,128)(2,1)S(1)} %reshape.252), channel_id=1, source_target_pairs={{0,8},{8,16},{16,24},{24,0},{1,9},{9,17},{17,25},{25,1},{2,10},{10... | collective-permute-start | bytes 786440 | tf_op jit(solution)/shard_map/ppermute | solution.py:41
  51.6 20.5 %collective-permute-start.12 = (bf16[128,1024]{1,0:T(8,128)(2,1)S(1)}, bf16[128,1024]{1,0:T(8,128)(2,1)S(1)}, u32[]{:S(2)}, u32[]{:S(2)}) collective-permute-start(bf16[128,1024]{1,0:T(8,128)(2,1)S(1)} %reshape.252), channel_id=1, source_target_pairs={{0,16},{8,24},{16,0},{24,8},{1,17},{9,25},{17,1},{25,9},{2,18},{10... | collective-permute-start | bytes 786440 | tf_op jit(solution)/shard_map/ppermute | solution.py:41
  52.3 19.8 %collective-permute-start.13 = (bf16[128,1024]{1,0:T(8,128)(2,1)S(1)}, bf16[128,1024]{1,0:T(8,128)(2,1)S(1)}, u32[]{:S(2)}, u32[]{:S(2)}) collective-permute-start(bf16[128,1024]{1,0:T(8,128)(2,1)S(1)} %reshape.252), channel_id=1, source_target_pairs={{0,24},{8,0},{16,8},{24,16},{1,25},{9,1},{17,9},{25,17},{2,26},{10... | collective-permute-start | bytes 786440 | tf_op jit(solution)/shard_map/ppermute | solution.py:41
  55.0 21.1 %collective-permute-start.14 = (bf16[3,128,1152]{2,1,0:T(8,128)(2,1)S(1)}, bf16[3,128,1152]{2,1,0:T(8,128)(2,1)S(1)}, u32[]{:S(2)}, u32[]{:S(2)}) collective-permute-start(bf16[3,128,1152]{2,1,0:T(8,128)(2,1)S(1)} %pad_maximum_fusion.1), channel_id=1, source_target_pairs={{0,4},{4,0},{1,5},{5,1},{2,6},{6,2},{3,7},{7,3},{8,12},{12,8},{9,1... | collective-permute-start | bytes 2654216 | tf_op jit(solution)/shard_map/ppermute | solution.py:41
  58.4 19.0 %copy-start = (bf16[2048,128]{1,0:T(8,128)(2,1)S(1)}, bf16[2048,128]{1,0:T(8,128)(2,1)}, u32[]{:S(2)}) copy-start(bf16[2048,128]{1,0:T(8,128)(2,1)} %refs_0_.1) | copy-start | bytes 1572868
  61.8 15.5 %copy-start.8 = (bf16[128,1024]{1,0:T(8,128)(2,1)}, bf16[128,1024]{1,0:T(8,128)(2,1)S(1)}, u32[]{:S(2)}) copy-start(bf16[128,1024]{1,0:T(8,128)(2,1)S(1)} %collective-permute-done.11) | copy-start | bytes 786436
  76.2 7.0 %collective-permute-start.17 = (bf16[512,1152]{1,0:T(8,128)(2,1)S(1)}, bf16[512,1152]{1,0:T(8,128)(2,1)}, u32[]{:S(2)}, u32[]{:S(2)}) collective-permute-start(bf16[512,1152]{1,0:T(8,128)(2,1)S(1)} %bitcast.136), channel_id=1, source_target_pairs={{0,2},{2,0},{1,3},{3,1},{4,6},{6,4},{5,7},{7,5},{8,10},{10,8},{9,1... | collective-permute-start | bytes 3538952 | tf_op jit(solution)/shard_map/ppermute | solution.py:41
  77.3 5.9 %collective-permute-start.16 = (bf16[512,1152]{1,0:T(8,128)(2,1)}, bf16[512,1152]{1,0:T(8,128)(2,1)}, u32[]{:S(2)}, u32[]{:S(2)}) collective-permute-start(bf16[512,1152]{1,0:T(8,128)(2,1)} %bitcast.25), channel_id=1, source_target_pairs={{0,2},{2,0},{1,3},{3,1},{4,6},{6,4},{5,7},{7,5},{8,10},{10,8},{9,1... | collective-permute-start | bytes 3538952 | tf_op jit(solution)/shard_map/ppermute | solution.py:41
  77.4 13.1 %collective-permute-start.18 = (bf16[2048,128]{1,0:T(8,128)(2,1)S(1)}, bf16[2048,128]{1,0:T(8,128)(2,1)S(1)}, u32[]{:S(2)}, u32[]{:S(2)}) collective-permute-start(bf16[2048,128]{1,0:T(8,128)(2,1)S(1)} %copy-done), channel_id=1, source_target_pairs={{0,4},{4,0},{1,5},{5,1},{2,6},{6,2},{3,7},{7,3},{8,12},{12,8},{9,1... | collective-permute-start | bytes 1572872 | tf_op jit(solution)/shard_map/ppermute | solution.py:41
  77.4 30.4 %collective-permute-start.23 = (bf16[2048,128]{1,0:T(8,128)(2,1)S(1)}, bf16[2048,128]{1,0:T(8,128)(2,1)S(1)}, u32[]{:S(2)}, u32[]{:S(2)}) collective-permute-start(bf16[2048,128]{1,0:T(8,128)(2,1)S(1)} %copy-done), channel_id=1, source_target_pairs={{0,16},{16,0},{1,17},{17,1},{2,18},{18,2},{3,19},{19,3},{4,20},{20... | collective-permute-start | bytes 1572872 | tf_op jit(solution)/shard_map/ppermute | solution.py:41
  80.9 12.6 %collective-permute-start.15 = (bf16[256,1024]{1,0:T(8,128)(2,1)S(1)}, bf16[256,1024]{1,0:T(8,128)(2,1)S(1)}, u32[]{:S(2)}, u32[]{:S(2)}) collective-permute-start(bf16[256,1024]{1,0:T(8,128)(2,1)S(1)} %constant_dynamic-update-slice_fusion.8), channel_id=1, source_target_pairs={{0,1},{1,0},{2,3},{3,2},{4,5},{5,4},{6,7},{7,6},{8,9},{9,8},{10,11... | collective-permute-start | bytes 1572872 | tf_op jit(solution)/shard_map/ppermute | solution.py:41
  93.7 11.7 %collective-permute-start.19 = (bf16[256,1024]{1,0:T(8,128)(2,1)S(1)}, bf16[256,1024]{1,0:T(8,128)(2,1)S(1)}, u32[]{:S(2)}, u32[]{:S(2)}) collective-permute-start(bf16[256,1024]{1,0:T(8,128)(2,1)S(1)} %pad_maximum_fusion.2), channel_id=1, source_target_pairs={{0,1},{1,0},{2,3},{3,2},{4,5},{5,4},{6,7},{7,6},{8,9},{9,8},{10,11... | collective-permute-start | bytes 1572872 | tf_op jit(solution)/shard_map/ppermute | solution.py:41
  97.2 10.6 %collective-permute-start.20 = (bf16[128,640]{1,0:T(8,128)(2,1)}, bf16[128,640]{1,0:T(8,128)(2,1)S(1)}, u32[]{:S(2)}, u32[]{:S(2)}) collective-permute-start(bf16[128,640]{1,0:T(8,128)(2,1)} %get-tuple-element.180), channel_id=1, source_target_pairs={{0,24},{8,0},{16,8},{24,16},{1,25},{9,1},{17,9},{25,17},{2,26},{10... | collective-permute-start | bytes 491528 | tf_op jit(solution)/shard_map/ppermute | solution.py:41
  99.5 15.4 %collective-permute-start.21 = (bf16[128,640]{1,0:T(8,128)(2,1)S(1)}, bf16[128,640]{1,0:T(8,128)(2,1)S(1)}, u32[]{:S(2)}, u32[]{:S(2)}) collective-permute-start(bf16[128,640]{1,0:T(8,128)(2,1)S(1)} %get-tuple-element.179), channel_id=1, source_target_pairs={{0,16},{8,24},{16,0},{24,8},{1,17},{9,25},{17,1},{25,9},{2,18},{10... | collective-permute-start | bytes 491528 | tf_op jit(solution)/shard_map/ppermute | solution.py:41
  107.8 7.0 %collective-permute-start.22 = (bf16[128,640]{1,0:T(8,128)(2,1)}, bf16[128,640]{1,0:T(8,128)(2,1)S(1)}, u32[]{:S(2)}, u32[]{:S(2)}) collective-permute-start(bf16[128,640]{1,0:T(8,128)(2,1)} %slice.213), channel_id=1, source_target_pairs={{0,8},{8,16},{16,24},{24,0},{1,9},{9,17},{17,25},{25,1},{2,10},{10... | collective-permute-start | bytes 491528 | tf_op jit(solution)/shard_map/ppermute | solution.py:41
  107.8 13.7 %copy-start.1 = (bf16[128,640]{1,0:T(8,128)(2,1)}, bf16[128,640]{1,0:T(8,128)(2,1)S(1)}, u32[]{:S(2)}) copy-start(bf16[128,640]{1,0:T(8,128)(2,1)S(1)} %collective-permute-done.20.refs_2_.refs_6_) | copy-start | bytes 491524
  115.6 15.7 %collective-permute-start.24 = (bf16[128,512]{1,0:T(8,128)(2,1)S(1)}, bf16[128,512]{1,0:T(8,128)(2,1)S(1)}, u32[]{:S(2)}, u32[]{:S(2)}) collective-permute-start(bf16[128,512]{1,0:T(8,128)(2,1)S(1)} %slice.176), channel_id=1, source_target_pairs={{0,8},{8,16},{16,24},{24,0},{1,9},{9,17},{17,25},{25,1},{2,10},{10... | collective-permute-start | bytes 393224 | tf_op jit(solution)/shard_map/ppermute | solution.py:41
  115.7 15.6 %collective-permute-start.25 = (bf16[128,512]{1,0:T(8,128)(2,1)S(1)}, bf16[128,512]{1,0:T(8,128)(2,1)S(1)}, u32[]{:S(2)}, u32[]{:S(2)}) collective-permute-start(bf16[128,512]{1,0:T(8,128)(2,1)S(1)} %get-tuple-element.178), channel_id=1, source_target_pairs={{0,16},{8,24},{16,0},{24,8},{1,17},{9,25},{17,1},{25,9},{2,18},{10... | collective-permute-start | bytes 393224 | tf_op jit(solution)/shard_map/ppermute | solution.py:41
  118.8 12.5 %collective-permute-start.26 = (bf16[128,512]{1,0:T(8,128)(2,1)S(1)}, bf16[128,512]{1,0:T(8,128)(2,1)S(1)}, u32[]{:S(2)}, u32[]{:S(2)}) collective-permute-start(bf16[128,512]{1,0:T(8,128)(2,1)S(1)} %get-tuple-element.177), channel_id=1, source_target_pairs={{0,24},{8,0},{16,8},{24,16},{1,25},{9,1},{17,9},{25,17},{2,26},{10... | collective-permute-start | bytes 393224 | tf_op jit(solution)/shard_map/ppermute | solution.py:41
  119.9 17.1 %collective-permute-start.31 = (bf16[2048,128]{1,0:T(8,128)(2,1)S(1)}, bf16[2048,128]{1,0:T(8,128)(2,1)S(1)}, u32[]{:S(2)}, u32[]{:S(2)}) collective-permute-start(bf16[2048,128]{1,0:T(8,128)(2,1)S(1)} %collective-permute-done.23.refs_4_), channel_id=1, source_target_pairs={{0,4},{4,0},{1,5},{5,1},{2,6},{6,2},{3,7},{7,3},{8,12},{12,8},{9,1... | collective-permute-start | bytes 1572872 | tf_op jit(solution)/shard_map/ppermute | solution.py:41
  133.0 12.9 %collective-permute-start.27 = (bf16[128,2048]{1,0:T(8,128)(2,1)S(1)}, bf16[128,2048]{1,0:T(8,128)(2,1)S(1)}, u32[]{:S(2)}, u32[]{:S(2)}) collective-permute-start(bf16[128,2048]{1,0:T(8,128)(2,1)S(1)} %get-tuple-element.167.own_ref), channel_id=1, source_target_pairs={{0,8},{8,0},{1,9},{9,1},{2,10},{10,2},{3,11},{11,3},{4,12},{12,4},... | collective-permute-start | bytes 1572872 | tf_op jit(solution)/shard_map/ppermute | solution.py:41
  133.3 13.8 %collective-permute-start.28 = (bf16[2048,128]{1,0:T(8,128)(2,1)S(1)}, bf16[2048,128]{1,0:T(8,128)(2,1)}, u32[]{:S(2)}, u32[]{:S(2)}) collective-permute-start(bf16[2048,128]{1,0:T(8,128)(2,1)S(1)} %copy-done), channel_id=1, source_target_pairs={{0,2},{2,0},{1,3},{3,1},{4,6},{6,4},{5,7},{7,5},{8,10},{10,8},{9,1... | collective-permute-start | bytes 1572872 | tf_op jit(solution)/shard_map/ppermute | solution.py:41
  136.5 10.6 %collective-permute-start.29 = (bf16[2048,128]{1,0:T(8,128)(2,1)S(1)}, bf16[2048,128]{1,0:T(8,128)(2,1)}, u32[]{:S(2)}, u32[]{:S(2)}) collective-permute-start(bf16[2048,128]{1,0:T(8,128)(2,1)S(1)} %collective-permute-done.18.refs_2_), channel_id=1, source_target_pairs={{0,2},{2,0},{1,3},{3,1},{4,6},{6,4},{5,7},{7,5},{8,10},{10,8},{9,1... | collective-permute-start | bytes 1572872 | tf_op jit(solution)/shard_map/ppermute | solution.py:41
  136.5 10.6 %collective-permute-start.30 = (bf16[2048,128]{1,0:T(8,128)(2,1)S(1)}, bf16[2048,128]{1,0:T(8,128)(2,1)}, u32[]{:S(2)}, u32[]{:S(2)}) collective-permute-start(bf16[2048,128]{1,0:T(8,128)(2,1)S(1)} %collective-permute-done.23.refs_4_), channel_id=1, source_target_pairs={{0,2},{2,0},{1,3},{3,1},{4,6},{6,4},{5,7},{7,5},{8,10},{10,8},{9,1... | collective-permute-start | bytes 1572872 | tf_op jit(solution)/shard_map/ppermute | solution.py:41
  137.0 10.1 %collective-permute-start.32 = (bf16[2048,128]{1,0:T(8,128)(2,1)S(1)}, bf16[2048,128]{1,0:T(8,128)(2,1)}, u32[]{:S(2)}, u32[]{:S(2)}) collective-permute-start(bf16[2048,128]{1,0:T(8,128)(2,1)S(1)} %collective-permute-done.31.refs_6_), channel_id=1, source_target_pairs={{0,2},{2,0},{1,3},{3,1},{4,6},{6,4},{5,7},{7,5},{8,10},{10,8},{9,1... | collective-permute-start | bytes 1572872 | tf_op jit(solution)/shard_map/ppermute | solution.py:41
  145.8 6.9 %collective-permute-start.34 = (f32[128]{0:T(128)S(1)}, f32[128]{0:T(128)S(1)}, u32[]{:S(2)}, u32[]{:S(2)}) collective-permute-start(f32[128]{0:T(128)S(1)} %get-tuple-element.168), channel_id=1, source_target_pairs={{0,1},{1,0},{2,3},{3,2},{4,5},{5,4},{6,7},{7,6},{8,9},{9,8},{10,11... | collective-permute-start | bytes 1544 | tf_op jit(solution)/shard_map/ppermute | solution.py:41
  150.0 4.9 %collective-permute-start.36 = (bf16[128,512]{1,0:T(8,128)(2,1)S(1)}, bf16[128,512]{1,0:T(8,128)(2,1)S(1)}, u32[]{:S(2)}, u32[]{:S(2)}) collective-permute-start(bf16[128,512]{1,0:T(8,128)(2,1)S(1)} %get-tuple-element.190), channel_id=1, source_target_pairs={{0,9},{1,8},{8,1},{9,0},{2,11},{3,10},{10,3},{11,2},{4,13},{5,12},... | collective-permute-start | bytes 393224 | tf_op jit(solution)/shard_map/ppermute | solution.py:704
  151.5 4.8 %collective-permute-start.35 = (bf16[128,512]{1,0:T(8,128)(2,1)S(1)}, bf16[128,512]{1,0:T(8,128)(2,1)S(1)}, u32[]{:S(2)}, u32[]{:S(2)}) collective-permute-start(bf16[128,512]{1,0:T(8,128)(2,1)S(1)} %get-tuple-element.191), channel_id=1, source_target_pairs={{0,8},{8,0},{1,9},{9,1},{2,10},{10,2},{3,11},{11,3},{4,12},{12,4},... | collective-permute-start | bytes 393224 | tf_op jit(solution)/shard_map/ppermute | solution.py:41
  151.6 5.4 %collective-permute-start.33 = (bf16[128,512]{1,0:T(8,128)(2,1)S(1)}, bf16[128,512]{1,0:T(8,128)(2,1)S(1)}, u32[]{:S(2)}, u32[]{:S(2)}) collective-permute-start(bf16[128,512]{1,0:T(8,128)(2,1)S(1)} %get-tuple-element.189), channel_id=1, source_target_pairs={{0,1},{1,0},{2,3},{3,2},{4,5},{5,4},{6,7},{7,6},{8,9},{9,8},{10,11... | collective-permute-start | bytes 393224 | tf_op jit(solution)/shard_map/ppermute | solution.py:41
  157.3 13.7 %copy-start.15 = (bf16[32,256]{1,0:T(8,128)(2,1)S(1)}, bf16[32,256]{1,0:T(8,128)(2,1)}, u32[]{:S(2)}) copy-start(bf16[32,256]{1,0:T(8,128)(2,1)} %get-tuple-element.137) | copy-start | bytes 49156
  158.3 8.0 %collective-permute-start.37 = (bf16[2,16,1024]{2,1,0:T(8,128)(2,1)S(1)}, bf16[2,16,1024]{2,1,0:T(8,128)(2,1)S(1)}, u32[]{:S(2)}, u32[]{:S(2)}) collective-permute-start(bf16[2,16,1024]{2,1,0:T(8,128)(2,1)S(1)} %bitcast.196), channel_id=1, source_target_pairs={{0,30},{2,0},{4,2},{6,4},{8,6},{10,8},{12,10},{14,12},{16,14},{18,... | collective-permute-start | bytes 196616 | tf_op jit(solution)/shard_map/ppermute | solution.py:41
  161.0 7.4 %collective-permute-start.38 = (bf16[2,16,1024]{2,1,0:T(8,128)(2,1)S(1)}, bf16[2,16,1024]{2,1,0:T(8,128)(2,1)S(1)}, u32[]{:S(2)}, u32[]{:S(2)}) collective-permute-start(bf16[2,16,1024]{2,1,0:T(8,128)(2,1)S(1)} %bitcast.195), channel_id=1, source_target_pairs={{0,28},{2,30},{4,0},{6,2},{8,4},{10,6},{12,8},{14,10},{16,12},{18,... | collective-permute-start | bytes 196616 | tf_op jit(solution)/shard_map/ppermute | solution.py:41
  163.5 8.2 %collective-permute-start.39 = (bf16[2,16,1024]{2,1,0:T(8,128)(2,1)S(1)}, bf16[2,16,1024]{2,1,0:T(8,128)(2,1)S(1)}, u32[]{:S(2)}, u32[]{:S(2)}) collective-permute-start(bf16[2,16,1024]{2,1,0:T(8,128)(2,1)S(1)} %bitcast.186), channel_id=1, source_target_pairs={{0,26},{2,28},{4,30},{6,0},{8,2},{10,4},{12,6},{14,8},{16,10},{18,... | collective-permute-start | bytes 196616 | tf_op jit(solution)/shard_map/ppermute | solution.py:41
  165.1 6.7 %collective-permute-start.40 = (bf16[2,16,1024]{2,1,0:T(8,128)(2,1)S(1)}, bf16[2,16,1024]{2,1,0:T(8,128)(2,1)S(1)}, u32[]{:S(2)}, u32[]{:S(2)}) collective-permute-start(bf16[2,16,1024]{2,1,0:T(8,128)(2,1)S(1)} %bitcast.188), channel_id=1, source_target_pairs={{0,24},{2,26},{4,28},{6,30},{8,0},{10,2},{12,4},{14,6},{16,8},{18,... | collective-permute-start | bytes 196616 | tf_op jit(solution)/shard_map/ppermute | solution.py:41
  165.2 6.7 %collective-permute-start.41 = (bf16[2,16,1024]{2,1,0:T(8,128)(2,1)S(1)}, bf16[2,16,1024]{2,1,0:T(8,128)(2,1)S(1)}, u32[]{:S(2)}, u32[]{:S(2)}) collective-permute-start(bf16[2,16,1024]{2,1,0:T(8,128)(2,1)S(1)} %bitcast.190), channel_id=1, source_target_pairs={{0,22},{2,24},{4,26},{6,28},{8,30},{10,0},{12,2},{14,4},{16,6},{18... | collective-permute-start | bytes 196616 | tf_op jit(solution)/shard_map/ppermute | solution.py:41
  166.3 6.5 %collective-permute-start.42 = (bf16[2,16,1024]{2,1,0:T(8,128)(2,1)S(1)}, bf16[2,16,1024]{2,1,0:T(8,128)(2,1)S(1)}, u32[]{:S(2)}, u32[]{:S(2)}) collective-permute-start(bf16[2,16,1024]{2,1,0:T(8,128)(2,1)S(1)} %bitcast.192), channel_id=1, source_target_pairs={{0,20},{2,22},{4,24},{6,26},{8,28},{10,30},{12,0},{14,2},{16,4},{1... | collective-permute-start | bytes 196616 | tf_op jit(solution)/shard_map/ppermute | solution.py:41
  168.4 8.8 %collective-permute-start.43 = (bf16[2,16,1024]{2,1,0:T(8,128)(2,1)S(1)}, bf16[2,16,1024]{2,1,0:T(8,128)(2,1)S(1)}, u32[]{:S(2)}, u32[]{:S(2)}) collective-permute-start(bf16[2,16,1024]{2,1,0:T(8,128)(2,1)S(1)} %bitcast.184), channel_id=1, source_target_pairs={{0,18},{2,20},{4,22},{6,24},{8,26},{10,28},{12,30},{14,0},{16,2},{... | collective-permute-start | bytes 196616 | tf_op jit(solution)/shard_map/ppermute | solution.py:41
  (20 other events, 133.9 us)

commit v5 on v4

--- a/solution.py
+++ b/solution.py
@@ -630,17 +630,11 @@
         packed_2 = rotate(early[rows:, :split], SLABS, -2)
         late = project(late_own, late_peer)
         packed_3 = rotate(late[:rows, :split], SLABS, -3)
-        early, late, packed_1, packed_2, packed_3, out_far = lax.optimization_barrier(
-            (early, late, packed_1, packed_2, packed_3, out_far)
-        )
+        out_across = swap(tie(out_far, late), "side")
+        gate = [late[rows:, split:], early[:rows, split:], early[rows:, split:], late[:rows, split:]]
         packed = [late[rows:, :split], packed_1, packed_2, packed_3]
-        gate = [
-            late[rows:, split:],
-            rotate(early[:rows, split:], SLABS, -1),
-            rotate(early[rows:, split:], SLABS, -2),
-            rotate(late[:rows, split:], SLABS, -3),
-        ]
-        out_across = swap(out_far, "side")
+        gate, packed = lax.optimization_barrier((gate, packed))
+        gate = [rotate(value, SLABS, -step) for step, value in enumerate(gate)]
         out_columns = []
         for column in (out_weight, out_side, out_far, out_across):
             out_columns += [column, swap(column, "core")]

time: 180 us -> 178 us (0.989)
  local copies, waits for them, and re-layouts: 19.1 us -> 15.8 us
  waiting for transfers between devices: 68.1 us -> 70 us
    ppermute x43, waiting for transfers between devices: 66 us -> 67.9 us  [rotate(): return lax.ppermute(value, axis, pairs)]
    unnamed x85 -> x81, local copies, waits for them, and re-layouts: 5.43 us -> 4.47 us
  transfers between devices with their start and end apart: 44 -> 44, of which waited for: 13 -> 14; matrix products, arithmetic and copies ran while one was open for 14% -> 13% of each run, Pallas kernels for 13% -> 13%
where the time goes in v5:
time: 178 us; the launch traced here: 177 us
  waiting for transfers between devices  70 us (39%)
  starting transfers between devices  53.5 us (30%)
  Pallas kernels  22.9 us (13%)
  local copies, waits for them, and re-layouts  15.8 us (9%)
  other arithmetic  9.11 us (5%)
  matrix products  4.33 us (2%)
    ppermute x43, waiting for transfers between devices, rotate(): return lax.ppermute(value, axis, pairs)  67.9 us
    ppermute x43, starting transfers between devices, rotate(): return lax.ppermute(value, axis, pairs)  52.5 us
    pallas_call x1, Pallas kernels, mix_requests(): pl.pallas_call(lambda *refs: mixer_kernel(sizes, *refs), grid_spec=grid_s...  9.72 us
    pallas_call x1, Pallas kernels, update_states(): pl.pallas_call(lambda *refs: update_kernel(sizes, *refs), grid=(steps,),...  8.75 us
    unnamed x81, local copies, waits for them, and re-layouts  4.47 us
  transfers between devices with their start and end apart: 44, of which 14 were waited for; matrix products, arithmetic and copies ran while one was open for 13% of the time, Pallas kernels for 13%

profile of v5, /device:TPU:1, one launch (start us, length us, event | category | flops | bytes accessed | tf_op | source)
XLA Modules:
  0.0 177.4 jit_solution(14422733985916228939)
XLA Ops:
  0.7 1.3 copy.74
  3.6 2.7 %collective-permute-start = (bf16[2,16,1024]{2,1,0:T(8,128)(2,1)S(1)}, bf16[2,16,1024]{2,1,0:T(8,128)(2,1)S(1)}, u32[]{:S(2)}, u32[]{:S(2)}) collective-permute-start(bf16[2,16,1024]{2,1,0:T(8,128)(2,1)S(1)} %bitcast.177), channel_id=1, source_target_pairs={{0,2},{2,4},{4,6},{6,8},{8,10},{10,12},{12,14},{14,16},{16,18},{18... | collective-permute-start | bytes 196616 | tf_op jit(solution)/shard_map/ppermute | solution.py:41
  6.3 1.3 collective-permute-start.1
  8.0 1.4 collective-permute-start.3
  9.4 2.5 %collective-permute-start.4 = (bf16[2,16,1024]{2,1,0:T(8,128)(2,1)S(1)}, bf16[2,16,1024]{2,1,0:T(8,128)(2,1)S(1)}, u32[]{:S(2)}, u32[]{:S(2)}) collective-permute-start(bf16[2,16,1024]{2,1,0:T(8,128)(2,1)S(1)} %bitcast.180), channel_id=1, source_target_pairs={{0,10},{2,12},{4,14},{6,16},{8,18},{10,20},{12,22},{14,24},{16,26}... | collective-permute-start | bytes 196616 | tf_op jit(solution)/shard_map/ppermute | solution.py:41
  15.4 2.1 %collective-permute-start.5 = (bf16[2,16,1024]{2,1,0:T(8,128)(2,1)S(1)}, bf16[2,16,1024]{2,1,0:T(8,128)(2,1)S(1)}, u32[]{:S(2)}, u32[]{:S(2)}) collective-permute-start(bf16[2,16,1024]{2,1,0:T(8,128)(2,1)S(1)} %bitcast.182), channel_id=1, source_target_pairs={{0,12},{2,14},{4,16},{6,18},{8,20},{10,22},{12,24},{14,26},{16,28}... | collective-permute-start | bytes 196616 | tf_op jit(solution)/shard_map/ppermute | solution.py:41
  18.7 1.9 %collective-permute-start.8 = (bf16[128,1152]{1,0:T(8,128)(2,1)S(1)}, bf16[128,1152]{1,0:T(8,128)(2,1)S(1)}, u32[]{:S(2)}, u32[]{:S(2)}) collective-permute-start(bf16[128,1152]{1,0:T(8,128)(2,1)S(1)} %bitcast.150), channel_id=1, source_target_pairs={{0,16},{8,24},{16,0},{24,8},{1,17},{9,25},{17,1},{25,9},{2,18},{10... | collective-permute-start | bytes 884744 | tf_op jit(solution)/shard_map/ppermute | solution.py:41
  20.9 1.6 collective-permute-start.9
  23.6 1.6 shard_map.210
  26.4 2.1 %collective-permute-start.6 = (bf16[2,16,1024]{2,1,0:T(8,128)(2,1)S(1)}, bf16[2,16,1024]{2,1,0:T(8,128)(2,1)S(1)}, u32[]{:S(2)}, u32[]{:S(2)}) collective-permute-start(bf16[2,16,1024]{2,1,0:T(8,128)(2,1)S(1)} %bitcast.181), channel_id=1, source_target_pairs={{0,14},{2,16},{4,18},{6,20},{8,22},{10,24},{12,26},{14,28},{16,30}... | collective-permute-start | bytes 196616 | tf_op jit(solution)/shard_map/ppermute | solution.py:41
  29.1 21.6 %collective-permute-done.6 = bf16[2,16,1024]{2,1,0:T(8,128)(2,1)S(1)} collective-permute-done((bf16[2,16,1024]{2,1,0:T(8,128)(2,1)S(1)}, bf16[2,16,1024]{2,1,0:T(8,128)(2,1)S(1)}, u32[]{:S(2)}, u32[]{:S(2)}) %collective-permute-start.6) | collective-permute-done | bytes 65568 | tf_op jit(solution)/shard_map/ppermute | solution.py:41
  52.3 2.6 %collective-permute-start.13 = (bf16[128,1024]{1,0:T(8,128)(2,1)S(1)}, bf16[128,1024]{1,0:T(8,128)(2,1)S(1)}, u32[]{:S(2)}, u32[]{:S(2)}) collective-permute-start(bf16[128,1024]{1,0:T(8,128)(2,1)S(1)} %reshape.252), channel_id=1, source_target_pairs={{0,24},{8,0},{16,8},{24,16},{1,25},{9,1},{17,9},{25,17},{2,26},{10... | collective-permute-start | bytes 786440 | tf_op jit(solution)/shard_map/ppermute | solution.py:41
  55.1 1.1 broadcast.204.clone
  59.3 2.5 %collective-permute-done.11 = bf16[128,1024]{1,0:T(8,128)(2,1)S(1)} collective-permute-done((bf16[128,1024]{1,0:T(8,128)(2,1)S(1)}, bf16[128,1024]{1,0:T(8,128)(2,1)S(1)}, u32[]{:S(2)}, u32[]{:S(2)}) %collective-permute-start.11) | collective-permute-done | bytes 262176 | tf_op jit(solution)/shard_map/ppermute | solution.py:41
  61.8 10.3 %collective-permute-done.12 = bf16[128,1024]{1,0:T(8,128)(2,1)S(1)} collective-permute-done((bf16[128,1024]{1,0:T(8,128)(2,1)S(1)}, bf16[128,1024]{1,0:T(8,128)(2,1)S(1)}, u32[]{:S(2)}, u32[]{:S(2)}) %collective-permute-start.12) | collective-permute-done | bytes 262176 | tf_op jit(solution)/shard_map/ppermute | solution.py:41
  72.1 4.0 %collective-permute-done.14 = bf16[3,128,1152]{2,1,0:T(8,128)(2,1)S(1)} collective-permute-done((bf16[3,128,1152]{2,1,0:T(8,128)(2,1)S(1)}, bf16[3,128,1152]{2,1,0:T(8,128)(2,1)S(1)}, u32[]{:S(2)}, u32[]{:S(2)}) %collective-permute-start.14) | collective-permute-done | bytes 884768 | tf_op jit(solution)/shard_map/ppermute | solution.py:41
  76.2 1.1 collective-permute-start.17
  77.4 1.5 collective-permute-start.29
  79.0 1.3 collective-permute-start.15
  80.3 1.0 pad_maximum_fusion.2
  81.8 2.9 %pad_maximum_fusion = bf16[2048,1152]{1,0:T(8,128)(2,1)S(1)} fusion(bf16[512,1152]{1,0:T(8,128)(2,1)} %collective-permute-done.17, bf16[512,1152]{1,0:T(8,128)(2,1)} %collective-permute-done.16, bf16[512,1152]{1,0:T(8,128)(2,1)S(1)} %bitcast.137, bf16[512,1152]{1,0:T(8,128)(2,1)} %bitcast.25), kind=kLoop, calls=%fused_computation.4 | loop fusion | flops 18874368 | bytes 9437184 | tf_op jit(solution)/shard_map/concatenate | solution.py:607
  84.7 5.8 %collective-permute-done.18.refs_2_ = bf16[2048,128]{1,0:T(8,128)(2,1)S(1)} collective-permute-done((bf16[2048,128]{1,0:T(8,128)(2,1)S(1)}, bf16[2048,128]{1,0:T(8,128)(2,1)S(1)}, u32[]{:S(2)}, u32[]{:S(2)}) %collective-permute-start.18) | collective-permute-done | bytes 524320 | tf_op jit(solution)/shard_map/ppermute | solution.py:41
  90.4 1.1 collective-permute-done.15
  91.5 1.2 collective-permute-start.19
  93.0 1.5 convolution_convert_fusion.4
  94.5 2.3 %collective-permute-start.20 = (bf16[128,640]{1,0:T(8,128)(2,1)S(1)}, bf16[128,640]{1,0:T(8,128)(2,1)S(1)}, u32[]{:S(2)}, u32[]{:S(2)}) collective-permute-start(bf16[128,640]{1,0:T(8,128)(2,1)S(1)} %get-tuple-element.182), channel_id=1, source_target_pairs={{0,24},{8,0},{16,8},{24,16},{1,25},{9,1},{17,9},{25,17},{2,26},{10... | collective-permute-start | bytes 491528 | tf_op jit(solution)/shard_map/ppermute | solution.py:41
  96.8 6.3 %collective-permute-done.19 = bf16[256,1024]{1,0:T(8,128)(2,1)S(1)} collective-permute-done((bf16[256,1024]{1,0:T(8,128)(2,1)S(1)}, bf16[256,1024]{1,0:T(8,128)(2,1)S(1)}, u32[]{:S(2)}, u32[]{:S(2)}) %collective-permute-start.19) | collective-permute-done | bytes 524320 | tf_op jit(solution)/shard_map/ppermute | solution.py:41
  103.3 1.6 convolution_convert_fusion.5
  106.1 1.2 collective-permute-start.31
  107.4 9.1 %collective-permute-done.21.refs_3_.refs_7_ = bf16[128,640]{1,0:T(8,128)(2,1)S(1)} collective-permute-done((bf16[128,640]{1,0:T(8,128)(2,1)S(1)}, bf16[128,640]{1,0:T(8,128)(2,1)S(1)}, u32[]{:S(2)}, u32[]{:S(2)}) %collective-permute-start.21) | collective-permute-done | bytes 163872 | tf_op jit(solution)/shard_map/ppermute | solution.py:41
  116.6 2.4 %collective-permute-start.24 = (bf16[128,512]{1,0:T(8,128)(2,1)S(1)}, bf16[128,512]{1,0:T(8,128)(2,1)S(1)}, u32[]{:S(2)}, u32[]{:S(2)}) collective-permute-start(bf16[128,512]{1,0:T(8,128)(2,1)S(1)} %get-tuple-element.130), channel_id=1, source_target_pairs={{0,16},{8,24},{16,0},{24,8},{1,17},{9,25},{17,1},{25,9},{2,18},{10... | collective-permute-start | bytes 393224 | tf_op jit(solution)/shard_map/ppermute | solution.py:41
  119.8 9.7 %shard_map.211 = (bf16[128,2048]{1,0:T(8,128)(2,1)}, bf16[2048,256]{1,0:T(8,128)(2,1)}, f32[128,128]{1,0:T(8,128)}, f32[128,128]{1,0:T(8,128)}, bf16[32,2048]{1,0:T(8,128)(2,1)}, /*index=5*/bf16[32,256]{1,0:T(8,128)(2,1)}) custom-call(s32[4]{0:T(128)} %and_select_fusion.1.refs_0_, bf16[128,640]{1,0:T(8,128)(2,1)} %get-tuple-element.118.refs_1_.refs_5_, ...), custom_call_target="tpu_custom_call" | custom-call | flops 2147483648 | bytes 16777216 | tf_op jit(solution)/shard_map/pallas_call | solution.py:391
  129.7 1.6 multiply_convert_fusion
  131.3 1.3 collective-permute-start.26
  132.5 1.7 collective-permute-start.27
  134.8 8.7 %shard_map.212 = f32[8,32,64,128]{3,2,1,0:T(8,128)} custom-call(bf16[2048,256]{1,0:T(8,128)(2,1)} %get-tuple-element.133.refs_0_, f32[128,128]{1,0:T(8,128)} %get-tuple-element.135.refs_1_, f32[128,128]{1,0:T(8,128)} %get-tuple-element.136.refs_2_, f32[8,32,64,128]{3,2,1,0:T(8,128)} %refs_3_.1), custom_call_target="tpu_custom_call" | custom-call | flops 2147483648 | bytes 16777216 | tf_op jit(solution)/shard_map/pallas_call | solution.py:293
  143.6 1.2 collective-permute-start.34
  144.8 2.9 %shard_map.213 = (f32[2,128,512]{2,1,0:T(8,128)S(1)}, bf16[2,2,128,512]{3,2,1,0:T(8,128)(2,1)S(1)}) custom-call(s32[4]{0:T(128)S(1)} %pad_add_fusion.place_ref, bf16[128,2048]{1,0:T(8,128)(2,1)S(1)} %get-tuple-element.173.own_ref, bf16[128,2048]{1,0:T(8,128)(2,1)S(1)} %collective-permute-done.26.peer_ref, bf16[2048,128]{1,0:T(8,128)(2,1)S(1)} %copy-done, ...), custom_call_target="tpu_custom_call" | custom-call | flops 1000 | bytes 1000 | tf_op jit(solution)/shard_map/pallas_call | solution.py:467
  147.7 1.0 collective-permute-start.36
  149.2 1.2 collective-permute-start.33
  150.4 2.1 %collective-permute-done.36 = bf16[128,512]{1,0:T(8,128)(2,1)S(1)} collective-permute-done((bf16[128,512]{1,0:T(8,128)(2,1)S(1)}, bf16[128,512]{1,0:T(8,128)(2,1)S(1)}, u32[]{:S(2)}, u32[]{:S(2)}) %collective-permute-start.36) | collective-permute-done | bytes 131104 | tf_op jit(solution)/shard_map/ppermute | solution.py:698
  153.0 1.0 collective-permute-done.33
  155.1 3.6 %collective-permute-start.37 = (bf16[2,16,1024]{2,1,0:T(8,128)(2,1)S(1)}, bf16[2,16,1024]{2,1,0:T(8,128)(2,1)S(1)}, u32[]{:S(2)}, u32[]{:S(2)}) collective-permute-start(bf16[2,16,1024]{2,1,0:T(8,128)(2,1)S(1)} %bitcast.196), channel_id=1, source_target_pairs={{0,30},{2,0},{4,2},{6,4},{8,6},{10,8},{12,10},{14,12},{16,14},{18,... | collective-permute-start | bytes 196616 | tf_op jit(solution)/shard_map/ppermute | solution.py:41
  158.8 3.5 %collective-permute-start.38 = (bf16[2,16,1024]{2,1,0:T(8,128)(2,1)S(1)}, bf16[2,16,1024]{2,1,0:T(8,128)(2,1)S(1)}, u32[]{:S(2)}, u32[]{:S(2)}) collective-permute-start(bf16[2,16,1024]{2,1,0:T(8,128)(2,1)S(1)} %bitcast.195), channel_id=1, source_target_pairs={{0,28},{2,30},{4,0},{6,2},{8,4},{10,6},{12,8},{14,10},{16,12},{18,... | collective-permute-start | bytes 196616 | tf_op jit(solution)/shard_map/ppermute | solution.py:41
  163.0 1.5 collective-permute-start.41
  164.5 1.4 collective-permute-start.42
  165.9 2.2 %collective-permute-start.43 = (bf16[2,16,1024]{2,1,0:T(8,128)(2,1)S(1)}, bf16[2,16,1024]{2,1,0:T(8,128)(2,1)S(1)}, u32[]{:S(2)}, u32[]{:S(2)}) collective-permute-start(bf16[2,16,1024]{2,1,0:T(8,128)(2,1)S(1)} %bitcast.184), channel_id=1, source_target_pairs={{0,18},{2,20},{4,22},{6,24},{8,26},{10,28},{12,30},{14,0},{16,2},{... | collective-permute-start | bytes 196616 | tf_op jit(solution)/shard_map/ppermute | solution.py:41
  170.2 5.1 %collective-permute-done.43 = bf16[2,16,1024]{2,1,0:T(8,128)(2,1)S(1)} collective-permute-done((bf16[2,16,1024]{2,1,0:T(8,128)(2,1)S(1)}, bf16[2,16,1024]{2,1,0:T(8,128)(2,1)S(1)}, u32[]{:S(2)}, u32[]{:S(2)}) %collective-permute-start.43) | collective-permute-done | bytes 65568 | tf_op jit(solution)/shard_map/ppermute | solution.py:41
  (210 shorter events, 25.3 us)
Async XLA Ops:
  3.6 11.8 %collective-permute-start = (bf16[2,16,1024]{2,1,0:T(8,128)(2,1)S(1)}, bf16[2,16,1024]{2,1,0:T(8,128)(2,1)S(1)}, u32[]{:S(2)}, u32[]{:S(2)}) collective-permute-start(bf16[2,16,1024]{2,1,0:T(8,128)(2,1)S(1)} %bitcast.177), channel_id=1, source_target_pairs={{0,2},{2,4},{4,6},{6,8},{8,10},{10,12},{12,14},{14,16},{16,18},{18... | collective-permute-start | bytes 196616 | tf_op jit(solution)/shard_map/ppermute | solution.py:41
  6.3 11.2 %collective-permute-start.1 = (bf16[2,16,1024]{2,1,0:T(8,128)(2,1)S(1)}, bf16[2,16,1024]{2,1,0:T(8,128)(2,1)S(1)}, u32[]{:S(2)}, u32[]{:S(2)}) collective-permute-start(bf16[2,16,1024]{2,1,0:T(8,128)(2,1)S(1)} %bitcast.176), channel_id=1, source_target_pairs={{0,4},{2,6},{4,8},{6,10},{8,12},{10,14},{12,16},{14,18},{16,20},{1... | collective-permute-start | bytes 196616 | tf_op jit(solution)/shard_map/ppermute | solution.py:41
  7.6 9.9 %collective-permute-start.2 = (bf16[2,16,1024]{2,1,0:T(8,128)(2,1)S(1)}, bf16[2,16,1024]{2,1,0:T(8,128)(2,1)S(1)}, u32[]{:S(2)}, u32[]{:S(2)}) collective-permute-start(bf16[2,16,1024]{2,1,0:T(8,128)(2,1)S(1)} %bitcast.178), channel_id=1, source_target_pairs={{0,6},{2,8},{4,10},{6,12},{8,14},{10,16},{12,18},{14,20},{16,22},{... | collective-permute-start | bytes 196616 | tf_op jit(solution)/shard_map/ppermute | solution.py:41
  8.0 9.5 %collective-permute-start.3 = (bf16[2,16,1024]{2,1,0:T(8,128)(2,1)S(1)}, bf16[2,16,1024]{2,1,0:T(8,128)(2,1)S(1)}, u32[]{:S(2)}, u32[]{:S(2)}) collective-permute-start(bf16[2,16,1024]{2,1,0:T(8,128)(2,1)S(1)} %bitcast.179), channel_id=1, source_target_pairs={{0,8},{2,10},{4,12},{6,14},{8,16},{10,18},{12,20},{14,22},{16,24},... | collective-permute-start | bytes 196616 | tf_op jit(solution)/shard_map/ppermute | solution.py:41
  9.4 8.1 %collective-permute-start.4 = (bf16[2,16,1024]{2,1,0:T(8,128)(2,1)S(1)}, bf16[2,16,1024]{2,1,0:T(8,128)(2,1)S(1)}, u32[]{:S(2)}, u32[]{:S(2)}) collective-permute-start(bf16[2,16,1024]{2,1,0:T(8,128)(2,1)S(1)} %bitcast.180), channel_id=1, source_target_pairs={{0,10},{2,12},{4,14},{6,16},{8,18},{10,20},{12,22},{14,24},{16,26}... | collective-permute-start | bytes 196616 | tf_op jit(solution)/shard_map/ppermute | solution.py:41
  15.4 11.0 %collective-permute-start.5 = (bf16[2,16,1024]{2,1,0:T(8,128)(2,1)S(1)}, bf16[2,16,1024]{2,1,0:T(8,128)(2,1)S(1)}, u32[]{:S(2)}, u32[]{:S(2)}) collective-permute-start(bf16[2,16,1024]{2,1,0:T(8,128)(2,1)S(1)} %bitcast.182), channel_id=1, source_target_pairs={{0,12},{2,14},{4,16},{6,18},{8,20},{10,22},{12,24},{14,26},{16,28}... | collective-permute-start | bytes 196616 | tf_op jit(solution)/shard_map/ppermute | solution.py:41
  18.1 32.6 %collective-permute-start.7 = (bf16[128,1152]{1,0:T(8,128)(2,1)S(1)}, bf16[128,1152]{1,0:T(8,128)(2,1)S(1)}, u32[]{:S(2)}, u32[]{:S(2)}) collective-permute-start(bf16[128,1152]{1,0:T(8,128)(2,1)S(1)} %bitcast.149), channel_id=1, source_target_pairs={{0,8},{8,16},{16,24},{24,0},{1,9},{9,17},{17,25},{25,1},{2,10},{10... | collective-permute-start | bytes 884744 | tf_op jit(solution)/shard_map/ppermute | solution.py:41
  18.7 31.9 %collective-permute-start.8 = (bf16[128,1152]{1,0:T(8,128)(2,1)S(1)}, bf16[128,1152]{1,0:T(8,128)(2,1)S(1)}, u32[]{:S(2)}, u32[]{:S(2)}) collective-permute-start(bf16[128,1152]{1,0:T(8,128)(2,1)S(1)} %bitcast.150), channel_id=1, source_target_pairs={{0,16},{8,24},{16,0},{24,8},{1,17},{9,25},{17,1},{25,9},{2,18},{10... | collective-permute-start | bytes 884744 | tf_op jit(solution)/shard_map/ppermute | solution.py:41
  20.9 29.8 %collective-permute-start.9 = (bf16[128,1152]{1,0:T(8,128)(2,1)S(1)}, bf16[128,1152]{1,0:T(8,128)(2,1)S(1)}, u32[]{:S(2)}, u32[]{:S(2)}) collective-permute-start(bf16[128,1152]{1,0:T(8,128)(2,1)S(1)} %bitcast.151), channel_id=1, source_target_pairs={{0,24},{8,0},{16,8},{24,16},{1,25},{9,1},{17,9},{25,17},{2,26},{10... | collective-permute-start | bytes 884744 | tf_op jit(solution)/shard_map/ppermute | solution.py:41
  22.4 28.2 %collective-permute-start.10 = (bf16[128,1152]{1,0:T(8,128)(2,1)S(1)}, bf16[128,1152]{1,0:T(8,128)(2,1)S(1)}, u32[]{:S(2)}, u32[]{:S(2)}) collective-permute-start(bf16[128,1152]{1,0:T(8,128)(2,1)S(1)} %bitcast.146), channel_id=1, source_target_pairs={{0,4},{4,0},{1,5},{5,1},{2,6},{6,2},{3,7},{7,3},{8,12},{12,8},{9,1... | collective-permute-start | bytes 884744 | tf_op jit(solution)/shard_map/ppermute | solution.py:41
  26.4 24.3 %collective-permute-start.6 = (bf16[2,16,1024]{2,1,0:T(8,128)(2,1)S(1)}, bf16[2,16,1024]{2,1,0:T(8,128)(2,1)S(1)}, u32[]{:S(2)}, u32[]{:S(2)}) collective-permute-start(bf16[2,16,1024]{2,1,0:T(8,128)(2,1)S(1)} %bitcast.181), channel_id=1, source_target_pairs={{0,14},{2,16},{4,18},{6,20},{8,22},{10,24},{12,26},{14,28},{16,30}... | collective-permute-start | bytes 196616 | tf_op jit(solution)/shard_map/ppermute | solution.py:41
  51.5 10.2 %collective-permute-start.11 = (bf16[128,1024]{1,0:T(8,128)(2,1)S(1)}, bf16[128,1024]{1,0:T(8,128)(2,1)S(1)}, u32[]{:S(2)}, u32[]{:S(2)}) collective-permute-start(bf16[128,1024]{1,0:T(8,128)(2,1)S(1)} %reshape.252), channel_id=1, source_target_pairs={{0,8},{8,16},{16,24},{24,0},{1,9},{9,17},{17,25},{25,1},{2,10},{10... | collective-permute-start | bytes 786440 | tf_op jit(solution)/shard_map/ppermute | solution.py:41
  51.6 20.5 %collective-permute-start.12 = (bf16[128,1024]{1,0:T(8,128)(2,1)S(1)}, bf16[128,1024]{1,0:T(8,128)(2,1)S(1)}, u32[]{:S(2)}, u32[]{:S(2)}) collective-permute-start(bf16[128,1024]{1,0:T(8,128)(2,1)S(1)} %reshape.252), channel_id=1, source_target_pairs={{0,16},{8,24},{16,0},{24,8},{1,17},{9,25},{17,1},{25,9},{2,18},{10... | collective-permute-start | bytes 786440 | tf_op jit(solution)/shard_map/ppermute | solution.py:41
  52.3 19.8 %collective-permute-start.13 = (bf16[128,1024]{1,0:T(8,128)(2,1)S(1)}, bf16[128,1024]{1,0:T(8,128)(2,1)S(1)}, u32[]{:S(2)}, u32[]{:S(2)}) collective-permute-start(bf16[128,1024]{1,0:T(8,128)(2,1)S(1)} %reshape.252), channel_id=1, source_target_pairs={{0,24},{8,0},{16,8},{24,16},{1,25},{9,1},{17,9},{25,17},{2,26},{10... | collective-permute-start | bytes 786440 | tf_op jit(solution)/shard_map/ppermute | solution.py:41
  55.0 21.1 %collective-permute-start.14 = (bf16[3,128,1152]{2,1,0:T(8,128)(2,1)S(1)}, bf16[3,128,1152]{2,1,0:T(8,128)(2,1)S(1)}, u32[]{:S(2)}, u32[]{:S(2)}) collective-permute-start(bf16[3,128,1152]{2,1,0:T(8,128)(2,1)S(1)} %pad_maximum_fusion.1), channel_id=1, source_target_pairs={{0,4},{4,0},{1,5},{5,1},{2,6},{6,2},{3,7},{7,3},{8,12},{12,8},{9,1... | collective-permute-start | bytes 2654216 | tf_op jit(solution)/shard_map/ppermute | solution.py:41
  58.4 19.0 %copy-start = (bf16[2048,128]{1,0:T(8,128)(2,1)S(1)}, bf16[2048,128]{1,0:T(8,128)(2,1)}, u32[]{:S(2)}) copy-start(bf16[2048,128]{1,0:T(8,128)(2,1)} %refs_0_.1) | copy-start | bytes 1572868
  76.2 5.1 %collective-permute-start.17 = (bf16[512,1152]{1,0:T(8,128)(2,1)S(1)}, bf16[512,1152]{1,0:T(8,128)(2,1)}, u32[]{:S(2)}, u32[]{:S(2)}) collective-permute-start(bf16[512,1152]{1,0:T(8,128)(2,1)S(1)} %bitcast.136), channel_id=1, source_target_pairs={{0,2},{2,0},{1,3},{3,1},{4,6},{6,4},{5,7},{7,5},{8,10},{10,8},{9,1... | collective-permute-start | bytes 3538952 | tf_op jit(solution)/shard_map/ppermute | solution.py:41
  77.3 4.5 %collective-permute-start.16 = (bf16[512,1152]{1,0:T(8,128)(2,1)}, bf16[512,1152]{1,0:T(8,128)(2,1)}, u32[]{:S(2)}, u32[]{:S(2)}) collective-permute-start(bf16[512,1152]{1,0:T(8,128)(2,1)} %bitcast.25), channel_id=1, source_target_pairs={{0,2},{2,0},{1,3},{3,1},{4,6},{6,4},{5,7},{7,5},{8,10},{10,8},{9,1... | collective-permute-start | bytes 3538952 | tf_op jit(solution)/shard_map/ppermute | solution.py:41
  77.4 13.1 %collective-permute-start.18 = (bf16[2048,128]{1,0:T(8,128)(2,1)S(1)}, bf16[2048,128]{1,0:T(8,128)(2,1)S(1)}, u32[]{:S(2)}, u32[]{:S(2)}) collective-permute-start(bf16[2048,128]{1,0:T(8,128)(2,1)S(1)} %copy-done), channel_id=1, source_target_pairs={{0,4},{4,0},{1,5},{5,1},{2,6},{6,2},{3,7},{7,3},{8,12},{12,8},{9,1... | collective-permute-start | bytes 1572872 | tf_op jit(solution)/shard_map/ppermute | solution.py:41
  77.4 28.7 %collective-permute-start.29 = (bf16[2048,128]{1,0:T(8,128)(2,1)S(1)}, bf16[2048,128]{1,0:T(8,128)(2,1)S(1)}, u32[]{:S(2)}, u32[]{:S(2)}) collective-permute-start(bf16[2048,128]{1,0:T(8,128)(2,1)S(1)} %copy-done), channel_id=1, source_target_pairs={{0,16},{16,0},{1,17},{17,1},{2,18},{18,2},{3,19},{19,3},{4,20},{20... | collective-permute-start | bytes 1572872 | tf_op jit(solution)/shard_map/ppermute | solution.py:41
  79.0 12.6 %collective-permute-start.15 = (bf16[256,1024]{1,0:T(8,128)(2,1)S(1)}, bf16[256,1024]{1,0:T(8,128)(2,1)S(1)}, u32[]{:S(2)}, u32[]{:S(2)}) collective-permute-start(bf16[256,1024]{1,0:T(8,128)(2,1)S(1)} %constant_dynamic-update-slice_fusion.8), channel_id=1, source_target_pairs={{0,1},{1,0},{2,3},{3,2},{4,5},{5,4},{6,7},{7,6},{8,9},{9,8},{10,11... | collective-permute-start | bytes 1572872 | tf_op jit(solution)/shard_map/ppermute | solution.py:41
  91.5 11.6 %collective-permute-start.19 = (bf16[256,1024]{1,0:T(8,128)(2,1)S(1)}, bf16[256,1024]{1,0:T(8,128)(2,1)S(1)}, u32[]{:S(2)}, u32[]{:S(2)}) collective-permute-start(bf16[256,1024]{1,0:T(8,128)(2,1)S(1)} %pad_maximum_fusion.2), channel_id=1, source_target_pairs={{0,1},{1,0},{2,3},{3,2},{4,5},{5,4},{6,7},{7,6},{8,9},{9,8},{10,11... | collective-permute-start | bytes 1572872 | tf_op jit(solution)/shard_map/ppermute | solution.py:41
  94.5 12.8 %collective-permute-start.20 = (bf16[128,640]{1,0:T(8,128)(2,1)S(1)}, bf16[128,640]{1,0:T(8,128)(2,1)S(1)}, u32[]{:S(2)}, u32[]{:S(2)}) collective-permute-start(bf16[128,640]{1,0:T(8,128)(2,1)S(1)} %get-tuple-element.182), channel_id=1, source_target_pairs={{0,24},{8,0},{16,8},{24,16},{1,25},{9,1},{17,9},{25,17},{2,26},{10... | collective-permute-start | bytes 491528 | tf_op jit(solution)/shard_map/ppermute | solution.py:41
  96.8 19.7 %collective-permute-start.21 = (bf16[128,640]{1,0:T(8,128)(2,1)S(1)}, bf16[128,640]{1,0:T(8,128)(2,1)S(1)}, u32[]{:S(2)}, u32[]{:S(2)}) collective-permute-start(bf16[128,640]{1,0:T(8,128)(2,1)S(1)} %get-tuple-element.181), channel_id=1, source_target_pairs={{0,16},{8,24},{16,0},{24,8},{1,17},{9,25},{17,1},{25,9},{2,18},{10... | collective-permute-start | bytes 491528 | tf_op jit(solution)/shard_map/ppermute | solution.py:41
  105.6 11.0 %collective-permute-start.22 = (bf16[128,640]{1,0:T(8,128)(2,1)S(1)}, bf16[128,640]{1,0:T(8,128)(2,1)S(1)}, u32[]{:S(2)}, u32[]{:S(2)}) collective-permute-start(bf16[128,640]{1,0:T(8,128)(2,1)S(1)} %get-tuple-element.179), channel_id=1, source_target_pairs={{0,8},{8,16},{16,24},{24,0},{1,9},{9,17},{17,25},{25,1},{2,10},{10... | collective-permute-start | bytes 491528 | tf_op jit(solution)/shard_map/ppermute | solution.py:41
  106.1 28.6 %collective-permute-start.31 = (bf16[2048,128]{1,0:T(8,128)(2,1)S(1)}, bf16[2048,128]{1,0:T(8,128)(2,1)S(1)}, u32[]{:S(2)}, u32[]{:S(2)}) collective-permute-start(bf16[2048,128]{1,0:T(8,128)(2,1)S(1)} %collective-permute-done.29.refs_4_), channel_id=1, source_target_pairs={{0,4},{4,0},{1,5},{5,1},{2,6},{6,2},{3,7},{7,3},{8,12},{12,8},{9,1... | collective-permute-start | bytes 1572872 | tf_op jit(solution)/shard_map/ppermute | solution.py:41
  116.5 13.2 %copy-start.15 = (f32[2048]{0:T(1024)S(1)}, f32[2048]{0:T(1024)}, u32[]{:S(2)}) copy-start(f32[2048]{0:T(1024)} %param.29) | copy-start | bytes 24580
  116.5 13.1 %collective-permute-start.23 = (bf16[128,512]{1,0:T(8,128)(2,1)S(1)}, bf16[128,512]{1,0:T(8,128)(2,1)S(1)}, u32[]{:S(2)}, u32[]{:S(2)}) collective-permute-start(bf16[128,512]{1,0:T(8,128)(2,1)S(1)} %get-tuple-element.129), channel_id=1, source_target_pairs={{0,8},{8,16},{16,24},{24,0},{1,9},{9,17},{17,25},{25,1},{2,10},{10... | collective-permute-start | bytes 393224 | tf_op jit(solution)/shard_map/ppermute | solution.py:41
  116.6 13.0 %collective-permute-start.24 = (bf16[128,512]{1,0:T(8,128)(2,1)S(1)}, bf16[128,512]{1,0:T(8,128)(2,1)S(1)}, u32[]{:S(2)}, u32[]{:S(2)}) collective-permute-start(bf16[128,512]{1,0:T(8,128)(2,1)S(1)} %get-tuple-element.130), channel_id=1, source_target_pairs={{0,16},{8,24},{16,0},{24,8},{1,17},{9,25},{17,1},{25,9},{2,18},{10... | collective-permute-start | bytes 393224 | tf_op jit(solution)/shard_map/ppermute | solution.py:41
  118.9 10.7 %collective-permute-start.25 = (bf16[128,512]{1,0:T(8,128)(2,1)S(1)}, bf16[128,512]{1,0:T(8,128)(2,1)S(1)}, u32[]{:S(2)}, u32[]{:S(2)}) collective-permute-start(bf16[128,512]{1,0:T(8,128)(2,1)S(1)} %get-tuple-element.131), channel_id=1, source_target_pairs={{0,24},{8,0},{16,8},{24,16},{1,25},{9,1},{17,9},{25,17},{2,26},{10... | collective-permute-start | bytes 393224 | tf_op jit(solution)/shard_map/ppermute | solution.py:41
  131.3 12.3 %collective-permute-start.26 = (bf16[128,2048]{1,0:T(8,128)(2,1)S(1)}, bf16[128,2048]{1,0:T(8,128)(2,1)S(1)}, u32[]{:S(2)}, u32[]{:S(2)}) collective-permute-start(bf16[128,2048]{1,0:T(8,128)(2,1)S(1)} %get-tuple-element.173.own_ref), channel_id=1, source_target_pairs={{0,8},{8,0},{1,9},{9,1},{2,10},{10,2},{3,11},{11,3},{4,12},{12,4},... | collective-permute-start | bytes 1572872 | tf_op jit(solution)/shard_map/ppermute | solution.py:41
  132.5 12.2 %collective-permute-start.27 = (bf16[2048,128]{1,0:T(8,128)(2,1)S(1)}, bf16[2048,128]{1,0:T(8,128)(2,1)}, u32[]{:S(2)}, u32[]{:S(2)}) collective-permute-start(bf16[2048,128]{1,0:T(8,128)(2,1)S(1)} %copy-done), channel_id=1, source_target_pairs={{0,2},{2,0},{1,3},{3,1},{4,6},{6,4},{5,7},{7,5},{8,10},{10,8},{9,1... | collective-permute-start | bytes 1572872 | tf_op jit(solution)/shard_map/ppermute | solution.py:41
  134.2 10.6 %collective-permute-start.30 = (bf16[2048,128]{1,0:T(8,128)(2,1)S(1)}, bf16[2048,128]{1,0:T(8,128)(2,1)}, u32[]{:S(2)}, u32[]{:S(2)}) collective-permute-start(bf16[2048,128]{1,0:T(8,128)(2,1)S(1)} %collective-permute-done.29.refs_4_), channel_id=1, source_target_pairs={{0,2},{2,0},{1,3},{3,1},{4,6},{6,4},{5,7},{7,5},{8,10},{10,8},{9,1... | collective-permute-start | bytes 1572872 | tf_op jit(solution)/shard_map/ppermute | solution.py:41
  134.2 10.6 %collective-permute-start.28 = (bf16[2048,128]{1,0:T(8,128)(2,1)S(1)}, bf16[2048,128]{1,0:T(8,128)(2,1)}, u32[]{:S(2)}, u32[]{:S(2)}) collective-permute-start(bf16[2048,128]{1,0:T(8,128)(2,1)S(1)} %collective-permute-done.18.refs_2_), channel_id=1, source_target_pairs={{0,2},{2,0},{1,3},{3,1},{4,6},{6,4},{5,7},{7,5},{8,10},{10,8},{9,1... | collective-permute-start | bytes 1572872 | tf_op jit(solution)/shard_map/ppermute | solution.py:41
  134.7 10.1 %collective-permute-start.32 = (bf16[2048,128]{1,0:T(8,128)(2,1)S(1)}, bf16[2048,128]{1,0:T(8,128)(2,1)}, u32[]{:S(2)}, u32[]{:S(2)}) collective-permute-start(bf16[2048,128]{1,0:T(8,128)(2,1)S(1)} %collective-permute-done.31.refs_6_), channel_id=1, source_target_pairs={{0,2},{2,0},{1,3},{3,1},{4,6},{6,4},{5,7},{7,5},{8,10},{10,8},{9,1... | collective-permute-start | bytes 1572872 | tf_op jit(solution)/shard_map/ppermute | solution.py:41
  143.6 6.9 %collective-permute-start.34 = (f32[128]{0:T(128)S(1)}, f32[128]{0:T(128)S(1)}, u32[]{:S(2)}, u32[]{:S(2)}) collective-permute-start(f32[128]{0:T(128)S(1)} %get-tuple-element.174), channel_id=1, source_target_pairs={{0,1},{1,0},{2,3},{3,2},{4,5},{5,4},{6,7},{7,6},{8,9},{9,8},{10,11... | collective-permute-start | bytes 1544 | tf_op jit(solution)/shard_map/ppermute | solution.py:41
  147.7 4.9 %collective-permute-start.36 = (bf16[128,512]{1,0:T(8,128)(2,1)S(1)}, bf16[128,512]{1,0:T(8,128)(2,1)S(1)}, u32[]{:S(2)}, u32[]{:S(2)}) collective-permute-start(bf16[128,512]{1,0:T(8,128)(2,1)S(1)} %get-tuple-element.196), channel_id=1, source_target_pairs={{0,9},{1,8},{8,1},{9,0},{2,11},{3,10},{10,3},{11,2},{4,13},{5,12},... | collective-permute-start | bytes 393224 | tf_op jit(solution)/shard_map/ppermute | solution.py:698
  148.8 4.2 %collective-permute-start.35 = (bf16[128,512]{1,0:T(8,128)(2,1)S(1)}, bf16[128,512]{1,0:T(8,128)(2,1)S(1)}, u32[]{:S(2)}, u32[]{:S(2)}) collective-permute-start(bf16[128,512]{1,0:T(8,128)(2,1)S(1)} %get-tuple-element.197), channel_id=1, source_target_pairs={{0,8},{8,0},{1,9},{9,1},{2,10},{10,2},{3,11},{11,3},{4,12},{12,4},... | collective-permute-start | bytes 393224 | tf_op jit(solution)/shard_map/ppermute | solution.py:41
  149.2 4.7 %collective-permute-start.33 = (bf16[128,512]{1,0:T(8,128)(2,1)S(1)}, bf16[128,512]{1,0:T(8,128)(2,1)S(1)}, u32[]{:S(2)}, u32[]{:S(2)}) collective-permute-start(bf16[128,512]{1,0:T(8,128)(2,1)S(1)} %get-tuple-element.195), channel_id=1, source_target_pairs={{0,1},{1,0},{2,3},{3,2},{4,5},{5,4},{6,7},{7,6},{8,9},{9,8},{10,11... | collective-permute-start | bytes 393224 | tf_op jit(solution)/shard_map/ppermute | solution.py:41
  154.0 14.0 %copy-start.10 = (bf16[32,2048]{1,0:T(8,128)(2,1)S(1)}, bf16[32,2048]{1,0:T(8,128)(2,1)}, u32[]{:S(2)}) copy-start(bf16[32,2048]{1,0:T(8,128)(2,1)} %get-tuple-element.142) | copy-start | bytes 393220
  154.2 14.7 %copy-start.13 = (bf16[32,256]{1,0:T(8,128)(2,1)S(1)}, bf16[32,256]{1,0:T(8,128)(2,1)}, u32[]{:S(2)}) copy-start(bf16[32,256]{1,0:T(8,128)(2,1)} %get-tuple-element.143) | copy-start | bytes 49156
  155.1 9.4 %collective-permute-start.37 = (bf16[2,16,1024]{2,1,0:T(8,128)(2,1)S(1)}, bf16[2,16,1024]{2,1,0:T(8,128)(2,1)S(1)}, u32[]{:S(2)}, u32[]{:S(2)}) collective-permute-start(bf16[2,16,1024]{2,1,0:T(8,128)(2,1)S(1)} %bitcast.196), channel_id=1, source_target_pairs={{0,30},{2,0},{4,2},{6,4},{8,6},{10,8},{12,10},{14,12},{16,14},{18,... | collective-permute-start | bytes 196616 | tf_op jit(solution)/shard_map/ppermute | solution.py:41
  158.8 7.1 %collective-permute-start.38 = (bf16[2,16,1024]{2,1,0:T(8,128)(2,1)S(1)}, bf16[2,16,1024]{2,1,0:T(8,128)(2,1)S(1)}, u32[]{:S(2)}, u32[]{:S(2)}) collective-permute-start(bf16[2,16,1024]{2,1,0:T(8,128)(2,1)S(1)} %bitcast.195), channel_id=1, source_target_pairs={{0,28},{2,30},{4,0},{6,2},{8,4},{10,6},{12,8},{14,10},{16,12},{18,... | collective-permute-start | bytes 196616 | tf_op jit(solution)/shard_map/ppermute | solution.py:41
  162.3 7.3 %collective-permute-start.39 = (bf16[2,16,1024]{2,1,0:T(8,128)(2,1)S(1)}, bf16[2,16,1024]{2,1,0:T(8,128)(2,1)S(1)}, u32[]{:S(2)}, u32[]{:S(2)}) collective-permute-start(bf16[2,16,1024]{2,1,0:T(8,128)(2,1)S(1)} %bitcast.186), channel_id=1, source_target_pairs={{0,26},{2,28},{4,30},{6,0},{8,2},{10,4},{12,6},{14,8},{16,10},{18,... | collective-permute-start | bytes 196616 | tf_op jit(solution)/shard_map/ppermute | solution.py:41
  162.6 7.1 %collective-permute-start.40 = (bf16[2,16,1024]{2,1,0:T(8,128)(2,1)S(1)}, bf16[2,16,1024]{2,1,0:T(8,128)(2,1)S(1)}, u32[]{:S(2)}, u32[]{:S(2)}) collective-permute-start(bf16[2,16,1024]{2,1,0:T(8,128)(2,1)S(1)} %bitcast.188), channel_id=1, source_target_pairs={{0,24},{2,26},{4,28},{6,30},{8,0},{10,2},{12,4},{14,6},{16,8},{18,... | collective-permute-start | bytes 196616 | tf_op jit(solution)/shard_map/ppermute | solution.py:41
  163.0 6.8 %collective-permute-start.41 = (bf16[2,16,1024]{2,1,0:T(8,128)(2,1)S(1)}, bf16[2,16,1024]{2,1,0:T(8,128)(2,1)S(1)}, u32[]{:S(2)}, u32[]{:S(2)}) collective-permute-start(bf16[2,16,1024]{2,1,0:T(8,128)(2,1)S(1)} %bitcast.190), channel_id=1, source_target_pairs={{0,22},{2,24},{4,26},{6,28},{8,30},{10,0},{12,2},{14,4},{16,6},{18... | collective-permute-start | bytes 196616 | tf_op jit(solution)/shard_map/ppermute | solution.py:41
  164.5 5.6 %collective-permute-start.42 = (bf16[2,16,1024]{2,1,0:T(8,128)(2,1)S(1)}, bf16[2,16,1024]{2,1,0:T(8,128)(2,1)S(1)}, u32[]{:S(2)}, u32[]{:S(2)}) collective-permute-start(bf16[2,16,1024]{2,1,0:T(8,128)(2,1)S(1)} %bitcast.192), channel_id=1, source_target_pairs={{0,20},{2,22},{4,24},{6,26},{8,28},{10,30},{12,0},{14,2},{16,4},{1... | collective-permute-start | bytes 196616 | tf_op jit(solution)/shard_map/ppermute | solution.py:41
  165.9 9.4 %collective-permute-start.43 = (bf16[2,16,1024]{2,1,0:T(8,128)(2,1)S(1)}, bf16[2,16,1024]{2,1,0:T(8,128)(2,1)S(1)}, u32[]{:S(2)}, u32[]{:S(2)}) collective-permute-start(bf16[2,16,1024]{2,1,0:T(8,128)(2,1)S(1)} %bitcast.184), channel_id=1, source_target_pairs={{0,18},{2,20},{4,22},{6,24},{8,26},{10,28},{12,30},{14,0},{16,2},{... | collective-permute-start | bytes 196616 | tf_op jit(solution)/shard_map/ppermute | solution.py:41
  (18 other events, 108.7 us)

commit v6 on v5

--- a/solution.py
+++ b/solution.py
@@ -444,37 +444,28 @@
     return lax.optimization_barrier((value,) + others)[0]
 
 
-def out_kernel(place_ref, own_ref, peer_ref, *refs):
-    weight_refs, own_out_ref, both_out_ref = refs[:8], refs[8], refs[9]
-    rows = own_ref.shape[0]
-    both = jnp.concatenate([own_ref[...], peer_ref[...]], axis=0)
+def out_kernel(place_ref, rows_ref, *refs):
+    weight_refs, out_ref = refs[:8], refs[8]
     for pair in range(4):
         weight = jnp.concatenate([weight_refs[2 * pair][...], weight_refs[2 * pair + 1][...]], axis=1)
-        total = jnp.dot(both, weight, preferred_element_type=F32)
+        total = jnp.dot(rows_ref[...], weight, preferred_element_type=F32)
         for at in range(2):
             start = place_ref[(2 * pair + at) % 4] * LANES
             lanes = pl.ds(pl.multiple_of(start, LANES), LANES)
             columns = slice(at * LANES, (at + 1) * LANES)
-            own_out_ref[pair // 2, :, lanes] = total[:rows, columns]
-            for group in range(2):
-                part = total[group * rows : (group + 1) * rows, columns]
-                both_out_ref[pair // 2, group, :, lanes] = part.astype(BF16)
-
-
-def project_out(own, peer, weights, place_of):
-    rows, depth = own.shape
+            out_ref[pair // 2, :, lanes] = total[:, columns].astype(out_ref.dtype)
+
+
+def project_out(rows, weights, place_of, dtype):
     whole = pl.BlockSpec(memory_space=pltpu.VMEM)
     return pl.pallas_call(
         out_kernel,
-        in_specs=[pl.BlockSpec(memory_space=pltpu.SMEM)] + [whole] * 10,
-        out_specs=[whole, whole],
-        out_shape=[
-            jax.ShapeDtypeStruct((2, rows, 4 * LANES), F32),
-            jax.ShapeDtypeStruct((2, 2, rows, 4 * LANES), BF16),
-        ],
+        in_specs=[pl.BlockSpec(memory_space=pltpu.SMEM)] + [whole] * 9,
+        out_specs=whole,
+        out_shape=jax.ShapeDtypeStruct((2, rows.shape[0], 4 * LANES), dtype),
         compiler_params=pltpu.CompilerParams(vmem_limit_bytes=24 * 1024 * 1024),
         cost_estimate=QUICK,
-    )(place_of, own, peer, *weights)
+    )(place_of, rows, *weights)
 
 
 def on_device(
@@ -687,12 +678,15 @@
         columns_at = jnp.stack(
             [2 * at_side + at_core for at_side in (side, 1 - side) for at_core in (core, 1 - core)]
         )
-        terms, given = project_out(scaled, tie(swap(scaled, "near"), new_states), out_columns, columns_at)
+        terms = project_out(scaled, out_columns, columns_at, F32)
+        given = project_out(
+            tie(swap(scaled, "near"), new_states, terms), out_columns, columns_at, BF16
+        )
         here = far == part
         mine = jnp.where(here, terms[0], terms[1])
-        other = jnp.where(here, given[1, 0], given[0, 0])
-        peer_mine = jnp.where(here, given[0, 1], given[1, 1])
-        peer_other = jnp.where(here, given[1, 1], given[0, 1])
+        other = jnp.where(here, terms[1], terms[0]).astype(BF16)
+        peer_mine = jnp.where(here, given[0], given[1])
+        peer_other = jnp.where(here, given[1], given[0])
         over_y = swap(other, "mdl")
         over_near = swap(peer_mine, "near")
         over_both = lax.ppermute(peer_other, ("near", "mdl"), [(0, 3), (1, 2), (2, 1), (3, 0)])

time: 178 us -> 217 us (1.22)
  waiting for transfers between devices: 70 us -> 107 us
  local copies, waits for them, and re-layouts: 15.8 us -> 19.6 us
  starting transfers between devices: 53.5 us -> 50.3 us
    ppermute x43, waiting for transfers between devices: 67.9 us -> 104 us  [rotate(): return lax.ppermute(value, axis, pairs)]
    ppermute x43, starting transfers between devices: 52.5 us -> 49 us  [rotate(): return lax.ppermute(value, axis, pairs)]
    dynamic_update_slice x8, local copies, waits for them, and re-layouts: 3.08 us -> 5.85 us  [place(): full = lax.dynamic_update_slice_in_dim(full, piece[None], slot, 0)]
    unnamed x81 -> x77, local copies, waits for them, and re-layouts: 4.47 us -> 4.47 us
  transfers between devices with their start and end apart: 44 -> 44, of which waited for: 14 -> 14; matrix products, arithmetic and copies ran while one was open for 13% -> 12% of each run, Pallas kernels for 13% -> 11%
where the time goes in v6:
time: 217 us
  waiting for transfers between devices  107 us (49%)
  starting transfers between devices  50.3 us (23%)
  Pallas kernels  24.3 us (11%)
  local copies, waits for them, and re-layouts  19.6 us (9%)
  other arithmetic  10.1 us (5%)
  matrix products  4.35 us (2%)
    ppermute x43, waiting for transfers between devices, rotate(): return lax.ppermute(value, axis, pairs)  104 us
    ppermute x43, starting transfers between devices, rotate(): return lax.ppermute(value, axis, pairs)  49 us
    pallas_call x1, Pallas kernels, mix_requests(): pl.pallas_call(lambda *refs: mixer_kernel(sizes, *refs), grid_spec=grid_s...  9.72 us
    pallas_call x1, Pallas kernels, update_states(): pl.pallas_call(lambda *refs: update_kernel(sizes, *refs), grid=(steps,),...  8.75 us
    dynamic_update_slice x8, local copies, waits for them, and re-layouts, place(): full = lax.dynamic_update_slice_in_dim(full, piece[None], slot, 0)  5.85 us
    unnamed x77, local copies, waits for them, and re-layouts  4.47 us
  transfers between devices with their start and end apart: 44, of which 14 were waited for; matrix products, arithmetic and copies ran while one was open for 12% of the time, Pallas kernels for 11%

profile of v6, /device:TPU:1, one launch (start us, length us, event | category | flops | bytes accessed | tf_op | source)
XLA Modules:
  0.0 217.0 jit_solution(10148501426668894571)
XLA Ops:
  0.7 1.3 copy.74
  3.6 2.7 %collective-permute-start = (bf16[2,16,1024]{2,1,0:T(8,128)(2,1)S(1)}, bf16[2,16,1024]{2,1,0:T(8,128)(2,1)S(1)}, u32[]{:S(2)}, u32[]{:S(2)}) collective-permute-start(bf16[2,16,1024]{2,1,0:T(8,128)(2,1)S(1)} %bitcast.175), channel_id=1, source_target_pairs={{0,2},{2,4},{4,6},{6,8},{8,10},{10,12},{12,14},{14,16},{16,18},{18... | collective-permute-start | bytes 196616 | tf_op jit(solution)/shard_map/ppermute | solution.py:41
  6.3 1.3 collective-permute-start.1
  8.0 1.4 collective-permute-start.3
  9.4 2.5 %collective-permute-start.4 = (bf16[2,16,1024]{2,1,0:T(8,128)(2,1)S(1)}, bf16[2,16,1024]{2,1,0:T(8,128)(2,1)S(1)}, u32[]{:S(2)}, u32[]{:S(2)}) collective-permute-start(bf16[2,16,1024]{2,1,0:T(8,128)(2,1)S(1)} %bitcast.178), channel_id=1, source_target_pairs={{0,10},{2,12},{4,14},{6,16},{8,18},{10,20},{12,22},{14,24},{16,26}... | collective-permute-start | bytes 196616 | tf_op jit(solution)/shard_map/ppermute | solution.py:41
  15.3 2.1 collective-permute-start.5
  18.7 1.9 collective-permute-start.8
  20.8 1.6 collective-permute-start.9
  23.5 1.6 shard_map.210
  26.4 2.2 collective-permute-start.6
  29.2 21.5 %collective-permute-done.6 = bf16[2,16,1024]{2,1,0:T(8,128)(2,1)S(1)} collective-permute-done((bf16[2,16,1024]{2,1,0:T(8,128)(2,1)S(1)}, bf16[2,16,1024]{2,1,0:T(8,128)(2,1)S(1)}, u32[]{:S(2)}, u32[]{:S(2)}) %collective-permute-start.6) | collective-permute-done | bytes 65568 | tf_op jit(solution)/shard_map/ppermute | solution.py:41
  52.2 2.6 %collective-permute-start.13 = (bf16[128,1024]{1,0:T(8,128)(2,1)S(1)}, bf16[128,1024]{1,0:T(8,128)(2,1)S(1)}, u32[]{:S(2)}, u32[]{:S(2)}) collective-permute-start(bf16[128,1024]{1,0:T(8,128)(2,1)S(1)} %reshape.253), channel_id=1, source_target_pairs={{0,24},{8,0},{16,8},{24,16},{1,25},{9,1},{17,9},{25,17},{2,26},{10... | collective-permute-start | bytes 786440 | tf_op jit(solution)/shard_map/ppermute | solution.py:41
  55.0 1.1 broadcast.204.clone
  61.8 10.3 %collective-permute-done.12 = bf16[128,1024]{1,0:T(8,128)(2,1)S(1)} collective-permute-done((bf16[128,1024]{1,0:T(8,128)(2,1)S(1)}, bf16[128,1024]{1,0:T(8,128)(2,1)S(1)}, u32[]{:S(2)}, u32[]{:S(2)}) %collective-permute-start.12) | collective-permute-done | bytes 262176 | tf_op jit(solution)/shard_map/ppermute | solution.py:41
  72.1 4.0 %collective-permute-done.14 = bf16[3,128,1152]{2,1,0:T(8,128)(2,1)S(1)} collective-permute-done((bf16[3,128,1152]{2,1,0:T(8,128)(2,1)S(1)}, bf16[3,128,1152]{2,1,0:T(8,128)(2,1)S(1)}, u32[]{:S(2)}, u32[]{:S(2)}) %collective-permute-start.14) | collective-permute-done | bytes 884768 | tf_op jit(solution)/shard_map/ppermute | solution.py:41
  79.3 1.5 collective-permute-start.28
  81.9 22.6 %collective-permute-done.28.refs_4_ = bf16[2048,128]{1,0:T(8,128)(2,1)S(1)} collective-permute-done((bf16[2048,128]{1,0:T(8,128)(2,1)S(1)}, bf16[2048,128]{1,0:T(8,128)(2,1)S(1)}, u32[]{:S(2)}, u32[]{:S(2)}) %collective-permute-start.28) | collective-permute-done | bytes 524320 | tf_op jit(solution)/shard_map/ppermute | solution.py:41
  104.4 1.4 collective-permute-start.29
  106.8 1.3 collective-permute-start.15
  108.2 3.1 %pad_maximum_fusion = bf16[2048,1152]{1,0:T(8,128)(2,1)S(1)} fusion(bf16[512,1152]{1,0:T(8,128)(2,1)} %collective-permute-done.17, bf16[512,1152]{1,0:T(8,128)(2,1)} %collective-permute-done.16, bf16[512,1152]{1,0:T(8,128)(2,1)} %bitcast.27, bf16[512,1152]{1,0:T(8,128)(2,1)} %bitcast.25), kind=kLoop, calls=%fused_computation.4 | loop fusion | flops 18874368 | bytes 9437184 | tf_op jit(solution)/shard_map/concatenate | solution.py:598
  111.3 9.1 %collective-permute-done.15 = bf16[256,1024]{1,0:T(8,128)(2,1)S(1)} collective-permute-done((bf16[256,1024]{1,0:T(8,128)(2,1)S(1)}, bf16[256,1024]{1,0:T(8,128)(2,1)S(1)}, u32[]{:S(2)}, u32[]{:S(2)}) %collective-permute-start.15) | collective-permute-done | bytes 524320 | tf_op jit(solution)/shard_map/ppermute | solution.py:41
  120.5 1.2 collective-permute-start.19
  121.9 1.6 convolution_convert_fusion.4
  123.5 1.2 collective-permute-start.20
  124.7 8.4 %collective-permute-done.19 = bf16[256,1024]{1,0:T(8,128)(2,1)S(1)} collective-permute-done((bf16[256,1024]{1,0:T(8,128)(2,1)S(1)}, bf16[256,1024]{1,0:T(8,128)(2,1)S(1)}, u32[]{:S(2)}, u32[]{:S(2)}) %collective-permute-start.19) | collective-permute-done | bytes 524320 | tf_op jit(solution)/shard_map/ppermute | solution.py:41
  133.3 1.6 convolution_convert_fusion.5
  135.6 5.9 %collective-permute-done.22.refs_4_.refs_8_ = bf16[128,640]{1,0:T(8,128)(2,1)S(1)} collective-permute-done((bf16[128,640]{1,0:T(8,128)(2,1)S(1)}, bf16[128,640]{1,0:T(8,128)(2,1)S(1)}, u32[]{:S(2)}, u32[]{:S(2)}) %collective-permute-start.22) | collective-permute-done | bytes 163872 | tf_op jit(solution)/shard_map/ppermute | solution.py:41
  141.6 3.2 %collective-permute-start.25 = (bf16[128,512]{1,0:T(8,128)(2,1)S(1)}, bf16[128,512]{1,0:T(8,128)(2,1)S(1)}, u32[]{:S(2)}, u32[]{:S(2)}) collective-permute-start(bf16[128,512]{1,0:T(8,128)(2,1)S(1)} %get-tuple-element.129), channel_id=1, source_target_pairs={{0,24},{8,0},{16,8},{24,16},{1,25},{9,1},{17,9},{25,17},{2,26},{10... | collective-permute-start | bytes 393224 | tf_op jit(solution)/shard_map/ppermute | solution.py:41
  144.8 9.7 %shard_map.211 = (bf16[128,2048]{1,0:T(8,128)(2,1)}, bf16[2048,256]{1,0:T(8,128)(2,1)}, f32[128,128]{1,0:T(8,128)}, f32[128,128]{1,0:T(8,128)}, bf16[32,2048]{1,0:T(8,128)(2,1)}, /*index=5*/bf16[32,256]{1,0:T(8,128)(2,1)}) custom-call(s32[4]{0:T(128)} %and_select_fusion.1.refs_0_, bf16[128,640]{1,0:T(8,128)(2,1)} %get-tuple-element.116.refs_1_.refs_5_, ...), custom_call_target="tpu_custom_call" | custom-call | flops 2147483648 | bytes 16777216 | tf_op jit(solution)/shard_map/pallas_call | solution.py:391
  154.5 3.5 %collective-permute-start.27 = (bf16[2048,128]{1,0:T(8,128)(2,1)S(1)}, bf16[2048,128]{1,0:T(8,128)(2,1)S(1)}, u32[]{:S(2)}, u32[]{:S(2)}) collective-permute-start(bf16[2048,128]{1,0:T(8,128)(2,1)S(1)} %collective-permute-done.18.refs_2_), channel_id=1, source_target_pairs={{0,2},{2,0},{1,3},{3,1},{4,6},{6,4},{5,7},{7,5},{8,10},{10,8},{9,1... | collective-permute-start | bytes 1572872 | tf_op jit(solution)/shard_map/ppermute | solution.py:41
  158.1 2.3 %multiply_convert_fusion = (bf16[128,2048]{1,0:T(8,128)(2,1)}, f32[128]{0:T(128)S(1)}) fusion(f32[2048]{0:T(1024)S(1)} %copy-done.13, bf16[128,512]{1,0:T(8,128)(2,1)S(1)} %get-tuple-element.192, bf16[128,512]{1,0:T(8,128)(2,1)S(1)} %get-tuple-element.193, bf16[128,512]{1,0:T(8,128)(2,1)S(1)} %get-tuple-element.194, ...), kind=kLoop, calls=%fused_computation.33 | loop fusion | flops 4456320 | bytes 1581568 | tf_op jit(solution)/shard_map/convert_element_type | solution.py:671
  160.4 11.2 %collective-permute-done.30.refs_6_ = bf16[2048,128]{1,0:T(8,128)(2,1)} collective-permute-done((bf16[2048,128]{1,0:T(8,128)(2,1)S(1)}, bf16[2048,128]{1,0:T(8,128)(2,1)}, u32[]{:S(2)}, u32[]{:S(2)}) %collective-permute-start.30) | collective-permute-done | bytes 524320 | tf_op jit(solution)/shard_map/ppermute | solution.py:41
  172.8 8.8 %shard_map.213 = f32[8,32,64,128]{3,2,1,0:T(8,128)} custom-call(bf16[2048,256]{1,0:T(8,128)(2,1)} %get-tuple-element.133.refs_0_, f32[128,128]{1,0:T(8,128)} %get-tuple-element.135.refs_1_, f32[128,128]{1,0:T(8,128)} %get-tuple-element.136.refs_2_, f32[8,32,64,128]{3,2,1,0:T(8,128)} %refs_3_.1), custom_call_target="tpu_custom_call" | custom-call | flops 2147483648 | bytes 16777216 | tf_op jit(solution)/shard_map/pallas_call | solution.py:293
  181.6 1.2 collective-permute-start.33
  182.8 2.2 shard_map.212
  185.0 1.3 collective-permute-done.34.rows_ref
  186.4 2.1 shard_map.214
  188.5 1.3 collective-permute-start.36
  189.8 1.2 collective-permute-start.35
  191.2 2.5 %collective-permute-done.36 = bf16[128,512]{1,0:T(8,128)(2,1)S(1)} collective-permute-done((bf16[128,512]{1,0:T(8,128)(2,1)S(1)}, bf16[128,512]{1,0:T(8,128)(2,1)S(1)}, u32[]{:S(2)}, u32[]{:S(2)}) %collective-permute-start.36) | collective-permute-done | bytes 131104 | tf_op jit(solution)/shard_map/ppermute | solution.py:692
  193.7 2.9 %collective-permute-done.35 = bf16[128,512]{1,0:T(8,128)(2,1)S(1)} collective-permute-done((bf16[128,512]{1,0:T(8,128)(2,1)S(1)}, bf16[128,512]{1,0:T(8,128)(2,1)S(1)}, u32[]{:S(2)}, u32[]{:S(2)}) %collective-permute-start.35) | collective-permute-done | bytes 131104 | tf_op jit(solution)/shard_map/ppermute | solution.py:41
  198.1 1.5 collective-permute-start.37
  199.6 1.4 collective-permute-start.38
  201.0 1.7 collective-permute-start.39
  202.7 1.3 collective-permute-start.40
  204.2 1.8 collective-permute-start.42
  206.0 1.3 collective-permute-start.43
  209.2 5.7 %collective-permute-done.43 = bf16[2,16,1024]{2,1,0:T(8,128)(2,1)S(1)} collective-permute-done((bf16[2,16,1024]{2,1,0:T(8,128)(2,1)S(1)}, bf16[2,16,1024]{2,1,0:T(8,128)(2,1)S(1)}, u32[]{:S(2)}, u32[]{:S(2)}) %collective-permute-start.43) | collective-permute-done | bytes 65568 | tf_op jit(solution)/shard_map/ppermute | solution.py:41
  (208 shorter events, 30.5 us)
Async XLA Ops:
  3.6 11.8 %collective-permute-start = (bf16[2,16,1024]{2,1,0:T(8,128)(2,1)S(1)}, bf16[2,16,1024]{2,1,0:T(8,128)(2,1)S(1)}, u32[]{:S(2)}, u32[]{:S(2)}) collective-permute-start(bf16[2,16,1024]{2,1,0:T(8,128)(2,1)S(1)} %bitcast.175), channel_id=1, source_target_pairs={{0,2},{2,4},{4,6},{6,8},{8,10},{10,12},{12,14},{14,16},{16,18},{18... | collective-permute-start | bytes 196616 | tf_op jit(solution)/shard_map/ppermute | solution.py:41
  6.3 11.2 %collective-permute-start.1 = (bf16[2,16,1024]{2,1,0:T(8,128)(2,1)S(1)}, bf16[2,16,1024]{2,1,0:T(8,128)(2,1)S(1)}, u32[]{:S(2)}, u32[]{:S(2)}) collective-permute-start(bf16[2,16,1024]{2,1,0:T(8,128)(2,1)S(1)} %bitcast.174), channel_id=1, source_target_pairs={{0,4},{2,6},{4,8},{6,10},{8,12},{10,14},{12,16},{14,18},{16,20},{1... | collective-permute-start | bytes 196616 | tf_op jit(solution)/shard_map/ppermute | solution.py:41
  7.6 9.9 %collective-permute-start.2 = (bf16[2,16,1024]{2,1,0:T(8,128)(2,1)S(1)}, bf16[2,16,1024]{2,1,0:T(8,128)(2,1)S(1)}, u32[]{:S(2)}, u32[]{:S(2)}) collective-permute-start(bf16[2,16,1024]{2,1,0:T(8,128)(2,1)S(1)} %bitcast.176), channel_id=1, source_target_pairs={{0,6},{2,8},{4,10},{6,12},{8,14},{10,16},{12,18},{14,20},{16,22},{... | collective-permute-start | bytes 196616 | tf_op jit(solution)/shard_map/ppermute | solution.py:41
  8.0 9.5 %collective-permute-start.3 = (bf16[2,16,1024]{2,1,0:T(8,128)(2,1)S(1)}, bf16[2,16,1024]{2,1,0:T(8,128)(2,1)S(1)}, u32[]{:S(2)}, u32[]{:S(2)}) collective-permute-start(bf16[2,16,1024]{2,1,0:T(8,128)(2,1)S(1)} %bitcast.177), channel_id=1, source_target_pairs={{0,8},{2,10},{4,12},{6,14},{8,16},{10,18},{12,20},{14,22},{16,24},... | collective-permute-start | bytes 196616 | tf_op jit(solution)/shard_map/ppermute | solution.py:41
  9.4 8.1 %collective-permute-start.4 = (bf16[2,16,1024]{2,1,0:T(8,128)(2,1)S(1)}, bf16[2,16,1024]{2,1,0:T(8,128)(2,1)S(1)}, u32[]{:S(2)}, u32[]{:S(2)}) collective-permute-start(bf16[2,16,1024]{2,1,0:T(8,128)(2,1)S(1)} %bitcast.178), channel_id=1, source_target_pairs={{0,10},{2,12},{4,14},{6,16},{8,18},{10,20},{12,22},{14,24},{16,26}... | collective-permute-start | bytes 196616 | tf_op jit(solution)/shard_map/ppermute | solution.py:41
  15.3 11.1 %collective-permute-start.5 = (bf16[2,16,1024]{2,1,0:T(8,128)(2,1)S(1)}, bf16[2,16,1024]{2,1,0:T(8,128)(2,1)S(1)}, u32[]{:S(2)}, u32[]{:S(2)}) collective-permute-start(bf16[2,16,1024]{2,1,0:T(8,128)(2,1)S(1)} %bitcast.180), channel_id=1, source_target_pairs={{0,12},{2,14},{4,16},{6,18},{8,20},{10,22},{12,24},{14,26},{16,28}... | collective-permute-start | bytes 196616 | tf_op jit(solution)/shard_map/ppermute | solution.py:41
  17.6 11.0 %copy-start.15 = (f32[32]{0:T(128)S(1)}, f32[32]{0:T(128)}, u32[]{:S(2)}) copy-start(f32[32]{0:T(128)} %param.24) | copy-start | bytes 388
  18.1 32.6 %collective-permute-start.7 = (bf16[128,1152]{1,0:T(8,128)(2,1)S(1)}, bf16[128,1152]{1,0:T(8,128)(2,1)S(1)}, u32[]{:S(2)}, u32[]{:S(2)}) collective-permute-start(bf16[128,1152]{1,0:T(8,128)(2,1)S(1)} %bitcast.147), channel_id=1, source_target_pairs={{0,8},{8,16},{16,24},{24,0},{1,9},{9,17},{17,25},{25,1},{2,10},{10... | collective-permute-start | bytes 884744 | tf_op jit(solution)/shard_map/ppermute | solution.py:41
  18.7 32.0 %collective-permute-start.8 = (bf16[128,1152]{1,0:T(8,128)(2,1)S(1)}, bf16[128,1152]{1,0:T(8,128)(2,1)S(1)}, u32[]{:S(2)}, u32[]{:S(2)}) collective-permute-start(bf16[128,1152]{1,0:T(8,128)(2,1)S(1)} %bitcast.148), channel_id=1, source_target_pairs={{0,16},{8,24},{16,0},{24,8},{1,17},{9,25},{17,1},{25,9},{2,18},{10... | collective-permute-start | bytes 884744 | tf_op jit(solution)/shard_map/ppermute | solution.py:41
  20.8 29.8 %collective-permute-start.9 = (bf16[128,1152]{1,0:T(8,128)(2,1)S(1)}, bf16[128,1152]{1,0:T(8,128)(2,1)S(1)}, u32[]{:S(2)}, u32[]{:S(2)}) collective-permute-start(bf16[128,1152]{1,0:T(8,128)(2,1)S(1)} %bitcast.149), channel_id=1, source_target_pairs={{0,24},{8,0},{16,8},{24,16},{1,25},{9,1},{17,9},{25,17},{2,26},{10... | collective-permute-start | bytes 884744 | tf_op jit(solution)/shard_map/ppermute | solution.py:41
  22.4 28.3 %collective-permute-start.10 = (bf16[128,1152]{1,0:T(8,128)(2,1)S(1)}, bf16[128,1152]{1,0:T(8,128)(2,1)S(1)}, u32[]{:S(2)}, u32[]{:S(2)}) collective-permute-start(bf16[128,1152]{1,0:T(8,128)(2,1)S(1)} %bitcast.144), channel_id=1, source_target_pairs={{0,4},{4,0},{1,5},{5,1},{2,6},{6,2},{3,7},{7,3},{8,12},{12,8},{9,1... | collective-permute-start | bytes 884744 | tf_op jit(solution)/shard_map/ppermute | solution.py:41
  26.4 24.2 %collective-permute-start.6 = (bf16[2,16,1024]{2,1,0:T(8,128)(2,1)S(1)}, bf16[2,16,1024]{2,1,0:T(8,128)(2,1)S(1)}, u32[]{:S(2)}, u32[]{:S(2)}) collective-permute-start(bf16[2,16,1024]{2,1,0:T(8,128)(2,1)S(1)} %bitcast.179), channel_id=1, source_target_pairs={{0,14},{2,16},{4,18},{6,20},{8,22},{10,24},{12,26},{14,28},{16,30}... | collective-permute-start | bytes 196616 | tf_op jit(solution)/shard_map/ppermute | solution.py:41
  51.5 10.3 %collective-permute-start.11 = (bf16[128,1024]{1,0:T(8,128)(2,1)S(1)}, bf16[128,1024]{1,0:T(8,128)(2,1)S(1)}, u32[]{:S(2)}, u32[]{:S(2)}) collective-permute-start(bf16[128,1024]{1,0:T(8,128)(2,1)S(1)} %reshape.253), channel_id=1, source_target_pairs={{0,8},{8,16},{16,24},{24,0},{1,9},{9,17},{17,25},{25,1},{2,10},{10... | collective-permute-start | bytes 786440 | tf_op jit(solution)/shard_map/ppermute | solution.py:41
  51.6 20.5 %collective-permute-start.12 = (bf16[128,1024]{1,0:T(8,128)(2,1)S(1)}, bf16[128,1024]{1,0:T(8,128)(2,1)S(1)}, u32[]{:S(2)}, u32[]{:S(2)}) collective-permute-start(bf16[128,1024]{1,0:T(8,128)(2,1)S(1)} %reshape.253), channel_id=1, source_target_pairs={{0,16},{8,24},{16,0},{24,8},{1,17},{9,25},{17,1},{25,9},{2,18},{10... | collective-permute-start | bytes 786440 | tf_op jit(solution)/shard_map/ppermute | solution.py:41
  52.2 19.8 %collective-permute-start.13 = (bf16[128,1024]{1,0:T(8,128)(2,1)S(1)}, bf16[128,1024]{1,0:T(8,128)(2,1)S(1)}, u32[]{:S(2)}, u32[]{:S(2)}) collective-permute-start(bf16[128,1024]{1,0:T(8,128)(2,1)S(1)} %reshape.253), channel_id=1, source_target_pairs={{0,24},{8,0},{16,8},{24,16},{1,25},{9,1},{17,9},{25,17},{2,26},{10... | collective-permute-start | bytes 786440 | tf_op jit(solution)/shard_map/ppermute | solution.py:41
  55.0 21.1 %collective-permute-start.14 = (bf16[3,128,1152]{2,1,0:T(8,128)(2,1)S(1)}, bf16[3,128,1152]{2,1,0:T(8,128)(2,1)S(1)}, u32[]{:S(2)}, u32[]{:S(2)}) collective-permute-start(bf16[3,128,1152]{2,1,0:T(8,128)(2,1)S(1)} %pad_maximum_fusion.1), channel_id=1, source_target_pairs={{0,4},{4,0},{1,5},{5,1},{2,6},{6,2},{3,7},{7,3},{8,12},{12,8},{9,1... | collective-permute-start | bytes 2654216 | tf_op jit(solution)/shard_map/ppermute | solution.py:41
  58.3 21.0 %copy-start = (bf16[2048,128]{1,0:T(8,128)(2,1)S(1)}, bf16[2048,128]{1,0:T(8,128)(2,1)}, u32[]{:S(2)}) copy-start(bf16[2048,128]{1,0:T(8,128)(2,1)} %refs_0_.3) | copy-start | bytes 1572868
  78.3 28.5 %collective-permute-start.17 = (bf16[512,1152]{1,0:T(8,128)(2,1)}, bf16[512,1152]{1,0:T(8,128)(2,1)}, u32[]{:S(2)}, u32[]{:S(2)}) collective-permute-start(bf16[512,1152]{1,0:T(8,128)(2,1)} %bitcast.27), channel_id=1, source_target_pairs={{0,2},{2,0},{1,3},{3,1},{4,6},{6,4},{5,7},{7,5},{8,10},{10,8},{9,1... | collective-permute-start | bytes 3538952 | tf_op jit(solution)/shard_map/ppermute | solution.py:41
  79.3 28.8 %collective-permute-start.16 = (bf16[512,1152]{1,0:T(8,128)(2,1)}, bf16[512,1152]{1,0:T(8,128)(2,1)}, u32[]{:S(2)}, u32[]{:S(2)}) collective-permute-start(bf16[512,1152]{1,0:T(8,128)(2,1)} %bitcast.25), channel_id=1, source_target_pairs={{0,2},{2,0},{1,3},{3,1},{4,6},{6,4},{5,7},{7,5},{8,10},{10,8},{9,1... | collective-permute-start | bytes 3538952 | tf_op jit(solution)/shard_map/ppermute | solution.py:41
  79.3 25.1 %collective-permute-start.28 = (bf16[2048,128]{1,0:T(8,128)(2,1)S(1)}, bf16[2048,128]{1,0:T(8,128)(2,1)S(1)}, u32[]{:S(2)}, u32[]{:S(2)}) collective-permute-start(bf16[2048,128]{1,0:T(8,128)(2,1)S(1)} %copy-done), channel_id=1, source_target_pairs={{0,16},{16,0},{1,17},{17,1},{2,18},{18,2},{3,19},{19,3},{4,20},{20... | collective-permute-start | bytes 1572872 | tf_op jit(solution)/shard_map/ppermute | solution.py:41
  80.8 30.5 %collective-permute-start.18 = (bf16[2048,128]{1,0:T(8,128)(2,1)S(1)}, bf16[2048,128]{1,0:T(8,128)(2,1)S(1)}, u32[]{:S(2)}, u32[]{:S(2)}) collective-permute-start(bf16[2048,128]{1,0:T(8,128)(2,1)S(1)} %copy-done), channel_id=1, source_target_pairs={{0,4},{4,0},{1,5},{5,1},{2,6},{6,2},{3,7},{7,3},{8,12},{12,8},{9,1... | collective-permute-start | bytes 1572872 | tf_op jit(solution)/shard_map/ppermute | solution.py:41
  80.8 100.8 %collective-permute-start.26 = (bf16[2048,128]{1,0:T(8,128)(2,1)S(1)}, bf16[2048,128]{1,0:T(8,128)(2,1)S(1)}, u32[]{:S(2)}, u32[]{:S(2)}) collective-permute-start(bf16[2048,128]{1,0:T(8,128)(2,1)S(1)} %copy-done), channel_id=1, source_target_pairs={{0,2},{2,0},{1,3},{3,1},{4,6},{6,4},{5,7},{7,5},{8,10},{10,8},{9,1... | collective-permute-start | bytes 1572872 | tf_op jit(solution)/shard_map/ppermute | solution.py:41
  104.4 78.4 %collective-permute-start.29 = (bf16[2048,128]{1,0:T(8,128)(2,1)S(1)}, bf16[2048,128]{1,0:T(8,128)(2,1)S(1)}, u32[]{:S(2)}, u32[]{:S(2)}) collective-permute-start(bf16[2048,128]{1,0:T(8,128)(2,1)S(1)} %collective-permute-done.28.refs_4_), channel_id=1, source_target_pairs={{0,2},{2,0},{1,3},{3,1},{4,6},{6,4},{5,7},{7,5},{8,10},{10,8},{9,1... | collective-permute-start | bytes 1572872 | tf_op jit(solution)/shard_map/ppermute | solution.py:41
  106.8 13.6 %collective-permute-start.15 = (bf16[256,1024]{1,0:T(8,128)(2,1)S(1)}, bf16[256,1024]{1,0:T(8,128)(2,1)S(1)}, u32[]{:S(2)}, u32[]{:S(2)}) collective-permute-start(bf16[256,1024]{1,0:T(8,128)(2,1)S(1)} %constant_dynamic-update-slice_fusion.8), channel_id=1, source_target_pairs={{0,1},{1,0},{2,3},{3,2},{4,5},{5,4},{6,7},{7,6},{8,9},{9,8},{10,11... | collective-permute-start | bytes 1572872 | tf_op jit(solution)/shard_map/ppermute | solution.py:41
  120.5 12.7 %collective-permute-start.19 = (bf16[256,1024]{1,0:T(8,128)(2,1)S(1)}, bf16[256,1024]{1,0:T(8,128)(2,1)S(1)}, u32[]{:S(2)}, u32[]{:S(2)}) collective-permute-start(bf16[256,1024]{1,0:T(8,128)(2,1)S(1)} %pad_maximum_fusion.2), channel_id=1, source_target_pairs={{0,1},{1,0},{2,3},{3,2},{4,5},{5,4},{6,7},{7,6},{8,9},{9,8},{10,11... | collective-permute-start | bytes 1572872 | tf_op jit(solution)/shard_map/ppermute | solution.py:41
  123.5 12.1 %collective-permute-start.20 = (bf16[128,640]{1,0:T(8,128)(2,1)S(1)}, bf16[128,640]{1,0:T(8,128)(2,1)S(1)}, u32[]{:S(2)}, u32[]{:S(2)}) collective-permute-start(bf16[128,640]{1,0:T(8,128)(2,1)S(1)} %get-tuple-element.178), channel_id=1, source_target_pairs={{0,24},{8,0},{16,8},{24,16},{1,25},{9,1},{17,9},{25,17},{2,26},{10... | collective-permute-start | bytes 491528 | tf_op jit(solution)/shard_map/ppermute | solution.py:41
  124.7 10.9 %collective-permute-start.21 = (bf16[128,640]{1,0:T(8,128)(2,1)S(1)}, bf16[128,640]{1,0:T(8,128)(2,1)S(1)}, u32[]{:S(2)}, u32[]{:S(2)}) collective-permute-start(bf16[128,640]{1,0:T(8,128)(2,1)S(1)} %get-tuple-element.177), channel_id=1, source_target_pairs={{0,16},{8,24},{16,0},{24,8},{1,17},{9,25},{17,1},{25,9},{2,18},{10... | collective-permute-start | bytes 491528 | tf_op jit(solution)/shard_map/ppermute | solution.py:41
  135.6 6.0 %collective-permute-start.22 = (bf16[128,640]{1,0:T(8,128)(2,1)S(1)}, bf16[128,640]{1,0:T(8,128)(2,1)S(1)}, u32[]{:S(2)}, u32[]{:S(2)}) collective-permute-start(bf16[128,640]{1,0:T(8,128)(2,1)S(1)} %get-tuple-element.175), channel_id=1, source_target_pairs={{0,8},{8,16},{16,24},{24,0},{1,9},{9,17},{17,25},{25,1},{2,10},{10... | collective-permute-start | bytes 491528 | tf_op jit(solution)/shard_map/ppermute | solution.py:41
  141.5 16.6 %copy-start.13 = (f32[2048]{0:T(1024)S(1)}, f32[2048]{0:T(1024)}, u32[]{:S(2)}) copy-start(f32[2048]{0:T(1024)} %param.29) | copy-start | bytes 24580
  141.5 13.0 %collective-permute-start.23 = (bf16[128,512]{1,0:T(8,128)(2,1)S(1)}, bf16[128,512]{1,0:T(8,128)(2,1)S(1)}, u32[]{:S(2)}, u32[]{:S(2)}) collective-permute-start(bf16[128,512]{1,0:T(8,128)(2,1)S(1)} %get-tuple-element.127), channel_id=1, source_target_pairs={{0,8},{8,16},{16,24},{24,0},{1,9},{9,17},{17,25},{25,1},{2,10},{10... | collective-permute-start | bytes 393224 | tf_op jit(solution)/shard_map/ppermute | solution.py:41
  141.5 16.5 %collective-permute-start.24 = (bf16[128,512]{1,0:T(8,128)(2,1)S(1)}, bf16[128,512]{1,0:T(8,128)(2,1)S(1)}, u32[]{:S(2)}, u32[]{:S(2)}) collective-permute-start(bf16[128,512]{1,0:T(8,128)(2,1)S(1)} %get-tuple-element.128), channel_id=1, source_target_pairs={{0,16},{8,24},{16,0},{24,8},{1,17},{9,25},{17,1},{25,9},{2,18},{10... | collective-permute-start | bytes 393224 | tf_op jit(solution)/shard_map/ppermute | solution.py:41
  141.6 16.4 %collective-permute-start.25 = (bf16[128,512]{1,0:T(8,128)(2,1)S(1)}, bf16[128,512]{1,0:T(8,128)(2,1)S(1)}, u32[]{:S(2)}, u32[]{:S(2)}) collective-permute-start(bf16[128,512]{1,0:T(8,128)(2,1)S(1)} %get-tuple-element.129), channel_id=1, source_target_pairs={{0,24},{8,0},{16,8},{24,16},{1,25},{9,1},{17,9},{25,17},{2,26},{10... | collective-permute-start | bytes 393224 | tf_op jit(solution)/shard_map/ppermute | solution.py:41
  154.5 28.3 %collective-permute-start.27 = (bf16[2048,128]{1,0:T(8,128)(2,1)S(1)}, bf16[2048,128]{1,0:T(8,128)(2,1)S(1)}, u32[]{:S(2)}, u32[]{:S(2)}) collective-permute-start(bf16[2048,128]{1,0:T(8,128)(2,1)S(1)} %collective-permute-done.18.refs_2_), channel_id=1, source_target_pairs={{0,2},{2,0},{1,3},{3,1},{4,6},{6,4},{5,7},{7,5},{8,10},{10,8},{9,1... | collective-permute-start | bytes 1572872 | tf_op jit(solution)/shard_map/ppermute | solution.py:41
  158.0 13.6 %collective-permute-start.30 = (bf16[2048,128]{1,0:T(8,128)(2,1)S(1)}, bf16[2048,128]{1,0:T(8,128)(2,1)}, u32[]{:S(2)}, u32[]{:S(2)}) collective-permute-start(bf16[2048,128]{1,0:T(8,128)(2,1)S(1)} %collective-permute-done.28.refs_4_), channel_id=1, source_target_pairs={{0,4},{4,0},{1,5},{5,1},{2,6},{6,2},{3,7},{7,3},{8,12},{12,8},{9,1... | collective-permute-start | bytes 1572872 | tf_op jit(solution)/shard_map/ppermute | solution.py:41
  171.6 11.2 %collective-permute-start.31 = (bf16[2048,128]{1,0:T(8,128)(2,1)}, bf16[2048,128]{1,0:T(8,128)(2,1)}, u32[]{:S(2)}, u32[]{:S(2)}) collective-permute-start(bf16[2048,128]{1,0:T(8,128)(2,1)} %collective-permute-done.30.refs_6_), channel_id=1, source_target_pairs={{0,2},{2,0},{1,3},{3,1},{4,6},{6,4},{5,7},{7,5},{8,10},{10,8},{9,1... | collective-permute-start | bytes 1572872 | tf_op jit(solution)/shard_map/ppermute | solution.py:41
  172.5 13.9 %collective-permute-start.34 = (bf16[128,2048]{1,0:T(8,128)(2,1)}, bf16[128,2048]{1,0:T(8,128)(2,1)}, u32[]{:S(2)}, u32[]{:S(2)}) collective-permute-start(bf16[128,2048]{1,0:T(8,128)(2,1)} %get-tuple-element.169.rows_ref), channel_id=1, source_target_pairs={{0,8},{8,0},{1,9},{9,1},{2,10},{10,2},{3,11},{11,3},{4,12},{12,4},... | collective-permute-start | bytes 1572872 | tf_op jit(solution)/shard_map/ppermute | solution.py:41
  181.6 9.6 %collective-permute-start.33 = (f32[128]{0:T(128)S(1)}, f32[128]{0:T(128)S(1)}, u32[]{:S(2)}, u32[]{:S(2)}) collective-permute-start(f32[128]{0:T(128)S(1)} %get-tuple-element.170), channel_id=1, source_target_pairs={{0,1},{1,0},{2,3},{3,2},{4,5},{5,4},{6,7},{7,6},{8,9},{9,8},{10,11... | collective-permute-start | bytes 1544 | tf_op jit(solution)/shard_map/ppermute | solution.py:41
  188.5 5.2 %collective-permute-start.36 = (bf16[128,512]{1,0:T(8,128)(2,1)S(1)}, bf16[128,512]{1,0:T(8,128)(2,1)S(1)}, u32[]{:S(2)}, u32[]{:S(2)}) collective-permute-start(bf16[128,512]{1,0:T(8,128)(2,1)S(1)} %get-tuple-element.212), channel_id=1, source_target_pairs={{0,9},{1,8},{8,1},{9,0},{2,11},{3,10},{10,3},{11,2},{4,13},{5,12},... | collective-permute-start | bytes 393224 | tf_op jit(solution)/shard_map/ppermute | solution.py:692
  189.8 6.8 %collective-permute-start.35 = (bf16[128,512]{1,0:T(8,128)(2,1)S(1)}, bf16[128,512]{1,0:T(8,128)(2,1)S(1)}, u32[]{:S(2)}, u32[]{:S(2)}) collective-permute-start(bf16[128,512]{1,0:T(8,128)(2,1)S(1)} %get-tuple-element.211), channel_id=1, source_target_pairs={{0,8},{8,0},{1,9},{9,1},{2,10},{10,2},{3,11},{11,3},{4,12},{12,4},... | collective-permute-start | bytes 393224 | tf_op jit(solution)/shard_map/ppermute | solution.py:41
  191.0 5.8 %collective-permute-start.32 = (bf16[128,512]{1,0:T(8,128)(2,1)S(1)}, bf16[128,512]{1,0:T(8,128)(2,1)S(1)}, u32[]{:S(2)}, u32[]{:S(2)}) collective-permute-start(bf16[128,512]{1,0:T(8,128)(2,1)S(1)} %fusion.24), channel_id=1, source_target_pairs={{0,1},{1,0},{2,3},{3,2},{4,5},{5,4},{6,7},{7,6},{8,9},{9,8},{10,11... | collective-permute-start | bytes 393224 | tf_op jit(solution)/shard_map/ppermute | solution.py:41
  197.1 11.0 %copy-start.11 = (bf16[32,256]{1,0:T(8,128)(2,1)S(1)}, bf16[32,256]{1,0:T(8,128)(2,1)}, u32[]{:S(2)}) copy-start(bf16[32,256]{1,0:T(8,128)(2,1)} %get-tuple-element.139) | copy-start | bytes 49156
  198.1 6.1 %collective-permute-start.37 = (bf16[2,16,1024]{2,1,0:T(8,128)(2,1)S(1)}, bf16[2,16,1024]{2,1,0:T(8,128)(2,1)S(1)}, u32[]{:S(2)}, u32[]{:S(2)}) collective-permute-start(bf16[2,16,1024]{2,1,0:T(8,128)(2,1)S(1)} %bitcast.194), channel_id=1, source_target_pairs={{0,30},{2,0},{4,2},{6,4},{8,6},{10,8},{12,10},{14,12},{16,14},{18,... | collective-permute-start | bytes 196616 | tf_op jit(solution)/shard_map/ppermute | solution.py:41
  199.6 6.4 %collective-permute-start.38 = (bf16[2,16,1024]{2,1,0:T(8,128)(2,1)S(1)}, bf16[2,16,1024]{2,1,0:T(8,128)(2,1)S(1)}, u32[]{:S(2)}, u32[]{:S(2)}) collective-permute-start(bf16[2,16,1024]{2,1,0:T(8,128)(2,1)S(1)} %bitcast.193), channel_id=1, source_target_pairs={{0,28},{2,30},{4,0},{6,2},{8,4},{10,6},{12,8},{14,10},{16,12},{18,... | collective-permute-start | bytes 196616 | tf_op jit(solution)/shard_map/ppermute | solution.py:41
  201.0 7.9 %collective-permute-start.39 = (bf16[2,16,1024]{2,1,0:T(8,128)(2,1)S(1)}, bf16[2,16,1024]{2,1,0:T(8,128)(2,1)S(1)}, u32[]{:S(2)}, u32[]{:S(2)}) collective-permute-start(bf16[2,16,1024]{2,1,0:T(8,128)(2,1)S(1)} %bitcast.184), channel_id=1, source_target_pairs={{0,26},{2,28},{4,30},{6,0},{8,2},{10,4},{12,6},{14,8},{16,10},{18,... | collective-permute-start | bytes 196616 | tf_op jit(solution)/shard_map/ppermute | solution.py:41
  202.7 6.3 %collective-permute-start.40 = (bf16[2,16,1024]{2,1,0:T(8,128)(2,1)S(1)}, bf16[2,16,1024]{2,1,0:T(8,128)(2,1)S(1)}, u32[]{:S(2)}, u32[]{:S(2)}) collective-permute-start(bf16[2,16,1024]{2,1,0:T(8,128)(2,1)S(1)} %bitcast.186), channel_id=1, source_target_pairs={{0,24},{2,26},{4,28},{6,30},{8,0},{10,2},{12,4},{14,6},{16,8},{18,... | collective-permute-start | bytes 196616 | tf_op jit(solution)/shard_map/ppermute | solution.py:41
  204.1 5.0 %collective-permute-start.41 = (bf16[2,16,1024]{2,1,0:T(8,128)(2,1)S(1)}, bf16[2,16,1024]{2,1,0:T(8,128)(2,1)S(1)}, u32[]{:S(2)}, u32[]{:S(2)}) collective-permute-start(bf16[2,16,1024]{2,1,0:T(8,128)(2,1)S(1)} %bitcast.188), channel_id=1, source_target_pairs={{0,22},{2,24},{4,26},{6,28},{8,30},{10,0},{12,2},{14,4},{16,6},{18... | collective-permute-start | bytes 196616 | tf_op jit(solution)/shard_map/ppermute | solution.py:41
  204.2 5.0 %collective-permute-start.42 = (bf16[2,16,1024]{2,1,0:T(8,128)(2,1)S(1)}, bf16[2,16,1024]{2,1,0:T(8,128)(2,1)S(1)}, u32[]{:S(2)}, u32[]{:S(2)}) collective-permute-start(bf16[2,16,1024]{2,1,0:T(8,128)(2,1)S(1)} %bitcast.190), channel_id=1, source_target_pairs={{0,20},{2,22},{4,24},{6,26},{8,28},{10,30},{12,0},{14,2},{16,4},{1... | collective-permute-start | bytes 196616 | tf_op jit(solution)/shard_map/ppermute | solution.py:41
  206.0 9.0 %collective-permute-start.43 = (bf16[2,16,1024]{2,1,0:T(8,128)(2,1)S(1)}, bf16[2,16,1024]{2,1,0:T(8,128)(2,1)S(1)}, u32[]{:S(2)}, u32[]{:S(2)}) collective-permute-start(bf16[2,16,1024]{2,1,0:T(8,128)(2,1)S(1)} %bitcast.182), channel_id=1, source_target_pairs={{0,18},{2,20},{4,22},{6,24},{8,26},{10,28},{12,30},{14,0},{16,2},{... | collective-permute-start | bytes 196616 | tf_op jit(solution)/shard_map/ppermute | solution.py:41
  (16 other events, 105.7 us)
